TPU v7x, 32 devices: a whole 2x2x4 slice. The times are simulated.
32 devices in a mesh: wide: 16 (over z, y, x), narrow: 2 (over core).
Axes of the slice: x: 2, y: 2, z: 4, core: 2. Of those that a mesh axis runs over, the one named last changes fastest.
Arguments:
- amplitudes: bfloat16 [256, 256, 128], P('wide', 'narrow'), may hold values from -6 to 6
- send_list: int32 [16, 32], P('wide'), may hold values from 0 to 15
- tile_positions: int32 [128, 16], P('wide', 'narrow'), may hold values from 0 to 31
- integrals: bfloat16 [128, 16, 128, 128], P('wide', 'narrow'), may hold values from -0.125 to 0.125
Outputs:
- ladder: bfloat16 [128, 256, 128], P('wide', 'narrow')
All inputs are finite; a program needn't handle non-finite values.
Results may differ from a plain program's by a relative error of at most 0.001.
Values may be sent and summed in bfloat16 or wider, within the bound.
No kernel may reach another device: no remote copies, remote signals or barrier semaphores. Data moves between devices by JAX's collectives and lax.ppermute only.
A program may use at most 64 MiB of HBM per device.

v0:
```python
import jax
import jax.numpy as jnp
from jax import lax
from jax.sharding import PartitionSpec as P


def on_device(amplitudes, send_list, tile_positions, integrals):
    outgoing = amplitudes[send_list[0]]
    tiles_dev = integrals.shape[0]
    received = lax.all_to_all(outgoing, "wide", split_axis=0, concat_axis=0, tiled=True)
    start_sum = jnp.zeros((tiles_dev, received.shape[1], integrals.shape[3]), jnp.float32)
    blocks = lax.all_gather(integrals, "narrow", axis=1, tiled=True)
    places = lax.all_gather(tile_positions, "narrow", axis=1, tiled=True)
    picked = received[places]
    total = start_sum + jnp.einsum(
        "xmpt,xmts->xps", picked, blocks, preferred_element_type=jnp.float32
    )
    return total.astype(jnp.bfloat16)


def solution(mesh):
    placed = (
        P("wide", "narrow", None),
        P("wide", None),
        P("wide", "narrow"),
        P("wide", "narrow", None, None),
    )
    return jax.shard_map(
        on_device, mesh=mesh, in_specs=placed, out_specs=P("wide", "narrow", None), check_vma=False
    )
```

profile of v0, /device:TPU:0, one launch (start us, length us, event | category | flops | bytes accessed | tf_op | source)
XLA Modules:
  0.0 57.7 jit_solution(17776949622150962364)
XLA Ops:
  6.5 0.0 copy-start
  6.5 0.0 copy-start.1
  6.5 0.0 all-gather.2.cloned.1.call-start
  6.5 0.7 %all-gather.2.cloned.1.call-update = ((bf16[8,8,128,128]{3,2,1,0:T(8,128)(2,1)}), bf16[8,16,128,128]{3,2,1,0:T(8,128)(2,1)}) async-update(((), (), s32[]{:S(2)}) %all-gather.2.cloned.1.call-start, bf16[8,8,128,128]{3,2,1,0:T(8,128)(2,1)} %param.7) | async-update | bytes 8388632
  7.3 0.7 %fusion.1 = s32[32]{0:T(128)S(1)} fusion(s32[1,32]{1,0:T(1,128)} %param.5), kind=kLoop, calls=%fused_computation.8 | loop fusion | flops 96 | bytes 256 | tf_op jit(solution)/shard_map/select_n | solution.py:8
  7.9 0.0 copy-done
  7.9 1.7 %gather_fusion = bf16[32,128,128]{2,1,0:T(8,128)(2,1)} fusion(bf16[16,128,128]{2,1,0:T(8,128)(2,1)S(1)} %copy-done, s32[1024]{0:T(1024)S(1)} %pad_clamp_fusion.1), kind=kCustom, calls=%fused_computation | custom fusion | bytes 2097280 | tf_op jit(solution)/shard_map/gather | solution.py:8
  9.6 8.3 %all-to-all-start = ((bf16[32,128,128]{2,1,0:T(8,128)(2,1)}), bf16[32,128,128]{2,1,0:T(8,128)(2,1)S(1)}, u32[]{:S(2)}, u32[]{:S(2)}) async-start(bf16[32,128,128]{2,1,0:T(8,128)(2,1)} %gather_fusion), calls=%async_computation | async-start | bytes 2097152 | tf_op jit(solution)/shard_map/all_to_all | solution.py:10
  17.9 0.0 copy-done.1
  17.9 0.1 copy.5
  18.0 1.8 %all_gather.6 = s32[8,16]{0,1:T(8,128)S(1)} all-gather(s32[8,8]{0,1:T(8,128)S(1)} %copy.5), channel_id=1, replica_groups=mesh['wide'=16,'narrow'=2] {'narrow'}, dimensions={1}, use_global_device_ids=true | all-gather | bytes 768 | tf_op jit(solution)/shard_map/all_gather | solution.py:13
  19.8 0.1 copy.6
  19.8 0.1 reshape.38
  19.9 22.4 %all-to-all-done = bf16[32,128,128]{2,1,0:T(8,128)(2,1)S(1)} async-done(((bf16[32,128,128]{2,1,0:T(8,128)(2,1)}), bf16[32,128,128]{2,1,0:T(8,128)(2,1)S(1)}, u32[]{:S(2)}, u32[]{:S(2)}) %all-to-all-start) | async-done | bytes 1048608 | tf_op jit(solution)/shard_map/all_to_all | solution.py:10
  42.3 3.1 %gather_fusion.1 = bf16[128,128,128]{2,1,0:T(8,128)(2,1)} fusion(bf16[32,128,128]{2,1,0:T(8,128)(2,1)S(1)} %all-to-all-done, s32[1024]{0:T(1024)S(1)} %pad_clamp_fusion), kind=kCustom, calls=%fused_computation.1 | custom fusion | bytes 8389120 | tf_op jit(solution)/shard_map/gather | solution.py:14
  45.4 0.0 all-gather.2.cloned.1.call-done
  45.4 5.4 %fusion = bf16[8,128,128]{2,1,0:T(8,128)(2,1)} fusion(bf16[8,16,128,128]{3,2,1,0:T(8,128)(2,1)} %bitcast.12, bf16[8,16,128,128]{3,2,1,0:T(8,128)(2,1)} %all-gather.2.cloned.1.call-done), kind=kOutput, calls=%fused_computation.3 | convolution fusion | flops 537001984 | bytes 8650752 | tf_op jit(solution)/shard_map/xmpt,xmts->xps/dot_general | solution.py:15
  (3 shorter events, 0.0 us)
Async XLA Ops:
  6.5 1.4 %copy-start = (bf16[16,128,128]{2,1,0:T(8,128)(2,1)S(1)}, bf16[16,128,128]{2,1,0:T(8,128)(2,1)}, u32[]{:S(2)}) copy-start(bf16[16,128,128]{2,1,0:T(8,128)(2,1)} %param.4) | copy-start | bytes 1572868
  6.5 11.4 %copy-start.1 = (s32[8,8]{1,0:T(8,128)S(1)}, s32[8,8]{1,0:T(8,128)}, u32[]{:S(2)}) copy-start(s32[8,8]{1,0:T(8,128)} %param.6) | copy-start | bytes 772
  6.5 38.9 %all-gather.2.cloned.1.call-start = ((), (), s32[]{:S(2)}) async-start(), calls=%async_computation.1 | async-start | bytes 6291456 | tf_op jit(solution)/shard_map/all_gather | solution.py:12
  9.6 32.8 %all-to-all-start = ((bf16[32,128,128]{2,1,0:T(8,128)(2,1)}), bf16[32,128,128]{2,1,0:T(8,128)(2,1)S(1)}, u32[]{:S(2)}, u32[]{:S(2)}) async-start(bf16[32,128,128]{2,1,0:T(8,128)(2,1)} %gather_fusion), calls=%async_computation | async-start | bytes 2097152 | tf_op jit(solution)/shard_map/all_to_all | solution.py:10
Sparse Core Ops, SparseCore 0:
  8.9 16.3 all-gather.1
where the time goes:
time: 57.9 us; the launch traced here: 57.7 us
  waiting for transfers between devices  23.1 us (40%)
  between operations  13.4 us (23%)
  starting transfers between devices  8.31 us (14%)
  matrix products  5.41 us (9%)
  local copies, waits for them, and re-layouts  4.94 us (9%)
  blocking collectives  1.78 us (3%)
  other arithmetic  0.68 us (1%)
    all_to_all x1, waiting for transfers between devices, on_device(): lax.all_to_all(outgoing, 'wide', split_axis=0, concat_axis=0, tiled=True)  22.4 us
    all_to_all x1, starting transfers between devices, on_device(): lax.all_to_all(outgoing, 'wide', split_axis=0, concat_axis=0, tiled=True)  8.31 us
    dot_general x1, matrix products, on_device(): jnp.einsum('xmpt,xmts->xps', picked, blocks, preferred_element_type=jnp.f...  5.41 us
    gather x1, local copies, waits for them, and re-layouts, on_device(): picked = received[places]  3.06 us
    all_gather x1, blocking collectives, on_device(): places = lax.all_gather(tile_positions, 'narrow', axis=1, tiled=True)  1.78 us
    gather x1, local copies, waits for them, and re-layouts, on_device(): outgoing = amplitudes[send_list[0]]  1.65 us
  transfers between devices with their start and end apart: 2, of which 1 were waited for; matrix products, arithmetic and copies ran while one was open for 10% of the time, Pallas kernels for 0%

commit v1 on v0

v1 whole, which is shorter than its diff:
```python
import functools

import jax
import jax.numpy as jnp
from jax import lax
from jax.experimental import pallas as pl
from jax.experimental.pallas import tpu as pltpu
from jax.sharding import PartitionSpec as P

VMEM_LIMIT = 48 * 1024 * 1024


def pick_outgoing(send_ref, amplitudes_ref, out_ref):
    for slot in range(out_ref.shape[0]):
        out_ref[slot] = amplitudes_ref[send_ref[0, slot]]


def contract(half_count, *refs):
    places = refs[:half_count]
    received_ref = refs[half_count]
    blocks = refs[half_count + 1 : 2 * half_count + 1]
    out_ref, stage, sems = refs[2 * half_count + 1 :]
    tiles, per_half, inner, columns = blocks[0].shape
    copies = []
    for x in range(tiles):
        total = None
        for place_ref, block_ref in zip(places, blocks):
            picked = jnp.concatenate(
                [received_ref[place_ref[x, k]] for k in range(per_half)], axis=1
            )
            part = jnp.dot(
                picked,
                block_ref[x].reshape(per_half * inner, columns),
                preferred_element_type=jnp.float32,
            )
            total = part if total is None else total + part
        stage[x] = total.astype(stage.dtype)
        copy = pltpu.make_async_copy(stage.at[x], out_ref.at[x], sems.at[x])
        copy.start()
        copies.append(copy)
    for copy in copies:
        copy.wait()


def on_device(narrow, amplitudes, send_list, tile_positions, integrals):
    smem = pl.BlockSpec(memory_space=pltpu.SMEM)
    vmem = pl.BlockSpec(memory_space=pltpu.VMEM)
    params = pltpu.CompilerParams(vmem_limit_bytes=VMEM_LIMIT)
    slots = send_list.shape[1]
    tile_bytes = amplitudes.shape[1] * amplitudes.shape[2] * 2
    outgoing = pl.pallas_call(
        pick_outgoing,
        out_shape=jax.ShapeDtypeStruct((slots,) + amplitudes.shape[1:], amplitudes.dtype),
        in_specs=[smem, vmem],
        out_specs=vmem,
        compiler_params=params,
        cost_estimate=pl.CostEstimate(flops=0, bytes_accessed=2 * slots * tile_bytes, transcendentals=0),
    )(send_list, amplitudes)
    if narrow == 2:
        swap = [(0, 1), (1, 0)]
        places = [tile_positions, lax.ppermute(tile_positions, "narrow", swap)]
        blocks = [integrals, lax.ppermute(integrals, "narrow", swap)]
    else:
        places = [lax.all_gather(tile_positions, "narrow", axis=1, tiled=True)]
        blocks = [lax.all_gather(integrals, "narrow", axis=1, tiled=True)]
    received = lax.all_to_all(outgoing, "wide", split_axis=0, concat_axis=0, tiled=True)
    tiles, pairs, columns = integrals.shape[0], amplitudes.shape[1], integrals.shape[3]
    count = len(blocks)
    return pl.pallas_call(
        functools.partial(contract, count),
        out_shape=jax.ShapeDtypeStruct((tiles, pairs, columns), jnp.bfloat16),
        in_specs=[smem] * count + [vmem] * (count + 1),
        out_specs=pl.BlockSpec(memory_space=pl.ANY),
        scratch_shapes=[
            pltpu.VMEM((tiles, pairs, columns), jnp.bfloat16),
            pltpu.SemaphoreType.DMA((tiles,)),
        ],
        compiler_params=params,
    )(*places, received, *blocks)


def solution(mesh):
    placed = (
        P("wide", "narrow", None),
        P("wide", None),
        P("wide", "narrow"),
        P("wide", "narrow", None, None),
    )
    return jax.shard_map(
        functools.partial(on_device, mesh.shape["narrow"]),
        mesh=mesh,
        in_specs=placed,
        out_specs=P("wide", "narrow", None),
        check_vma=False,
    )
```

time: 57.9 us -> 40.4 us (0.70)
  between operations: 13.4 us -> 0.02 us
  matrix products: 5.41 us -> 0 us
  Pallas kernels: 0 us -> 5.13 us
  local copies, waits for them, and re-layouts: 4.94 us -> 1.88 us
  blocking collectives: 1.78 us -> 0 us
  waiting for transfers between devices: 23.1 us -> 24.6 us
  other arithmetic: 0.68 us -> 0 us
    dot_general x1 -> x0, matrix products: 5.41 us -> none  [on_device(): jnp.einsum('xmpt,xmts->xps', picked, blocks, preferred_element_type=jnp.f...]
    pallas_call x0 -> x2, Pallas kernels: none -> 5.13 us  [the longest x1 3.53 us: on_device(): pl.pallas_call(functools.partial(contract, count), out_shape=jax.ShapeDty...]
    gather x2 -> x0, local copies, waits for them, and re-layouts: 4.71 us -> none  [the longest x1 3.06 us: on_device(): picked = received[places]]
    unnamed x5 -> x8, local copies, waits for them, and re-layouts: 0.08 us -> 1.88 us
    all_gather x1 -> x0, blocking collectives: 1.78 us -> none  [on_device(): places = lax.all_gather(tile_positions, 'narrow', axis=1, tiled=True)]
    ppermute x0 -> x2, waiting for transfers between devices: none -> 1.1 us  [the longest x1 1.1 us: on_device(): places = [tile_positions, lax.ppermute(tile_positions, 'narrow', swap)]]
    all_to_all x1, waiting for transfers between devices: 22.4 us -> 23.4 us  [on_device(): lax.all_to_all(outgoing, 'wide', split_axis=0, concat_axis=0, tiled=True)]
    unnamed x1 -> x0, waiting for transfers between devices: 0.71 us -> none
  transfers between devices with their start and end apart: 2 -> 3, of which waited for: 1 -> 2; matrix products, arithmetic and copies ran while one was open for 10% -> 0% of each run, Pallas kernels for 0% -> 4%
where the time goes in v1:
time: 40.4 us; the launch traced here: 40 us
  waiting for transfers between devices  24.6 us (61%)
  starting transfers between devices  8.43 us (21%)
  Pallas kernels  5.13 us (13%)
  local copies, waits for them, and re-layouts  1.88 us (5%)
    all_to_all x1, waiting for transfers between devices, on_device(): lax.all_to_all(outgoing, 'wide', split_axis=0, concat_axis=0, tiled=True)  23.4 us
    all_to_all x1, starting transfers between devices, on_device(): lax.all_to_all(outgoing, 'wide', split_axis=0, concat_axis=0, tiled=True)  7.85 us
    pallas_call x1, Pallas kernels, on_device(): pl.pallas_call(functools.partial(contract, count), out_shape=jax.ShapeDty...  3.53 us
    unnamed x8, local copies, waits for them, and re-layouts  1.88 us
    pallas_call x1, Pallas kernels, on_device(): pl.pallas_call(pick_outgoing, out_shape=jax.ShapeDtypeStruct((slots,) + a...  1.6 us
    ppermute x1, waiting for transfers between devices, on_device(): places = [tile_positions, lax.ppermute(tile_positions, 'narrow', swap)]  1.1 us
  transfers between devices with their start and end apart: 3, of which 2 were waited for; matrix products, arithmetic and copies ran while one was open for 0% of the time, Pallas kernels for 4%

profile of v1, /device:TPU:0, one launch (start us, length us, event | category | flops | bytes accessed | tf_op | source)
XLA Modules:
  0.0 40.0 jit_solution(6783527216759573874)
XLA Ops:
  0.0 0.0 copy-start
  0.0 0.5 %collective-permute-start.1 = (bf16[8,8,128,128]{3,2,1,0:T(8,128)(2,1)}, bf16[8,8,128,128]{3,2,1,0:T(8,128)(2,1)}, u32[]{:S(2)}, u32[]{:S(2)}) collective-permute-start(bf16[8,8,128,128]{3,2,1,0:T(8,128)(2,1)} %refs_3_.1), channel_id=1, source_target_pairs={{0,1},{1,0},{2,3},{3,2},{4,5},{5,4},{6,7},{7,6},{8,9},{9,8},{10,11... | collective-permute-start | bytes 6291464 | tf_op jit(solution)/shard_map/ppermute | solution.py:62
  0.5 0.0 copy-start.1
  0.5 1.2 %copy-done.1 = bf16[16,128,128]{2,1,0:T(8,128)(2,1)S(1)} copy-done((bf16[16,128,128]{2,1,0:T(8,128)(2,1)S(1)}, bf16[16,128,128]{2,1,0:T(8,128)(2,1)}, u32[]{:S(2)}) %copy-start.1) | copy-done | bytes 524312
  1.7 0.0 copy-start.3
  1.7 0.7 %copy-done.3 = s32[1,32]{1,0:T(1,128)S(1)} copy-done((s32[1,32]{1,0:T(1,128)S(1)}, s32[1,32]{1,0:T(1,128)}, u32[]{:S(2)}) %copy-start.3) | copy-done | bytes 152
  2.3 0.0 copy-start.2
  2.3 1.6 %shard_map.46 = bf16[32,128,128]{2,1,0:T(8,128)(2,1)} custom-call(s32[1,32]{1,0:T(1,128)S(1)} %copy-done.3, bf16[16,128,128]{2,1,0:T(8,128)(2,1)S(1)} %copy-done.1), custom_call_target="tpu_custom_call" | custom-call | bytes 2097152 | tf_op jit(solution)/shard_map/pallas_call | solution.py:51
  3.9 7.9 %all-to-all-start = ((bf16[32,128,128]{2,1,0:T(8,128)(2,1)}), bf16[32,128,128]{2,1,0:T(8,128)(2,1)S(1)}, u32[]{:S(2)}, u32[]{:S(2)}) async-start(bf16[32,128,128]{2,1,0:T(8,128)(2,1)} %shard_map.46), calls=%async_computation | async-start | bytes 2097152 | tf_op jit(solution)/shard_map/all_to_all | solution.py:66
  11.8 0.0 copy-done.2
  11.8 0.1 collective-permute-start
  11.9 1.1 %collective-permute-done.refs_1_ = s32[8,8]{1,0:T(8,128)S(1)} collective-permute-done((s32[8,8]{1,0:T(8,128)S(1)}, s32[8,8]{1,0:T(8,128)S(1)}, u32[]{:S(2)}, u32[]{:S(2)}) %collective-permute-start) | collective-permute-done | bytes 288 | tf_op jit(solution)/shard_map/ppermute | solution.py:61
  13.0 23.4 %all-to-all-done.refs_2_ = bf16[32,128,128]{2,1,0:T(8,128)(2,1)S(1)} async-done(((bf16[32,128,128]{2,1,0:T(8,128)(2,1)}), bf16[32,128,128]{2,1,0:T(8,128)(2,1)S(1)}, u32[]{:S(2)}, u32[]{:S(2)}) %all-to-all-start) | async-done | bytes 1048608 | tf_op jit(solution)/shard_map/all_to_all | solution.py:66
  36.5 0.0 collective-permute-done.1.refs_4_
  36.5 0.0 copy-done
  36.5 3.5 %shard_map.47 = bf16[8,128,128]{2,1,0:T(8,128)(2,1)} custom-call(s32[8,8]{1,0:T(8,128)S(1)} %copy-done.2, s32[8,8]{1,0:T(8,128)S(1)} %collective-permute-done.refs_1_, bf16[32,128,128]{2,1,0:T(8,128)(2,1)S(1)} %all-to-all-done.refs_2_, bf16[8,8,128,128]{3,2,1,0:T(8,128)(2,1)S(1)} %copy-done, bf16[8,8,128,128]{3,2,1,0:T(8,128)(2,1)} %collective-permute-done.1.refs_4_), custom_call_target="tpu_custom_call" | custom-call | tf_op jit(solution)/shard_map/pallas_call | solution.py:69
Async XLA Ops:
  0.0 36.5 %copy-start = (bf16[8,8,128,128]{3,2,1,0:T(8,128)(2,1)S(1)}, bf16[8,8,128,128]{3,2,1,0:T(8,128)(2,1)}, u32[]{:S(2)}) copy-start(bf16[8,8,128,128]{3,2,1,0:T(8,128)(2,1)} %refs_3_.1) | copy-start | bytes 6291460
  0.0 36.5 %collective-permute-start.1 = (bf16[8,8,128,128]{3,2,1,0:T(8,128)(2,1)}, bf16[8,8,128,128]{3,2,1,0:T(8,128)(2,1)}, u32[]{:S(2)}, u32[]{:S(2)}) collective-permute-start(bf16[8,8,128,128]{3,2,1,0:T(8,128)(2,1)} %refs_3_.1), channel_id=1, source_target_pairs={{0,1},{1,0},{2,3},{3,2},{4,5},{5,4},{6,7},{7,6},{8,9},{9,8},{10,11... | collective-permute-start | bytes 6291464 | tf_op jit(solution)/shard_map/ppermute | solution.py:62
  0.5 1.2 %copy-start.1 = (bf16[16,128,128]{2,1,0:T(8,128)(2,1)S(1)}, bf16[16,128,128]{2,1,0:T(8,128)(2,1)}, u32[]{:S(2)}) copy-start(bf16[16,128,128]{2,1,0:T(8,128)(2,1)} %amplitudes_ref.1) | copy-start | bytes 1572868
  1.7 0.7 %copy-start.3 = (s32[1,32]{1,0:T(1,128)S(1)}, s32[1,32]{1,0:T(1,128)}, u32[]{:S(2)}) copy-start(s32[1,32]{1,0:T(1,128)} %send_ref.1) | copy-start | bytes 388
  2.3 9.5 %copy-start.2 = (s32[8,8]{1,0:T(8,128)S(1)}, s32[8,8]{1,0:T(8,128)}, u32[]{:S(2)}) copy-start(s32[8,8]{1,0:T(8,128)} %refs_0_.1) | copy-start | bytes 772
  3.9 32.5 %all-to-all-start = ((bf16[32,128,128]{2,1,0:T(8,128)(2,1)}), bf16[32,128,128]{2,1,0:T(8,128)(2,1)S(1)}, u32[]{:S(2)}, u32[]{:S(2)}) async-start(bf16[32,128,128]{2,1,0:T(8,128)(2,1)} %shard_map.46), calls=%async_computation | async-start | bytes 2097152 | tf_op jit(solution)/shard_map/all_to_all | solution.py:66
  11.8 1.2 %collective-permute-start = (s32[8,8]{1,0:T(8,128)S(1)}, s32[8,8]{1,0:T(8,128)S(1)}, u32[]{:S(2)}, u32[]{:S(2)}) collective-permute-start(s32[8,8]{1,0:T(8,128)S(1)} %copy-done.2), channel_id=1, source_target_pairs={{0,1},{1,0},{2,3},{3,2},{4,5},{5,4},{6,7},{7,6},{8,9},{9,8},{10,11... | collective-permute-start | bytes 776 | tf_op jit(solution)/shard_map/ppermute | solution.py:61

commit v2 on v1

v2 whole, which is shorter than its diff:
```python
import functools

import jax
import jax.numpy as jnp
from jax import lax
from jax.experimental import pallas as pl
from jax.experimental.pallas import tpu as pltpu
from jax.sharding import PartitionSpec as P

VMEM_LIMIT = 48 * 1024 * 1024
DIRECT_WIDE = 16


def pick_outgoing(partners, send_ref, amplitudes_ref, *refs):
    out_refs = refs[: len(partners)]
    sends, held, sems = refs[len(partners) :]
    fetch_sends = pltpu.make_async_copy(send_ref, sends, sems.at[0])
    fetch_tiles = pltpu.make_async_copy(amplitudes_ref, held, sems.at[1])
    fetch_sends.start()
    fetch_tiles.start()
    fetch_sends.wait()
    fetch_tiles.wait()
    me = lax.axis_index("wide")
    for partner, out_ref in zip(partners, out_refs):
        cap = out_ref.shape[0]
        for slot in range(cap):
            out_ref[slot] = held[sends[0, (me ^ partner) * cap + slot]]


def contract(partners, half_count, *refs):
    places = refs[:half_count]
    pieces = refs[half_count : half_count + len(partners)]
    blocks = refs[half_count + len(partners) : 2 * half_count + len(partners)]
    out_ref, received, stage, sems = refs[2 * half_count + len(partners) :]
    tiles, per_half, inner, columns = blocks[0].shape
    me = lax.axis_index("wide")
    for partner, piece_ref in zip(partners, pieces):
        cap = piece_ref.shape[0]
        received[pl.ds((me ^ partner) * cap, cap)] = piece_ref[...]
    copies = []
    for x in range(tiles):
        total = None
        for place_ref, block_ref in zip(places, blocks):
            picked = jnp.concatenate(
                [received[place_ref[x, k]] for k in range(per_half)], axis=1
            )
            part = jnp.dot(
                picked,
                block_ref[x].reshape(per_half * inner, columns),
                preferred_element_type=jnp.float32,
            )
            total = part if total is None else total + part
        stage[x] = total.astype(stage.dtype)
        copy = pltpu.make_async_copy(stage.at[x], out_ref.at[x], sems.at[x])
        copy.start()
        copies.append(copy)
    for copy in copies:
        copy.wait()


def on_device(wide, narrow, amplitudes, send_list, tile_positions, integrals):
    smem = pl.BlockSpec(memory_space=pltpu.SMEM)
    vmem = pl.BlockSpec(memory_space=pltpu.VMEM)
    anywhere = pl.BlockSpec(memory_space=pl.ANY)
    hbm = pl.BlockSpec(memory_space=pltpu.HBM)
    params = pltpu.CompilerParams(vmem_limit_bytes=VMEM_LIMIT)
    cap = send_list.shape[1] // wide
    pairs, columns = amplitudes.shape[1:]
    tiles = integrals.shape[0]
    piece = jax.ShapeDtypeStruct((cap, pairs, columns), amplitudes.dtype)
    partners = tuple(range(wide - 1, -1, -1))
    outgoing = pl.pallas_call(
        functools.partial(pick_outgoing, partners),
        out_shape=[piece] * wide,
        in_specs=[hbm, hbm],
        out_specs=[vmem] * wide,
        scratch_shapes=[
            pltpu.SMEM(send_list.shape, send_list.dtype),
            pltpu.VMEM(amplitudes.shape, amplitudes.dtype),
            pltpu.SemaphoreType.DMA((2,)),
        ],
        compiler_params=params,
    )(send_list, amplitudes)
    if wide <= DIRECT_WIDE:
        pieces = [
            lax.ppermute(sent, "wide", [(d, d ^ partner) for d in range(wide)]) if partner else sent
            for partner, sent in zip(partners, outgoing)
        ]
    else:
        me = lax.axis_index("wide")
        stacked = jnp.stack(outgoing[::-1])[jnp.arange(wide) ^ me]
        arrived = lax.all_to_all(stacked, "wide", split_axis=0, concat_axis=0, tiled=True)
        arrived = arrived[jnp.arange(wide) ^ me]
        pieces = [arrived[partner] for partner in partners]
    if narrow == 2:
        swap = [(0, 1), (1, 0)]
        places = [tile_positions, lax.ppermute(tile_positions, "narrow", swap)]
        blocks = [integrals, lax.ppermute(integrals, "narrow", swap)]
    else:
        places = [lax.all_gather(tile_positions, "narrow", axis=1, tiled=True)]
        blocks = [lax.all_gather(integrals, "narrow", axis=1, tiled=True)]
    count = len(blocks)
    return pl.pallas_call(
        functools.partial(contract, partners, count),
        out_shape=jax.ShapeDtypeStruct((tiles, pairs, columns), jnp.bfloat16),
        in_specs=[smem] * count + [vmem] * (count + wide),
        out_specs=anywhere,
        scratch_shapes=[
            pltpu.VMEM((cap * wide, pairs, columns), amplitudes.dtype),
            pltpu.VMEM((tiles, pairs, columns), jnp.bfloat16),
            pltpu.SemaphoreType.DMA((tiles,)),
        ],
        compiler_params=params,
    )(*places, *pieces, *blocks)


def solution(mesh):
    placed = (
        P("wide", "narrow", None),
        P("wide", None),
        P("wide", "narrow"),
        P("wide", "narrow", None, None),
    )
    return jax.shard_map(
        functools.partial(on_device, mesh.shape["wide"], mesh.shape["narrow"]),
        mesh=mesh,
        in_specs=placed,
        out_specs=P("wide", "narrow", None),
        check_vma=False,
    )
```

time: 40.4 us -> 47.5 us (1.18)
  starting transfers between devices: 8.43 us -> 28.2 us
  waiting for transfers between devices: 24.6 us -> 11.7 us
  local copies, waits for them, and re-layouts: 1.88 us -> 3.97 us
  Pallas kernels: 5.13 us -> 3.37 us
    ppermute x0 -> x15, starting transfers between devices: none -> 27.7 us  [on_device(): lax.ppermute(sent, 'wide', [(d, d ^ partner) for d in range(wide)])]
    all_to_all x1 -> x0, waiting for transfers between devices: 23.4 us -> none  [on_device(): lax.all_to_all(outgoing, 'wide', split_axis=0, concat_axis=0, tiled=True)]
    ppermute x0 -> x15, waiting for transfers between devices: none -> 10.4 us  [on_device(): lax.ppermute(sent, 'wide', [(d, d ^ partner) for d in range(wide)])]
    all_to_all x1 -> x0, starting transfers between devices: 7.85 us -> none  [on_device(): lax.all_to_all(outgoing, 'wide', split_axis=0, concat_axis=0, tiled=True)]
    unnamed x8, local copies, waits for them, and re-layouts: 1.88 us -> 3.97 us
    pallas_call x2, Pallas kernels: 5.13 us -> 3.37 us  [the longest x1 2.73 us: on_device(): pl.pallas_call(functools.partial(contract, partners, count), out_shape=ja...]
  transfers between devices with their start and end apart: 3 -> 17, of which waited for: 2 -> 8; matrix products, arithmetic and copies ran while one was open for 0% -> 0% of each run, Pallas kernels for 4% -> 1%
where the time goes in v2:
time: 47.5 us; the launch traced here: 47.3 us
  starting transfers between devices  28.2 us (59%)
  waiting for transfers between devices  11.7 us (25%)
  local copies, waits for them, and re-layouts  3.97 us (8%)
  Pallas kernels  3.37 us (7%)
    ppermute x15, starting transfers between devices, on_device(): lax.ppermute(sent, 'wide', [(d, d ^ partner) for d in range(wide)])  27.7 us
    ppermute x15, waiting for transfers between devices, on_device(): lax.ppermute(sent, 'wide', [(d, d ^ partner) for d in range(wide)])  10.4 us
    unnamed x8, local copies, waits for them, and re-layouts  3.97 us
    pallas_call x1, Pallas kernels, on_device(): pl.pallas_call(functools.partial(contract, partners, count), out_shape=ja...  2.73 us
    ppermute x1, waiting for transfers between devices, on_device(): places = [tile_positions, lax.ppermute(tile_positions, 'narrow', swap)]  1.37 us
  transfers between devices with their start and end apart: 17, of which 8 were waited for; matrix products, arithmetic and copies ran while one was open for 0% of the time, Pallas kernels for 1%

profile of v2, /device:TPU:0, one launch (start us, length us, event | category | flops | bytes accessed | tf_op | source)
XLA Modules:
  0.0 47.3 jit_solution(5746162343667162909)
XLA Ops:
  0.0 0.5 collective-permute-start.16
  0.5 0.0 copy-start.1
  0.5 1.0 %copy-done.1 = bf16[16,128,128]{2,1,0:T(8,128)(2,1)S(1)} copy-done((bf16[16,128,128]{2,1,0:T(8,128)(2,1)S(1)}, bf16[16,128,128]{2,1,0:T(8,128)(2,1)}, u32[]{:S(2)}) %copy-start.1) | copy-done | bytes 524312
  1.5 0.0 copy-start.3
  1.5 0.7 %copy-done.3 = s32[1,32]{1,0:T(1,128)S(1)} copy-done((s32[1,32]{1,0:T(1,128)S(1)}, s32[1,32]{1,0:T(1,128)}, u32[]{:S(2)}) %copy-start.3) | copy-done | bytes 152
  2.2 0.6 %shard_map.46 = (bf16[2,128,128]{2,1,0:T(8,128)(2,1)S(1)}, bf16[2,128,128]{2,1,0:T(8,128)(2,1)S(1)}, bf16[2,128,128]{2,1,0:T(8,128)(2,1)S(1)}, bf16[2,128,128]{2...) custom-call(s32[1,32]{1,0:T(1,128)S(1)} %copy-done.3, ...), custom_call_target="tpu_custom_call" | custom-call | tf_op jit(solution)/shard_map/pallas_call | solution.py:72
  2.8 6.5 %collective-permute-start.1 = (bf16[2,128,128]{2,1,0:T(8,128)(2,1)S(1)}, bf16[2,128,128]{2,1,0:T(8,128)(2,1)S(1)}, u32[]{:S(2)}, u32[]{:S(2)}) collective-permute-start(bf16[2,128,128]{2,1,0:T(8,128)(2,1)S(1)} %get-tuple-element.21), channel_id=1, source_target_pairs={{0,30},{2,28},{4,26},{6,24},{8,22},{10,20},{12,18},{14,16},{16,14}... | collective-permute-start | bytes 196616 | tf_op jit(solution)/shard_map/ppermute | solution.py:86
  9.3 0.2 collective-permute-start.2
  9.5 3.6 %collective-permute-start.3 = (bf16[2,128,128]{2,1,0:T(8,128)(2,1)S(1)}, bf16[2,128,128]{2,1,0:T(8,128)(2,1)S(1)}, u32[]{:S(2)}, u32[]{:S(2)}) collective-permute-start(bf16[2,128,128]{2,1,0:T(8,128)(2,1)S(1)} %get-tuple-element.23), channel_id=1, source_target_pairs={{0,26},{2,24},{4,30},{6,28},{8,18},{10,16},{12,22},{14,20},{16,10}... | collective-permute-start | bytes 196616 | tf_op jit(solution)/shard_map/ppermute | solution.py:86
  13.1 0.0 collective-permute-start
  13.1 1.4 %collective-permute-done.refs_1_ = s32[8,8]{1,0:T(8,128)S(1)} collective-permute-done((s32[8,8]{1,0:T(8,128)}, s32[8,8]{1,0:T(8,128)S(1)}, u32[]{:S(2)}, u32[]{:S(2)}) %collective-permute-start) | collective-permute-done | bytes 288 | tf_op jit(solution)/shard_map/ppermute | solution.py:97
  14.5 0.2 collective-permute-start.4
  14.6 0.0 collective-permute-done.1.refs_2_
  14.6 0.9 %collective-permute-start.5 = (bf16[2,128,128]{2,1,0:T(8,128)(2,1)S(1)}, bf16[2,128,128]{2,1,0:T(8,128)(2,1)S(1)}, u32[]{:S(2)}, u32[]{:S(2)}) collective-permute-start(bf16[2,128,128]{2,1,0:T(8,128)(2,1)S(1)} %get-tuple-element.25), channel_id=1, source_target_pairs={{0,22},{2,20},{4,18},{6,16},{8,30},{10,28},{12,26},{14,24},{16,6},... | collective-permute-start | bytes 196616 | tf_op jit(solution)/shard_map/ppermute | solution.py:86
  15.6 1.5 %collective-permute-done.2.refs_3_ = bf16[2,128,128]{2,1,0:T(8,128)(2,1)S(1)} collective-permute-done((bf16[2,128,128]{2,1,0:T(8,128)(2,1)S(1)}, bf16[2,128,128]{2,1,0:T(8,128)(2,1)S(1)}, u32[]{:S(2)}, u32[]{:S(2)}) %collective-permute-start.2) | collective-permute-done | bytes 65568 | tf_op jit(solution)/shard_map/ppermute | solution.py:86
  17.1 5.6 %collective-permute-start.6 = (bf16[2,128,128]{2,1,0:T(8,128)(2,1)S(1)}, bf16[2,128,128]{2,1,0:T(8,128)(2,1)S(1)}, u32[]{:S(2)}, u32[]{:S(2)}) collective-permute-start(bf16[2,128,128]{2,1,0:T(8,128)(2,1)S(1)} %get-tuple-element.26), channel_id=1, source_target_pairs={{0,20},{2,22},{4,16},{6,18},{8,28},{10,30},{12,24},{14,26},{16,4},... | collective-permute-start | bytes 196616 | tf_op jit(solution)/shard_map/ppermute | solution.py:86
  22.7 0.0 collective-permute-done.3.refs_4_
  22.7 2.0 %collective-permute-start.7 = (bf16[2,128,128]{2,1,0:T(8,128)(2,1)S(1)}, bf16[2,128,128]{2,1,0:T(8,128)(2,1)S(1)}, u32[]{:S(2)}, u32[]{:S(2)}) collective-permute-start(bf16[2,128,128]{2,1,0:T(8,128)(2,1)S(1)} %get-tuple-element.27), channel_id=1, source_target_pairs={{0,18},{2,16},{4,22},{6,20},{8,26},{10,24},{12,30},{14,28},{16,2},... | collective-permute-start | bytes 196616 | tf_op jit(solution)/shard_map/ppermute | solution.py:86
  24.7 0.0 collective-permute-done.4.refs_5_
  24.7 0.5 %collective-permute-start.8 = (bf16[2,128,128]{2,1,0:T(8,128)(2,1)S(1)}, bf16[2,128,128]{2,1,0:T(8,128)(2,1)S(1)}, u32[]{:S(2)}, u32[]{:S(2)}) collective-permute-start(bf16[2,128,128]{2,1,0:T(8,128)(2,1)S(1)} %get-tuple-element.28), channel_id=1, source_target_pairs={{0,16},{2,18},{4,20},{6,22},{8,24},{10,26},{12,28},{14,30},{16,0},... | collective-permute-start | bytes 196616 | tf_op jit(solution)/shard_map/ppermute | solution.py:86
  25.2 3.6 %collective-permute-done.5.refs_6_ = bf16[2,128,128]{2,1,0:T(8,128)(2,1)S(1)} collective-permute-done((bf16[2,128,128]{2,1,0:T(8,128)(2,1)S(1)}, bf16[2,128,128]{2,1,0:T(8,128)(2,1)S(1)}, u32[]{:S(2)}, u32[]{:S(2)}) %collective-permute-start.5) | collective-permute-done | bytes 65568 | tf_op jit(solution)/shard_map/ppermute | solution.py:86
  28.7 0.0 collective-permute-start.9
  28.7 1.3 %collective-permute-done.6.refs_7_ = bf16[2,128,128]{2,1,0:T(8,128)(2,1)S(1)} collective-permute-done((bf16[2,128,128]{2,1,0:T(8,128)(2,1)S(1)}, bf16[2,128,128]{2,1,0:T(8,128)(2,1)S(1)}, u32[]{:S(2)}, u32[]{:S(2)}) %collective-permute-start.6) | collective-permute-done | bytes 65568 | tf_op jit(solution)/shard_map/ppermute | solution.py:86
  30.1 1.6 %collective-permute-start.10 = (bf16[2,128,128]{2,1,0:T(8,128)(2,1)S(1)}, bf16[2,128,128]{2,1,0:T(8,128)(2,1)S(1)}, u32[]{:S(2)}, u32[]{:S(2)}) collective-permute-start(bf16[2,128,128]{2,1,0:T(8,128)(2,1)S(1)} %get-tuple-element.30), channel_id=1, source_target_pairs={{0,12},{2,14},{4,8},{6,10},{8,4},{10,6},{12,0},{14,2},{16,28},{18,... | collective-permute-start | bytes 196616 | tf_op jit(solution)/shard_map/ppermute | solution.py:86
  31.6 0.0 collective-permute-done.7.refs_8_
  31.6 1.2 %collective-permute-start.11 = (bf16[2,128,128]{2,1,0:T(8,128)(2,1)S(1)}, bf16[2,128,128]{2,1,0:T(8,128)(2,1)S(1)}, u32[]{:S(2)}, u32[]{:S(2)}) collective-permute-start(bf16[2,128,128]{2,1,0:T(8,128)(2,1)S(1)} %get-tuple-element.31), channel_id=1, source_target_pairs={{0,10},{2,8},{4,14},{6,12},{8,2},{10,0},{12,6},{14,4},{16,26},{18,... | collective-permute-start | bytes 196616 | tf_op jit(solution)/shard_map/ppermute | solution.py:86
  32.8 0.0 collective-permute-done.8.refs_9_
  32.8 1.8 %collective-permute-start.12 = (bf16[2,128,128]{2,1,0:T(8,128)(2,1)S(1)}, bf16[2,128,128]{2,1,0:T(8,128)(2,1)S(1)}, u32[]{:S(2)}, u32[]{:S(2)}) collective-permute-start(bf16[2,128,128]{2,1,0:T(8,128)(2,1)S(1)} %get-tuple-element.32), channel_id=1, source_target_pairs={{0,8},{2,10},{4,12},{6,14},{8,0},{10,2},{12,4},{14,6},{16,24},{18,... | collective-permute-start | bytes 196616 | tf_op jit(solution)/shard_map/ppermute | solution.py:86
  34.6 0.7 %collective-permute-done.9.refs_10_ = bf16[2,128,128]{2,1,0:T(8,128)(2,1)S(1)} collective-permute-done((bf16[2,128,128]{2,1,0:T(8,128)(2,1)S(1)}, bf16[2,128,128]{2,1,0:T(8,128)(2,1)S(1)}, u32[]{:S(2)}, u32[]{:S(2)}) %collective-permute-start.9) | collective-permute-done | bytes 65568 | tf_op jit(solution)/shard_map/ppermute | solution.py:86
  35.3 2.3 %collective-permute-start.13 = (bf16[2,128,128]{2,1,0:T(8,128)(2,1)S(1)}, bf16[2,128,128]{2,1,0:T(8,128)(2,1)S(1)}, u32[]{:S(2)}, u32[]{:S(2)}) collective-permute-start(bf16[2,128,128]{2,1,0:T(8,128)(2,1)S(1)} %get-tuple-element.33), channel_id=1, source_target_pairs={{0,6},{2,4},{4,2},{6,0},{8,14},{10,12},{12,10},{14,8},{16,22},{18,... | collective-permute-start | bytes 196616 | tf_op jit(solution)/shard_map/ppermute | solution.py:86
  37.6 0.0 collective-permute-done.10.refs_11_
  37.6 0.4 collective-permute-start.14
  38.0 0.0 collective-permute-done.11.refs_12_
  38.0 1.0 %collective-permute-start.15 = (bf16[2,128,128]{2,1,0:T(8,128)(2,1)S(1)}, bf16[2,128,128]{2,1,0:T(8,128)(2,1)S(1)}, u32[]{:S(2)}, u32[]{:S(2)}) collective-permute-start(bf16[2,128,128]{2,1,0:T(8,128)(2,1)S(1)} %get-tuple-element.35), channel_id=1, source_target_pairs={{0,2},{2,0},{4,6},{6,4},{8,10},{10,8},{12,14},{14,12},{16,18},{18,... | collective-permute-start | bytes 196616 | tf_op jit(solution)/shard_map/ppermute | solution.py:86
  39.0 0.0 collective-permute-done.12.refs_13_
  39.0 1.4 %collective-permute-done.13.refs_14_ = bf16[2,128,128]{2,1,0:T(8,128)(2,1)S(1)} collective-permute-done((bf16[2,128,128]{2,1,0:T(8,128)(2,1)S(1)}, bf16[2,128,128]{2,1,0:T(8,128)(2,1)S(1)}, u32[]{:S(2)}, u32[]{:S(2)}) %collective-permute-start.13) | collective-permute-done | bytes 65568 | tf_op jit(solution)/shard_map/ppermute | solution.py:86
  40.4 1.5 %collective-permute-done.14.refs_15_ = bf16[2,128,128]{2,1,0:T(8,128)(2,1)S(1)} collective-permute-done((bf16[2,128,128]{2,1,0:T(8,128)(2,1)S(1)}, bf16[2,128,128]{2,1,0:T(8,128)(2,1)S(1)}, u32[]{:S(2)}, u32[]{:S(2)}) %collective-permute-start.14) | collective-permute-done | bytes 65568 | tf_op jit(solution)/shard_map/ppermute | solution.py:86
  41.9 0.4 collective-permute-done.15.refs_16_
  42.3 0.0 collective-permute-done.16.refs_19_
  42.3 0.0 copy-start
  42.3 1.6 %copy-done = bf16[8,8,128,128]{3,2,1,0:T(8,128)(2,1)S(1)} copy-done((bf16[8,8,128,128]{3,2,1,0:T(8,128)(2,1)S(1)}, bf16[8,8,128,128]{3,2,1,0:T(8,128)(2,1)}, u32[]{:S(2)}) %copy-start) | copy-done | bytes 2097176
  43.9 0.0 copy-start.2
  43.9 0.7 %copy-done.2 = s32[8,8]{1,0:T(8,128)S(1)} copy-done((s32[8,8]{1,0:T(8,128)S(1)}, s32[8,8]{1,0:T(8,128)}, u32[]{:S(2)}) %copy-start.2) | copy-done | bytes 280
  44.6 2.7 %shard_map.47 = bf16[8,128,128]{2,1,0:T(8,128)(2,1)} custom-call(s32[8,8]{1,0:T(8,128)S(1)} %copy-done.2, s32[8,8]{1,0:T(8,128)S(1)} %collective-permute-done.refs_1_, bf16[2,128,128]{2,1,0:T(8,128)(2,1)S(1)} %collective-permute-done.1.refs_2_, bf16[2,128,128]{2,1,0:T(8,128)(2,1)S(1)} %collective-permute-done.2.refs_3_, ...), custom_call_target="tpu_custom_call" | custom-call | tf_op jit(solution)/shard_map/pallas_call | solution.py:103
Async XLA Ops:
  0.0 42.3 %collective-permute-start.16 = (bf16[8,8,128,128]{3,2,1,0:T(8,128)(2,1)}, bf16[8,8,128,128]{3,2,1,0:T(8,128)(2,1)S(1)}, u32[]{:S(2)}, u32[]{:S(2)}) collective-permute-start(bf16[8,8,128,128]{3,2,1,0:T(8,128)(2,1)} %refs_18_.1), channel_id=1, source_target_pairs={{0,1},{1,0},{2,3},{3,2},{4,5},{5,4},{6,7},{7,6},{8,9},{9,8},{10,11... | collective-permute-start | bytes 6291464 | tf_op jit(solution)/shard_map/ppermute | solution.py:98
  0.5 1.0 %copy-start.1 = (bf16[16,128,128]{2,1,0:T(8,128)(2,1)S(1)}, bf16[16,128,128]{2,1,0:T(8,128)(2,1)}, u32[]{:S(2)}) copy-start(bf16[16,128,128]{2,1,0:T(8,128)(2,1)} %amplitudes_ref.1) | copy-start | bytes 1572868
  1.5 0.7 %copy-start.3 = (s32[1,32]{1,0:T(1,128)S(1)}, s32[1,32]{1,0:T(1,128)}, u32[]{:S(2)}) copy-start(s32[1,32]{1,0:T(1,128)} %send_ref.1) | copy-start | bytes 388
  2.8 11.8 %collective-permute-start.1 = (bf16[2,128,128]{2,1,0:T(8,128)(2,1)S(1)}, bf16[2,128,128]{2,1,0:T(8,128)(2,1)S(1)}, u32[]{:S(2)}, u32[]{:S(2)}) collective-permute-start(bf16[2,128,128]{2,1,0:T(8,128)(2,1)S(1)} %get-tuple-element.21), channel_id=1, source_target_pairs={{0,30},{2,28},{4,26},{6,24},{8,22},{10,20},{12,18},{14,16},{16,14}... | collective-permute-start | bytes 196616 | tf_op jit(solution)/shard_map/ppermute | solution.py:86
  9.3 7.7 %collective-permute-start.2 = (bf16[2,128,128]{2,1,0:T(8,128)(2,1)S(1)}, bf16[2,128,128]{2,1,0:T(8,128)(2,1)S(1)}, u32[]{:S(2)}, u32[]{:S(2)}) collective-permute-start(bf16[2,128,128]{2,1,0:T(8,128)(2,1)S(1)} %get-tuple-element.22), channel_id=1, source_target_pairs={{0,28},{2,30},{4,24},{6,26},{8,20},{10,22},{12,16},{14,18},{16,12}... | collective-permute-start | bytes 196616 | tf_op jit(solution)/shard_map/ppermute | solution.py:86
  9.5 13.1 %collective-permute-start.3 = (bf16[2,128,128]{2,1,0:T(8,128)(2,1)S(1)}, bf16[2,128,128]{2,1,0:T(8,128)(2,1)S(1)}, u32[]{:S(2)}, u32[]{:S(2)}) collective-permute-start(bf16[2,128,128]{2,1,0:T(8,128)(2,1)S(1)} %get-tuple-element.23), channel_id=1, source_target_pairs={{0,26},{2,24},{4,30},{6,28},{8,18},{10,16},{12,22},{14,20},{16,10}... | collective-permute-start | bytes 196616 | tf_op jit(solution)/shard_map/ppermute | solution.py:86
  13.1 1.4 %collective-permute-start = (s32[8,8]{1,0:T(8,128)}, s32[8,8]{1,0:T(8,128)S(1)}, u32[]{:S(2)}, u32[]{:S(2)}) collective-permute-start(s32[8,8]{1,0:T(8,128)} %refs_0_.1), channel_id=1, source_target_pairs={{0,1},{1,0},{2,3},{3,2},{4,5},{5,4},{6,7},{7,6},{8,9},{9,8},{10,11... | collective-permute-start | bytes 776 | tf_op jit(solution)/shard_map/ppermute | solution.py:97
  14.5 10.2 %collective-permute-start.4 = (bf16[2,128,128]{2,1,0:T(8,128)(2,1)S(1)}, bf16[2,128,128]{2,1,0:T(8,128)(2,1)S(1)}, u32[]{:S(2)}, u32[]{:S(2)}) collective-permute-start(bf16[2,128,128]{2,1,0:T(8,128)(2,1)S(1)} %get-tuple-element.24), channel_id=1, source_target_pairs={{0,24},{2,26},{4,28},{6,30},{8,16},{10,18},{12,20},{14,22},{16,8},... | collective-permute-start | bytes 196616 | tf_op jit(solution)/shard_map/ppermute | solution.py:86
  14.6 14.1 %collective-permute-start.5 = (bf16[2,128,128]{2,1,0:T(8,128)(2,1)S(1)}, bf16[2,128,128]{2,1,0:T(8,128)(2,1)S(1)}, u32[]{:S(2)}, u32[]{:S(2)}) collective-permute-start(bf16[2,128,128]{2,1,0:T(8,128)(2,1)S(1)} %get-tuple-element.25), channel_id=1, source_target_pairs={{0,22},{2,20},{4,18},{6,16},{8,30},{10,28},{12,26},{14,24},{16,6},... | collective-permute-start | bytes 196616 | tf_op jit(solution)/shard_map/ppermute | solution.py:86
  17.1 13.0 %collective-permute-start.6 = (bf16[2,128,128]{2,1,0:T(8,128)(2,1)S(1)}, bf16[2,128,128]{2,1,0:T(8,128)(2,1)S(1)}, u32[]{:S(2)}, u32[]{:S(2)}) collective-permute-start(bf16[2,128,128]{2,1,0:T(8,128)(2,1)S(1)} %get-tuple-element.26), channel_id=1, source_target_pairs={{0,20},{2,22},{4,16},{6,18},{8,28},{10,30},{12,24},{14,26},{16,4},... | collective-permute-start | bytes 196616 | tf_op jit(solution)/shard_map/ppermute | solution.py:86
  22.7 9.0 %collective-permute-start.7 = (bf16[2,128,128]{2,1,0:T(8,128)(2,1)S(1)}, bf16[2,128,128]{2,1,0:T(8,128)(2,1)S(1)}, u32[]{:S(2)}, u32[]{:S(2)}) collective-permute-start(bf16[2,128,128]{2,1,0:T(8,128)(2,1)S(1)} %get-tuple-element.27), channel_id=1, source_target_pairs={{0,18},{2,16},{4,22},{6,20},{8,26},{10,24},{12,30},{14,28},{16,2},... | collective-permute-start | bytes 196616 | tf_op jit(solution)/shard_map/ppermute | solution.py:86
  24.7 8.1 %collective-permute-start.8 = (bf16[2,128,128]{2,1,0:T(8,128)(2,1)S(1)}, bf16[2,128,128]{2,1,0:T(8,128)(2,1)S(1)}, u32[]{:S(2)}, u32[]{:S(2)}) collective-permute-start(bf16[2,128,128]{2,1,0:T(8,128)(2,1)S(1)} %get-tuple-element.28), channel_id=1, source_target_pairs={{0,16},{2,18},{4,20},{6,22},{8,24},{10,26},{12,28},{14,30},{16,0},... | collective-permute-start | bytes 196616 | tf_op jit(solution)/shard_map/ppermute | solution.py:86
  28.7 6.5 %collective-permute-start.9 = (bf16[2,128,128]{2,1,0:T(8,128)(2,1)S(1)}, bf16[2,128,128]{2,1,0:T(8,128)(2,1)S(1)}, u32[]{:S(2)}, u32[]{:S(2)}) collective-permute-start(bf16[2,128,128]{2,1,0:T(8,128)(2,1)S(1)} %get-tuple-element.29), channel_id=1, source_target_pairs={{0,14},{2,12},{4,10},{6,8},{8,6},{10,4},{12,2},{14,0},{16,30},{18,... | collective-permute-start | bytes 196616 | tf_op jit(solution)/shard_map/ppermute | solution.py:86
  30.1 7.5 %collective-permute-start.10 = (bf16[2,128,128]{2,1,0:T(8,128)(2,1)S(1)}, bf16[2,128,128]{2,1,0:T(8,128)(2,1)S(1)}, u32[]{:S(2)}, u32[]{:S(2)}) collective-permute-start(bf16[2,128,128]{2,1,0:T(8,128)(2,1)S(1)} %get-tuple-element.30), channel_id=1, source_target_pairs={{0,12},{2,14},{4,8},{6,10},{8,4},{10,6},{12,0},{14,2},{16,28},{18,... | collective-permute-start | bytes 196616 | tf_op jit(solution)/shard_map/ppermute | solution.py:86
  31.6 6.4 %collective-permute-start.11 = (bf16[2,128,128]{2,1,0:T(8,128)(2,1)S(1)}, bf16[2,128,128]{2,1,0:T(8,128)(2,1)S(1)}, u32[]{:S(2)}, u32[]{:S(2)}) collective-permute-start(bf16[2,128,128]{2,1,0:T(8,128)(2,1)S(1)} %get-tuple-element.31), channel_id=1, source_target_pairs={{0,10},{2,8},{4,14},{6,12},{8,2},{10,0},{12,6},{14,4},{16,26},{18,... | collective-permute-start | bytes 196616 | tf_op jit(solution)/shard_map/ppermute | solution.py:86
  32.8 6.2 %collective-permute-start.12 = (bf16[2,128,128]{2,1,0:T(8,128)(2,1)S(1)}, bf16[2,128,128]{2,1,0:T(8,128)(2,1)S(1)}, u32[]{:S(2)}, u32[]{:S(2)}) collective-permute-start(bf16[2,128,128]{2,1,0:T(8,128)(2,1)S(1)} %get-tuple-element.32), channel_id=1, source_target_pairs={{0,8},{2,10},{4,12},{6,14},{8,0},{10,2},{12,4},{14,6},{16,24},{18,... | collective-permute-start | bytes 196616 | tf_op jit(solution)/shard_map/ppermute | solution.py:86
  35.3 5.2 %collective-permute-start.13 = (bf16[2,128,128]{2,1,0:T(8,128)(2,1)S(1)}, bf16[2,128,128]{2,1,0:T(8,128)(2,1)S(1)}, u32[]{:S(2)}, u32[]{:S(2)}) collective-permute-start(bf16[2,128,128]{2,1,0:T(8,128)(2,1)S(1)} %get-tuple-element.33), channel_id=1, source_target_pairs={{0,6},{2,4},{4,2},{6,0},{8,14},{10,12},{12,10},{14,8},{16,22},{18,... | collective-permute-start | bytes 196616 | tf_op jit(solution)/shard_map/ppermute | solution.py:86
  37.6 4.3 %collective-permute-start.14 = (bf16[2,128,128]{2,1,0:T(8,128)(2,1)S(1)}, bf16[2,128,128]{2,1,0:T(8,128)(2,1)S(1)}, u32[]{:S(2)}, u32[]{:S(2)}) collective-permute-start(bf16[2,128,128]{2,1,0:T(8,128)(2,1)S(1)} %get-tuple-element.34), channel_id=1, source_target_pairs={{0,4},{2,6},{4,0},{6,2},{8,12},{10,14},{12,8},{14,10},{16,20},{18,... | collective-permute-start | bytes 196616 | tf_op jit(solution)/shard_map/ppermute | solution.py:86
  38.0 4.3 %collective-permute-start.15 = (bf16[2,128,128]{2,1,0:T(8,128)(2,1)S(1)}, bf16[2,128,128]{2,1,0:T(8,128)(2,1)S(1)}, u32[]{:S(2)}, u32[]{:S(2)}) collective-permute-start(bf16[2,128,128]{2,1,0:T(8,128)(2,1)S(1)} %get-tuple-element.35), channel_id=1, source_target_pairs={{0,2},{2,0},{4,6},{6,4},{8,10},{10,8},{12,14},{14,12},{16,18},{18,... | collective-permute-start | bytes 196616 | tf_op jit(solution)/shard_map/ppermute | solution.py:86
  42.3 1.6 %copy-start = (bf16[8,8,128,128]{3,2,1,0:T(8,128)(2,1)S(1)}, bf16[8,8,128,128]{3,2,1,0:T(8,128)(2,1)}, u32[]{:S(2)}) copy-start(bf16[8,8,128,128]{3,2,1,0:T(8,128)(2,1)} %refs_18_.1) | copy-start | bytes 6291460
  43.9 0.7 %copy-start.2 = (s32[8,8]{1,0:T(8,128)S(1)}, s32[8,8]{1,0:T(8,128)}, u32[]{:S(2)}) copy-start(s32[8,8]{1,0:T(8,128)} %refs_0_.1) | copy-start | bytes 772

commit v3 on v2

v3 whole, which is shorter than its diff:
```python
import functools

import jax
import jax.numpy as jnp
from jax import lax
from jax.experimental import pallas as pl
from jax.experimental.pallas import tpu as pltpu
from jax.sharding import PartitionSpec as P

VMEM_LIMIT = 48 * 1024 * 1024
SMEM = pl.BlockSpec(memory_space=pltpu.SMEM)
VMEM = pl.BlockSpec(memory_space=pltpu.VMEM)
ANYWHERE = pl.BlockSpec(memory_space=pl.ANY)
PARAMS = pltpu.CompilerParams(vmem_limit_bytes=VMEM_LIMIT)


def device_of(me, half, spot):
    return ((me // half[0] + half[1]) % 2) * half[0] + spot


def pick_outgoing(plan, near, cap, send_ref, amplitudes_ref, *refs):
    out_refs = refs[: len(plan)]
    sends, held, sems = refs[len(plan) :]
    fetch_sends = pltpu.make_async_copy(send_ref, sends, sems.at[0])
    fetch_tiles = pltpu.make_async_copy(amplitudes_ref, held, sems.at[1])
    fetch_sends.start()
    fetch_tiles.start()
    fetch_sends.wait()
    fetch_tiles.wait()
    me = lax.axis_index("wide")
    for wanted, out_ref in zip(plan, out_refs):
        for place, (half, spot, slot) in enumerate(wanted):
            out_ref[place] = held[sends[0, device_of(me, (near, half), spot) * cap + slot]]


def take_crossing(count, both_ref, out_ref):
    for spot in range(out_ref.shape[0] // count):
        out_ref[pl.ds(spot * count, count)] = both_ref[pl.ds((2 * spot + 1) * count, count)]


def join_halves(count, own_ref, crossed_ref, out_ref):
    for spot in range(own_ref.shape[0] // count):
        here = pl.ds(spot * count, count)
        out_ref[pl.ds(2 * spot * count, count)] = own_ref[here]
        out_ref[pl.ds((2 * spot + 1) * count, count)] = crossed_ref[here]


def stage_own(after_ref, places_ref, blocks_ref, places_out, blocks_out, sems):
    copies = [
        pltpu.make_async_copy(places_ref, places_out, sems.at[0]),
        pltpu.make_async_copy(blocks_ref, blocks_out, sems.at[1]),
    ]
    for copy in copies:
        copy.start()
    for copy in copies:
        copy.wait()


def contract(plan, near, cap, half_count, *refs):
    places = refs[:half_count]
    pieces = refs[half_count : half_count + len(plan)]
    blocks = refs[half_count + len(plan) : 2 * half_count + len(plan)]
    out_ref, received, stage, sems = refs[2 * half_count + len(plan) :]
    tiles, per_half, inner, columns = blocks[0].shape
    me = lax.axis_index("wide")
    for origin, piece_ref in zip(plan, pieces):
        for place, spot in origin:
            half, device, slot = spot
            received[device_of(me, (near, half), device) * cap + slot] = piece_ref[place]
    copies = []
    for x in range(tiles):
        total = None
        for place_ref, block_ref in zip(places, blocks):
            picked = jnp.concatenate(
                [received[place_ref[x, k]] for k in range(per_half)], axis=1
            )
            part = jnp.dot(
                picked,
                block_ref[x].reshape(per_half * inner, columns),
                preferred_element_type=jnp.float32,
            )
            total = part if total is None else total + part
        stage[x] = total.astype(stage.dtype)
        copy = pltpu.make_async_copy(stage.at[x], out_ref.at[x], sems.at[x])
        copy.start()
        copies.append(copy)
    for copy in copies:
        copy.wait()


def rearranged(body, shape, *arrays):
    return pl.pallas_call(
        body,
        out_shape=jax.ShapeDtypeStruct(shape, arrays[0].dtype),
        in_specs=[VMEM] * len(arrays),
        out_specs=VMEM,
        compiler_params=PARAMS,
    )(*arrays)


def on_device(wide, narrow, amplitudes, send_list, tile_positions, integrals):
    cap = send_list.shape[1] // wide
    pairs, columns = amplitudes.shape[1:]
    tiles = integrals.shape[0]
    near = wide // 2
    early, late = range(cap // 2), range(cap // 2, cap)
    groups = [list(range(near)), list(range(near, wide))]
    opposite = [(d, (d + near) % wide) for d in range(wide)]

    def cross(array):
        return lax.ppermute(array, "wide", opposite)

    def spread(array):
        return lax.all_to_all(
            array, "wide", split_axis=0, concat_axis=0, axis_index_groups=groups, tiled=True
        )

    def both(slots):
        return [(half, spot, slot) for spot in range(near) for half in (0, 1) for slot in slots]

    asked = [
        [(1, spot, slot) for spot in range(near) for slot in early],
        both(late),
        [(0, spot, slot) for spot in range(near) for slot in early],
    ]
    cross_first, spread_first, kept = pl.pallas_call(
        functools.partial(pick_outgoing, asked, near, cap),
        out_shape=[jax.ShapeDtypeStruct((len(p), pairs, columns), amplitudes.dtype) for p in asked],
        in_specs=[ANYWHERE, ANYWHERE],
        out_specs=[VMEM] * len(asked),
        scratch_shapes=[
            pltpu.SMEM(send_list.shape, send_list.dtype),
            pltpu.VMEM(amplitudes.shape, amplitudes.dtype),
            pltpu.SemaphoreType.DMA((2,)),
        ],
        compiler_params=PARAMS,
    )(send_list, amplitudes)
    tile = (pairs, columns)
    crossed = cross(cross_first)
    spread_late = spread(spread_first)
    second = rearranged(functools.partial(take_crossing, len(late)), (near * len(late),) + tile, spread_late)
    crossed_late = cross(second)
    joined = rearranged(
        functools.partial(join_halves, len(early)), (2 * near * len(early),) + tile, kept, crossed
    )
    spread_early = spread(joined)
    pieces = [spread_late, crossed_late, spread_early]
    plan = [
        [(i, place) for i, place in enumerate(both(late)) if place[0] == 0],
        list(enumerate((1, spot, slot) for spot in range(near) for slot in late)),
        list(enumerate(both(early))),
    ]
    tied, started = lax.optimization_barrier((integrals, second))
    staged = pl.pallas_call(
        stage_own,
        out_shape=[
            jax.ShapeDtypeStruct(tile_positions.shape, tile_positions.dtype),
            jax.ShapeDtypeStruct(integrals.shape, integrals.dtype),
        ],
        in_specs=[ANYWHERE] * 3,
        out_specs=[VMEM, VMEM],
        scratch_shapes=[pltpu.SemaphoreType.DMA((2,))],
        compiler_params=PARAMS,
        cost_estimate=pl.CostEstimate(flops=0, bytes_accessed=2 * integrals.size * 2, transcendentals=0),
    )
    if narrow == 2:
        swap = [(0, 1), (1, 0)]
        own_places, own_blocks = staged(started, tile_positions, tied)
        places = [own_places, lax.ppermute(tile_positions, "narrow", swap)]
        blocks = [own_blocks, lax.ppermute(tied, "narrow", swap)]
    else:
        places = [lax.all_gather(tile_positions, "narrow", axis=1, tiled=True)]
        blocks = [lax.all_gather(tied, "narrow", axis=1, tiled=True)]
    count = len(blocks)
    return pl.pallas_call(
        functools.partial(contract, plan, near, cap, count),
        out_shape=jax.ShapeDtypeStruct((tiles, pairs, columns), jnp.bfloat16),
        in_specs=[SMEM] * count + [VMEM] * (count + len(pieces)),
        out_specs=ANYWHERE,
        scratch_shapes=[
            pltpu.VMEM((cap * wide, pairs, columns), amplitudes.dtype),
            pltpu.VMEM((tiles, pairs, columns), jnp.bfloat16),
            pltpu.SemaphoreType.DMA((tiles,)),
        ],
        compiler_params=PARAMS,
    )(*places, *pieces, *blocks)


def solution(mesh):
    placed = (
        P("wide", "narrow", None),
        P("wide", None),
        P("wide", "narrow"),
        P("wide", "narrow", None, None),
    )
    return jax.shard_map(
        functools.partial(on_device, mesh.shape["wide"], mesh.shape["narrow"]),
        mesh=mesh,
        in_specs=placed,
        out_specs=P("wide", "narrow", None),
        check_vma=False,
    )
```

time: 47.5 us -> 58.7 us (1.24)
  starting transfers between devices: 28.2 us -> 7.5 us
  blocking collectives: 0 us -> 15.4 us
  waiting for transfers between devices: 11.7 us -> 23.6 us
  local copies, waits for them, and re-layouts: 3.97 us -> 6.41 us
  Pallas kernels: 3.37 us -> 5.3 us
    ppermute x17 -> x4, starting transfers between devices: 28.2 us -> 4.01 us  [the longest x2 3.93 us: cross(): return lax.ppermute(array, 'wide', opposite)]
    all_to_all x0 -> x1, blocking collectives: none -> 15.4 us  [spread(): lax.all_to_all(array, 'wide', split_axis=0, concat_axis=0, axis_index_gro...]
    ppermute x17 -> x4, waiting for transfers between devices: 11.7 us -> 21.4 us  [the longest x2 21.4 us: cross(): return lax.ppermute(array, 'wide', opposite)]
    all_to_all x0 -> x1, starting transfers between devices: none -> 3.49 us  [spread(): lax.all_to_all(array, 'wide', split_axis=0, concat_axis=0, axis_index_gro...]
    unnamed x8 -> x16, local copies, waits for them, and re-layouts: 3.97 us -> 6.41 us
    all_to_all x0 -> x1, waiting for transfers between devices: none -> 2.27 us  [spread(): lax.all_to_all(array, 'wide', split_axis=0, concat_axis=0, axis_index_gro...]
    pallas_call x2 -> x5, Pallas kernels: 3.37 us -> 5.3 us  [the longest x1 3.64 us: on_device(): pl.pallas_call(functools.partial(contract, plan, near, cap, count), out_s...]
  transfers between devices with their start and end apart: 17 -> 5, of which waited for: 8 -> 3; matrix products, arithmetic and copies ran while one was open for 0% -> 0% of each run, Pallas kernels for 1% -> 2%
where the time goes in v3:
time: 58.7 us; the launch traced here: 58.3 us
  waiting for transfers between devices  23.6 us (40%)
  blocking collectives  15.4 us (26%)
  starting transfers between devices  7.5 us (13%)
  local copies, waits for them, and re-layouts  6.41 us (11%)
  Pallas kernels  5.3 us (9%)
    ppermute x2, waiting for transfers between devices, cross(): return lax.ppermute(array, 'wide', opposite)  21.4 us
    all_to_all x1, blocking collectives, spread(): lax.all_to_all(array, 'wide', split_axis=0, concat_axis=0, axis_index_gro...  15.4 us
    unnamed x16, local copies, waits for them, and re-layouts  6.41 us
    ppermute x2, starting transfers between devices, cross(): return lax.ppermute(array, 'wide', opposite)  3.93 us
    pallas_call x1, Pallas kernels, on_device(): pl.pallas_call(functools.partial(contract, plan, near, cap, count), out_s...  3.64 us
    all_to_all x1, starting transfers between devices, spread(): lax.all_to_all(array, 'wide', split_axis=0, concat_axis=0, axis_index_gro...  3.49 us
    all_to_all x1, waiting for transfers between devices, spread(): lax.all_to_all(array, 'wide', split_axis=0, concat_axis=0, axis_index_gro...  2.27 us
  transfers between devices with their start and end apart: 5, of which 3 were waited for; matrix products, arithmetic and copies ran while one was open for 0% of the time, Pallas kernels for 2%

profile of v3, /device:TPU:0, one launch (start us, length us, event | category | flops | bytes accessed | tf_op | source)
XLA Modules:
  0.0 58.3 jit_solution(8680860131664048168)
XLA Ops:
  0.0 0.0 copy-start
  0.0 0.0 copy-start.3
  0.0 1.2 %copy-done.3 = bf16[16,128,128]{2,1,0:T(8,128)(2,1)S(1)} copy-done((bf16[16,128,128]{2,1,0:T(8,128)(2,1)S(1)}, bf16[16,128,128]{2,1,0:T(8,128)(2,1)}, u32[]{:S(2)}) %copy-start.3) | copy-done | bytes 524312
  1.2 0.0 copy-start.7
  1.2 0.7 %copy-done.7 = s32[1,32]{1,0:T(1,128)S(1)} copy-done((s32[1,32]{1,0:T(1,128)S(1)}, s32[1,32]{1,0:T(1,128)}, u32[]{:S(2)}) %copy-start.7) | copy-done | bytes 152
  1.9 0.6 %shard_map.46 = (bf16[8,128,128]{2,1,0:T(8,128)(2,1)S(1)}, bf16[16,128,128]{2,1,0:T(8,128)(2,1)S(1)}, bf16[8,128,128]{2,1,0:T(8,128)(2,1)S(1)}) custom-call(s32[1,32]{1,0:T(1,128)S(1)} %copy-done.7, bf16[16,128,128]{2,1,0:T(8,128)(2,1)S(1)} %copy-done.3), custom_call_target="tpu_custom_call" | custom-call | tf_op jit(solution)/shard_map/pallas_call | solution.py:126
  2.5 0.0 copy-start.6
  2.5 15.4 %all_to_all.10.both_ref.refs_2_ = bf16[16,128,128]{2,1,0:T(8,128)(2,1)S(1)} all-to-all(bf16[16,128,128]{2,1,0:T(8,128)(2,1)S(1)} %get-tuple-element.12), channel_id=1, replica_groups={{0,2,4,6,8,10,12,14},{16,18,20,22,24,26,28,30},{1,3,5,7,9,11,13,15},{17..., dimensions={0} | all-to-all | bytes 1048576 | tf_op jit(solution)/shard_map/all_to_all | solution.py:114
  17.9 0.0 copy-done
  18.0 0.1 collective-permute-start.3
  18.0 2.7 %collective-permute-start.2 = (bf16[8,128,128]{2,1,0:T(8,128)(2,1)S(1)}, bf16[8,128,128]{2,1,0:T(8,128)(2,1)S(1)}, u32[]{:S(2)}, u32[]{:S(2)}) collective-permute-start(bf16[8,128,128]{2,1,0:T(8,128)(2,1)S(1)} %get-tuple-element.17), channel_id=1, source_target_pairs={{0,16},{2,18},{4,20},{6,22},{8,24},{10,26},{12,28},{14,30},{16,0},... | collective-permute-start | bytes 786440 | tf_op jit(solution)/shard_map/ppermute | solution.py:111
  20.7 12.6 %collective-permute-done.2.crossed_ref = bf16[8,128,128]{2,1,0:T(8,128)(2,1)S(1)} collective-permute-done((bf16[8,128,128]{2,1,0:T(8,128)(2,1)S(1)}, bf16[8,128,128]{2,1,0:T(8,128)(2,1)S(1)}, u32[]{:S(2)}, u32[]{:S(2)}) %collective-permute-start.2) | collective-permute-done | bytes 262176 | tf_op jit(solution)/shard_map/ppermute | solution.py:111
  33.3 0.8 %shard_map.49 = bf16[16,128,128]{2,1,0:T(8,128)(2,1)} custom-call(bf16[8,128,128]{2,1,0:T(8,128)(2,1)S(1)} %get-tuple-element.16.own_ref, bf16[8,128,128]{2,1,0:T(8,128)(2,1)S(1)} %collective-permute-done.2.crossed_ref), custom_call_target="tpu_custom_call" | custom-call | tf_op jit(solution)/shard_map/pallas_call | solution.py:92
  34.1 3.5 %all-to-all-start.1 = ((bf16[16,128,128]{2,1,0:T(8,128)(2,1)}), bf16[16,128,128]{2,1,0:T(8,128)(2,1)S(1)}, u32[]{:S(2)}, u32[]{:S(2)}) async-start(bf16[16,128,128]{2,1,0:T(8,128)(2,1)} %shard_map.49), calls=%async_computation.1 | async-start | bytes 1048576 | tf_op jit(solution)/shard_map/all_to_all | solution.py:114
  37.6 1.3 %collective-permute-start.1 = (bf16[8,128,128]{2,1,0:T(8,128)(2,1)S(1)}, bf16[8,128,128]{2,1,0:T(8,128)(2,1)S(1)}, u32[]{:S(2)}, u32[]{:S(2)}) collective-permute-start(bf16[8,128,128]{2,1,0:T(8,128)(2,1)S(1)} %shard_map.47.after_ref), channel_id=1, source_target_pairs={{0,16},{2,18},{4,20},{6,22},{8,24},{10,26},{12,28},{14,30},{16,0},... | collective-permute-start | bytes 786440 | tf_op jit(solution)/shard_map/ppermute | solution.py:111
  38.9 0.0 copy-done.6
  38.9 0.0 collective-permute-start
  38.9 0.2 shard_map.48
  39.1 0.0 copy-start.1
  39.1 1.3 %copy-done.1 = bf16[8,8,128,128]{3,2,1,0:T(8,128)(2,1)} copy-done((bf16[8,8,128,128]{3,2,1,0:T(8,128)(2,1)}, bf16[8,8,128,128]{3,2,1,0:T(8,128)(2,1)S(1)}, u32[]{:S(2)}) %copy-start.1) | copy-done | bytes 2097176
  40.4 0.0 collective-permute-done.refs_1_
  40.4 8.8 %collective-permute-done.1.refs_3_ = bf16[8,128,128]{2,1,0:T(8,128)(2,1)S(1)} collective-permute-done((bf16[8,128,128]{2,1,0:T(8,128)(2,1)S(1)}, bf16[8,128,128]{2,1,0:T(8,128)(2,1)S(1)}, u32[]{:S(2)}, u32[]{:S(2)}) %collective-permute-start.1) | collective-permute-done | bytes 262176 | tf_op jit(solution)/shard_map/ppermute | solution.py:111
  49.2 0.0 copy-start.4
  49.2 0.7 %copy-done.4 = bf16[8,128,128]{2,1,0:T(8,128)(2,1)} copy-done((bf16[8,128,128]{2,1,0:T(8,128)(2,1)}, bf16[8,128,128]{2,1,0:T(8,128)(2,1)S(1)}, u32[]{:S(2)}) %copy-start.4) | copy-done | bytes 262168
  49.9 2.3 %all-to-all-done.1.refs_4_ = bf16[16,128,128]{2,1,0:T(8,128)(2,1)S(1)} async-done(((bf16[16,128,128]{2,1,0:T(8,128)(2,1)}), bf16[16,128,128]{2,1,0:T(8,128)(2,1)S(1)}, u32[]{:S(2)}, u32[]{:S(2)}) %all-to-all-start.1) | async-done | bytes 524320 | tf_op jit(solution)/shard_map/all_to_all | solution.py:114
  52.1 0.0 collective-permute-done.3.refs_6_
  52.1 0.0 copy-start.2
  52.1 1.6 %copy-done.2 = bf16[8,8,128,128]{3,2,1,0:T(8,128)(2,1)S(1)} copy-done((bf16[8,8,128,128]{3,2,1,0:T(8,128)(2,1)S(1)}, bf16[8,8,128,128]{3,2,1,0:T(8,128)(2,1)}, u32[]{:S(2)}) %copy-start.2) | copy-done | bytes 2097176
  53.7 0.0 copy-start.5
  53.7 0.9 %copy-done.5 = bf16[8,128,128]{2,1,0:T(8,128)(2,1)S(1)} copy-done((bf16[8,128,128]{2,1,0:T(8,128)(2,1)S(1)}, bf16[8,128,128]{2,1,0:T(8,128)(2,1)}, u32[]{:S(2)}) %copy-start.5) | copy-done | bytes 262168
  54.7 3.6 %shard_map.50 = bf16[8,128,128]{2,1,0:T(8,128)(2,1)} custom-call(s32[8,8]{1,0:T(8,128)S(1)} %get-tuple-element.15.refs_0_, s32[8,8]{1,0:T(8,128)S(1)} %collective-permute-done.refs_1_, bf16[16,128,128]{2,1,0:T(8,128)(2,1)S(1)} %all_to_all.10.both_ref.refs_2_, bf16[8,128,128]{2,1,0:T(8,128)(2,1)S(1)} %copy-done.5, ...), custom_call_target="tpu_custom_call" | custom-call | tf_op jit(solution)/shard_map/pallas_call | solution.py:175
  (1 shorter events, 0.0 us)
Async XLA Ops:
  0.0 17.9 %copy-start = (bf16[8,8,128,128]{3,2,1,0:T(8,128)(2,1)S(1)}, bf16[8,8,128,128]{3,2,1,0:T(8,128)(2,1)}, u32[]{:S(2)}) copy-start(bf16[8,8,128,128]{3,2,1,0:T(8,128)(2,1)} %blocks_ref) | copy-start | bytes 6291460
  0.0 1.2 %copy-start.3 = (bf16[16,128,128]{2,1,0:T(8,128)(2,1)S(1)}, bf16[16,128,128]{2,1,0:T(8,128)(2,1)}, u32[]{:S(2)}) copy-start(bf16[16,128,128]{2,1,0:T(8,128)(2,1)} %amplitudes_ref.1) | copy-start | bytes 1572868
  1.2 0.7 %copy-start.7 = (s32[1,32]{1,0:T(1,128)S(1)}, s32[1,32]{1,0:T(1,128)}, u32[]{:S(2)}) copy-start(s32[1,32]{1,0:T(1,128)} %send_ref.1) | copy-start | bytes 388
  2.5 36.4 %copy-start.6 = (s32[8,8]{1,0:T(8,128)S(1)}, s32[8,8]{1,0:T(8,128)}, u32[]{:S(2)}) copy-start(s32[8,8]{1,0:T(8,128)} %places_ref.1) | copy-start | bytes 772
  18.0 34.2 %collective-permute-start.3 = (bf16[8,8,128,128]{3,2,1,0:T(8,128)(2,1)S(1)}, bf16[8,8,128,128]{3,2,1,0:T(8,128)(2,1)}, u32[]{:S(2)}, u32[]{:S(2)}) collective-permute-start(bf16[8,8,128,128]{3,2,1,0:T(8,128)(2,1)S(1)} %copy-done), channel_id=1, source_target_pairs={{0,1},{1,0},{2,3},{3,2},{4,5},{5,4},{6,7},{7,6},{8,9},{9,8},{10,11... | collective-permute-start | bytes 6291464 | tf_op jit(solution)/shard_map/ppermute | solution.py:170
  18.0 15.2 %collective-permute-start.2 = (bf16[8,128,128]{2,1,0:T(8,128)(2,1)S(1)}, bf16[8,128,128]{2,1,0:T(8,128)(2,1)S(1)}, u32[]{:S(2)}, u32[]{:S(2)}) collective-permute-start(bf16[8,128,128]{2,1,0:T(8,128)(2,1)S(1)} %get-tuple-element.17), channel_id=1, source_target_pairs={{0,16},{2,18},{4,20},{6,22},{8,24},{10,26},{12,28},{14,30},{16,0},... | collective-permute-start | bytes 786440 | tf_op jit(solution)/shard_map/ppermute | solution.py:111
  34.1 18.0 %all-to-all-start.1 = ((bf16[16,128,128]{2,1,0:T(8,128)(2,1)}), bf16[16,128,128]{2,1,0:T(8,128)(2,1)S(1)}, u32[]{:S(2)}, u32[]{:S(2)}) async-start(bf16[16,128,128]{2,1,0:T(8,128)(2,1)} %shard_map.49), calls=%async_computation.1 | async-start | bytes 1048576 | tf_op jit(solution)/shard_map/all_to_all | solution.py:114
  37.6 11.6 %collective-permute-start.1 = (bf16[8,128,128]{2,1,0:T(8,128)(2,1)S(1)}, bf16[8,128,128]{2,1,0:T(8,128)(2,1)S(1)}, u32[]{:S(2)}, u32[]{:S(2)}) collective-permute-start(bf16[8,128,128]{2,1,0:T(8,128)(2,1)S(1)} %shard_map.47.after_ref), channel_id=1, source_target_pairs={{0,16},{2,18},{4,20},{6,22},{8,24},{10,26},{12,28},{14,30},{16,0},... | collective-permute-start | bytes 786440 | tf_op jit(solution)/shard_map/ppermute | solution.py:111
  38.9 1.5 %collective-permute-start = (s32[8,8]{1,0:T(8,128)S(1)}, s32[8,8]{1,0:T(8,128)S(1)}, u32[]{:S(2)}, u32[]{:S(2)}) collective-permute-start(s32[8,8]{1,0:T(8,128)S(1)} %copy-done.6), channel_id=1, source_target_pairs={{0,1},{1,0},{2,3},{3,2},{4,5},{5,4},{6,7},{7,6},{8,9},{9,8},{10,11... | collective-permute-start | bytes 776 | tf_op jit(solution)/shard_map/ppermute | solution.py:169
  39.1 1.3 %copy-start.1 = (bf16[8,8,128,128]{3,2,1,0:T(8,128)(2,1)}, bf16[8,8,128,128]{3,2,1,0:T(8,128)(2,1)S(1)}, u32[]{:S(2)}) copy-start(bf16[8,8,128,128]{3,2,1,0:T(8,128)(2,1)S(1)} %get-tuple-element.18.refs_5_) | copy-start | bytes 6291460
  49.2 0.7 %copy-start.4 = (bf16[8,128,128]{2,1,0:T(8,128)(2,1)}, bf16[8,128,128]{2,1,0:T(8,128)(2,1)S(1)}, u32[]{:S(2)}) copy-start(bf16[8,128,128]{2,1,0:T(8,128)(2,1)S(1)} %collective-permute-done.1.refs_3_) | copy-start | bytes 786436
  52.1 1.6 %copy-start.2 = (bf16[8,8,128,128]{3,2,1,0:T(8,128)(2,1)S(1)}, bf16[8,8,128,128]{3,2,1,0:T(8,128)(2,1)}, u32[]{:S(2)}) copy-start(bf16[8,8,128,128]{3,2,1,0:T(8,128)(2,1)} %copy-done.1) | copy-start | bytes 6291460
  53.7 0.9 %copy-start.5 = (bf16[8,128,128]{2,1,0:T(8,128)(2,1)S(1)}, bf16[8,128,128]{2,1,0:T(8,128)(2,1)}, u32[]{:S(2)}) copy-start(bf16[8,128,128]{2,1,0:T(8,128)(2,1)} %copy-done.4) | copy-start | bytes 786436

commit v4 on v3

--- a/solution.py
+++ b/solution.py
@@ -45,23 +45,22 @@
         out_ref[pl.ds((2 * spot + 1) * count, count)] = crossed_ref[here]
 
 
-def stage_own(after_ref, places_ref, blocks_ref, places_out, blocks_out, sems):
-    copies = [
-        pltpu.make_async_copy(places_ref, places_out, sems.at[0]),
-        pltpu.make_async_copy(blocks_ref, blocks_out, sems.at[1]),
-    ]
-    for copy in copies:
-        copy.start()
-    for copy in copies:
-        copy.wait()
-
-
 def contract(plan, near, cap, half_count, *refs):
     places = refs[:half_count]
     pieces = refs[half_count : half_count + len(plan)]
     blocks = refs[half_count + len(plan) : 2 * half_count + len(plan)]
-    out_ref, received, stage, sems = refs[2 * half_count + len(plan) :]
+    out_ref, received, stage, out_sems, in_sems = refs[2 * half_count + len(plan) :][:5]
+    fetched = refs[2 * half_count + len(plan) + 5 :]
     tiles, per_half, inner, columns = blocks[0].shape
+    fetches = [
+        [
+            pltpu.make_async_copy(block_ref.at[x], held.at[x], in_sems.at[half, x])
+            for half, (block_ref, held) in enumerate(zip(blocks, fetched))
+        ]
+        for x in range(tiles)
+    ]
+    for fetch in sum(fetches, []):
+        fetch.start()
     me = lax.axis_index("wide")
     for origin, piece_ref in zip(plan, pieces):
         for place, spot in origin:
@@ -70,7 +69,8 @@
     copies = []
     for x in range(tiles):
         total = None
-        for place_ref, block_ref in zip(places, blocks):
+        for place_ref, block_ref, fetch in zip(places, fetched, fetches[x]):
+            fetch.wait()
             picked = jnp.concatenate(
                 [received[place_ref[x, k]] for k in range(per_half)], axis=1
             )
@@ -81,7 +81,7 @@
             )
             total = part if total is None else total + part
         stage[x] = total.astype(stage.dtype)
-        copy = pltpu.make_async_copy(stage.at[x], out_ref.at[x], sems.at[x])
+        copy = pltpu.make_async_copy(stage.at[x], out_ref.at[x], out_sems.at[x])
         copy.start()
         copies.append(copy)
     for copy in copies:
@@ -150,38 +150,26 @@
         list(enumerate((1, spot, slot) for spot in range(near) for slot in late)),
         list(enumerate(both(early))),
     ]
-    tied, started = lax.optimization_barrier((integrals, second))
-    staged = pl.pallas_call(
-        stage_own,
-        out_shape=[
-            jax.ShapeDtypeStruct(tile_positions.shape, tile_positions.dtype),
-            jax.ShapeDtypeStruct(integrals.shape, integrals.dtype),
-        ],
-        in_specs=[ANYWHERE] * 3,
-        out_specs=[VMEM, VMEM],
-        scratch_shapes=[pltpu.SemaphoreType.DMA((2,))],
-        compiler_params=PARAMS,
-        cost_estimate=pl.CostEstimate(flops=0, bytes_accessed=2 * integrals.size * 2, transcendentals=0),
-    )
     if narrow == 2:
         swap = [(0, 1), (1, 0)]
-        own_places, own_blocks = staged(started, tile_positions, tied)
-        places = [own_places, lax.ppermute(tile_positions, "narrow", swap)]
-        blocks = [own_blocks, lax.ppermute(tied, "narrow", swap)]
+        places = [tile_positions, lax.ppermute(tile_positions, "narrow", swap)]
+        blocks = [integrals, lax.ppermute(integrals, "narrow", swap)]
     else:
         places = [lax.all_gather(tile_positions, "narrow", axis=1, tiled=True)]
-        blocks = [lax.all_gather(tied, "narrow", axis=1, tiled=True)]
+        blocks = [lax.all_gather(integrals, "narrow", axis=1, tiled=True)]
     count = len(blocks)
     return pl.pallas_call(
         functools.partial(contract, plan, near, cap, count),
         out_shape=jax.ShapeDtypeStruct((tiles, pairs, columns), jnp.bfloat16),
-        in_specs=[SMEM] * count + [VMEM] * (count + len(pieces)),
+        in_specs=[SMEM] * count + [VMEM] * len(pieces) + [ANYWHERE] * count,
         out_specs=ANYWHERE,
         scratch_shapes=[
             pltpu.VMEM((cap * wide, pairs, columns), amplitudes.dtype),
             pltpu.VMEM((tiles, pairs, columns), jnp.bfloat16),
             pltpu.SemaphoreType.DMA((tiles,)),
-        ],
+            pltpu.SemaphoreType.DMA((count, tiles)),
+        ]
+        + [pltpu.VMEM(block.shape, block.dtype) for block in blocks],
         compiler_params=PARAMS,
     )(*places, *pieces, *blocks)
 

time: 58.7 us -> 50 us (0.85)
  blocking collectives: 15.4 us -> 0 us
  starting transfers between devices: 7.5 us -> 16.9 us
  local copies, waits for them, and re-layouts: 6.41 us -> 1.71 us
  Pallas kernels: 5.3 us -> 7.45 us
    all_to_all x1 -> x0, blocking collectives: 15.4 us -> none  [spread(): lax.all_to_all(array, 'wide', split_axis=0, concat_axis=0, axis_index_gro...]
    all_to_all x1 -> x2, starting transfers between devices: 3.49 us -> 11.3 us  [spread(): lax.all_to_all(array, 'wide', split_axis=0, concat_axis=0, axis_index_gro...]
    unnamed x16 -> x8, local copies, waits for them, and re-layouts: 6.41 us -> 1.71 us
    ppermute x2, waiting for transfers between devices: 21.4 us -> 16.8 us  [cross(): return lax.ppermute(array, 'wide', opposite)]
    all_to_all x1 -> x2, waiting for transfers between devices: 2.27 us -> 5.61 us  [spread(): lax.all_to_all(array, 'wide', split_axis=0, concat_axis=0, axis_index_gro...]
    pallas_call x1, Pallas kernels: 3.64 us -> 5.13 us  [on_device(): pl.pallas_call(functools.partial(contract, plan, near, cap, count), out_s...]
    ppermute x2, starting transfers between devices: 3.93 us -> 5.14 us  [cross(): return lax.ppermute(array, 'wide', opposite)]
    ppermute x2, waiting for transfers between devices: 0.01 us -> 1.17 us  [the longest x1 1.16 us: on_device(): places = [tile_positions, lax.ppermute(tile_positions, 'narrow', swap)]]
  transfers between devices with their start and end apart: 5 -> 6, of which waited for: 3 -> 5; matrix products, arithmetic and copies ran while one was open for 0% -> 0% of each run, Pallas kernels for 2% -> 5%
where the time goes in v4:
time: 50 us; the launch traced here: 49.7 us
  waiting for transfers between devices  23.6 us (47%)
  starting transfers between devices  16.9 us (34%)
  Pallas kernels  7.45 us (15%)
  local copies, waits for them, and re-layouts  1.71 us (3%)
    ppermute x2, waiting for transfers between devices, cross(): return lax.ppermute(array, 'wide', opposite)  16.8 us
    all_to_all x2, starting transfers between devices, spread(): lax.all_to_all(array, 'wide', split_axis=0, concat_axis=0, axis_index_gro...  11.3 us
    all_to_all x2, waiting for transfers between devices, spread(): lax.all_to_all(array, 'wide', split_axis=0, concat_axis=0, axis_index_gro...  5.61 us
    ppermute x2, starting transfers between devices, cross(): return lax.ppermute(array, 'wide', opposite)  5.14 us
    pallas_call x1, Pallas kernels, on_device(): pl.pallas_call(functools.partial(contract, plan, near, cap, count), out_s...  5.13 us
    unnamed x8, local copies, waits for them, and re-layouts  1.71 us
    pallas_call x1, Pallas kernels, on_device(): pl.pallas_call(functools.partial(pick_outgoing, asked, near, cap), out_sh...  1.46 us
    ppermute x1, waiting for transfers between devices, on_device(): places = [tile_positions, lax.ppermute(tile_positions, 'narrow', swap)]  1.16 us
  transfers between devices with their start and end apart: 6, of which 5 were waited for; matrix products, arithmetic and copies ran while one was open for 0% of the time, Pallas kernels for 5%

profile of v4, /device:TPU:0, one launch (start us, length us, event | category | flops | bytes accessed | tf_op | source)
XLA Modules:
  0.0 49.7 jit_solution(8190254962342904082)
XLA Ops:
  0.0 0.5 collective-permute-start.3
  0.5 0.0 copy-start.1
  0.5 1.0 %copy-done.1 = bf16[16,128,128]{2,1,0:T(8,128)(2,1)S(1)} copy-done((bf16[16,128,128]{2,1,0:T(8,128)(2,1)S(1)}, bf16[16,128,128]{2,1,0:T(8,128)(2,1)}, u32[]{:S(2)}) %copy-start.1) | copy-done | bytes 524312
  1.5 0.0 copy-start.3
  1.5 0.7 %copy-done.3 = s32[1,32]{1,0:T(1,128)S(1)} copy-done((s32[1,32]{1,0:T(1,128)S(1)}, s32[1,32]{1,0:T(1,128)}, u32[]{:S(2)}) %copy-start.3) | copy-done | bytes 152
  2.2 1.5 %shard_map.46 = (bf16[8,128,128]{2,1,0:T(8,128)(2,1)S(1)}, bf16[16,128,128]{2,1,0:T(8,128)(2,1)}, bf16[8,128,128]{2,1,0:T(8,128)(2,1)S(1)}) custom-call(s32[1,32]{1,0:T(1,128)S(1)} %copy-done.3, bf16[16,128,128]{2,1,0:T(8,128)(2,1)S(1)} %copy-done.1), custom_call_target="tpu_custom_call" | custom-call | tf_op jit(solution)/shard_map/pallas_call | solution.py:126
  3.6 0.0 copy-start.2
  3.6 0.0 copy-start
  3.6 5.9 %all-to-all-start = ((bf16[16,128,128]{2,1,0:T(8,128)(2,1)}), bf16[16,128,128]{2,1,0:T(8,128)(2,1)S(1)}, u32[]{:S(2)}, u32[]{:S(2)}) async-start(bf16[16,128,128]{2,1,0:T(8,128)(2,1)} %get-tuple-element.8), calls=%async_computation | async-start | bytes 1048576 | tf_op jit(solution)/shard_map/all_to_all | solution.py:114
  9.5 2.6 %collective-permute-start.2 = (bf16[8,128,128]{2,1,0:T(8,128)(2,1)S(1)}, bf16[8,128,128]{2,1,0:T(8,128)(2,1)S(1)}, u32[]{:S(2)}, u32[]{:S(2)}) collective-permute-start(bf16[8,128,128]{2,1,0:T(8,128)(2,1)S(1)} %get-tuple-element.10), channel_id=1, source_target_pairs={{0,16},{2,18},{4,20},{6,22},{8,24},{10,26},{12,28},{14,30},{16,0},... | collective-permute-start | bytes 786440 | tf_op jit(solution)/shard_map/ppermute | solution.py:111
  12.1 9.5 %collective-permute-done.2.crossed_ref = bf16[8,128,128]{2,1,0:T(8,128)(2,1)S(1)} collective-permute-done((bf16[8,128,128]{2,1,0:T(8,128)(2,1)S(1)}, bf16[8,128,128]{2,1,0:T(8,128)(2,1)S(1)}, u32[]{:S(2)}, u32[]{:S(2)}) %collective-permute-start.2) | collective-permute-done | bytes 262176 | tf_op jit(solution)/shard_map/ppermute | solution.py:111
  21.6 0.8 %shard_map.48 = bf16[16,128,128]{2,1,0:T(8,128)(2,1)} custom-call(bf16[8,128,128]{2,1,0:T(8,128)(2,1)S(1)} %get-tuple-element.9.own_ref, bf16[8,128,128]{2,1,0:T(8,128)(2,1)S(1)} %collective-permute-done.2.crossed_ref), custom_call_target="tpu_custom_call" | custom-call | tf_op jit(solution)/shard_map/pallas_call | solution.py:92
  22.5 2.4 %all-to-all-done.both_ref.refs_2_ = bf16[16,128,128]{2,1,0:T(8,128)(2,1)S(1)} async-done(((bf16[16,128,128]{2,1,0:T(8,128)(2,1)}), bf16[16,128,128]{2,1,0:T(8,128)(2,1)S(1)}, u32[]{:S(2)}, u32[]{:S(2)}) %all-to-all-start) | async-done | bytes 524320 | tf_op jit(solution)/shard_map/all_to_all | solution.py:114
  24.9 5.4 %all-to-all-start.1 = ((bf16[16,128,128]{2,1,0:T(8,128)(2,1)}), bf16[16,128,128]{2,1,0:T(8,128)(2,1)S(1)}, u32[]{:S(2)}, u32[]{:S(2)}) async-start(bf16[16,128,128]{2,1,0:T(8,128)(2,1)} %shard_map.48), calls=%async_computation.1 | async-start | bytes 1048576 | tf_op jit(solution)/shard_map/all_to_all | solution.py:114
  30.3 2.6 %collective-permute-start.1 = (bf16[8,128,128]{2,1,0:T(8,128)(2,1)S(1)}, bf16[8,128,128]{2,1,0:T(8,128)(2,1)S(1)}, u32[]{:S(2)}, u32[]{:S(2)}) collective-permute-start(bf16[8,128,128]{2,1,0:T(8,128)(2,1)S(1)} %shard_map.47), channel_id=1, source_target_pairs={{0,16},{2,18},{4,20},{6,22},{8,24},{10,26},{12,28},{14,30},{16,0},... | collective-permute-start | bytes 786440 | tf_op jit(solution)/shard_map/ppermute | solution.py:111
  32.9 0.0 copy-done.2
  32.9 0.0 collective-permute-start
  32.9 1.2 %collective-permute-done.refs_1_ = s32[8,8]{1,0:T(8,128)S(1)} collective-permute-done((s32[8,8]{1,0:T(8,128)S(1)}, s32[8,8]{1,0:T(8,128)S(1)}, u32[]{:S(2)}, u32[]{:S(2)}) %collective-permute-start) | collective-permute-done | bytes 288 | tf_op jit(solution)/shard_map/ppermute | solution.py:155
  34.0 7.3 %collective-permute-done.1.refs_3_ = bf16[8,128,128]{2,1,0:T(8,128)(2,1)S(1)} collective-permute-done((bf16[8,128,128]{2,1,0:T(8,128)(2,1)S(1)}, bf16[8,128,128]{2,1,0:T(8,128)(2,1)S(1)}, u32[]{:S(2)}, u32[]{:S(2)}) %collective-permute-start.1) | collective-permute-done | bytes 262176 | tf_op jit(solution)/shard_map/ppermute | solution.py:111
  41.3 3.2 %all-to-all-done.1.refs_4_ = bf16[16,128,128]{2,1,0:T(8,128)(2,1)S(1)} async-done(((bf16[16,128,128]{2,1,0:T(8,128)(2,1)}), bf16[16,128,128]{2,1,0:T(8,128)(2,1)S(1)}, u32[]{:S(2)}, u32[]{:S(2)}) %all-to-all-start.1) | async-done | bytes 524320 | tf_op jit(solution)/shard_map/all_to_all | solution.py:114
  44.6 0.0 collective-permute-done.3.refs_6_
  44.6 0.0 copy-done
  44.6 5.1 %shard_map.49 = bf16[8,128,128]{2,1,0:T(8,128)(2,1)} custom-call(s32[8,8]{1,0:T(8,128)S(1)} %copy-done.2, s32[8,8]{1,0:T(8,128)S(1)} %collective-permute-done.refs_1_, bf16[16,128,128]{2,1,0:T(8,128)(2,1)S(1)} %all-to-all-done.both_ref.refs_2_, bf16[8,128,128]{2,1,0:T(8,128)(2,1)S(1)} %collective-permute-done.1.refs_3_, ...), custom_call_target="tpu_custom_call" | custom-call | tf_op jit(solution)/shard_map/pallas_call | solution.py:161
  (1 shorter events, 0.0 us)
Async XLA Ops:
  0.0 44.6 %collective-permute-start.3 = (bf16[8,8,128,128]{3,2,1,0:T(8,128)(2,1)}, bf16[8,8,128,128]{3,2,1,0:T(8,128)(2,1)}, u32[]{:S(2)}, u32[]{:S(2)}) collective-permute-start(bf16[8,8,128,128]{3,2,1,0:T(8,128)(2,1)} %refs_5_.1), channel_id=1, source_target_pairs={{0,1},{1,0},{2,3},{3,2},{4,5},{5,4},{6,7},{7,6},{8,9},{9,8},{10,11... | collective-permute-start | bytes 6291464 | tf_op jit(solution)/shard_map/ppermute | solution.py:156
  0.5 1.0 %copy-start.1 = (bf16[16,128,128]{2,1,0:T(8,128)(2,1)S(1)}, bf16[16,128,128]{2,1,0:T(8,128)(2,1)}, u32[]{:S(2)}) copy-start(bf16[16,128,128]{2,1,0:T(8,128)(2,1)} %amplitudes_ref.1) | copy-start | bytes 1572868
  1.5 0.7 %copy-start.3 = (s32[1,32]{1,0:T(1,128)S(1)}, s32[1,32]{1,0:T(1,128)}, u32[]{:S(2)}) copy-start(s32[1,32]{1,0:T(1,128)} %send_ref.1) | copy-start | bytes 388
  3.6 29.3 %copy-start.2 = (s32[8,8]{1,0:T(8,128)S(1)}, s32[8,8]{1,0:T(8,128)}, u32[]{:S(2)}) copy-start(s32[8,8]{1,0:T(8,128)} %refs_0_.1) | copy-start | bytes 772
  3.6 40.9 %copy-start = (bf16[8,8,128,128]{3,2,1,0:T(8,128)(2,1)S(1)}, bf16[8,8,128,128]{3,2,1,0:T(8,128)(2,1)}, u32[]{:S(2)}) copy-start(bf16[8,8,128,128]{3,2,1,0:T(8,128)(2,1)} %refs_5_.1) | copy-start | bytes 6291460
  3.6 21.2 %all-to-all-start = ((bf16[16,128,128]{2,1,0:T(8,128)(2,1)}), bf16[16,128,128]{2,1,0:T(8,128)(2,1)S(1)}, u32[]{:S(2)}, u32[]{:S(2)}) async-start(bf16[16,128,128]{2,1,0:T(8,128)(2,1)} %get-tuple-element.8), calls=%async_computation | async-start | bytes 1048576 | tf_op jit(solution)/shard_map/all_to_all | solution.py:114
  9.5 12.1 %collective-permute-start.2 = (bf16[8,128,128]{2,1,0:T(8,128)(2,1)S(1)}, bf16[8,128,128]{2,1,0:T(8,128)(2,1)S(1)}, u32[]{:S(2)}, u32[]{:S(2)}) collective-permute-start(bf16[8,128,128]{2,1,0:T(8,128)(2,1)S(1)} %get-tuple-element.10), channel_id=1, source_target_pairs={{0,16},{2,18},{4,20},{6,22},{8,24},{10,26},{12,28},{14,30},{16,0},... | collective-permute-start | bytes 786440 | tf_op jit(solution)/shard_map/ppermute | solution.py:111
  24.9 19.7 %all-to-all-start.1 = ((bf16[16,128,128]{2,1,0:T(8,128)(2,1)}), bf16[16,128,128]{2,1,0:T(8,128)(2,1)S(1)}, u32[]{:S(2)}, u32[]{:S(2)}) async-start(bf16[16,128,128]{2,1,0:T(8,128)(2,1)} %shard_map.48), calls=%async_computation.1 | async-start | bytes 1048576 | tf_op jit(solution)/shard_map/all_to_all | solution.py:114
  30.3 11.0 %collective-permute-start.1 = (bf16[8,128,128]{2,1,0:T(8,128)(2,1)S(1)}, bf16[8,128,128]{2,1,0:T(8,128)(2,1)S(1)}, u32[]{:S(2)}, u32[]{:S(2)}) collective-permute-start(bf16[8,128,128]{2,1,0:T(8,128)(2,1)S(1)} %shard_map.47), channel_id=1, source_target_pairs={{0,16},{2,18},{4,20},{6,22},{8,24},{10,26},{12,28},{14,30},{16,0},... | collective-permute-start | bytes 786440 | tf_op jit(solution)/shard_map/ppermute | solution.py:111
  32.9 1.2 %collective-permute-start = (s32[8,8]{1,0:T(8,128)S(1)}, s32[8,8]{1,0:T(8,128)S(1)}, u32[]{:S(2)}, u32[]{:S(2)}) collective-permute-start(s32[8,8]{1,0:T(8,128)S(1)} %copy-done.2), channel_id=1, source_target_pairs={{0,1},{1,0},{2,3},{3,2},{4,5},{5,4},{6,7},{7,6},{8,9},{9,8},{10,11... | collective-permute-start | bytes 776 | tf_op jit(solution)/shard_map/ppermute | solution.py:155

commit v5 on v2

v5 whole, which is shorter than its diff:
```python
import functools
import math

import jax
import jax.numpy as jnp
from jax import lax
from jax.experimental import pallas as pl
from jax.experimental.pallas import tpu as pltpu
from jax.sharding import PartitionSpec as P

SMEM = pl.BlockSpec(memory_space=pltpu.SMEM)
VMEM = pl.BlockSpec(memory_space=pltpu.VMEM)
ANYWHERE = pl.BlockSpec(memory_space=pl.ANY)


GRANT = pltpu.CompilerParams(vmem_limit_bytes=48 * 1024 * 1024)


def pick_outgoing(plan, cap, send_ref, amplitudes_ref, *refs):
    out_refs = refs[: len(plan)]
    sends, held, sems = refs[len(plan) :]
    fetch_sends = pltpu.make_async_copy(send_ref, sends, sems.at[0])
    fetch_tiles = pltpu.make_async_copy(amplitudes_ref, held, sems.at[1])
    fetch_tiles.start()
    fetch_sends.start()
    fetch_sends.wait()
    fetch_tiles.wait()
    me = lax.axis_index("wide")
    for wanted, out_ref in zip(plan, out_refs):
        for place, (partner, slot) in enumerate(wanted):
            out_ref[place] = held[sends[0, (me ^ partner) * cap + slot]]


def regroup(ins, width, staged, *refs):
    in_refs, stage_in = refs[:ins], refs[ins : ins + staged]
    out_refs = refs[ins + staged :]
    copies = []
    if staged:
        out_refs, stage_out, sems = out_refs[: -staged - 1], out_refs[-staged - 1 : -1], out_refs[-1]
        for number in range(staged):
            copy = pltpu.make_async_copy(stage_in[number], stage_out[number], sems.at[number])
            copy.start()
            copies.append(copy)
    for j, out_ref in enumerate(out_refs):
        for i, in_ref in enumerate(in_refs):
            out_ref[i * width : (i + 1) * width] = in_ref[(j + 1) * width : (j + 2) * width]
    for copy in copies:
        copy.wait()


def contract(plan, cap, count, *refs):
    places = refs[:count]
    pieces = refs[count : count + len(plan)]
    blocks = list(refs[count + len(plan) : 2 * count + len(plan)])
    out_ref, received, stage, sems = refs[2 * count + len(plan) :]
    tiles, per_block, inner, columns = blocks[0].shape
    me = lax.axis_index("wide")
    for origin, piece_ref in zip(plan, pieces):
        for place, (partner, slot) in origin:
            received[(me ^ partner) * cap + slot] = piece_ref[place]
    copies = []
    for x in range(tiles):
        total = None
        for place_ref, block_ref in zip(places, blocks):
            picked = jnp.concatenate(
                [received[place_ref[x, k]] for k in range(per_block)], axis=1
            )
            part = jnp.dot(
                picked,
                block_ref[x].reshape(per_block * inner, columns),
                preferred_element_type=jnp.float32,
            )
            total = part if total is None else total + part
        stage[x] = total.astype(stage.dtype)
        copy = pltpu.make_async_copy(stage.at[x], out_ref.at[x], sems.at[x])
        copy.start()
        copies.append(copy)
    for copy in copies:
        copy.wait()


def regrouped(arrays, width, count, staged=()):
    shape = jax.ShapeDtypeStruct((len(arrays) * width,) + arrays[0].shape[1:], arrays[0].dtype)
    outs = pl.pallas_call(
        functools.partial(regroup, len(arrays), width, len(staged)),
        out_shape=[shape] * count + [jax.ShapeDtypeStruct(s.shape, s.dtype) for s in staged],
        in_specs=[VMEM] * len(arrays) + [ANYWHERE] * len(staged),
        out_specs=[VMEM] * (count + len(staged)),
        scratch_shapes=[pltpu.SemaphoreType.DMA((len(staged),))] if staged else [],
        compiler_params=GRANT,
    )(*arrays, *staged)
    return list(outs[:count]), list(outs[count:])


def on_device(wide, narrow, amplitudes, send_list, tile_positions, integrals):
    cap = send_list.shape[1] // wide
    pairs, columns = amplitudes.shape[1:]
    tiles = integrals.shape[0]
    near = math.isqrt(wide)
    far = wide // near
    early, late = range(cap // 2), range(cap // 2, cap)

    def exchange(array, partner):
        return lax.ppermute(array, "wide", [(d, d ^ partner) for d in range(wide)])

    along = [[(a + near * b, s) for a in range(near) for s in early] for b in range(far)]
    across = [[(a + near * b, s) for b in range(far) for s in late] for a in range(near)]
    plan = along + across
    outgoing = pl.pallas_call(
        functools.partial(pick_outgoing, plan, cap),
        out_shape=[jax.ShapeDtypeStruct((len(p), pairs, columns), amplitudes.dtype) for p in plan],
        in_specs=[ANYWHERE, ANYWHERE],
        out_specs=[VMEM] * len(plan),
        scratch_shapes=[
            pltpu.SMEM(send_list.shape, send_list.dtype),
            pltpu.VMEM(amplitudes.shape, amplitudes.dtype),
            pltpu.SemaphoreType.DMA((2,)),
        ],
        compiler_params=GRANT,
    )(send_list, amplitudes)
    if narrow == 2:
        swap = [(0, 1), (1, 0)]
        places = [tile_positions, lax.ppermute(tile_positions, "narrow", swap)]
        blocks = [integrals, lax.ppermute(integrals, "narrow", swap)]
    else:
        places = [lax.all_gather(tile_positions, "narrow", axis=1, tiled=True)]
        blocks = [lax.all_gather(integrals, "narrow", axis=1, tiled=True)]
    first_along, first_across = outgoing[:far], outgoing[far:]
    got_across = [first_across[0]] + [None] * (near - 1)
    got_along = [first_along[0]] + [None] * (far - 1)
    for a in range(near - 1, 0, -1):
        got_across[a] = exchange(first_across[a], a)
    for b in range(far - 1, 0, -1):
        got_along[b] = exchange(first_along[b], near * b)
    second_along, kept = regrouped(got_across, len(late), far - 1, (places[0], blocks[0]) if narrow == 2 else ())
    if narrow == 2:
        places[0], blocks[0] = kept
    second_along, blocks[-1] = lax.optimization_barrier((second_along, blocks[-1]))
    got_along[0], second_along[-1] = lax.optimization_barrier((got_along[0], second_along[-1]))
    last_along = [exchange(second_along[b - 1], near * b) for b in range(far - 1, 0, -1)]
    second_across, _ = regrouped(got_along, len(early), near - 1)
    last_across = [exchange(second_across[a - 1], a) for a in range(near - 1, 0, -1)]
    pieces = got_across + got_along[:1] + got_along[:0:-1] + last_along + last_across
    origins = [list(enumerate((a, s) for s in late)) for a in range(near)]
    origins += [list(enumerate((near * b, s) for s in early)) for b in [0, *range(far - 1, 0, -1)]]
    origins += [list(enumerate((a + near * b, s) for a in range(near) for s in late)) for b in range(far - 1, 0, -1)]
    origins += [list(enumerate((a + near * b, s) for b in range(far) for s in early)) for a in range(near - 1, 0, -1)]
    count = len(blocks)
    return pl.pallas_call(
        functools.partial(contract, origins, cap, count),
        out_shape=jax.ShapeDtypeStruct((tiles, pairs, columns), jnp.bfloat16),
        in_specs=[SMEM] * count + [VMEM] * (len(pieces) + count),
        out_specs=ANYWHERE,
        scratch_shapes=[
            pltpu.VMEM((cap * wide, pairs, columns), amplitudes.dtype),
            pltpu.VMEM((tiles, pairs, columns), jnp.bfloat16),
            pltpu.SemaphoreType.DMA((tiles,)),
        ],
        compiler_params=GRANT,
    )(*places, *pieces, *blocks)


def solution(mesh):
    placed = (
        P("wide", "narrow", None),
        P("wide", None),
        P("wide", "narrow"),
        P("wide", "narrow", None, None),
    )
    return jax.shard_map(
        functools.partial(on_device, mesh.shape["wide"], mesh.shape["narrow"]),
        mesh=mesh,
        in_specs=placed,
        out_specs=P("wide", "narrow", None),
        check_vma=False,
    )
```

time: 47.5 us -> 39.6 us (0.83)
  starting transfers between devices: 28.2 us -> 19.2 us
  waiting for transfers between devices: 11.7 us -> 12.7 us
  Pallas kernels: 3.37 us -> 4.13 us
  local copies, waits for them, and re-layouts: 3.97 us -> 3.29 us
    ppermute x15 -> x12, starting transfers between devices: 27.7 us -> 18.7 us  [exchange(): return lax.ppermute(array, 'wide', [(d, d ^ partner) for d in range(wide)])]
    ppermute x15 -> x12, waiting for transfers between devices: 10.4 us -> 12.7 us  [exchange(): return lax.ppermute(array, 'wide', [(d, d ^ partner) for d in range(wide)])]
    ppermute x1, waiting for transfers between devices: 1.37 us -> 0.01 us  [on_device(): places = [tile_positions, lax.ppermute(tile_positions, 'narrow', swap)]]
    pallas_call x2 -> x4, Pallas kernels: 3.37 us -> 4.13 us  [the longest x1 2.73 us: on_device(): pl.pallas_call(functools.partial(contract, origins, cap, count), out_shap...]
    unnamed x8 -> x6, local copies, waits for them, and re-layouts: 3.97 us -> 3.29 us
  transfers between devices with their start and end apart: 17 -> 14, of which waited for: 8 -> 6; matrix products, arithmetic and copies ran while one was open for 0% -> 0% of each run, Pallas kernels for 1% -> 4%
where the time goes in v5:
time: 39.6 us; the launch traced here: 39.3 us
  starting transfers between devices  19.2 us (48%)
  waiting for transfers between devices  12.7 us (32%)
  Pallas kernels  4.13 us (10%)
  local copies, waits for them, and re-layouts  3.29 us (8%)
    ppermute x12, starting transfers between devices, exchange(): return lax.ppermute(array, 'wide', [(d, d ^ partner) for d in range(wide)])  18.7 us
    ppermute x12, waiting for transfers between devices, exchange(): return lax.ppermute(array, 'wide', [(d, d ^ partner) for d in range(wide)])  12.7 us
    unnamed x6, local copies, waits for them, and re-layouts  3.29 us
    pallas_call x1, Pallas kernels, on_device(): pl.pallas_call(functools.partial(contract, origins, cap, count), out_shap...  2.73 us
  transfers between devices with their start and end apart: 14, of which 6 were waited for; matrix products, arithmetic and copies ran while one was open for 0% of the time, Pallas kernels for 4%

profile of v5, /device:TPU:0, one launch (start us, length us, event | category | flops | bytes accessed | tf_op | source)
XLA Modules:
  0.0 39.3 jit_solution(3331048379884813515)
XLA Ops:
  0.0 0.5 %collective-permute-start.4 = (bf16[8,8,128,128]{3,2,1,0:T(8,128)(2,1)}, bf16[8,8,128,128]{3,2,1,0:T(8,128)(2,1)S(1)}, u32[]{:S(2)}, u32[]{:S(2)}) collective-permute-start(bf16[8,8,128,128]{3,2,1,0:T(8,128)(2,1)} %refs_5_.1), channel_id=1, source_target_pairs={{0,1},{1,0},{2,3},{3,2},{4,5},{5,4},{6,7},{7,6},{8,9},{9,8},{10,11... | collective-permute-start | bytes 6291464 | tf_op jit(solution)/shard_map/ppermute | solution.py:124
  0.5 0.0 copy-start.1
  0.5 1.0 %copy-done.1 = bf16[16,128,128]{2,1,0:T(8,128)(2,1)S(1)} copy-done((bf16[16,128,128]{2,1,0:T(8,128)(2,1)S(1)}, bf16[16,128,128]{2,1,0:T(8,128)(2,1)}, u32[]{:S(2)}) %copy-start.1) | copy-done | bytes 524312
  1.5 0.0 copy-start.2
  1.5 0.7 %copy-done.2 = s32[1,32]{1,0:T(1,128)S(1)} copy-done((s32[1,32]{1,0:T(1,128)S(1)}, s32[1,32]{1,0:T(1,128)}, u32[]{:S(2)}) %copy-start.2) | copy-done | bytes 152
  2.2 0.7 %shard_map.46 = (bf16[4,128,128]{2,1,0:T(8,128)(2,1)S(1)}, bf16[4,128,128]{2,1,0:T(8,128)(2,1)S(1)}, bf16[4,128,128]{2,1,0:T(8,128)(2,1)S(1)}, bf16[4,128,128]{2...) custom-call(s32[1,32]{1,0:T(1,128)S(1)} %copy-done.2, ...), custom_call_target="tpu_custom_call" | custom-call | tf_op jit(solution)/shard_map/pallas_call | solution.py:109
  2.8 2.6 %collective-permute-start = (bf16[4,128,128]{2,1,0:T(8,128)(2,1)S(1)}, bf16[4,128,128]{2,1,0:T(8,128)(2,1)S(1)}, u32[]{:S(2)}, u32[]{:S(2)}) collective-permute-start(bf16[4,128,128]{2,1,0:T(8,128)(2,1)S(1)} %get-tuple-element.28), channel_id=1, source_target_pairs={{0,2},{2,0},{4,6},{6,4},{8,10},{10,8},{12,14},{14,12},{16,18},{18,... | collective-permute-start | bytes 393224 | tf_op jit(solution)/shard_map/ppermute | solution.py:104
  5.4 1.5 %collective-permute-start.1 = (bf16[4,128,128]{2,1,0:T(8,128)(2,1)S(1)}, bf16[4,128,128]{2,1,0:T(8,128)(2,1)S(1)}, u32[]{:S(2)}, u32[]{:S(2)}) collective-permute-start(bf16[4,128,128]{2,1,0:T(8,128)(2,1)S(1)} %get-tuple-element.29), channel_id=1, source_target_pairs={{0,4},{2,6},{4,0},{6,2},{8,12},{10,14},{12,8},{14,10},{16,20},{18,... | collective-permute-start | bytes 393224 | tf_op jit(solution)/shard_map/ppermute | solution.py:104
  6.9 0.0 collective-permute-start.2
  6.9 4.1 %collective-permute-start.5 = (bf16[4,128,128]{2,1,0:T(8,128)(2,1)S(1)}, bf16[4,128,128]{2,1,0:T(8,128)(2,1)S(1)}, u32[]{:S(2)}, u32[]{:S(2)}) collective-permute-start(bf16[4,128,128]{2,1,0:T(8,128)(2,1)S(1)} %get-tuple-element.38), channel_id=1, source_target_pairs={{0,24},{2,26},{4,28},{6,30},{8,16},{10,18},{12,20},{14,22},{16,8},... | collective-permute-start | bytes 393224 | tf_op jit(solution)/shard_map/ppermute | solution.py:104
  11.0 0.0 collective-permute-done.refs_1_.refs_3_
  11.0 1.8 %collective-permute-start.6 = (bf16[4,128,128]{2,1,0:T(8,128)(2,1)S(1)}, bf16[4,128,128]{2,1,0:T(8,128)(2,1)S(1)}, u32[]{:S(2)}, u32[]{:S(2)}) collective-permute-start(bf16[4,128,128]{2,1,0:T(8,128)(2,1)S(1)} %get-tuple-element.39), channel_id=1, source_target_pairs={{0,16},{2,18},{4,20},{6,22},{8,24},{10,26},{12,28},{14,30},{16,0},... | collective-permute-start | bytes 393224 | tf_op jit(solution)/shard_map/ppermute | solution.py:104
  12.8 1.0 %collective-permute-done.1.refs_2_.refs_4_ = bf16[4,128,128]{2,1,0:T(8,128)(2,1)S(1)} collective-permute-done((bf16[4,128,128]{2,1,0:T(8,128)(2,1)S(1)}, bf16[4,128,128]{2,1,0:T(8,128)(2,1)S(1)}, u32[]{:S(2)}, u32[]{:S(2)}) %collective-permute-start.1) | collective-permute-done | bytes 131104 | tf_op jit(solution)/shard_map/ppermute | solution.py:104
  13.8 1.6 %collective-permute-start.7 = (bf16[4,128,128]{2,1,0:T(8,128)(2,1)S(1)}, bf16[4,128,128]{2,1,0:T(8,128)(2,1)S(1)}, u32[]{:S(2)}, u32[]{:S(2)}) collective-permute-start(bf16[4,128,128]{2,1,0:T(8,128)(2,1)S(1)} %get-tuple-element.40), channel_id=1, source_target_pairs={{0,8},{2,10},{4,12},{6,14},{8,0},{10,2},{12,4},{14,6},{16,24},{18,... | collective-permute-start | bytes 393224 | tf_op jit(solution)/shard_map/ppermute | solution.py:104
  15.4 0.0 collective-permute-done.2.refs_3_.refs_5_
  15.4 0.0 copy-start
  15.4 1.6 %copy-done = bf16[8,8,128,128]{3,2,1,0:T(8,128)(2,1)S(1)} copy-done((bf16[8,8,128,128]{3,2,1,0:T(8,128)(2,1)S(1)}, bf16[8,8,128,128]{3,2,1,0:T(8,128)(2,1)}, u32[]{:S(2)}) %copy-start) | copy-done | bytes 2097176
  17.0 0.7 %shard_map.47 = (bf16[4,128,128]{2,1,0:T(8,128)(2,1)S(1)}, bf16[4,128,128]{2,1,0:T(8,128)(2,1)S(1)}, bf16[4,128,128]{2,1,0:T(8,128)(2,1)S(1)}, s32[8,8]{1,0:T(8,128)S(1)}, bf16[8,8,128,128]{3,2,1,0:T(8,128)(2,1)S(1)}) custom-call(bf16[4,128,128]{2,1,0:T(8,128)(2,1)S(1)} %get-tuple-element.27.refs_0_.refs_2_, ...), custom_call_target="tpu_custom_call" | custom-call | tf_op jit(solution)/shard_map/pallas_call | solution.py:84
  17.7 0.0 collective-permute-done.4.refs_17_
  17.7 2.5 %collective-permute-start.8 = (bf16[4,128,128]{2,1,0:T(8,128)(2,1)S(1)}, bf16[4,128,128]{2,1,0:T(8,128)(2,1)S(1)}, u32[]{:S(2)}, u32[]{:S(2)}) collective-permute-start(bf16[4,128,128]{2,1,0:T(8,128)(2,1)S(1)} %get-tuple-element.41), channel_id=1, source_target_pairs={{0,24},{2,26},{4,28},{6,30},{8,16},{10,18},{12,20},{14,22},{16,8},... | collective-permute-start | bytes 393224 | tf_op jit(solution)/shard_map/ppermute | solution.py:104
  20.3 0.0 collective-permute-start.3
  20.3 0.0 collective-permute-done.5.refs_3_.refs_7_
  20.3 1.1 %collective-permute-start.9 = (bf16[4,128,128]{2,1,0:T(8,128)(2,1)S(1)}, bf16[4,128,128]{2,1,0:T(8,128)(2,1)S(1)}, u32[]{:S(2)}, u32[]{:S(2)}) collective-permute-start(bf16[4,128,128]{2,1,0:T(8,128)(2,1)S(1)} %get-tuple-element.42), channel_id=1, source_target_pairs={{0,16},{2,18},{4,20},{6,22},{8,24},{10,26},{12,28},{14,30},{16,0},... | collective-permute-start | bytes 393224 | tf_op jit(solution)/shard_map/ppermute | solution.py:104
  21.4 7.1 %collective-permute-done.6.refs_2_.refs_8_ = bf16[4,128,128]{2,1,0:T(8,128)(2,1)S(1)} collective-permute-done((bf16[4,128,128]{2,1,0:T(8,128)(2,1)S(1)}, bf16[4,128,128]{2,1,0:T(8,128)(2,1)S(1)}, u32[]{:S(2)}, u32[]{:S(2)}) %collective-permute-start.6) | collective-permute-done | bytes 131104 | tf_op jit(solution)/shard_map/ppermute | solution.py:104
  28.5 0.0 collective-permute-start.10
  28.5 0.0 collective-permute-done.7.refs_1_.refs_9_
  28.5 2.5 %collective-permute-start.11 = (bf16[4,128,128]{2,1,0:T(8,128)(2,1)S(1)}, bf16[4,128,128]{2,1,0:T(8,128)(2,1)S(1)}, u32[]{:S(2)}, u32[]{:S(2)}) collective-permute-start(bf16[4,128,128]{2,1,0:T(8,128)(2,1)S(1)} %get-tuple-element.44), channel_id=1, source_target_pairs={{0,6},{2,4},{4,2},{6,0},{8,14},{10,12},{12,10},{14,8},{16,22},{18,... | collective-permute-start | bytes 393224 | tf_op jit(solution)/shard_map/ppermute | solution.py:104
  31.0 0.0 collective-permute-done.3.refs_1_
  31.0 0.5 %collective-permute-start.12 = (bf16[4,128,128]{2,1,0:T(8,128)(2,1)S(1)}, bf16[4,128,128]{2,1,0:T(8,128)(2,1)S(1)}, u32[]{:S(2)}, u32[]{:S(2)}) collective-permute-start(bf16[4,128,128]{2,1,0:T(8,128)(2,1)S(1)} %get-tuple-element.45), channel_id=1, source_target_pairs={{0,4},{2,6},{4,0},{6,2},{8,12},{10,14},{12,8},{14,10},{16,20},{18,... | collective-permute-start | bytes 393224 | tf_op jit(solution)/shard_map/ppermute | solution.py:104
  31.6 0.0 collective-permute-done.8.refs_10_
  31.6 0.5 %collective-permute-start.13 = (bf16[4,128,128]{2,1,0:T(8,128)(2,1)S(1)}, bf16[4,128,128]{2,1,0:T(8,128)(2,1)S(1)}, u32[]{:S(2)}, u32[]{:S(2)}) collective-permute-start(bf16[4,128,128]{2,1,0:T(8,128)(2,1)S(1)} %get-tuple-element.46), channel_id=1, source_target_pairs={{0,2},{2,0},{4,6},{6,4},{8,10},{10,8},{12,14},{14,12},{16,18},{18,... | collective-permute-start | bytes 393224 | tf_op jit(solution)/shard_map/ppermute | solution.py:104
  32.1 1.1 %collective-permute-done.9.refs_11_ = bf16[4,128,128]{2,1,0:T(8,128)(2,1)S(1)} collective-permute-done((bf16[4,128,128]{2,1,0:T(8,128)(2,1)S(1)}, bf16[4,128,128]{2,1,0:T(8,128)(2,1)S(1)}, u32[]{:S(2)}, u32[]{:S(2)}) %collective-permute-start.9) | collective-permute-done | bytes 131104 | tf_op jit(solution)/shard_map/ppermute | solution.py:104
  33.2 1.3 %collective-permute-done.10.refs_12_ = bf16[4,128,128]{2,1,0:T(8,128)(2,1)S(1)} collective-permute-done((bf16[4,128,128]{2,1,0:T(8,128)(2,1)S(1)}, bf16[4,128,128]{2,1,0:T(8,128)(2,1)S(1)}, u32[]{:S(2)}, u32[]{:S(2)}) %collective-permute-start.10) | collective-permute-done | bytes 131104 | tf_op jit(solution)/shard_map/ppermute | solution.py:104
  34.5 1.1 %collective-permute-done.11.refs_13_ = bf16[4,128,128]{2,1,0:T(8,128)(2,1)S(1)} collective-permute-done((bf16[4,128,128]{2,1,0:T(8,128)(2,1)S(1)}, bf16[4,128,128]{2,1,0:T(8,128)(2,1)S(1)}, u32[]{:S(2)}, u32[]{:S(2)}) %collective-permute-start.11) | collective-permute-done | bytes 131104 | tf_op jit(solution)/shard_map/ppermute | solution.py:104
  35.6 1.0 %collective-permute-done.12.refs_14_ = bf16[4,128,128]{2,1,0:T(8,128)(2,1)S(1)} collective-permute-done((bf16[4,128,128]{2,1,0:T(8,128)(2,1)S(1)}, bf16[4,128,128]{2,1,0:T(8,128)(2,1)S(1)}, u32[]{:S(2)}, u32[]{:S(2)}) %collective-permute-start.12) | collective-permute-done | bytes 131104 | tf_op jit(solution)/shard_map/ppermute | solution.py:104
  36.6 0.0 collective-permute-done.13.refs_15_
  36.6 2.7 %shard_map.49 = bf16[8,128,128]{2,1,0:T(8,128)(2,1)} custom-call(s32[8,8]{1,0:T(8,128)S(1)} %get-tuple-element.31.refs_0_, s32[8,8]{1,0:T(8,128)S(1)} %collective-permute-done.3.refs_1_, bf16[4,128,128]{2,1,0:T(8,128)(2,1)S(1)} %get-tuple-element.27.refs_0_.refs_2_, bf16[4,128,128]{2,1,0:T(8,128)(2,1)S(1)} %collective-permute-done.refs_1_.refs_3_, ...), custom_call_target="tpu_custom_call" | custom-call | tf_op jit(solution)/shard_map/pallas_call | solution.py:149
  (1 shorter events, 0.0 us)
Async XLA Ops:
  0.0 17.7 %collective-permute-start.4 = (bf16[8,8,128,128]{3,2,1,0:T(8,128)(2,1)}, bf16[8,8,128,128]{3,2,1,0:T(8,128)(2,1)S(1)}, u32[]{:S(2)}, u32[]{:S(2)}) collective-permute-start(bf16[8,8,128,128]{3,2,1,0:T(8,128)(2,1)} %refs_5_.1), channel_id=1, source_target_pairs={{0,1},{1,0},{2,3},{3,2},{4,5},{5,4},{6,7},{7,6},{8,9},{9,8},{10,11... | collective-permute-start | bytes 6291464 | tf_op jit(solution)/shard_map/ppermute | solution.py:124
  0.5 1.0 %copy-start.1 = (bf16[16,128,128]{2,1,0:T(8,128)(2,1)S(1)}, bf16[16,128,128]{2,1,0:T(8,128)(2,1)}, u32[]{:S(2)}) copy-start(bf16[16,128,128]{2,1,0:T(8,128)(2,1)} %amplitudes_ref.1) | copy-start | bytes 1572868
  1.5 0.7 %copy-start.2 = (s32[1,32]{1,0:T(1,128)S(1)}, s32[1,32]{1,0:T(1,128)}, u32[]{:S(2)}) copy-start(s32[1,32]{1,0:T(1,128)} %send_ref.1) | copy-start | bytes 388
  2.8 8.2 %collective-permute-start = (bf16[4,128,128]{2,1,0:T(8,128)(2,1)S(1)}, bf16[4,128,128]{2,1,0:T(8,128)(2,1)S(1)}, u32[]{:S(2)}, u32[]{:S(2)}) collective-permute-start(bf16[4,128,128]{2,1,0:T(8,128)(2,1)S(1)} %get-tuple-element.28), channel_id=1, source_target_pairs={{0,2},{2,0},{4,6},{6,4},{8,10},{10,8},{12,14},{14,12},{16,18},{18,... | collective-permute-start | bytes 393224 | tf_op jit(solution)/shard_map/ppermute | solution.py:104
  5.4 8.4 %collective-permute-start.1 = (bf16[4,128,128]{2,1,0:T(8,128)(2,1)S(1)}, bf16[4,128,128]{2,1,0:T(8,128)(2,1)S(1)}, u32[]{:S(2)}, u32[]{:S(2)}) collective-permute-start(bf16[4,128,128]{2,1,0:T(8,128)(2,1)S(1)} %get-tuple-element.29), channel_id=1, source_target_pairs={{0,4},{2,6},{4,0},{6,2},{8,12},{10,14},{12,8},{14,10},{16,20},{18,... | collective-permute-start | bytes 393224 | tf_op jit(solution)/shard_map/ppermute | solution.py:104
  6.9 8.5 %collective-permute-start.2 = (bf16[4,128,128]{2,1,0:T(8,128)(2,1)S(1)}, bf16[4,128,128]{2,1,0:T(8,128)(2,1)S(1)}, u32[]{:S(2)}, u32[]{:S(2)}) collective-permute-start(bf16[4,128,128]{2,1,0:T(8,128)(2,1)S(1)} %get-tuple-element.30), channel_id=1, source_target_pairs={{0,6},{2,4},{4,2},{6,0},{8,14},{10,12},{12,10},{14,8},{16,22},{18,... | collective-permute-start | bytes 393224 | tf_op jit(solution)/shard_map/ppermute | solution.py:104
  6.9 13.3 %collective-permute-start.5 = (bf16[4,128,128]{2,1,0:T(8,128)(2,1)S(1)}, bf16[4,128,128]{2,1,0:T(8,128)(2,1)S(1)}, u32[]{:S(2)}, u32[]{:S(2)}) collective-permute-start(bf16[4,128,128]{2,1,0:T(8,128)(2,1)S(1)} %get-tuple-element.38), channel_id=1, source_target_pairs={{0,24},{2,26},{4,28},{6,30},{8,16},{10,18},{12,20},{14,22},{16,8},... | collective-permute-start | bytes 393224 | tf_op jit(solution)/shard_map/ppermute | solution.py:104
  11.0 17.5 %collective-permute-start.6 = (bf16[4,128,128]{2,1,0:T(8,128)(2,1)S(1)}, bf16[4,128,128]{2,1,0:T(8,128)(2,1)S(1)}, u32[]{:S(2)}, u32[]{:S(2)}) collective-permute-start(bf16[4,128,128]{2,1,0:T(8,128)(2,1)S(1)} %get-tuple-element.39), channel_id=1, source_target_pairs={{0,16},{2,18},{4,20},{6,22},{8,24},{10,26},{12,28},{14,30},{16,0},... | collective-permute-start | bytes 393224 | tf_op jit(solution)/shard_map/ppermute | solution.py:104
  13.8 14.7 %collective-permute-start.7 = (bf16[4,128,128]{2,1,0:T(8,128)(2,1)S(1)}, bf16[4,128,128]{2,1,0:T(8,128)(2,1)S(1)}, u32[]{:S(2)}, u32[]{:S(2)}) collective-permute-start(bf16[4,128,128]{2,1,0:T(8,128)(2,1)S(1)} %get-tuple-element.40), channel_id=1, source_target_pairs={{0,8},{2,10},{4,12},{6,14},{8,0},{10,2},{12,4},{14,6},{16,24},{18,... | collective-permute-start | bytes 393224 | tf_op jit(solution)/shard_map/ppermute | solution.py:104
  15.4 1.6 %copy-start = (bf16[8,8,128,128]{3,2,1,0:T(8,128)(2,1)S(1)}, bf16[8,8,128,128]{3,2,1,0:T(8,128)(2,1)}, u32[]{:S(2)}) copy-start(bf16[8,8,128,128]{3,2,1,0:T(8,128)(2,1)} %refs_5_.1) | copy-start | bytes 6291460
  17.7 13.8 %collective-permute-start.8 = (bf16[4,128,128]{2,1,0:T(8,128)(2,1)S(1)}, bf16[4,128,128]{2,1,0:T(8,128)(2,1)S(1)}, u32[]{:S(2)}, u32[]{:S(2)}) collective-permute-start(bf16[4,128,128]{2,1,0:T(8,128)(2,1)S(1)} %get-tuple-element.41), channel_id=1, source_target_pairs={{0,24},{2,26},{4,28},{6,30},{8,16},{10,18},{12,20},{14,22},{16,8},... | collective-permute-start | bytes 393224 | tf_op jit(solution)/shard_map/ppermute | solution.py:104
  20.3 10.8 %collective-permute-start.3 = (s32[8,8]{1,0:T(8,128)}, s32[8,8]{1,0:T(8,128)S(1)}, u32[]{:S(2)}, u32[]{:S(2)}) collective-permute-start(s32[8,8]{1,0:T(8,128)} %refs_4_.1), channel_id=1, source_target_pairs={{0,1},{1,0},{2,3},{3,2},{4,5},{5,4},{6,7},{7,6},{8,9},{9,8},{10,11... | collective-permute-start | bytes 776 | tf_op jit(solution)/shard_map/ppermute | solution.py:123
  20.3 13.0 %collective-permute-start.9 = (bf16[4,128,128]{2,1,0:T(8,128)(2,1)S(1)}, bf16[4,128,128]{2,1,0:T(8,128)(2,1)S(1)}, u32[]{:S(2)}, u32[]{:S(2)}) collective-permute-start(bf16[4,128,128]{2,1,0:T(8,128)(2,1)S(1)} %get-tuple-element.42), channel_id=1, source_target_pairs={{0,16},{2,18},{4,20},{6,22},{8,24},{10,26},{12,28},{14,30},{16,0},... | collective-permute-start | bytes 393224 | tf_op jit(solution)/shard_map/ppermute | solution.py:104
  28.5 6.0 %collective-permute-start.10 = (bf16[4,128,128]{2,1,0:T(8,128)(2,1)S(1)}, bf16[4,128,128]{2,1,0:T(8,128)(2,1)S(1)}, u32[]{:S(2)}, u32[]{:S(2)}) collective-permute-start(bf16[4,128,128]{2,1,0:T(8,128)(2,1)S(1)} %get-tuple-element.43), channel_id=1, source_target_pairs={{0,8},{2,10},{4,12},{6,14},{8,0},{10,2},{12,4},{14,6},{16,24},{18,... | collective-permute-start | bytes 393224 | tf_op jit(solution)/shard_map/ppermute | solution.py:104
  28.5 7.1 %collective-permute-start.11 = (bf16[4,128,128]{2,1,0:T(8,128)(2,1)S(1)}, bf16[4,128,128]{2,1,0:T(8,128)(2,1)S(1)}, u32[]{:S(2)}, u32[]{:S(2)}) collective-permute-start(bf16[4,128,128]{2,1,0:T(8,128)(2,1)S(1)} %get-tuple-element.44), channel_id=1, source_target_pairs={{0,6},{2,4},{4,2},{6,0},{8,14},{10,12},{12,10},{14,8},{16,22},{18,... | collective-permute-start | bytes 393224 | tf_op jit(solution)/shard_map/ppermute | solution.py:104
  31.0 5.5 %collective-permute-start.12 = (bf16[4,128,128]{2,1,0:T(8,128)(2,1)S(1)}, bf16[4,128,128]{2,1,0:T(8,128)(2,1)S(1)}, u32[]{:S(2)}, u32[]{:S(2)}) collective-permute-start(bf16[4,128,128]{2,1,0:T(8,128)(2,1)S(1)} %get-tuple-element.45), channel_id=1, source_target_pairs={{0,4},{2,6},{4,0},{6,2},{8,12},{10,14},{12,8},{14,10},{16,20},{18,... | collective-permute-start | bytes 393224 | tf_op jit(solution)/shard_map/ppermute | solution.py:104
  31.6 5.0 %collective-permute-start.13 = (bf16[4,128,128]{2,1,0:T(8,128)(2,1)S(1)}, bf16[4,128,128]{2,1,0:T(8,128)(2,1)S(1)}, u32[]{:S(2)}, u32[]{:S(2)}) collective-permute-start(bf16[4,128,128]{2,1,0:T(8,128)(2,1)S(1)} %get-tuple-element.46), channel_id=1, source_target_pairs={{0,2},{2,0},{4,6},{6,4},{8,10},{10,8},{12,14},{14,12},{16,18},{18,... | collective-permute-start | bytes 393224 | tf_op jit(solution)/shard_map/ppermute | solution.py:104

commit v6 on v5

--- a/solution.py
+++ b/solution.py
@@ -1,5 +1,4 @@
 import functools
-import math
 
 import jax
 import jax.numpy as jnp
@@ -31,21 +30,27 @@
             out_ref[place] = held[sends[0, (me ^ partner) * cap + slot]]
 
 
-def regroup(ins, width, staged, *refs):
-    in_refs, stage_in = refs[:ins], refs[ins : ins + staged]
-    out_refs = refs[ins + staged :]
+def take_opposite(count, staged, *refs):
+    near_refs, stage_in = refs[:count], refs[count : count + staged]
+    out_ref, stage_out, sems = refs[count + staged], refs[count + staged + 1 : count + 2 * staged + 1], refs[-1]
     copies = []
-    if staged:
-        out_refs, stage_out, sems = out_refs[: -staged - 1], out_refs[-staged - 1 : -1], out_refs[-1]
-        for number in range(staged):
-            copy = pltpu.make_async_copy(stage_in[number], stage_out[number], sems.at[number])
-            copy.start()
-            copies.append(copy)
-    for j, out_ref in enumerate(out_refs):
-        for i, in_ref in enumerate(in_refs):
-            out_ref[i * width : (i + 1) * width] = in_ref[(j + 1) * width : (j + 2) * width]
+    for number in range(staged):
+        copy = pltpu.make_async_copy(stage_in[number], stage_out[number], sems.at[number])
+        copy.start()
+        copies.append(copy)
+    width = out_ref.shape[0] // count
+    for spot, near_ref in enumerate(near_refs):
+        out_ref[spot * width : (spot + 1) * width] = near_ref[width:]
     for copy in copies:
         copy.wait()
+
+
+def join_halves(kept_ref, crossed_ref, *out_refs):
+    width = out_refs[0].shape[0] // 2
+    for spot, out_ref in enumerate(out_refs, 1):
+        here = slice(spot * width, (spot + 1) * width)
+        out_ref[:width] = kept_ref[here]
+        out_ref[width:] = crossed_ref[here]
 
 
 def contract(plan, cap, count, *refs):
@@ -79,33 +84,21 @@
         copy.wait()
 
 
-def regrouped(arrays, width, count, staged=()):
-    shape = jax.ShapeDtypeStruct((len(arrays) * width,) + arrays[0].shape[1:], arrays[0].dtype)
-    outs = pl.pallas_call(
-        functools.partial(regroup, len(arrays), width, len(staged)),
-        out_shape=[shape] * count + [jax.ShapeDtypeStruct(s.shape, s.dtype) for s in staged],
-        in_specs=[VMEM] * len(arrays) + [ANYWHERE] * len(staged),
-        out_specs=[VMEM] * (count + len(staged)),
-        scratch_shapes=[pltpu.SemaphoreType.DMA((len(staged),))] if staged else [],
-        compiler_params=GRANT,
-    )(*arrays, *staged)
-    return list(outs[:count]), list(outs[count:])
-
-
 def on_device(wide, narrow, amplitudes, send_list, tile_positions, integrals):
     cap = send_list.shape[1] // wide
     pairs, columns = amplitudes.shape[1:]
     tiles = integrals.shape[0]
-    near = math.isqrt(wide)
-    far = wide // near
+    near = wide // 2
+    spots = sorted(range(near), key=lambda a: (a.bit_count(), a))
     early, late = range(cap // 2), range(cap // 2, cap)
 
     def exchange(array, partner):
         return lax.ppermute(array, "wide", [(d, d ^ partner) for d in range(wide)])
 
-    along = [[(a + near * b, s) for a in range(near) for s in early] for b in range(far)]
-    across = [[(a + near * b, s) for b in range(far) for s in late] for a in range(near)]
-    plan = along + across
+    spread = [[(h * near + a, s) for h in (0, 1) for s in late] for a in spots]
+    facing = [(near + a, s) for a in spots for s in early]
+    kept = [(a, s) for a in spots for s in early]
+    plan = spread + [facing, kept]
     outgoing = pl.pallas_call(
         functools.partial(pick_outgoing, plan, cap),
         out_shape=[jax.ShapeDtypeStruct((len(p), pairs, columns), amplitudes.dtype) for p in plan],
@@ -125,26 +118,36 @@
     else:
         places = [lax.all_gather(tile_positions, "narrow", axis=1, tiled=True)]
         blocks = [lax.all_gather(integrals, "narrow", axis=1, tiled=True)]
-    first_along, first_across = outgoing[:far], outgoing[far:]
-    got_across = [first_across[0]] + [None] * (near - 1)
-    got_along = [first_along[0]] + [None] * (far - 1)
-    for a in range(near - 1, 0, -1):
-        got_across[a] = exchange(first_across[a], a)
-    for b in range(far - 1, 0, -1):
-        got_along[b] = exchange(first_along[b], near * b)
-    second_along, kept = regrouped(got_across, len(late), far - 1, (places[0], blocks[0]) if narrow == 2 else ())
-    if narrow == 2:
-        places[0], blocks[0] = kept
-    second_along, blocks[-1] = lax.optimization_barrier((second_along, blocks[-1]))
-    got_along[0], second_along[-1] = lax.optimization_barrier((got_along[0], second_along[-1]))
-    last_along = [exchange(second_along[b - 1], near * b) for b in range(far - 1, 0, -1)]
-    second_across, _ = regrouped(got_along, len(early), near - 1)
-    last_across = [exchange(second_across[a - 1], a) for a in range(near - 1, 0, -1)]
-    pieces = got_across + got_along[:1] + got_along[:0:-1] + last_along + last_across
-    origins = [list(enumerate((a, s) for s in late)) for a in range(near)]
-    origins += [list(enumerate((near * b, s) for s in early)) for b in [0, *range(far - 1, 0, -1)]]
-    origins += [list(enumerate((a + near * b, s) for a in range(near) for s in late)) for b in range(far - 1, 0, -1)]
-    origins += [list(enumerate((a + near * b, s) for b in range(far) for s in early)) for a in range(near - 1, 0, -1)]
+    cross_first, kept_tiles = outgoing[near:]
+    crossed = exchange(cross_first, near)
+    spread_late = [outgoing[0]] + [exchange(outgoing[i], a) for i, a in enumerate(spots) if a]
+    staged = [places[0], blocks[0]] if narrow == 2 else []
+    cross_second, *staged = pl.pallas_call(
+        functools.partial(take_opposite, near, len(staged)),
+        out_shape=[jax.ShapeDtypeStruct(cross_first.shape, cross_first.dtype)]
+        + [jax.ShapeDtypeStruct(s.shape, s.dtype) for s in staged],
+        in_specs=[VMEM] * near + [ANYWHERE] * len(staged),
+        out_specs=[VMEM] * (1 + len(staged)),
+        scratch_shapes=[pltpu.SemaphoreType.DMA((2,))],
+        compiler_params=GRANT,
+    )(*spread_late, *staged)
+    if staged:
+        places[0], blocks[0] = staged
+    cross_second, blocks[-1], crossed = lax.optimization_barrier((cross_second, blocks[-1])) + (crossed,)
+    crossed_late = exchange(cross_second, near)
+    joined = pl.pallas_call(
+        join_halves,
+        out_shape=[jax.ShapeDtypeStruct(outgoing[0].shape, outgoing[0].dtype)] * (near - 1),
+        in_specs=[VMEM, VMEM],
+        out_specs=[VMEM] * (near - 1),
+        compiler_params=GRANT,
+    )(kept_tiles, crossed)
+    spread_early = [exchange(joined[i - 1], a) for i, a in enumerate(spots) if a]
+    pieces = spread_late + [kept_tiles, crossed] + spread_early + [crossed_late]
+    origins = [list(enumerate((a, s) for s in late)) for a in spots]
+    origins += [list(enumerate((0, s) for s in early)), list(enumerate((near, s) for s in early))]
+    origins += [list(enumerate((h * near + a, s) for h in (0, 1) for s in early)) for a in spots[1:]]
+    origins += [list(enumerate((near + a, s) for a in spots for s in late))]
     count = len(blocks)
     return pl.pallas_call(
         functools.partial(contract, origins, cap, count),

time: 39.6 us -> 47.2 us (1.19)
  starting transfers between devices: 19.2 us -> 23.4 us
  waiting for transfers between devices: 12.7 us -> 15.9 us
  local copies, waits for them, and re-layouts: 3.29 us -> 3.97 us
  Pallas kernels: 4.13 us -> 3.63 us
    ppermute x12 -> x16, starting transfers between devices: 18.7 us -> 22.9 us  [exchange(): return lax.ppermute(array, 'wide', [(d, d ^ partner) for d in range(wide)])]
    ppermute x12 -> x16, waiting for transfers between devices: 12.7 us -> 14.8 us  [exchange(): return lax.ppermute(array, 'wide', [(d, d ^ partner) for d in range(wide)])]
    ppermute x1, waiting for transfers between devices: 0.01 us -> 1.16 us  [on_device(): places = [tile_positions, lax.ppermute(tile_positions, 'narrow', swap)]]
    unnamed x6 -> x8, local copies, waits for them, and re-layouts: 3.29 us -> 3.97 us
    pallas_call x2, Pallas kernels: 0.73 us -> 0.21 us  [the longest x1 0.18 us: on_device(): pl.pallas_call(functools.partial(take_opposite, near, len(staged)), out_s...]
  transfers between devices with their start and end apart: 14 -> 18, of which waited for: 6 -> 7; matrix products, arithmetic and copies ran while one was open for 0% -> 0% of each run, Pallas kernels for 4% -> 2%
where the time goes in v6:
time: 47.2 us; the launch traced here: 47 us
  starting transfers between devices  23.4 us (50%)
  waiting for transfers between devices  15.9 us (34%)
  local copies, waits for them, and re-layouts  3.97 us (8%)
  Pallas kernels  3.63 us (8%)
    ppermute x16, starting transfers between devices, exchange(): return lax.ppermute(array, 'wide', [(d, d ^ partner) for d in range(wide)])  22.9 us
    ppermute x16, waiting for transfers between devices, exchange(): return lax.ppermute(array, 'wide', [(d, d ^ partner) for d in range(wide)])  14.8 us
    unnamed x8, local copies, waits for them, and re-layouts  3.97 us
    pallas_call x1, Pallas kernels, on_device(): pl.pallas_call(functools.partial(contract, origins, cap, count), out_shap...  2.74 us
    ppermute x1, waiting for transfers between devices, on_device(): places = [tile_positions, lax.ppermute(tile_positions, 'narrow', swap)]  1.16 us
  transfers between devices with their start and end apart: 18, of which 7 were waited for; matrix products, arithmetic and copies ran while one was open for 0% of the time, Pallas kernels for 2%

profile of v6, /device:TPU:0, one launch (start us, length us, event | category | flops | bytes accessed | tf_op | source)
XLA Modules:
  0.0 47.0 jit_solution(5941884071147897988)
XLA Ops:
  0.0 0.5 collective-permute-start.16
  0.5 0.0 copy-start.1
  0.5 1.0 %copy-done.1 = bf16[16,128,128]{2,1,0:T(8,128)(2,1)S(1)} copy-done((bf16[16,128,128]{2,1,0:T(8,128)(2,1)S(1)}, bf16[16,128,128]{2,1,0:T(8,128)(2,1)}, u32[]{:S(2)}) %copy-start.1) | copy-done | bytes 524312
  1.5 0.0 copy-start.3
  1.5 0.7 %copy-done.3 = s32[1,32]{1,0:T(1,128)S(1)} copy-done((s32[1,32]{1,0:T(1,128)S(1)}, s32[1,32]{1,0:T(1,128)}, u32[]{:S(2)}) %copy-start.3) | copy-done | bytes 152
  2.2 0.7 %shard_map.46 = (bf16[2,128,128]{2,1,0:T(8,128)(2,1)S(1)}, bf16[2,128,128]{2,1,0:T(8,128)(2,1)S(1)}, bf16[2,128,128]{2,1,0:T(8,128)(2,1)S(1)}, bf16[2,128,128]{2...) custom-call(s32[1,32]{1,0:T(1,128)S(1)} %copy-done.3, ...), custom_call_target="tpu_custom_call" | custom-call | tf_op jit(solution)/shard_map/pallas_call | solution.py:102
  2.8 2.6 %collective-permute-start = (bf16[2,128,128]{2,1,0:T(8,128)(2,1)S(1)}, bf16[2,128,128]{2,1,0:T(8,128)(2,1)S(1)}, u32[]{:S(2)}, u32[]{:S(2)}) collective-permute-start(bf16[2,128,128]{2,1,0:T(8,128)(2,1)S(1)} %get-tuple-element.28), channel_id=1, source_target_pairs={{0,2},{2,0},{4,6},{6,4},{8,10},{10,8},{12,14},{14,12},{16,18},{18,... | collective-permute-start | bytes 196616 | tf_op jit(solution)/shard_map/ppermute | solution.py:96
  5.4 1.5 %collective-permute-start.1 = (bf16[2,128,128]{2,1,0:T(8,128)(2,1)S(1)}, bf16[2,128,128]{2,1,0:T(8,128)(2,1)S(1)}, u32[]{:S(2)}, u32[]{:S(2)}) collective-permute-start(bf16[2,128,128]{2,1,0:T(8,128)(2,1)S(1)} %get-tuple-element.29), channel_id=1, source_target_pairs={{0,4},{2,6},{4,0},{6,2},{8,12},{10,14},{12,8},{14,10},{16,20},{18,... | collective-permute-start | bytes 196616 | tf_op jit(solution)/shard_map/ppermute | solution.py:96
  6.9 1.6 %collective-permute-start.2 = (bf16[2,128,128]{2,1,0:T(8,128)(2,1)S(1)}, bf16[2,128,128]{2,1,0:T(8,128)(2,1)S(1)}, u32[]{:S(2)}, u32[]{:S(2)}) collective-permute-start(bf16[2,128,128]{2,1,0:T(8,128)(2,1)S(1)} %get-tuple-element.30), channel_id=1, source_target_pairs={{0,8},{2,10},{4,12},{6,14},{8,0},{10,2},{12,4},{14,6},{16,24},{18,... | collective-permute-start | bytes 196616 | tf_op jit(solution)/shard_map/ppermute | solution.py:96
  8.5 2.6 %collective-permute-start.8 = (bf16[8,128,128]{2,1,0:T(8,128)(2,1)S(1)}, bf16[8,128,128]{2,1,0:T(8,128)(2,1)S(1)}, u32[]{:S(2)}, u32[]{:S(2)}) collective-permute-start(bf16[8,128,128]{2,1,0:T(8,128)(2,1)S(1)} %get-tuple-element.37), channel_id=1, source_target_pairs={{0,16},{2,18},{4,20},{6,22},{8,24},{10,26},{12,28},{14,30},{16,0},... | collective-permute-start | bytes 786440 | tf_op jit(solution)/shard_map/ppermute | solution.py:96
  11.1 0.0 collective-permute-done.refs_1_.refs_3_
  11.1 0.5 %collective-permute-start.3 = (bf16[2,128,128]{2,1,0:T(8,128)(2,1)S(1)}, bf16[2,128,128]{2,1,0:T(8,128)(2,1)S(1)}, u32[]{:S(2)}, u32[]{:S(2)}) collective-permute-start(bf16[2,128,128]{2,1,0:T(8,128)(2,1)S(1)} %get-tuple-element.31), channel_id=1, source_target_pairs={{0,6},{2,4},{4,2},{6,0},{8,14},{10,12},{12,10},{14,8},{16,22},{18,... | collective-permute-start | bytes 196616 | tf_op jit(solution)/shard_map/ppermute | solution.py:96
  11.6 0.0 collective-permute-done.1.refs_2_.refs_4_
  11.6 1.4 %collective-permute-start.4 = (bf16[2,128,128]{2,1,0:T(8,128)(2,1)S(1)}, bf16[2,128,128]{2,1,0:T(8,128)(2,1)S(1)}, u32[]{:S(2)}, u32[]{:S(2)}) collective-permute-start(bf16[2,128,128]{2,1,0:T(8,128)(2,1)S(1)} %get-tuple-element.32), channel_id=1, source_target_pairs={{0,10},{2,8},{4,14},{6,12},{8,2},{10,0},{12,6},{14,4},{16,26},{18,... | collective-permute-start | bytes 196616 | tf_op jit(solution)/shard_map/ppermute | solution.py:96
  12.9 0.0 collective-permute-done.2.refs_3_.refs_5_
  12.9 2.5 %collective-permute-start.5 = (bf16[2,128,128]{2,1,0:T(8,128)(2,1)S(1)}, bf16[2,128,128]{2,1,0:T(8,128)(2,1)S(1)}, u32[]{:S(2)}, u32[]{:S(2)}) collective-permute-start(bf16[2,128,128]{2,1,0:T(8,128)(2,1)S(1)} %get-tuple-element.33), channel_id=1, source_target_pairs={{0,12},{2,14},{4,8},{6,10},{8,4},{10,6},{12,0},{14,2},{16,28},{18,... | collective-permute-start | bytes 196616 | tf_op jit(solution)/shard_map/ppermute | solution.py:96
  15.5 1.7 %collective-permute-done.3.refs_4_.refs_6_ = bf16[2,128,128]{2,1,0:T(8,128)(2,1)S(1)} collective-permute-done((bf16[2,128,128]{2,1,0:T(8,128)(2,1)S(1)}, bf16[2,128,128]{2,1,0:T(8,128)(2,1)S(1)}, u32[]{:S(2)}, u32[]{:S(2)}) %collective-permute-start.3) | collective-permute-done | bytes 65568 | tf_op jit(solution)/shard_map/ppermute | solution.py:96
  17.2 0.0 collective-permute-start.6
  17.2 2.0 %collective-permute-done.4.refs_5_.refs_7_ = bf16[2,128,128]{2,1,0:T(8,128)(2,1)S(1)} collective-permute-done((bf16[2,128,128]{2,1,0:T(8,128)(2,1)S(1)}, bf16[2,128,128]{2,1,0:T(8,128)(2,1)S(1)}, u32[]{:S(2)}, u32[]{:S(2)}) %collective-permute-start.4) | collective-permute-done | bytes 65568 | tf_op jit(solution)/shard_map/ppermute | solution.py:96
  19.2 4.3 %collective-permute-done.5.refs_6_.refs_8_ = bf16[2,128,128]{2,1,0:T(8,128)(2,1)S(1)} collective-permute-done((bf16[2,128,128]{2,1,0:T(8,128)(2,1)S(1)}, bf16[2,128,128]{2,1,0:T(8,128)(2,1)S(1)}, u32[]{:S(2)}, u32[]{:S(2)}) %collective-permute-start.5) | collective-permute-done | bytes 65568 | tf_op jit(solution)/shard_map/ppermute | solution.py:96
  23.6 0.8 %collective-permute-done.6.refs_7_.refs_9_ = bf16[2,128,128]{2,1,0:T(8,128)(2,1)S(1)} collective-permute-done((bf16[2,128,128]{2,1,0:T(8,128)(2,1)S(1)}, bf16[2,128,128]{2,1,0:T(8,128)(2,1)S(1)}, u32[]{:S(2)}, u32[]{:S(2)}) %collective-permute-start.6) | collective-permute-done | bytes 65568 | tf_op jit(solution)/shard_map/ppermute | solution.py:96
  24.4 0.0 copy-start
  24.4 1.6 %copy-done = bf16[8,8,128,128]{3,2,1,0:T(8,128)(2,1)S(1)} copy-done((bf16[8,8,128,128]{3,2,1,0:T(8,128)(2,1)S(1)}, bf16[8,8,128,128]{3,2,1,0:T(8,128)(2,1)}, u32[]{:S(2)}) %copy-start) | copy-done | bytes 2097176
  26.0 0.0 copy-start.2
  26.0 0.7 %copy-done.2 = s32[8,8]{1,0:T(8,128)S(1)} copy-done((s32[8,8]{1,0:T(8,128)S(1)}, s32[8,8]{1,0:T(8,128)}, u32[]{:S(2)}) %copy-start.2) | copy-done | bytes 280
  26.7 0.2 shard_map.47
  26.8 0.0 collective-permute-done.16.refs_21_
  26.9 0.1 collective-permute-start.17
  26.9 0.0 collective-permute-done.8.crossed_ref.refs_11_
  27.0 1.2 %collective-permute-start.10 = (bf16[2,128,128]{2,1,0:T(8,128)(2,1)S(1)}, bf16[2,128,128]{2,1,0:T(8,128)(2,1)S(1)}, u32[]{:S(2)}, u32[]{:S(2)}) collective-permute-start(bf16[2,128,128]{2,1,0:T(8,128)(2,1)S(1)} %get-tuple-element.39), channel_id=1, source_target_pairs={{0,4},{2,6},{4,0},{6,2},{8,12},{10,14},{12,8},{14,10},{16,20},{18,... | collective-permute-start | bytes 196616 | tf_op jit(solution)/shard_map/ppermute | solution.py:96
  28.1 2.8 %collective-permute-start.11 = (bf16[2,128,128]{2,1,0:T(8,128)(2,1)S(1)}, bf16[2,128,128]{2,1,0:T(8,128)(2,1)S(1)}, u32[]{:S(2)}, u32[]{:S(2)}) collective-permute-start(bf16[2,128,128]{2,1,0:T(8,128)(2,1)S(1)} %get-tuple-element.40), channel_id=1, source_target_pairs={{0,8},{2,10},{4,12},{6,14},{8,0},{10,2},{12,4},{14,6},{16,24},{18,... | collective-permute-start | bytes 196616 | tf_op jit(solution)/shard_map/ppermute | solution.py:96
  30.9 1.7 %collective-permute-start.12 = (bf16[2,128,128]{2,1,0:T(8,128)(2,1)S(1)}, bf16[2,128,128]{2,1,0:T(8,128)(2,1)S(1)}, u32[]{:S(2)}, u32[]{:S(2)}) collective-permute-start(bf16[2,128,128]{2,1,0:T(8,128)(2,1)S(1)} %get-tuple-element.41), channel_id=1, source_target_pairs={{0,6},{2,4},{4,2},{6,0},{8,14},{10,12},{12,10},{14,8},{16,22},{18,... | collective-permute-start | bytes 196616 | tf_op jit(solution)/shard_map/ppermute | solution.py:96
  32.7 0.0 collective-permute-start.7
  32.7 1.2 %collective-permute-done.7.refs_1_ = s32[8,8]{1,0:T(8,128)S(1)} collective-permute-done((s32[8,8]{1,0:T(8,128)S(1)}, s32[8,8]{1,0:T(8,128)S(1)}, u32[]{:S(2)}, u32[]{:S(2)}) %collective-permute-start.7) | collective-permute-done | bytes 288 | tf_op jit(solution)/shard_map/ppermute | solution.py:116
  33.8 0.0 collective-permute-start.13
  33.8 0.0 collective-permute-done.10.refs_13_
  33.9 2.7 %collective-permute-start.14 = (bf16[2,128,128]{2,1,0:T(8,128)(2,1)S(1)}, bf16[2,128,128]{2,1,0:T(8,128)(2,1)S(1)}, u32[]{:S(2)}, u32[]{:S(2)}) collective-permute-start(bf16[2,128,128]{2,1,0:T(8,128)(2,1)S(1)} %get-tuple-element.43), channel_id=1, source_target_pairs={{0,12},{2,14},{4,8},{6,10},{8,4},{10,6},{12,0},{14,2},{16,28},{18,... | collective-permute-start | bytes 196616 | tf_op jit(solution)/shard_map/ppermute | solution.py:96
  36.5 0.0 collective-permute-done.11.refs_14_
  36.5 1.1 %collective-permute-start.15 = (bf16[2,128,128]{2,1,0:T(8,128)(2,1)S(1)}, bf16[2,128,128]{2,1,0:T(8,128)(2,1)S(1)}, u32[]{:S(2)}, u32[]{:S(2)}) collective-permute-start(bf16[2,128,128]{2,1,0:T(8,128)(2,1)S(1)} %get-tuple-element.44), channel_id=1, source_target_pairs={{0,14},{2,12},{4,10},{6,8},{8,6},{10,4},{12,2},{14,0},{16,30},{18,... | collective-permute-start | bytes 196616 | tf_op jit(solution)/shard_map/ppermute | solution.py:96
  37.7 0.0 collective-permute-done.12.refs_15_
  37.7 0.7 %collective-permute-start.9 = (bf16[2,128,128]{2,1,0:T(8,128)(2,1)S(1)}, bf16[2,128,128]{2,1,0:T(8,128)(2,1)S(1)}, u32[]{:S(2)}, u32[]{:S(2)}) collective-permute-start(bf16[2,128,128]{2,1,0:T(8,128)(2,1)S(1)} %get-tuple-element.38), channel_id=1, source_target_pairs={{0,2},{2,0},{4,6},{6,4},{8,10},{10,8},{12,14},{14,12},{16,18},{18,... | collective-permute-start | bytes 196616 | tf_op jit(solution)/shard_map/ppermute | solution.py:96
  38.4 4.2 %collective-permute-done.13.refs_16_ = bf16[2,128,128]{2,1,0:T(8,128)(2,1)S(1)} collective-permute-done((bf16[2,128,128]{2,1,0:T(8,128)(2,1)S(1)}, bf16[2,128,128]{2,1,0:T(8,128)(2,1)S(1)}, u32[]{:S(2)}, u32[]{:S(2)}) %collective-permute-start.13) | collective-permute-done | bytes 65568 | tf_op jit(solution)/shard_map/ppermute | solution.py:96
  42.6 1.6 %collective-permute-done.14.refs_17_ = bf16[2,128,128]{2,1,0:T(8,128)(2,1)S(1)} collective-permute-done((bf16[2,128,128]{2,1,0:T(8,128)(2,1)S(1)}, bf16[2,128,128]{2,1,0:T(8,128)(2,1)S(1)}, u32[]{:S(2)}, u32[]{:S(2)}) %collective-permute-start.14) | collective-permute-done | bytes 65568 | tf_op jit(solution)/shard_map/ppermute | solution.py:96
  44.2 0.0 collective-permute-done.15.refs_18_
  44.2 0.0 collective-permute-done.9.refs_12_
  44.2 0.0 collective-permute-done.17.refs_19_
  44.2 2.7 %shard_map.49 = bf16[8,128,128]{2,1,0:T(8,128)(2,1)} custom-call(s32[8,8]{1,0:T(8,128)S(1)} %get-tuple-element.35.refs_0_, s32[8,8]{1,0:T(8,128)S(1)} %collective-permute-done.7.refs_1_, bf16[2,128,128]{2,1,0:T(8,128)(2,1)S(1)} %get-tuple-element.27.refs_0_.refs_2_, bf16[2,128,128]{2,1,0:T(8,128)(2,1)S(1)} %collective-permute-done.refs_1_.refs_3_, ...), custom_call_target="tpu_custom_call" | custom-call | tf_op jit(solution)/shard_map/pallas_call | solution.py:152
  (1 shorter events, 0.0 us)
Async XLA Ops:
  0.0 26.8 %collective-permute-start.16 = (bf16[8,8,128,128]{3,2,1,0:T(8,128)(2,1)}, bf16[8,8,128,128]{3,2,1,0:T(8,128)(2,1)S(1)}, u32[]{:S(2)}, u32[]{:S(2)}) collective-permute-start(bf16[8,8,128,128]{3,2,1,0:T(8,128)(2,1)} %refs_9_.1), channel_id=1, source_target_pairs={{0,1},{1,0},{2,3},{3,2},{4,5},{5,4},{6,7},{7,6},{8,9},{9,8},{10,11... | collective-permute-start | bytes 6291464 | tf_op jit(solution)/shard_map/ppermute | solution.py:117
  0.5 1.0 %copy-start.1 = (bf16[16,128,128]{2,1,0:T(8,128)(2,1)S(1)}, bf16[16,128,128]{2,1,0:T(8,128)(2,1)}, u32[]{:S(2)}) copy-start(bf16[16,128,128]{2,1,0:T(8,128)(2,1)} %amplitudes_ref.1) | copy-start | bytes 1572868
  1.5 0.7 %copy-start.3 = (s32[1,32]{1,0:T(1,128)S(1)}, s32[1,32]{1,0:T(1,128)}, u32[]{:S(2)}) copy-start(s32[1,32]{1,0:T(1,128)} %send_ref.1) | copy-start | bytes 388
  2.8 8.2 %collective-permute-start = (bf16[2,128,128]{2,1,0:T(8,128)(2,1)S(1)}, bf16[2,128,128]{2,1,0:T(8,128)(2,1)S(1)}, u32[]{:S(2)}, u32[]{:S(2)}) collective-permute-start(bf16[2,128,128]{2,1,0:T(8,128)(2,1)S(1)} %get-tuple-element.28), channel_id=1, source_target_pairs={{0,2},{2,0},{4,6},{6,4},{8,10},{10,8},{12,14},{14,12},{16,18},{18,... | collective-permute-start | bytes 196616 | tf_op jit(solution)/shard_map/ppermute | solution.py:96
  5.4 6.2 %collective-permute-start.1 = (bf16[2,128,128]{2,1,0:T(8,128)(2,1)S(1)}, bf16[2,128,128]{2,1,0:T(8,128)(2,1)S(1)}, u32[]{:S(2)}, u32[]{:S(2)}) collective-permute-start(bf16[2,128,128]{2,1,0:T(8,128)(2,1)S(1)} %get-tuple-element.29), channel_id=1, source_target_pairs={{0,4},{2,6},{4,0},{6,2},{8,12},{10,14},{12,8},{14,10},{16,20},{18,... | collective-permute-start | bytes 196616 | tf_op jit(solution)/shard_map/ppermute | solution.py:96
  6.9 6.0 %collective-permute-start.2 = (bf16[2,128,128]{2,1,0:T(8,128)(2,1)S(1)}, bf16[2,128,128]{2,1,0:T(8,128)(2,1)S(1)}, u32[]{:S(2)}, u32[]{:S(2)}) collective-permute-start(bf16[2,128,128]{2,1,0:T(8,128)(2,1)S(1)} %get-tuple-element.30), channel_id=1, source_target_pairs={{0,8},{2,10},{4,12},{6,14},{8,0},{10,2},{12,4},{14,6},{16,24},{18,... | collective-permute-start | bytes 196616 | tf_op jit(solution)/shard_map/ppermute | solution.py:96
  8.5 18.5 %collective-permute-start.8 = (bf16[8,128,128]{2,1,0:T(8,128)(2,1)S(1)}, bf16[8,128,128]{2,1,0:T(8,128)(2,1)S(1)}, u32[]{:S(2)}, u32[]{:S(2)}) collective-permute-start(bf16[8,128,128]{2,1,0:T(8,128)(2,1)S(1)} %get-tuple-element.37), channel_id=1, source_target_pairs={{0,16},{2,18},{4,20},{6,22},{8,24},{10,26},{12,28},{14,30},{16,0},... | collective-permute-start | bytes 786440 | tf_op jit(solution)/shard_map/ppermute | solution.py:96
  11.1 6.1 %collective-permute-start.3 = (bf16[2,128,128]{2,1,0:T(8,128)(2,1)S(1)}, bf16[2,128,128]{2,1,0:T(8,128)(2,1)S(1)}, u32[]{:S(2)}, u32[]{:S(2)}) collective-permute-start(bf16[2,128,128]{2,1,0:T(8,128)(2,1)S(1)} %get-tuple-element.31), channel_id=1, source_target_pairs={{0,6},{2,4},{4,2},{6,0},{8,14},{10,12},{12,10},{14,8},{16,22},{18,... | collective-permute-start | bytes 196616 | tf_op jit(solution)/shard_map/ppermute | solution.py:96
  11.6 7.7 %collective-permute-start.4 = (bf16[2,128,128]{2,1,0:T(8,128)(2,1)S(1)}, bf16[2,128,128]{2,1,0:T(8,128)(2,1)S(1)}, u32[]{:S(2)}, u32[]{:S(2)}) collective-permute-start(bf16[2,128,128]{2,1,0:T(8,128)(2,1)S(1)} %get-tuple-element.32), channel_id=1, source_target_pairs={{0,10},{2,8},{4,14},{6,12},{8,2},{10,0},{12,6},{14,4},{16,26},{18,... | collective-permute-start | bytes 196616 | tf_op jit(solution)/shard_map/ppermute | solution.py:96
  12.9 10.6 %collective-permute-start.5 = (bf16[2,128,128]{2,1,0:T(8,128)(2,1)S(1)}, bf16[2,128,128]{2,1,0:T(8,128)(2,1)S(1)}, u32[]{:S(2)}, u32[]{:S(2)}) collective-permute-start(bf16[2,128,128]{2,1,0:T(8,128)(2,1)S(1)} %get-tuple-element.33), channel_id=1, source_target_pairs={{0,12},{2,14},{4,8},{6,10},{8,4},{10,6},{12,0},{14,2},{16,28},{18,... | collective-permute-start | bytes 196616 | tf_op jit(solution)/shard_map/ppermute | solution.py:96
  17.2 7.2 %collective-permute-start.6 = (bf16[2,128,128]{2,1,0:T(8,128)(2,1)S(1)}, bf16[2,128,128]{2,1,0:T(8,128)(2,1)S(1)}, u32[]{:S(2)}, u32[]{:S(2)}) collective-permute-start(bf16[2,128,128]{2,1,0:T(8,128)(2,1)S(1)} %get-tuple-element.34), channel_id=1, source_target_pairs={{0,14},{2,12},{4,10},{6,8},{8,6},{10,4},{12,2},{14,0},{16,30},{18,... | collective-permute-start | bytes 196616 | tf_op jit(solution)/shard_map/ppermute | solution.py:96
  24.4 1.6 %copy-start = (bf16[8,8,128,128]{3,2,1,0:T(8,128)(2,1)S(1)}, bf16[8,8,128,128]{3,2,1,0:T(8,128)(2,1)}, u32[]{:S(2)}) copy-start(bf16[8,8,128,128]{3,2,1,0:T(8,128)(2,1)} %refs_9_.1) | copy-start | bytes 6291460
  26.0 0.7 %copy-start.2 = (s32[8,8]{1,0:T(8,128)S(1)}, s32[8,8]{1,0:T(8,128)}, u32[]{:S(2)}) copy-start(s32[8,8]{1,0:T(8,128)} %refs_8_.1) | copy-start | bytes 772
  26.9 17.4 %collective-permute-start.17 = (bf16[8,128,128]{2,1,0:T(8,128)(2,1)S(1)}, bf16[8,128,128]{2,1,0:T(8,128)(2,1)S(1)}, u32[]{:S(2)}, u32[]{:S(2)}) collective-permute-start(bf16[8,128,128]{2,1,0:T(8,128)(2,1)S(1)} %get-tuple-element.46), channel_id=1, source_target_pairs={{0,16},{2,18},{4,20},{6,22},{8,24},{10,26},{12,28},{14,30},{16,0},... | collective-permute-start | bytes 786440 | tf_op jit(solution)/shard_map/ppermute | solution.py:96
  27.0 6.9 %collective-permute-start.10 = (bf16[2,128,128]{2,1,0:T(8,128)(2,1)S(1)}, bf16[2,128,128]{2,1,0:T(8,128)(2,1)S(1)}, u32[]{:S(2)}, u32[]{:S(2)}) collective-permute-start(bf16[2,128,128]{2,1,0:T(8,128)(2,1)S(1)} %get-tuple-element.39), channel_id=1, source_target_pairs={{0,4},{2,6},{4,0},{6,2},{8,12},{10,14},{12,8},{14,10},{16,20},{18,... | collective-permute-start | bytes 196616 | tf_op jit(solution)/shard_map/ppermute | solution.py:96
  28.1 8.4 %collective-permute-start.11 = (bf16[2,128,128]{2,1,0:T(8,128)(2,1)S(1)}, bf16[2,128,128]{2,1,0:T(8,128)(2,1)S(1)}, u32[]{:S(2)}, u32[]{:S(2)}) collective-permute-start(bf16[2,128,128]{2,1,0:T(8,128)(2,1)S(1)} %get-tuple-element.40), channel_id=1, source_target_pairs={{0,8},{2,10},{4,12},{6,14},{8,0},{10,2},{12,4},{14,6},{16,24},{18,... | collective-permute-start | bytes 196616 | tf_op jit(solution)/shard_map/ppermute | solution.py:96
  30.9 6.7 %collective-permute-start.12 = (bf16[2,128,128]{2,1,0:T(8,128)(2,1)S(1)}, bf16[2,128,128]{2,1,0:T(8,128)(2,1)S(1)}, u32[]{:S(2)}, u32[]{:S(2)}) collective-permute-start(bf16[2,128,128]{2,1,0:T(8,128)(2,1)S(1)} %get-tuple-element.41), channel_id=1, source_target_pairs={{0,6},{2,4},{4,2},{6,0},{8,14},{10,12},{12,10},{14,8},{16,22},{18,... | collective-permute-start | bytes 196616 | tf_op jit(solution)/shard_map/ppermute | solution.py:96
  32.7 1.2 %collective-permute-start.7 = (s32[8,8]{1,0:T(8,128)S(1)}, s32[8,8]{1,0:T(8,128)S(1)}, u32[]{:S(2)}, u32[]{:S(2)}) collective-permute-start(s32[8,8]{1,0:T(8,128)S(1)} %copy-done.2), channel_id=1, source_target_pairs={{0,1},{1,0},{2,3},{3,2},{4,5},{5,4},{6,7},{7,6},{8,9},{9,8},{10,11... | collective-permute-start | bytes 776 | tf_op jit(solution)/shard_map/ppermute | solution.py:116
  33.8 8.8 %collective-permute-start.13 = (bf16[2,128,128]{2,1,0:T(8,128)(2,1)S(1)}, bf16[2,128,128]{2,1,0:T(8,128)(2,1)S(1)}, u32[]{:S(2)}, u32[]{:S(2)}) collective-permute-start(bf16[2,128,128]{2,1,0:T(8,128)(2,1)S(1)} %get-tuple-element.42), channel_id=1, source_target_pairs={{0,10},{2,8},{4,14},{6,12},{8,2},{10,0},{12,6},{14,4},{16,26},{18,... | collective-permute-start | bytes 196616 | tf_op jit(solution)/shard_map/ppermute | solution.py:96
  33.9 10.4 %collective-permute-start.14 = (bf16[2,128,128]{2,1,0:T(8,128)(2,1)S(1)}, bf16[2,128,128]{2,1,0:T(8,128)(2,1)S(1)}, u32[]{:S(2)}, u32[]{:S(2)}) collective-permute-start(bf16[2,128,128]{2,1,0:T(8,128)(2,1)S(1)} %get-tuple-element.43), channel_id=1, source_target_pairs={{0,12},{2,14},{4,8},{6,10},{8,4},{10,6},{12,0},{14,2},{16,28},{18,... | collective-permute-start | bytes 196616 | tf_op jit(solution)/shard_map/ppermute | solution.py:96
  36.5 7.7 %collective-permute-start.15 = (bf16[2,128,128]{2,1,0:T(8,128)(2,1)S(1)}, bf16[2,128,128]{2,1,0:T(8,128)(2,1)S(1)}, u32[]{:S(2)}, u32[]{:S(2)}) collective-permute-start(bf16[2,128,128]{2,1,0:T(8,128)(2,1)S(1)} %get-tuple-element.44), channel_id=1, source_target_pairs={{0,14},{2,12},{4,10},{6,8},{8,6},{10,4},{12,2},{14,0},{16,30},{18,... | collective-permute-start | bytes 196616 | tf_op jit(solution)/shard_map/ppermute | solution.py:96
  37.7 6.6 %collective-permute-start.9 = (bf16[2,128,128]{2,1,0:T(8,128)(2,1)S(1)}, bf16[2,128,128]{2,1,0:T(8,128)(2,1)S(1)}, u32[]{:S(2)}, u32[]{:S(2)}) collective-permute-start(bf16[2,128,128]{2,1,0:T(8,128)(2,1)S(1)} %get-tuple-element.38), channel_id=1, source_target_pairs={{0,2},{2,0},{4,6},{6,4},{8,10},{10,8},{12,14},{14,12},{16,18},{18,... | collective-permute-start | bytes 196616 | tf_op jit(solution)/shard_map/ppermute | solution.py:96

commit v7 on v5

--- a/solution.py
+++ b/solution.py
@@ -13,6 +13,8 @@
 ANYWHERE = pl.BlockSpec(memory_space=pl.ANY)
 
 
+PARTS = 4
+LATE = 3
 GRANT = pltpu.CompilerParams(vmem_limit_bytes=48 * 1024 * 1024)
 
 
@@ -27,8 +29,10 @@
     fetch_tiles.wait()
     me = lax.axis_index("wide")
     for wanted, out_ref in zip(plan, out_refs):
-        for place, (partner, slot) in enumerate(wanted):
-            out_ref[place] = held[sends[0, (me ^ partner) * cap + slot]]
+        rows = out_ref.shape[1]
+        for place, (partner, (slot, part)) in enumerate(wanted):
+            tile = sends[0, (me ^ partner) * cap + slot]
+            out_ref[place] = held[tile, part * rows : (part + 1) * rows]
 
 
 def regroup(ins, width, staged, *refs):
@@ -56,8 +60,9 @@
     tiles, per_block, inner, columns = blocks[0].shape
     me = lax.axis_index("wide")
     for origin, piece_ref in zip(plan, pieces):
-        for place, (partner, slot) in origin:
-            received[(me ^ partner) * cap + slot] = piece_ref[place]
+        rows = piece_ref.shape[1]
+        for place, (partner, (slot, part)) in origin:
+            received[(me ^ partner) * cap + slot, part * rows : (part + 1) * rows] = piece_ref[place]
     copies = []
     for x in range(tiles):
         total = None
@@ -98,7 +103,8 @@
     tiles = integrals.shape[0]
     near = math.isqrt(wide)
     far = wide // near
-    early, late = range(cap // 2), range(cap // 2, cap)
+    units = [(slot, part) for slot in range(cap) for part in range(PARTS)]
+    early, late = units[:-LATE], units[-LATE:]
 
     def exchange(array, partner):
         return lax.ppermute(array, "wide", [(d, d ^ partner) for d in range(wide)])
@@ -108,7 +114,7 @@
     plan = along + across
     outgoing = pl.pallas_call(
         functools.partial(pick_outgoing, plan, cap),
-        out_shape=[jax.ShapeDtypeStruct((len(p), pairs, columns), amplitudes.dtype) for p in plan],
+        out_shape=[jax.ShapeDtypeStruct((len(p), pairs // PARTS, columns), amplitudes.dtype) for p in plan],
         in_specs=[ANYWHERE, ANYWHERE],
         out_specs=[VMEM] * len(plan),
         scratch_shapes=[
@@ -138,6 +144,7 @@
     second_along, blocks[-1] = lax.optimization_barrier((second_along, blocks[-1]))
     got_along[0], second_along[-1] = lax.optimization_barrier((got_along[0], second_along[-1]))
     last_along = [exchange(second_along[b - 1], near * b) for b in range(far - 1, 0, -1)]
+    got_along[0], places[-1] = lax.optimization_barrier((got_along[0], places[-1]))
     second_across, _ = regrouped(got_along, len(early), near - 1)
     last_across = [exchange(second_across[a - 1], a) for a in range(near - 1, 0, -1)]
     pieces = got_across + got_along[:1] + got_along[:0:-1] + last_along + last_across

time: 39.6 us -> 40.9 us (1.033)
  starting transfers between devices: 19.2 us -> 21.1 us
  waiting for transfers between devices: 12.7 us -> 11.9 us
  local copies, waits for them, and re-layouts: 3.29 us -> 3.97 us
  Pallas kernels: 4.13 us -> 3.68 us
    ppermute x12, waiting for transfers between devices: 12.7 us -> 10.8 us  [exchange(): return lax.ppermute(array, 'wide', [(d, d ^ partner) for d in range(wide)])]
    ppermute x12, starting transfers between devices: 18.7 us -> 20.6 us  [exchange(): return lax.ppermute(array, 'wide', [(d, d ^ partner) for d in range(wide)])]
    ppermute x1, waiting for transfers between devices: 0.01 us -> 1.16 us  [on_device(): places = [tile_positions, lax.ppermute(tile_positions, 'narrow', swap)]]
    unnamed x6 -> x8, local copies, waits for them, and re-layouts: 3.29 us -> 3.97 us
    pallas_call x2, Pallas kernels: 0.73 us -> 0.22 us  [regrouped(): pl.pallas_call(functools.partial(regroup, len(arrays), width, len(staged)...]
  transfers between devices with their start and end apart: 14 -> 14, of which waited for: 6 -> 5; matrix products, arithmetic and copies ran while one was open for 0% -> 0% of each run, Pallas kernels for 4% -> 2%
where the time goes in v7:
time: 40.9 us; the launch traced here: 40.7 us
  starting transfers between devices  21.1 us (52%)
  waiting for transfers between devices  11.9 us (29%)
  local copies, waits for them, and re-layouts  3.97 us (10%)
  Pallas kernels  3.68 us (9%)
    ppermute x12, starting transfers between devices, exchange(): return lax.ppermute(array, 'wide', [(d, d ^ partner) for d in range(wide)])  20.6 us
    ppermute x12, waiting for transfers between devices, exchange(): return lax.ppermute(array, 'wide', [(d, d ^ partner) for d in range(wide)])  10.8 us
    unnamed x8, local copies, waits for them, and re-layouts  3.97 us
    pallas_call x1, Pallas kernels, on_device(): pl.pallas_call(functools.partial(contract, origins, cap, count), out_shap...  2.74 us
    ppermute x1, waiting for transfers between devices, on_device(): places = [tile_positions, lax.ppermute(tile_positions, 'narrow', swap)]  1.16 us
  transfers between devices with their start and end apart: 14, of which 5 were waited for; matrix products, arithmetic and copies ran while one was open for 0% of the time, Pallas kernels for 2%

profile of v7, /device:TPU:0, one launch (start us, length us, event | category | flops | bytes accessed | tf_op | source)
XLA Modules:
  0.0 40.7 jit_solution(2036848655460421992)
XLA Ops:
  0.0 0.5 %collective-permute-start.3 = (bf16[8,8,128,128]{3,2,1,0:T(8,128)(2,1)}, bf16[8,8,128,128]{3,2,1,0:T(8,128)(2,1)S(1)}, u32[]{:S(2)}, u32[]{:S(2)}) collective-permute-start(bf16[8,8,128,128]{3,2,1,0:T(8,128)(2,1)} %refs_5_.1), channel_id=1, source_target_pairs={{0,1},{1,0},{2,3},{3,2},{4,5},{5,4},{6,7},{7,6},{8,9},{9,8},{10,11... | collective-permute-start | bytes 6291464 | tf_op jit(solution)/shard_map/ppermute | solution.py:130
  0.5 0.0 copy-start.1
  0.5 1.0 %copy-done.1 = bf16[16,128,128]{2,1,0:T(8,128)(2,1)S(1)} copy-done((bf16[16,128,128]{2,1,0:T(8,128)(2,1)S(1)}, bf16[16,128,128]{2,1,0:T(8,128)(2,1)}, u32[]{:S(2)}) %copy-start.1) | copy-done | bytes 524312
  1.5 0.0 copy-start.3
  1.5 0.7 %copy-done.3 = s32[1,32]{1,0:T(1,128)S(1)} copy-done((s32[1,32]{1,0:T(1,128)S(1)}, s32[1,32]{1,0:T(1,128)}, u32[]{:S(2)}) %copy-start.3) | copy-done | bytes 152
  2.2 0.7 %shard_map.46 = (bf16[20,32,128]{2,1,0:T(8,128)(2,1)S(1)}, bf16[20,32,128]{2,1,0:T(8,128)(2,1)S(1)}, bf16[20,32,128]{2,1,0:T(8,128)(2,1)S(1)}, bf16[20,32,128]{2...) custom-call(s32[1,32]{1,0:T(1,128)S(1)} %copy-done.3, ...), custom_call_target="tpu_custom_call" | custom-call | tf_op jit(solution)/shard_map/pallas_call | solution.py:115
  2.9 2.6 %collective-permute-start = (bf16[12,32,128]{2,1,0:T(8,128)(2,1)S(1)}, bf16[12,32,128]{2,1,0:T(8,128)(2,1)S(1)}, u32[]{:S(2)}, u32[]{:S(2)}) collective-permute-start(bf16[12,32,128]{2,1,0:T(8,128)(2,1)S(1)} %get-tuple-element.30), channel_id=1, source_target_pairs={{0,2},{2,0},{4,6},{6,4},{8,10},{10,8},{12,14},{14,12},{16,18},{18,... | collective-permute-start | bytes 294920 | tf_op jit(solution)/shard_map/ppermute | solution.py:110
  5.4 1.5 %collective-permute-start.1 = (bf16[12,32,128]{2,1,0:T(8,128)(2,1)S(1)}, bf16[12,32,128]{2,1,0:T(8,128)(2,1)S(1)}, u32[]{:S(2)}, u32[]{:S(2)}) collective-permute-start(bf16[12,32,128]{2,1,0:T(8,128)(2,1)S(1)} %get-tuple-element.31), channel_id=1, source_target_pairs={{0,4},{2,6},{4,0},{6,2},{8,12},{10,14},{12,8},{14,10},{16,20},{18,... | collective-permute-start | bytes 294920 | tf_op jit(solution)/shard_map/ppermute | solution.py:110
  7.0 3.6 %collective-permute-start.5 = (bf16[20,32,128]{2,1,0:T(8,128)(2,1)S(1)}, bf16[20,32,128]{2,1,0:T(8,128)(2,1)S(1)}, u32[]{:S(2)}, u32[]{:S(2)}) collective-permute-start(bf16[20,32,128]{2,1,0:T(8,128)(2,1)S(1)} %get-tuple-element.42), channel_id=1, source_target_pairs={{0,24},{2,26},{4,28},{6,30},{8,16},{10,18},{12,20},{14,22},{16,8},... | collective-permute-start | bytes 491528 | tf_op jit(solution)/shard_map/ppermute | solution.py:110
  10.6 0.0 collective-permute-start.6
  10.6 0.0 collective-permute-done.refs_1_.refs_3_
  10.6 0.8 %collective-permute-start.7 = (bf16[20,32,128]{2,1,0:T(8,128)(2,1)S(1)}, bf16[20,32,128]{2,1,0:T(8,128)(2,1)S(1)}, u32[]{:S(2)}, u32[]{:S(2)}) collective-permute-start(bf16[20,32,128]{2,1,0:T(8,128)(2,1)S(1)} %get-tuple-element.44), channel_id=1, source_target_pairs={{0,8},{2,10},{4,12},{6,14},{8,0},{10,2},{12,4},{14,6},{16,24},{18,... | collective-permute-start | bytes 491528 | tf_op jit(solution)/shard_map/ppermute | solution.py:110
  11.4 0.0 collective-permute-done.1.refs_2_.refs_4_
  11.4 1.8 %collective-permute-start.2 = (bf16[12,32,128]{2,1,0:T(8,128)(2,1)S(1)}, bf16[12,32,128]{2,1,0:T(8,128)(2,1)S(1)}, u32[]{:S(2)}, u32[]{:S(2)}) collective-permute-start(bf16[12,32,128]{2,1,0:T(8,128)(2,1)S(1)} %get-tuple-element.32), channel_id=1, source_target_pairs={{0,6},{2,4},{4,2},{6,0},{8,14},{10,12},{12,10},{14,8},{16,22},{18,... | collective-permute-start | bytes 294920 | tf_op jit(solution)/shard_map/ppermute | solution.py:110
  13.2 3.7 %collective-permute-done.2.refs_3_.refs_5_ = bf16[12,32,128]{2,1,0:T(8,128)(2,1)S(1)} collective-permute-done((bf16[12,32,128]{2,1,0:T(8,128)(2,1)S(1)}, bf16[12,32,128]{2,1,0:T(8,128)(2,1)S(1)}, u32[]{:S(2)}, u32[]{:S(2)}) %collective-permute-start.2) | collective-permute-done | bytes 98336 | tf_op jit(solution)/shard_map/ppermute | solution.py:110
  16.9 0.0 copy-start
  16.9 1.6 %copy-done = bf16[8,8,128,128]{3,2,1,0:T(8,128)(2,1)S(1)} copy-done((bf16[8,8,128,128]{3,2,1,0:T(8,128)(2,1)S(1)}, bf16[8,8,128,128]{3,2,1,0:T(8,128)(2,1)}, u32[]{:S(2)}) %copy-start) | copy-done | bytes 2097176
  18.5 0.0 copy-start.2
  18.5 0.7 %copy-done.2 = s32[8,8]{1,0:T(8,128)S(1)} copy-done((s32[8,8]{1,0:T(8,128)S(1)}, s32[8,8]{1,0:T(8,128)}, u32[]{:S(2)}) %copy-start.2) | copy-done | bytes 280
  19.2 0.2 shard_map.47
  19.3 0.0 collective-permute-done.3.refs_17_
  19.4 3.7 %collective-permute-start.8 = (bf16[12,32,128]{2,1,0:T(8,128)(2,1)S(1)}, bf16[12,32,128]{2,1,0:T(8,128)(2,1)S(1)}, u32[]{:S(2)}, u32[]{:S(2)}) collective-permute-start(bf16[12,32,128]{2,1,0:T(8,128)(2,1)S(1)} %get-tuple-element.45), channel_id=1, source_target_pairs={{0,24},{2,26},{4,28},{6,30},{8,16},{10,18},{12,20},{14,22},{16,8},... | collective-permute-start | bytes 294920 | tf_op jit(solution)/shard_map/ppermute | solution.py:110
  23.0 0.0 collective-permute-start.4
  23.0 1.2 %collective-permute-done.4.refs_1_ = s32[8,8]{1,0:T(8,128)S(1)} collective-permute-done((s32[8,8]{1,0:T(8,128)S(1)}, s32[8,8]{1,0:T(8,128)S(1)}, u32[]{:S(2)}, u32[]{:S(2)}) %collective-permute-start.4) | collective-permute-done | bytes 288 | tf_op jit(solution)/shard_map/ppermute | solution.py:129
  24.2 0.0 collective-permute-done.5.refs_3_.refs_7_
  24.2 3.4 %collective-permute-done.6.refs_2_.refs_8_ = bf16[20,32,128]{2,1,0:T(8,128)(2,1)S(1)} collective-permute-done((bf16[20,32,128]{2,1,0:T(8,128)(2,1)S(1)}, bf16[20,32,128]{2,1,0:T(8,128)(2,1)S(1)}, u32[]{:S(2)}, u32[]{:S(2)}) %collective-permute-start.6) | collective-permute-done | bytes 163872 | tf_op jit(solution)/shard_map/ppermute | solution.py:110
  27.6 0.0 collective-permute-done.7.refs_1_.refs_9_
  27.7 0.5 %collective-permute-start.11 = (bf16[20,32,128]{2,1,0:T(8,128)(2,1)S(1)}, bf16[20,32,128]{2,1,0:T(8,128)(2,1)S(1)}, u32[]{:S(2)}, u32[]{:S(2)}) collective-permute-start(bf16[20,32,128]{2,1,0:T(8,128)(2,1)S(1)} %get-tuple-element.48), channel_id=1, source_target_pairs={{0,6},{2,4},{4,2},{6,0},{8,14},{10,12},{12,10},{14,8},{16,22},{18,... | collective-permute-start | bytes 491528 | tf_op jit(solution)/shard_map/ppermute | solution.py:110
  28.2 1.5 %collective-permute-start.12 = (bf16[20,32,128]{2,1,0:T(8,128)(2,1)S(1)}, bf16[20,32,128]{2,1,0:T(8,128)(2,1)S(1)}, u32[]{:S(2)}, u32[]{:S(2)}) collective-permute-start(bf16[20,32,128]{2,1,0:T(8,128)(2,1)S(1)} %get-tuple-element.49), channel_id=1, source_target_pairs={{0,4},{2,6},{4,0},{6,2},{8,12},{10,14},{12,8},{14,10},{16,20},{18,... | collective-permute-start | bytes 491528 | tf_op jit(solution)/shard_map/ppermute | solution.py:110
  29.7 1.5 %collective-permute-start.13 = (bf16[20,32,128]{2,1,0:T(8,128)(2,1)S(1)}, bf16[20,32,128]{2,1,0:T(8,128)(2,1)S(1)}, u32[]{:S(2)}, u32[]{:S(2)}) collective-permute-start(bf16[20,32,128]{2,1,0:T(8,128)(2,1)S(1)} %get-tuple-element.50), channel_id=1, source_target_pairs={{0,2},{2,0},{4,6},{6,4},{8,10},{10,8},{12,14},{14,12},{16,18},{18,... | collective-permute-start | bytes 491528 | tf_op jit(solution)/shard_map/ppermute | solution.py:110
  31.2 0.0 collective-permute-start.9
  31.2 0.0 collective-permute-done.8.refs_10_
  31.2 3.1 %collective-permute-start.10 = (bf16[12,32,128]{2,1,0:T(8,128)(2,1)S(1)}, bf16[12,32,128]{2,1,0:T(8,128)(2,1)S(1)}, u32[]{:S(2)}, u32[]{:S(2)}) collective-permute-start(bf16[12,32,128]{2,1,0:T(8,128)(2,1)S(1)} %get-tuple-element.47), channel_id=1, source_target_pairs={{0,8},{2,10},{4,12},{6,14},{8,0},{10,2},{12,4},{14,6},{16,24},{18,... | collective-permute-start | bytes 294920 | tf_op jit(solution)/shard_map/ppermute | solution.py:110
  34.3 3.2 %collective-permute-done.9.refs_11_ = bf16[12,32,128]{2,1,0:T(8,128)(2,1)S(1)} collective-permute-done((bf16[12,32,128]{2,1,0:T(8,128)(2,1)S(1)}, bf16[12,32,128]{2,1,0:T(8,128)(2,1)S(1)}, u32[]{:S(2)}, u32[]{:S(2)}) %collective-permute-start.9) | collective-permute-done | bytes 98336 | tf_op jit(solution)/shard_map/ppermute | solution.py:110
  37.5 0.4 %collective-permute-done.10.refs_12_ = bf16[12,32,128]{2,1,0:T(8,128)(2,1)S(1)} collective-permute-done((bf16[12,32,128]{2,1,0:T(8,128)(2,1)S(1)}, bf16[12,32,128]{2,1,0:T(8,128)(2,1)S(1)}, u32[]{:S(2)}, u32[]{:S(2)}) %collective-permute-start.10) | collective-permute-done | bytes 98336 | tf_op jit(solution)/shard_map/ppermute | solution.py:110
  38.0 0.0 collective-permute-done.11.refs_13_
  38.0 0.0 collective-permute-done.12.refs_14_
  38.0 0.0 collective-permute-done.13.refs_15_
  38.0 2.7 %shard_map.49 = bf16[8,128,128]{2,1,0:T(8,128)(2,1)} custom-call(s32[8,8]{1,0:T(8,128)S(1)} %get-tuple-element.33.refs_0_, s32[8,8]{1,0:T(8,128)S(1)} %collective-permute-done.4.refs_1_, bf16[12,32,128]{2,1,0:T(8,128)(2,1)S(1)} %get-tuple-element.29.refs_0_.refs_2_, bf16[12,32,128]{2,1,0:T(8,128)(2,1)S(1)} %collective-permute-done.refs_1_.refs_3_, ...), custom_call_target="tpu_custom_call" | custom-call | tf_op jit(solution)/shard_map/pallas_call | solution.py:156
  (1 shorter events, 0.0 us)
Async XLA Ops:
  0.0 19.3 %collective-permute-start.3 = (bf16[8,8,128,128]{3,2,1,0:T(8,128)(2,1)}, bf16[8,8,128,128]{3,2,1,0:T(8,128)(2,1)S(1)}, u32[]{:S(2)}, u32[]{:S(2)}) collective-permute-start(bf16[8,8,128,128]{3,2,1,0:T(8,128)(2,1)} %refs_5_.1), channel_id=1, source_target_pairs={{0,1},{1,0},{2,3},{3,2},{4,5},{5,4},{6,7},{7,6},{8,9},{9,8},{10,11... | collective-permute-start | bytes 6291464 | tf_op jit(solution)/shard_map/ppermute | solution.py:130
  0.5 1.0 %copy-start.1 = (bf16[16,128,128]{2,1,0:T(8,128)(2,1)S(1)}, bf16[16,128,128]{2,1,0:T(8,128)(2,1)}, u32[]{:S(2)}) copy-start(bf16[16,128,128]{2,1,0:T(8,128)(2,1)} %amplitudes_ref.1) | copy-start | bytes 1572868
  1.5 0.7 %copy-start.3 = (s32[1,32]{1,0:T(1,128)S(1)}, s32[1,32]{1,0:T(1,128)}, u32[]{:S(2)}) copy-start(s32[1,32]{1,0:T(1,128)} %send_ref.1) | copy-start | bytes 388
  2.9 7.7 %collective-permute-start = (bf16[12,32,128]{2,1,0:T(8,128)(2,1)S(1)}, bf16[12,32,128]{2,1,0:T(8,128)(2,1)S(1)}, u32[]{:S(2)}, u32[]{:S(2)}) collective-permute-start(bf16[12,32,128]{2,1,0:T(8,128)(2,1)S(1)} %get-tuple-element.30), channel_id=1, source_target_pairs={{0,2},{2,0},{4,6},{6,4},{8,10},{10,8},{12,14},{14,12},{16,18},{18,... | collective-permute-start | bytes 294920 | tf_op jit(solution)/shard_map/ppermute | solution.py:110
  5.4 5.9 %collective-permute-start.1 = (bf16[12,32,128]{2,1,0:T(8,128)(2,1)S(1)}, bf16[12,32,128]{2,1,0:T(8,128)(2,1)S(1)}, u32[]{:S(2)}, u32[]{:S(2)}) collective-permute-start(bf16[12,32,128]{2,1,0:T(8,128)(2,1)S(1)} %get-tuple-element.31), channel_id=1, source_target_pairs={{0,4},{2,6},{4,0},{6,2},{8,12},{10,14},{12,8},{14,10},{16,20},{18,... | collective-permute-start | bytes 294920 | tf_op jit(solution)/shard_map/ppermute | solution.py:110
  7.0 17.2 %collective-permute-start.5 = (bf16[20,32,128]{2,1,0:T(8,128)(2,1)S(1)}, bf16[20,32,128]{2,1,0:T(8,128)(2,1)S(1)}, u32[]{:S(2)}, u32[]{:S(2)}) collective-permute-start(bf16[20,32,128]{2,1,0:T(8,128)(2,1)S(1)} %get-tuple-element.42), channel_id=1, source_target_pairs={{0,24},{2,26},{4,28},{6,30},{8,16},{10,18},{12,20},{14,22},{16,8},... | collective-permute-start | bytes 491528 | tf_op jit(solution)/shard_map/ppermute | solution.py:110
  10.6 17.0 %collective-permute-start.6 = (bf16[20,32,128]{2,1,0:T(8,128)(2,1)S(1)}, bf16[20,32,128]{2,1,0:T(8,128)(2,1)S(1)}, u32[]{:S(2)}, u32[]{:S(2)}) collective-permute-start(bf16[20,32,128]{2,1,0:T(8,128)(2,1)S(1)} %get-tuple-element.43), channel_id=1, source_target_pairs={{0,16},{2,18},{4,20},{6,22},{8,24},{10,26},{12,28},{14,30},{16,0},... | collective-permute-start | bytes 491528 | tf_op jit(solution)/shard_map/ppermute | solution.py:110
  10.6 17.0 %collective-permute-start.7 = (bf16[20,32,128]{2,1,0:T(8,128)(2,1)S(1)}, bf16[20,32,128]{2,1,0:T(8,128)(2,1)S(1)}, u32[]{:S(2)}, u32[]{:S(2)}) collective-permute-start(bf16[20,32,128]{2,1,0:T(8,128)(2,1)S(1)} %get-tuple-element.44), channel_id=1, source_target_pairs={{0,8},{2,10},{4,12},{6,14},{8,0},{10,2},{12,4},{14,6},{16,24},{18,... | collective-permute-start | bytes 491528 | tf_op jit(solution)/shard_map/ppermute | solution.py:110
  11.4 5.5 %collective-permute-start.2 = (bf16[12,32,128]{2,1,0:T(8,128)(2,1)S(1)}, bf16[12,32,128]{2,1,0:T(8,128)(2,1)S(1)}, u32[]{:S(2)}, u32[]{:S(2)}) collective-permute-start(bf16[12,32,128]{2,1,0:T(8,128)(2,1)S(1)} %get-tuple-element.32), channel_id=1, source_target_pairs={{0,6},{2,4},{4,2},{6,0},{8,14},{10,12},{12,10},{14,8},{16,22},{18,... | collective-permute-start | bytes 294920 | tf_op jit(solution)/shard_map/ppermute | solution.py:110
  16.9 1.6 %copy-start = (bf16[8,8,128,128]{3,2,1,0:T(8,128)(2,1)S(1)}, bf16[8,8,128,128]{3,2,1,0:T(8,128)(2,1)}, u32[]{:S(2)}) copy-start(bf16[8,8,128,128]{3,2,1,0:T(8,128)(2,1)} %refs_5_.1) | copy-start | bytes 6291460
  18.5 0.7 %copy-start.2 = (s32[8,8]{1,0:T(8,128)S(1)}, s32[8,8]{1,0:T(8,128)}, u32[]{:S(2)}) copy-start(s32[8,8]{1,0:T(8,128)} %refs_4_.1) | copy-start | bytes 772
  19.4 11.9 %collective-permute-start.8 = (bf16[12,32,128]{2,1,0:T(8,128)(2,1)S(1)}, bf16[12,32,128]{2,1,0:T(8,128)(2,1)S(1)}, u32[]{:S(2)}, u32[]{:S(2)}) collective-permute-start(bf16[12,32,128]{2,1,0:T(8,128)(2,1)S(1)} %get-tuple-element.45), channel_id=1, source_target_pairs={{0,24},{2,26},{4,28},{6,30},{8,16},{10,18},{12,20},{14,22},{16,8},... | collective-permute-start | bytes 294920 | tf_op jit(solution)/shard_map/ppermute | solution.py:110
  23.0 1.2 %collective-permute-start.4 = (s32[8,8]{1,0:T(8,128)S(1)}, s32[8,8]{1,0:T(8,128)S(1)}, u32[]{:S(2)}, u32[]{:S(2)}) collective-permute-start(s32[8,8]{1,0:T(8,128)S(1)} %copy-done.2), channel_id=1, source_target_pairs={{0,1},{1,0},{2,3},{3,2},{4,5},{5,4},{6,7},{7,6},{8,9},{9,8},{10,11... | collective-permute-start | bytes 776 | tf_op jit(solution)/shard_map/ppermute | solution.py:129
  27.7 10.3 %collective-permute-start.11 = (bf16[20,32,128]{2,1,0:T(8,128)(2,1)S(1)}, bf16[20,32,128]{2,1,0:T(8,128)(2,1)S(1)}, u32[]{:S(2)}, u32[]{:S(2)}) collective-permute-start(bf16[20,32,128]{2,1,0:T(8,128)(2,1)S(1)} %get-tuple-element.48), channel_id=1, source_target_pairs={{0,6},{2,4},{4,2},{6,0},{8,14},{10,12},{12,10},{14,8},{16,22},{18,... | collective-permute-start | bytes 491528 | tf_op jit(solution)/shard_map/ppermute | solution.py:110
  28.2 9.8 %collective-permute-start.12 = (bf16[20,32,128]{2,1,0:T(8,128)(2,1)S(1)}, bf16[20,32,128]{2,1,0:T(8,128)(2,1)S(1)}, u32[]{:S(2)}, u32[]{:S(2)}) collective-permute-start(bf16[20,32,128]{2,1,0:T(8,128)(2,1)S(1)} %get-tuple-element.49), channel_id=1, source_target_pairs={{0,4},{2,6},{4,0},{6,2},{8,12},{10,14},{12,8},{14,10},{16,20},{18,... | collective-permute-start | bytes 491528 | tf_op jit(solution)/shard_map/ppermute | solution.py:110
  29.7 8.3 %collective-permute-start.13 = (bf16[20,32,128]{2,1,0:T(8,128)(2,1)S(1)}, bf16[20,32,128]{2,1,0:T(8,128)(2,1)S(1)}, u32[]{:S(2)}, u32[]{:S(2)}) collective-permute-start(bf16[20,32,128]{2,1,0:T(8,128)(2,1)S(1)} %get-tuple-element.50), channel_id=1, source_target_pairs={{0,2},{2,0},{4,6},{6,4},{8,10},{10,8},{12,14},{14,12},{16,18},{18,... | collective-permute-start | bytes 491528 | tf_op jit(solution)/shard_map/ppermute | solution.py:110
  31.2 6.3 %collective-permute-start.9 = (bf16[12,32,128]{2,1,0:T(8,128)(2,1)S(1)}, bf16[12,32,128]{2,1,0:T(8,128)(2,1)S(1)}, u32[]{:S(2)}, u32[]{:S(2)}) collective-permute-start(bf16[12,32,128]{2,1,0:T(8,128)(2,1)S(1)} %get-tuple-element.46), channel_id=1, source_target_pairs={{0,16},{2,18},{4,20},{6,22},{8,24},{10,26},{12,28},{14,30},{16,0},... | collective-permute-start | bytes 294920 | tf_op jit(solution)/shard_map/ppermute | solution.py:110
  31.2 6.7 %collective-permute-start.10 = (bf16[12,32,128]{2,1,0:T(8,128)(2,1)S(1)}, bf16[12,32,128]{2,1,0:T(8,128)(2,1)S(1)}, u32[]{:S(2)}, u32[]{:S(2)}) collective-permute-start(bf16[12,32,128]{2,1,0:T(8,128)(2,1)S(1)} %get-tuple-element.47), channel_id=1, source_target_pairs={{0,8},{2,10},{4,12},{6,14},{8,0},{10,2},{12,4},{14,6},{16,24},{18,... | collective-permute-start | bytes 294920 | tf_op jit(solution)/shard_map/ppermute | solution.py:110

commit v8 on v7

--- a/solution.py
+++ b/solution.py
@@ -30,26 +30,16 @@
     me = lax.axis_index("wide")
     for wanted, out_ref in zip(plan, out_refs):
         rows = out_ref.shape[1]
-        for place, (partner, (slot, part)) in enumerate(wanted):
-            tile = sends[0, (me ^ partner) * cap + slot]
+        for place, (relative, partner, (slot, part)) in enumerate(wanted):
+            tile = sends[0, (relative * me ^ partner) * cap + slot]
             out_ref[place] = held[tile, part * rows : (part + 1) * rows]
 
 
-def regroup(ins, width, staged, *refs):
-    in_refs, stage_in = refs[:ins], refs[ins : ins + staged]
-    out_refs = refs[ins + staged :]
-    copies = []
-    if staged:
-        out_refs, stage_out, sems = out_refs[: -staged - 1], out_refs[-staged - 1 : -1], out_refs[-1]
-        for number in range(staged):
-            copy = pltpu.make_async_copy(stage_in[number], stage_out[number], sems.at[number])
-            copy.start()
-            copies.append(copy)
+def regroup(ins, width, *refs):
+    in_refs, out_refs = refs[:ins], refs[ins:]
     for j, out_ref in enumerate(out_refs):
         for i, in_ref in enumerate(in_refs):
             out_ref[i * width : (i + 1) * width] = in_ref[(j + 1) * width : (j + 2) * width]
-    for copy in copies:
-        copy.wait()
 
 
 def contract(plan, cap, count, *refs):
@@ -61,8 +51,8 @@
     me = lax.axis_index("wide")
     for origin, piece_ref in zip(plan, pieces):
         rows = piece_ref.shape[1]
-        for place, (partner, (slot, part)) in origin:
-            received[(me ^ partner) * cap + slot, part * rows : (part + 1) * rows] = piece_ref[place]
+        for place, (relative, partner, (slot, part)) in origin:
+            received[(relative * me ^ partner) * cap + slot, part * rows : (part + 1) * rows] = piece_ref[place]
     copies = []
     for x in range(tiles):
         total = None
@@ -84,17 +74,15 @@
         copy.wait()
 
 
-def regrouped(arrays, width, count, staged=()):
+def regrouped(arrays, width, count):
     shape = jax.ShapeDtypeStruct((len(arrays) * width,) + arrays[0].shape[1:], arrays[0].dtype)
-    outs = pl.pallas_call(
-        functools.partial(regroup, len(arrays), width, len(staged)),
-        out_shape=[shape] * count + [jax.ShapeDtypeStruct(s.shape, s.dtype) for s in staged],
-        in_specs=[VMEM] * len(arrays) + [ANYWHERE] * len(staged),
-        out_specs=[VMEM] * (count + len(staged)),
-        scratch_shapes=[pltpu.SemaphoreType.DMA((len(staged),))] if staged else [],
+    return pl.pallas_call(
+        functools.partial(regroup, len(arrays), width),
+        out_shape=[shape] * count,
+        in_specs=[VMEM] * len(arrays),
+        out_specs=[VMEM] * count,
         compiler_params=GRANT,
-    )(*arrays, *staged)
-    return list(outs[:count]), list(outs[count:])
+    )(*arrays)
 
 
 def on_device(wide, narrow, amplitudes, send_list, tile_positions, integrals):
@@ -109,9 +97,9 @@
     def exchange(array, partner):
         return lax.ppermute(array, "wide", [(d, d ^ partner) for d in range(wide)])
 
-    along = [[(a + near * b, s) for a in range(near) for s in early] for b in range(far)]
-    across = [[(a + near * b, s) for b in range(far) for s in late] for a in range(near)]
-    plan = along + across
+    along = [[(1, a + near * b, s) for a in range(near) for s in early] for b in range(far)]
+    everyone = [(0, d, s) for d in range(wide) for s in late]
+    plan = along + [everyone]
     outgoing = pl.pallas_call(
         functools.partial(pick_outgoing, plan, cap),
         out_shape=[jax.ShapeDtypeStruct((len(p), pairs // PARTS, columns), amplitudes.dtype) for p in plan],
@@ -131,27 +119,16 @@
     else:
         places = [lax.all_gather(tile_positions, "narrow", axis=1, tiled=True)]
         blocks = [lax.all_gather(integrals, "narrow", axis=1, tiled=True)]
-    first_along, first_across = outgoing[:far], outgoing[far:]
-    got_across = [first_across[0]] + [None] * (near - 1)
-    got_along = [first_along[0]] + [None] * (far - 1)
-    for a in range(near - 1, 0, -1):
-        got_across[a] = exchange(first_across[a], a)
+    got_along = [outgoing[0]] + [None] * (far - 1)
     for b in range(far - 1, 0, -1):
-        got_along[b] = exchange(first_along[b], near * b)
-    second_along, kept = regrouped(got_across, len(late), far - 1, (places[0], blocks[0]) if narrow == 2 else ())
-    if narrow == 2:
-        places[0], blocks[0] = kept
-    second_along, blocks[-1] = lax.optimization_barrier((second_along, blocks[-1]))
-    got_along[0], second_along[-1] = lax.optimization_barrier((got_along[0], second_along[-1]))
-    last_along = [exchange(second_along[b - 1], near * b) for b in range(far - 1, 0, -1)]
-    got_along[0], places[-1] = lax.optimization_barrier((got_along[0], places[-1]))
-    second_across, _ = regrouped(got_along, len(early), near - 1)
-    last_across = [exchange(second_across[a - 1], a) for a in range(near - 1, 0, -1)]
-    pieces = got_across + got_along[:1] + got_along[:0:-1] + last_along + last_across
-    origins = [list(enumerate((a, s) for s in late)) for a in range(near)]
-    origins += [list(enumerate((near * b, s) for s in early)) for b in [0, *range(far - 1, 0, -1)]]
-    origins += [list(enumerate((a + near * b, s) for a in range(near) for s in late)) for b in range(far - 1, 0, -1)]
-    origins += [list(enumerate((a + near * b, s) for b in range(far) for s in early)) for a in range(near - 1, 0, -1)]
+        got_along[b] = exchange(outgoing[b], near * b)
+    direct = lax.all_to_all(outgoing[far], "wide", split_axis=0, concat_axis=0, tiled=True)
+    across = regrouped(got_along, len(early), near - 1)
+    got_across = [exchange(across[a - 1], a) for a in range(near - 1, 0, -1)]
+    pieces = [direct] + got_along[:1] + got_along[:0:-1] + got_across
+    origins = [list(enumerate(everyone))]
+    origins += [list(enumerate((1, near * b, s) for s in early)) for b in [0, *range(far - 1, 0, -1)]]
+    origins += [list(enumerate((1, a + near * b, s) for b in range(far) for s in early)) for a in range(near - 1, 0, -1)]
     count = len(blocks)
     return pl.pallas_call(
         functools.partial(contract, origins, cap, count),

time: 40.9 us -> 54.8 us (1.34)
  waiting for transfers between devices: 11.9 us -> 28.3 us
  starting transfers between devices: 21.1 us -> 16.3 us
  local copies, waits for them, and re-layouts: 3.97 us -> 5.55 us
  Pallas kernels: 3.68 us -> 4.24 us
    ppermute x12 -> x6, waiting for transfers between devices: 10.8 us -> 26.9 us  [exchange(): return lax.ppermute(array, 'wide', [(d, d ^ partner) for d in range(wide)])]
    ppermute x12 -> x6, starting transfers between devices: 20.6 us -> 8.01 us  [exchange(): return lax.ppermute(array, 'wide', [(d, d ^ partner) for d in range(wide)])]
    all_to_all x0 -> x1, starting transfers between devices: none -> 7.88 us  [on_device(): lax.all_to_all(outgoing[far], 'wide', split_axis=0, concat_axis=0, tiled=...]
    unnamed x8 -> x12, local copies, waits for them, and re-layouts: 3.97 us -> 5.55 us
    pallas_call x1, Pallas kernels: 0.73 us -> 1.5 us  [on_device(): pl.pallas_call(functools.partial(pick_outgoing, plan, cap), out_shape=[ja...]
  transfers between devices with their start and end apart: 14 -> 9, of which waited for: 5 -> 5; matrix products, arithmetic and copies ran while one was open for 0% -> 0% of each run, Pallas kernels for 2% -> 3%
where the time goes in v8:
time: 54.8 us; the launch traced here: 54.5 us
  waiting for transfers between devices  28.3 us (52%)
  starting transfers between devices  16.3 us (30%)
  local copies, waits for them, and re-layouts  5.55 us (10%)
  Pallas kernels  4.24 us (8%)
    ppermute x6, waiting for transfers between devices, exchange(): return lax.ppermute(array, 'wide', [(d, d ^ partner) for d in range(wide)])  26.9 us
    ppermute x6, starting transfers between devices, exchange(): return lax.ppermute(array, 'wide', [(d, d ^ partner) for d in range(wide)])  8.01 us
    all_to_all x1, starting transfers between devices, on_device(): lax.all_to_all(outgoing[far], 'wide', split_axis=0, concat_axis=0, tiled=...  7.88 us
    unnamed x12, local copies, waits for them, and re-layouts  5.55 us
    pallas_call x1, Pallas kernels, on_device(): pl.pallas_call(functools.partial(contract, origins, cap, count), out_shap...  2.7 us
    pallas_call x1, Pallas kernels, on_device(): pl.pallas_call(functools.partial(pick_outgoing, plan, cap), out_shape=[ja...  1.5 us
    ppermute x1, waiting for transfers between devices, on_device(): places = [tile_positions, lax.ppermute(tile_positions, 'narrow', swap)]  1.37 us
  transfers between devices with their start and end apart: 9, of which 5 were waited for; matrix products, arithmetic and copies ran while one was open for 0% of the time, Pallas kernels for 3%

profile of v8, /device:TPU:0, one launch (start us, length us, event | category | flops | bytes accessed | tf_op | source)
XLA Modules:
  0.0 54.5 jit_solution(17903179897511414264)
XLA Ops:
  0.0 0.5 collective-permute-start.7
  0.5 0.0 copy-start.1
  0.5 1.0 %copy-done.1 = bf16[16,128,128]{2,1,0:T(8,128)(2,1)S(1)} copy-done((bf16[16,128,128]{2,1,0:T(8,128)(2,1)S(1)}, bf16[16,128,128]{2,1,0:T(8,128)(2,1)}, u32[]{:S(2)}) %copy-start.1) | copy-done | bytes 524312
  1.5 0.0 copy-start.5
  1.5 0.7 %copy-done.5 = s32[1,32]{1,0:T(1,128)S(1)} copy-done((s32[1,32]{1,0:T(1,128)S(1)}, s32[1,32]{1,0:T(1,128)}, u32[]{:S(2)}) %copy-start.5) | copy-done | bytes 152
  2.2 1.5 %shard_map.46 = (bf16[20,32,128]{2,1,0:T(8,128)(2,1)S(1)}, bf16[20,32,128]{2,1,0:T(8,128)(2,1)S(1)}, bf16[20,32,128]{2,1,0:T(8,128)(2,1)S(1)}, bf16[20,32,128]{2,1,0:T(8,128)(2,1)}, bf16[48,32,128]{2,1,0:T(8,128)(2,1)}) custom-call(s32[1,32]{1,0:T(1,128)S(1)} %copy-done.5, bf16[16,128,128]{2,1,0:T(8,128)(2,1)S(1)} %copy-done.1), custom_call_target="tpu_custom_call" | custom-call | tf_op jit(solution)/shard_map/pallas_call | solution.py:103
  3.7 7.9 %all-to-all-start = ((bf16[48,32,128]{2,1,0:T(8,128)(2,1)}), bf16[48,32,128]{2,1,0:T(8,128)(2,1)S(1)}, u32[]{:S(2)}, u32[]{:S(2)}) async-start(bf16[48,32,128]{2,1,0:T(8,128)(2,1)} %get-tuple-element.13), calls=%async_computation | async-start | bytes 786432 | tf_op jit(solution)/shard_map/all_to_all | solution.py:125
  11.5 3.8 %collective-permute-start.1 = (bf16[20,32,128]{2,1,0:T(8,128)(2,1)}, bf16[20,32,128]{2,1,0:T(8,128)(2,1)S(1)}, u32[]{:S(2)}, u32[]{:S(2)}) collective-permute-start(bf16[20,32,128]{2,1,0:T(8,128)(2,1)} %get-tuple-element.15), channel_id=1, source_target_pairs={{0,24},{2,26},{4,28},{6,30},{8,16},{10,18},{12,20},{14,22},{16,8},... | collective-permute-start | bytes 491528 | tf_op jit(solution)/shard_map/ppermute | solution.py:98
  15.3 0.0 collective-permute-start.2
  15.3 0.7 %collective-permute-start.3 = (bf16[20,32,128]{2,1,0:T(8,128)(2,1)S(1)}, bf16[20,32,128]{2,1,0:T(8,128)(2,1)S(1)}, u32[]{:S(2)}, u32[]{:S(2)}) collective-permute-start(bf16[20,32,128]{2,1,0:T(8,128)(2,1)S(1)} %get-tuple-element.17), channel_id=1, source_target_pairs={{0,8},{2,10},{4,12},{6,14},{8,0},{10,2},{12,4},{14,6},{16,24},{18,... | collective-permute-start | bytes 491528 | tf_op jit(solution)/shard_map/ppermute | solution.py:98
  16.0 10.9 %collective-permute-done.1.refs_3_.refs_4_ = bf16[20,32,128]{2,1,0:T(8,128)(2,1)S(1)} collective-permute-done((bf16[20,32,128]{2,1,0:T(8,128)(2,1)}, bf16[20,32,128]{2,1,0:T(8,128)(2,1)S(1)}, u32[]{:S(2)}, u32[]{:S(2)}) %collective-permute-start.1) | collective-permute-done | bytes 163872 | tf_op jit(solution)/shard_map/ppermute | solution.py:98
  26.9 10.9 %collective-permute-done.2.refs_2_.refs_5_ = bf16[20,32,128]{2,1,0:T(8,128)(2,1)S(1)} collective-permute-done((bf16[20,32,128]{2,1,0:T(8,128)(2,1)S(1)}, bf16[20,32,128]{2,1,0:T(8,128)(2,1)S(1)}, u32[]{:S(2)}, u32[]{:S(2)}) %collective-permute-start.2) | collective-permute-done | bytes 163872 | tf_op jit(solution)/shard_map/ppermute | solution.py:98
  37.8 0.0 collective-permute-done.3.refs_1_.refs_6_
  37.9 2.4 %collective-permute-start.4 = (bf16[20,32,128]{2,1,0:T(8,128)(2,1)S(1)}, bf16[20,32,128]{2,1,0:T(8,128)(2,1)S(1)}, u32[]{:S(2)}, u32[]{:S(2)}) collective-permute-start(bf16[20,32,128]{2,1,0:T(8,128)(2,1)S(1)} %get-tuple-element.18), channel_id=1, source_target_pairs={{0,6},{2,4},{4,2},{6,0},{8,14},{10,12},{12,10},{14,8},{16,22},{18,... | collective-permute-start | bytes 491528 | tf_op jit(solution)/shard_map/ppermute | solution.py:98
  40.3 0.6 %collective-permute-start.5 = (bf16[20,32,128]{2,1,0:T(8,128)(2,1)S(1)}, bf16[20,32,128]{2,1,0:T(8,128)(2,1)S(1)}, u32[]{:S(2)}, u32[]{:S(2)}) collective-permute-start(bf16[20,32,128]{2,1,0:T(8,128)(2,1)S(1)} %get-tuple-element.19), channel_id=1, source_target_pairs={{0,4},{2,6},{4,0},{6,2},{8,12},{10,14},{12,8},{14,10},{16,20},{18,... | collective-permute-start | bytes 491528 | tf_op jit(solution)/shard_map/ppermute | solution.py:98
  40.9 0.6 %collective-permute-start.6 = (bf16[20,32,128]{2,1,0:T(8,128)(2,1)S(1)}, bf16[20,32,128]{2,1,0:T(8,128)(2,1)S(1)}, u32[]{:S(2)}, u32[]{:S(2)}) collective-permute-start(bf16[20,32,128]{2,1,0:T(8,128)(2,1)S(1)} %get-tuple-element.20), channel_id=1, source_target_pairs={{0,2},{2,0},{4,6},{6,4},{8,10},{10,8},{12,14},{14,12},{16,18},{18,... | collective-permute-start | bytes 491528 | tf_op jit(solution)/shard_map/ppermute | solution.py:98
  41.4 0.0 collective-permute-start
  41.4 1.4 %collective-permute-done.refs_1_ = s32[8,8]{1,0:T(8,128)S(1)} collective-permute-done((s32[8,8]{1,0:T(8,128)}, s32[8,8]{1,0:T(8,128)S(1)}, u32[]{:S(2)}, u32[]{:S(2)}) %collective-permute-start) | collective-permute-done | bytes 288 | tf_op jit(solution)/shard_map/ppermute | solution.py:117
  42.8 2.7 %collective-permute-done.4.refs_7_ = bf16[20,32,128]{2,1,0:T(8,128)(2,1)S(1)} collective-permute-done((bf16[20,32,128]{2,1,0:T(8,128)(2,1)S(1)}, bf16[20,32,128]{2,1,0:T(8,128)(2,1)S(1)}, u32[]{:S(2)}, u32[]{:S(2)}) %collective-permute-start.4) | collective-permute-done | bytes 163872 | tf_op jit(solution)/shard_map/ppermute | solution.py:98
  45.5 2.3 %collective-permute-done.5.refs_8_ = bf16[20,32,128]{2,1,0:T(8,128)(2,1)S(1)} collective-permute-done((bf16[20,32,128]{2,1,0:T(8,128)(2,1)S(1)}, bf16[20,32,128]{2,1,0:T(8,128)(2,1)S(1)}, u32[]{:S(2)}, u32[]{:S(2)}) %collective-permute-start.5) | collective-permute-done | bytes 163872 | tf_op jit(solution)/shard_map/ppermute | solution.py:98
  47.9 0.0 collective-permute-done.6.refs_9_
  47.9 0.0 copy-start.2
  47.9 0.7 %copy-done.2 = bf16[20,32,128]{2,1,0:T(8,128)(2,1)} copy-done((bf16[20,32,128]{2,1,0:T(8,128)(2,1)}, bf16[20,32,128]{2,1,0:T(8,128)(2,1)S(1)}, u32[]{:S(2)}) %copy-start.2) | copy-done | bytes 163864
  48.5 0.0 all-to-all-done.refs_2_
  48.5 0.0 collective-permute-done.7.refs_11_
  48.6 0.0 copy-start
  48.6 1.6 %copy-done = bf16[8,8,128,128]{3,2,1,0:T(8,128)(2,1)S(1)} copy-done((bf16[8,8,128,128]{3,2,1,0:T(8,128)(2,1)S(1)}, bf16[8,8,128,128]{3,2,1,0:T(8,128)(2,1)}, u32[]{:S(2)}) %copy-start) | copy-done | bytes 2097176
  50.1 0.0 copy-start.3
  50.1 0.9 %copy-done.3 = bf16[20,32,128]{2,1,0:T(8,128)(2,1)S(1)} copy-done((bf16[20,32,128]{2,1,0:T(8,128)(2,1)S(1)}, bf16[20,32,128]{2,1,0:T(8,128)(2,1)}, u32[]{:S(2)}) %copy-start.3) | copy-done | bytes 163864
  51.1 0.0 copy-start.4
  51.1 0.7 %copy-done.4 = s32[8,8]{1,0:T(8,128)S(1)} copy-done((s32[8,8]{1,0:T(8,128)S(1)}, s32[8,8]{1,0:T(8,128)}, u32[]{:S(2)}) %copy-start.4) | copy-done | bytes 280
  51.8 2.7 %shard_map.48 = bf16[8,128,128]{2,1,0:T(8,128)(2,1)} custom-call(s32[8,8]{1,0:T(8,128)S(1)} %copy-done.4, s32[8,8]{1,0:T(8,128)S(1)} %collective-permute-done.refs_1_, bf16[48,32,128]{2,1,0:T(8,128)(2,1)S(1)} %all-to-all-done.refs_2_, bf16[20,32,128]{2,1,0:T(8,128)(2,1)S(1)} %get-tuple-element.14.refs_0_.refs_3_, ...), custom_call_target="tpu_custom_call" | custom-call | tf_op jit(solution)/shard_map/pallas_call | solution.py:133
  (1 shorter events, 0.0 us)
Async XLA Ops:
  0.0 48.6 %collective-permute-start.7 = (bf16[8,8,128,128]{3,2,1,0:T(8,128)(2,1)}, bf16[8,8,128,128]{3,2,1,0:T(8,128)(2,1)S(1)}, u32[]{:S(2)}, u32[]{:S(2)}) collective-permute-start(bf16[8,8,128,128]{3,2,1,0:T(8,128)(2,1)} %refs_10_.1), channel_id=1, source_target_pairs={{0,1},{1,0},{2,3},{3,2},{4,5},{5,4},{6,7},{7,6},{8,9},{9,8},{10,11... | collective-permute-start | bytes 6291464 | tf_op jit(solution)/shard_map/ppermute | solution.py:118
  0.5 1.0 %copy-start.1 = (bf16[16,128,128]{2,1,0:T(8,128)(2,1)S(1)}, bf16[16,128,128]{2,1,0:T(8,128)(2,1)}, u32[]{:S(2)}) copy-start(bf16[16,128,128]{2,1,0:T(8,128)(2,1)} %amplitudes_ref.1) | copy-start | bytes 1572868
  1.5 0.7 %copy-start.5 = (s32[1,32]{1,0:T(1,128)S(1)}, s32[1,32]{1,0:T(1,128)}, u32[]{:S(2)}) copy-start(s32[1,32]{1,0:T(1,128)} %send_ref.1) | copy-start | bytes 388
  3.7 44.9 %all-to-all-start = ((bf16[48,32,128]{2,1,0:T(8,128)(2,1)}), bf16[48,32,128]{2,1,0:T(8,128)(2,1)S(1)}, u32[]{:S(2)}, u32[]{:S(2)}) async-start(bf16[48,32,128]{2,1,0:T(8,128)(2,1)} %get-tuple-element.13), calls=%async_computation | async-start | bytes 786432 | tf_op jit(solution)/shard_map/all_to_all | solution.py:125
  11.5 15.4 %collective-permute-start.1 = (bf16[20,32,128]{2,1,0:T(8,128)(2,1)}, bf16[20,32,128]{2,1,0:T(8,128)(2,1)S(1)}, u32[]{:S(2)}, u32[]{:S(2)}) collective-permute-start(bf16[20,32,128]{2,1,0:T(8,128)(2,1)} %get-tuple-element.15), channel_id=1, source_target_pairs={{0,24},{2,26},{4,28},{6,30},{8,16},{10,18},{12,20},{14,22},{16,8},... | collective-permute-start | bytes 491528 | tf_op jit(solution)/shard_map/ppermute | solution.py:98
  15.3 22.5 %collective-permute-start.2 = (bf16[20,32,128]{2,1,0:T(8,128)(2,1)S(1)}, bf16[20,32,128]{2,1,0:T(8,128)(2,1)S(1)}, u32[]{:S(2)}, u32[]{:S(2)}) collective-permute-start(bf16[20,32,128]{2,1,0:T(8,128)(2,1)S(1)} %get-tuple-element.16), channel_id=1, source_target_pairs={{0,16},{2,18},{4,20},{6,22},{8,24},{10,26},{12,28},{14,30},{16,0},... | collective-permute-start | bytes 491528 | tf_op jit(solution)/shard_map/ppermute | solution.py:98
  15.3 22.5 %collective-permute-start.3 = (bf16[20,32,128]{2,1,0:T(8,128)(2,1)S(1)}, bf16[20,32,128]{2,1,0:T(8,128)(2,1)S(1)}, u32[]{:S(2)}, u32[]{:S(2)}) collective-permute-start(bf16[20,32,128]{2,1,0:T(8,128)(2,1)S(1)} %get-tuple-element.17), channel_id=1, source_target_pairs={{0,8},{2,10},{4,12},{6,14},{8,0},{10,2},{12,4},{14,6},{16,24},{18,... | collective-permute-start | bytes 491528 | tf_op jit(solution)/shard_map/ppermute | solution.py:98
  37.9 7.6 %collective-permute-start.4 = (bf16[20,32,128]{2,1,0:T(8,128)(2,1)S(1)}, bf16[20,32,128]{2,1,0:T(8,128)(2,1)S(1)}, u32[]{:S(2)}, u32[]{:S(2)}) collective-permute-start(bf16[20,32,128]{2,1,0:T(8,128)(2,1)S(1)} %get-tuple-element.18), channel_id=1, source_target_pairs={{0,6},{2,4},{4,2},{6,0},{8,14},{10,12},{12,10},{14,8},{16,22},{18,... | collective-permute-start | bytes 491528 | tf_op jit(solution)/shard_map/ppermute | solution.py:98
  40.3 7.6 %collective-permute-start.5 = (bf16[20,32,128]{2,1,0:T(8,128)(2,1)S(1)}, bf16[20,32,128]{2,1,0:T(8,128)(2,1)S(1)}, u32[]{:S(2)}, u32[]{:S(2)}) collective-permute-start(bf16[20,32,128]{2,1,0:T(8,128)(2,1)S(1)} %get-tuple-element.19), channel_id=1, source_target_pairs={{0,4},{2,6},{4,0},{6,2},{8,12},{10,14},{12,8},{14,10},{16,20},{18,... | collective-permute-start | bytes 491528 | tf_op jit(solution)/shard_map/ppermute | solution.py:98
  40.9 7.0 %collective-permute-start.6 = (bf16[20,32,128]{2,1,0:T(8,128)(2,1)S(1)}, bf16[20,32,128]{2,1,0:T(8,128)(2,1)S(1)}, u32[]{:S(2)}, u32[]{:S(2)}) collective-permute-start(bf16[20,32,128]{2,1,0:T(8,128)(2,1)S(1)} %get-tuple-element.20), channel_id=1, source_target_pairs={{0,2},{2,0},{4,6},{6,4},{8,10},{10,8},{12,14},{14,12},{16,18},{18,... | collective-permute-start | bytes 491528 | tf_op jit(solution)/shard_map/ppermute | solution.py:98
  41.4 1.4 %collective-permute-start = (s32[8,8]{1,0:T(8,128)}, s32[8,8]{1,0:T(8,128)S(1)}, u32[]{:S(2)}, u32[]{:S(2)}) collective-permute-start(s32[8,8]{1,0:T(8,128)} %refs_0_.1), channel_id=1, source_target_pairs={{0,1},{1,0},{2,3},{3,2},{4,5},{5,4},{6,7},{7,6},{8,9},{9,8},{10,11... | collective-permute-start | bytes 776 | tf_op jit(solution)/shard_map/ppermute | solution.py:117
  47.9 0.7 %copy-start.2 = (bf16[20,32,128]{2,1,0:T(8,128)(2,1)}, bf16[20,32,128]{2,1,0:T(8,128)(2,1)S(1)}, u32[]{:S(2)}) copy-start(bf16[20,32,128]{2,1,0:T(8,128)(2,1)S(1)} %collective-permute-done.6.refs_9_) | copy-start | bytes 491524
  48.6 1.6 %copy-start = (bf16[8,8,128,128]{3,2,1,0:T(8,128)(2,1)S(1)}, bf16[8,8,128,128]{3,2,1,0:T(8,128)(2,1)}, u32[]{:S(2)}) copy-start(bf16[8,8,128,128]{3,2,1,0:T(8,128)(2,1)} %refs_10_.1) | copy-start | bytes 6291460
  50.1 0.9 %copy-start.3 = (bf16[20,32,128]{2,1,0:T(8,128)(2,1)S(1)}, bf16[20,32,128]{2,1,0:T(8,128)(2,1)}, u32[]{:S(2)}) copy-start(bf16[20,32,128]{2,1,0:T(8,128)(2,1)} %copy-done.2) | copy-start | bytes 491524
  51.1 0.7 %copy-start.4 = (s32[8,8]{1,0:T(8,128)S(1)}, s32[8,8]{1,0:T(8,128)}, u32[]{:S(2)}) copy-start(s32[8,8]{1,0:T(8,128)} %refs_0_.1) | copy-start | bytes 772

commit v9 on v7

--- a/solution.py
+++ b/solution.py
@@ -14,7 +14,7 @@
 
 
 PARTS = 4
-LATE = 3
+LATE = 5
 GRANT = pltpu.CompilerParams(vmem_limit_bytes=48 * 1024 * 1024)
 
 
@@ -138,20 +138,29 @@
         got_across[a] = exchange(first_across[a], a)
     for b in range(far - 1, 0, -1):
         got_along[b] = exchange(first_along[b], near * b)
-    second_along, kept = regrouped(got_across, len(late), far - 1, (places[0], blocks[0]) if narrow == 2 else ())
-    if narrow == 2:
-        places[0], blocks[0] = kept
+    second_along, _ = regrouped(got_across, len(late), far - 1)
     second_along, blocks[-1] = lax.optimization_barrier((second_along, blocks[-1]))
     got_along[0], second_along[-1] = lax.optimization_barrier((got_along[0], second_along[-1]))
     last_along = [exchange(second_along[b - 1], near * b) for b in range(far - 1, 0, -1)]
-    got_along[0], places[-1] = lax.optimization_barrier((got_along[0], places[-1]))
-    second_across, _ = regrouped(got_along, len(early), near - 1)
-    last_across = [exchange(second_across[a - 1], a) for a in range(near - 1, 0, -1)]
+    if narrow == 2:
+        got_along[0], places[-1] = lax.optimization_barrier((got_along[0], places[-1]))
+    sets = [range(far // 2), range(far - 1, far // 2 - 1, -1)]
+    last_across = []
+    for members in sets:
+        staged = (places[0], blocks[0]) if narrow == 2 and members is sets[1] else ()
+        second_across, staged = regrouped([got_along[b] for b in members], len(early), near - 1, staged)
+        if staged:
+            places[0], blocks[0] = staged
+        last_across += [exchange(second_across[a - 1], a) for a in range(near - 1, 0, -1)]
     pieces = got_across + got_along[:1] + got_along[:0:-1] + last_along + last_across
     origins = [list(enumerate((a, s) for s in late)) for a in range(near)]
     origins += [list(enumerate((near * b, s) for s in early)) for b in [0, *range(far - 1, 0, -1)]]
     origins += [list(enumerate((a + near * b, s) for a in range(near) for s in late)) for b in range(far - 1, 0, -1)]
-    origins += [list(enumerate((a + near * b, s) for b in range(far) for s in early)) for a in range(near - 1, 0, -1)]
+    origins += [
+        list(enumerate((a + near * b, s) for b in members for s in early))
+        for members in sets
+        for a in range(near - 1, 0, -1)
+    ]
     count = len(blocks)
     return pl.pallas_call(
         functools.partial(contract, origins, cap, count),

time: 40.9 us -> 46.3 us (1.13)
  starting transfers between devices: 21.1 us -> 27.2 us
  waiting for transfers between devices: 11.9 us -> 11.2 us
    ppermute x12 -> x15, starting transfers between devices: 20.6 us -> 26.7 us  [exchange(): return lax.ppermute(array, 'wide', [(d, d ^ partner) for d in range(wide)])]
    ppermute x1, waiting for transfers between devices: 1.16 us -> 0.01 us  [on_device(): places = [tile_positions, lax.ppermute(tile_positions, 'narrow', swap)]]
    ppermute x12 -> x15, waiting for transfers between devices: 10.8 us -> 11.2 us  [exchange(): return lax.ppermute(array, 'wide', [(d, d ^ partner) for d in range(wide)])]
  transfers between devices with their start and end apart: 14 -> 17, of which waited for: 5 -> 8; matrix products, arithmetic and copies ran while one was open for 0% -> 0% of each run, Pallas kernels for 2% -> 2%
where the time goes in v9:
time: 46.3 us; the launch traced here: 46.1 us
  starting transfers between devices  27.2 us (59%)
  waiting for transfers between devices  11.2 us (24%)
  local copies, waits for them, and re-layouts  3.97 us (9%)
  Pallas kernels  3.69 us (8%)
    ppermute x15, starting transfers between devices, exchange(): return lax.ppermute(array, 'wide', [(d, d ^ partner) for d in range(wide)])  26.7 us
    ppermute x15, waiting for transfers between devices, exchange(): return lax.ppermute(array, 'wide', [(d, d ^ partner) for d in range(wide)])  11.2 us
    unnamed x8, local copies, waits for them, and re-layouts  3.97 us
    pallas_call x1, Pallas kernels, on_device(): pl.pallas_call(functools.partial(contract, origins, cap, count), out_shap...  2.74 us
  transfers between devices with their start and end apart: 17, of which 8 were waited for; matrix products, arithmetic and copies ran while one was open for 0% of the time, Pallas kernels for 2%

profile of v9, /device:TPU:0, one launch (start us, length us, event | category | flops | bytes accessed | tf_op | source)
XLA Modules:
  0.0 46.1 jit_solution(10369074350857976686)
XLA Ops:
  0.0 0.5 collective-permute-start.5
  0.5 0.0 copy-start.1
  0.5 1.0 %copy-done.1 = bf16[16,128,128]{2,1,0:T(8,128)(2,1)S(1)} copy-done((bf16[16,128,128]{2,1,0:T(8,128)(2,1)S(1)}, bf16[16,128,128]{2,1,0:T(8,128)(2,1)}, u32[]{:S(2)}) %copy-start.1) | copy-done | bytes 524312
  1.5 0.0 copy-start.3
  1.5 0.7 %copy-done.3 = s32[1,32]{1,0:T(1,128)S(1)} copy-done((s32[1,32]{1,0:T(1,128)S(1)}, s32[1,32]{1,0:T(1,128)}, u32[]{:S(2)}) %copy-start.3) | copy-done | bytes 152
  2.2 0.7 %shard_map.46 = (bf16[12,32,128]{2,1,0:T(8,128)(2,1)S(1)}, bf16[12,32,128]{2,1,0:T(8,128)(2,1)S(1)}, bf16[12,32,128]{2,1,0:T(8,128)(2,1)S(1)}, bf16[12,32,128]{2...) custom-call(s32[1,32]{1,0:T(1,128)S(1)} %copy-done.3, ...), custom_call_target="tpu_custom_call" | custom-call | tf_op jit(solution)/shard_map/pallas_call | solution.py:115
  2.9 2.6 %collective-permute-start.2 = (bf16[20,32,128]{2,1,0:T(8,128)(2,1)S(1)}, bf16[20,32,128]{2,1,0:T(8,128)(2,1)S(1)}, u32[]{:S(2)}, u32[]{:S(2)}) collective-permute-start(bf16[20,32,128]{2,1,0:T(8,128)(2,1)S(1)} %get-tuple-element.37), channel_id=1, source_target_pairs={{0,2},{2,0},{4,6},{6,4},{8,10},{10,8},{12,14},{14,12},{16,18},{18,... | collective-permute-start | bytes 491528 | tf_op jit(solution)/shard_map/ppermute | solution.py:110
  5.4 1.5 %collective-permute-start.3 = (bf16[20,32,128]{2,1,0:T(8,128)(2,1)S(1)}, bf16[20,32,128]{2,1,0:T(8,128)(2,1)S(1)}, u32[]{:S(2)}, u32[]{:S(2)}) collective-permute-start(bf16[20,32,128]{2,1,0:T(8,128)(2,1)S(1)} %get-tuple-element.38), channel_id=1, source_target_pairs={{0,4},{2,6},{4,0},{6,2},{8,12},{10,14},{12,8},{14,10},{16,20},{18,... | collective-permute-start | bytes 491528 | tf_op jit(solution)/shard_map/ppermute | solution.py:110
  7.0 0.0 collective-permute-start.4
  7.0 4.1 %collective-permute-start = (bf16[12,32,128]{2,1,0:T(8,128)(2,1)S(1)}, bf16[12,32,128]{2,1,0:T(8,128)(2,1)S(1)}, u32[]{:S(2)}, u32[]{:S(2)}) collective-permute-start(bf16[12,32,128]{2,1,0:T(8,128)(2,1)S(1)} %get-tuple-element.32), channel_id=1, source_target_pairs={{0,24},{2,26},{4,28},{6,30},{8,16},{10,18},{12,20},{14,22},{16,8},... | collective-permute-start | bytes 294920 | tf_op jit(solution)/shard_map/ppermute | solution.py:110
  11.0 0.0 collective-permute-done.2.refs_1_.refs_3_
  11.0 2.5 %collective-permute-start.1 = (bf16[12,32,128]{2,1,0:T(8,128)(2,1)S(1)}, bf16[12,32,128]{2,1,0:T(8,128)(2,1)S(1)}, u32[]{:S(2)}, u32[]{:S(2)}) collective-permute-start(bf16[12,32,128]{2,1,0:T(8,128)(2,1)S(1)} %get-tuple-element.33), channel_id=1, source_target_pairs={{0,16},{2,18},{4,20},{6,22},{8,24},{10,26},{12,28},{14,30},{16,0},... | collective-permute-start | bytes 294920 | tf_op jit(solution)/shard_map/ppermute | solution.py:110
  13.5 1.7 %collective-permute-done.3.refs_2_.refs_4_ = bf16[20,32,128]{2,1,0:T(8,128)(2,1)S(1)} collective-permute-done((bf16[20,32,128]{2,1,0:T(8,128)(2,1)S(1)}, bf16[20,32,128]{2,1,0:T(8,128)(2,1)S(1)}, u32[]{:S(2)}, u32[]{:S(2)}) %collective-permute-start.3) | collective-permute-done | bytes 163872 | tf_op jit(solution)/shard_map/ppermute | solution.py:110
  15.3 1.6 %collective-permute-start.7 = (bf16[12,32,128]{2,1,0:T(8,128)(2,1)S(1)}, bf16[12,32,128]{2,1,0:T(8,128)(2,1)S(1)}, u32[]{:S(2)}, u32[]{:S(2)}) collective-permute-start(bf16[12,32,128]{2,1,0:T(8,128)(2,1)S(1)} %get-tuple-element.47), channel_id=1, source_target_pairs={{0,8},{2,10},{4,12},{6,14},{8,0},{10,2},{12,4},{14,6},{16,24},{18,... | collective-permute-start | bytes 294920 | tf_op jit(solution)/shard_map/ppermute | solution.py:110
  16.9 0.0 collective-permute-done.4.refs_3_.refs_5_
  16.9 0.0 collective-permute-done.5.refs_20_
  16.9 2.5 %collective-permute-start.8 = (bf16[20,32,128]{2,1,0:T(8,128)(2,1)S(1)}, bf16[20,32,128]{2,1,0:T(8,128)(2,1)S(1)}, u32[]{:S(2)}, u32[]{:S(2)}) collective-permute-start(bf16[20,32,128]{2,1,0:T(8,128)(2,1)S(1)} %get-tuple-element.48), channel_id=1, source_target_pairs={{0,24},{2,26},{4,28},{6,30},{8,16},{10,18},{12,20},{14,22},{16,8},... | collective-permute-start | bytes 491528 | tf_op jit(solution)/shard_map/ppermute | solution.py:110
  19.5 0.2 collective-permute-start.9
  19.6 0.0 collective-permute-done.refs_0_.refs_7_
  19.7 1.7 %collective-permute-start.10 = (bf16[20,32,128]{2,1,0:T(8,128)(2,1)S(1)}, bf16[20,32,128]{2,1,0:T(8,128)(2,1)S(1)}, u32[]{:S(2)}, u32[]{:S(2)}) collective-permute-start(bf16[20,32,128]{2,1,0:T(8,128)(2,1)S(1)} %get-tuple-element.50), channel_id=1, source_target_pairs={{0,8},{2,10},{4,12},{6,14},{8,0},{10,2},{12,4},{14,6},{16,24},{18,... | collective-permute-start | bytes 491528 | tf_op jit(solution)/shard_map/ppermute | solution.py:110
  21.4 0.1 collective-permute-done.1.refs_1_.refs_8_
  21.4 0.0 collective-permute-start.6
  21.4 0.0 copy-start
  21.4 1.6 %copy-done = bf16[8,8,128,128]{3,2,1,0:T(8,128)(2,1)S(1)} copy-done((bf16[8,8,128,128]{3,2,1,0:T(8,128)(2,1)S(1)}, bf16[8,8,128,128]{3,2,1,0:T(8,128)(2,1)}, u32[]{:S(2)}) %copy-start) | copy-done | bytes 2097176
  23.0 0.0 copy-start.2
  23.0 0.7 %copy-done.2 = s32[8,8]{1,0:T(8,128)S(1)} copy-done((s32[8,8]{1,0:T(8,128)S(1)}, s32[8,8]{1,0:T(8,128)}, u32[]{:S(2)}) %copy-start.2) | copy-done | bytes 280
  23.7 0.2 shard_map.47
  23.9 0.0 collective-permute-done.6.refs_1_
  23.9 6.3 %collective-permute-start.14 = (bf16[6,32,128]{2,1,0:T(8,128)(2,1)S(1)}, bf16[6,32,128]{2,1,0:T(8,128)(2,1)S(1)}, u32[]{:S(2)}, u32[]{:S(2)}) collective-permute-start(bf16[6,32,128]{2,1,0:T(8,128)(2,1)S(1)} %get-tuple-element.54), channel_id=1, source_target_pairs={{0,6},{2,4},{4,2},{6,0},{8,14},{10,12},{12,10},{14,8},{16,22},{18,... | collective-permute-start | bytes 147464 | tf_op jit(solution)/shard_map/ppermute | solution.py:110
  30.2 0.0 collective-permute-done.7.refs_1_.refs_9_
  30.2 0.0 collective-permute-start.15
  30.2 2.4 %collective-permute-done.14.refs_16_ = bf16[6,32,128]{2,1,0:T(8,128)(2,1)S(1)} collective-permute-done((bf16[6,32,128]{2,1,0:T(8,128)(2,1)S(1)}, bf16[6,32,128]{2,1,0:T(8,128)(2,1)S(1)}, u32[]{:S(2)}, u32[]{:S(2)}) %collective-permute-start.14) | collective-permute-done | bytes 49184 | tf_op jit(solution)/shard_map/ppermute | solution.py:110
  32.6 0.0 collective-permute-start.16
  32.6 1.7 %collective-permute-done.15.refs_17_ = bf16[6,32,128]{2,1,0:T(8,128)(2,1)S(1)} collective-permute-done((bf16[6,32,128]{2,1,0:T(8,128)(2,1)S(1)}, bf16[6,32,128]{2,1,0:T(8,128)(2,1)S(1)}, u32[]{:S(2)}, u32[]{:S(2)}) %collective-permute-start.15) | collective-permute-done | bytes 49184 | tf_op jit(solution)/shard_map/ppermute | solution.py:110
  34.3 1.2 %collective-permute-start.11 = (bf16[6,32,128]{2,1,0:T(8,128)(2,1)S(1)}, bf16[6,32,128]{2,1,0:T(8,128)(2,1)S(1)}, u32[]{:S(2)}, u32[]{:S(2)}) collective-permute-start(bf16[6,32,128]{2,1,0:T(8,128)(2,1)S(1)} %get-tuple-element.51), channel_id=1, source_target_pairs={{0,6},{2,4},{4,2},{6,0},{8,14},{10,12},{12,10},{14,8},{16,22},{18,... | collective-permute-start | bytes 147464 | tf_op jit(solution)/shard_map/ppermute | solution.py:110
  35.5 1.2 %collective-permute-done.16.refs_18_ = bf16[6,32,128]{2,1,0:T(8,128)(2,1)S(1)} collective-permute-done((bf16[6,32,128]{2,1,0:T(8,128)(2,1)S(1)}, bf16[6,32,128]{2,1,0:T(8,128)(2,1)S(1)}, u32[]{:S(2)}, u32[]{:S(2)}) %collective-permute-start.16) | collective-permute-done | bytes 49184 | tf_op jit(solution)/shard_map/ppermute | solution.py:110
  36.7 1.8 %collective-permute-start.12 = (bf16[6,32,128]{2,1,0:T(8,128)(2,1)S(1)}, bf16[6,32,128]{2,1,0:T(8,128)(2,1)S(1)}, u32[]{:S(2)}, u32[]{:S(2)}) collective-permute-start(bf16[6,32,128]{2,1,0:T(8,128)(2,1)S(1)} %get-tuple-element.52), channel_id=1, source_target_pairs={{0,4},{2,6},{4,0},{6,2},{8,12},{10,14},{12,8},{14,10},{16,20},{18,... | collective-permute-start | bytes 147464 | tf_op jit(solution)/shard_map/ppermute | solution.py:110
  38.4 0.8 %collective-permute-done.11.refs_13_ = bf16[6,32,128]{2,1,0:T(8,128)(2,1)S(1)} collective-permute-done((bf16[6,32,128]{2,1,0:T(8,128)(2,1)S(1)}, bf16[6,32,128]{2,1,0:T(8,128)(2,1)S(1)}, u32[]{:S(2)}, u32[]{:S(2)}) %collective-permute-start.11) | collective-permute-done | bytes 49184 | tf_op jit(solution)/shard_map/ppermute | solution.py:110
  39.2 0.8 %collective-permute-start.13 = (bf16[6,32,128]{2,1,0:T(8,128)(2,1)S(1)}, bf16[6,32,128]{2,1,0:T(8,128)(2,1)S(1)}, u32[]{:S(2)}, u32[]{:S(2)}) collective-permute-start(bf16[6,32,128]{2,1,0:T(8,128)(2,1)S(1)} %get-tuple-element.53), channel_id=1, source_target_pairs={{0,2},{2,0},{4,6},{6,4},{8,10},{10,8},{12,14},{14,12},{16,18},{18,... | collective-permute-start | bytes 147464 | tf_op jit(solution)/shard_map/ppermute | solution.py:110
  40.0 0.7 %collective-permute-done.12.refs_14_ = bf16[6,32,128]{2,1,0:T(8,128)(2,1)S(1)} collective-permute-done((bf16[6,32,128]{2,1,0:T(8,128)(2,1)S(1)}, bf16[6,32,128]{2,1,0:T(8,128)(2,1)S(1)}, u32[]{:S(2)}, u32[]{:S(2)}) %collective-permute-start.12) | collective-permute-done | bytes 49184 | tf_op jit(solution)/shard_map/ppermute | solution.py:110
  40.8 2.6 %collective-permute-done.13.refs_15_ = bf16[6,32,128]{2,1,0:T(8,128)(2,1)S(1)} collective-permute-done((bf16[6,32,128]{2,1,0:T(8,128)(2,1)S(1)}, bf16[6,32,128]{2,1,0:T(8,128)(2,1)S(1)}, u32[]{:S(2)}, u32[]{:S(2)}) %collective-permute-start.13) | collective-permute-done | bytes 49184 | tf_op jit(solution)/shard_map/ppermute | solution.py:110
  43.3 0.0 collective-permute-done.8.refs_10_
  43.3 0.0 collective-permute-done.9.refs_11_
  43.3 0.0 collective-permute-done.10.refs_12_
  43.3 2.7 %shard_map.50 = bf16[8,128,128]{2,1,0:T(8,128)(2,1)} custom-call(s32[8,8]{1,0:T(8,128)S(1)} %get-tuple-element.34.refs_0_, s32[8,8]{1,0:T(8,128)S(1)} %collective-permute-done.6.refs_1_, bf16[20,32,128]{2,1,0:T(8,128)(2,1)S(1)} %get-tuple-element.36.refs_0_.refs_2_, bf16[20,32,128]{2,1,0:T(8,128)(2,1)S(1)} %collective-permute-done.2.refs_1_.refs_3_, ...), custom_call_target="tpu_custom_call" | custom-call | tf_op jit(solution)/shard_map/pallas_call | solution.py:165
  (2 shorter events, 0.0 us)
Async XLA Ops:
  0.0 16.9 %collective-permute-start.5 = (bf16[8,8,128,128]{3,2,1,0:T(8,128)(2,1)}, bf16[8,8,128,128]{3,2,1,0:T(8,128)(2,1)S(1)}, u32[]{:S(2)}, u32[]{:S(2)}) collective-permute-start(bf16[8,8,128,128]{3,2,1,0:T(8,128)(2,1)} %refs_3_.1), channel_id=1, source_target_pairs={{0,1},{1,0},{2,3},{3,2},{4,5},{5,4},{6,7},{7,6},{8,9},{9,8},{10,11... | collective-permute-start | bytes 6291464 | tf_op jit(solution)/shard_map/ppermute | solution.py:130
  0.5 1.0 %copy-start.1 = (bf16[16,128,128]{2,1,0:T(8,128)(2,1)S(1)}, bf16[16,128,128]{2,1,0:T(8,128)(2,1)}, u32[]{:S(2)}) copy-start(bf16[16,128,128]{2,1,0:T(8,128)(2,1)} %amplitudes_ref.1) | copy-start | bytes 1572868
  1.5 0.7 %copy-start.3 = (s32[1,32]{1,0:T(1,128)S(1)}, s32[1,32]{1,0:T(1,128)}, u32[]{:S(2)}) copy-start(s32[1,32]{1,0:T(1,128)} %send_ref.1) | copy-start | bytes 388
  2.9 8.2 %collective-permute-start.2 = (bf16[20,32,128]{2,1,0:T(8,128)(2,1)S(1)}, bf16[20,32,128]{2,1,0:T(8,128)(2,1)S(1)}, u32[]{:S(2)}, u32[]{:S(2)}) collective-permute-start(bf16[20,32,128]{2,1,0:T(8,128)(2,1)S(1)} %get-tuple-element.37), channel_id=1, source_target_pairs={{0,2},{2,0},{4,6},{6,4},{8,10},{10,8},{12,14},{14,12},{16,18},{18,... | collective-permute-start | bytes 491528 | tf_op jit(solution)/shard_map/ppermute | solution.py:110
  5.4 9.8 %collective-permute-start.3 = (bf16[20,32,128]{2,1,0:T(8,128)(2,1)S(1)}, bf16[20,32,128]{2,1,0:T(8,128)(2,1)S(1)}, u32[]{:S(2)}, u32[]{:S(2)}) collective-permute-start(bf16[20,32,128]{2,1,0:T(8,128)(2,1)S(1)} %get-tuple-element.38), channel_id=1, source_target_pairs={{0,4},{2,6},{4,0},{6,2},{8,12},{10,14},{12,8},{14,10},{16,20},{18,... | collective-permute-start | bytes 491528 | tf_op jit(solution)/shard_map/ppermute | solution.py:110
  7.0 9.9 %collective-permute-start.4 = (bf16[20,32,128]{2,1,0:T(8,128)(2,1)S(1)}, bf16[20,32,128]{2,1,0:T(8,128)(2,1)S(1)}, u32[]{:S(2)}, u32[]{:S(2)}) collective-permute-start(bf16[20,32,128]{2,1,0:T(8,128)(2,1)S(1)} %get-tuple-element.39), channel_id=1, source_target_pairs={{0,6},{2,4},{4,2},{6,0},{8,14},{10,12},{12,10},{14,8},{16,22},{18,... | collective-permute-start | bytes 491528 | tf_op jit(solution)/shard_map/ppermute | solution.py:110
  7.0 12.7 %collective-permute-start = (bf16[12,32,128]{2,1,0:T(8,128)(2,1)S(1)}, bf16[12,32,128]{2,1,0:T(8,128)(2,1)S(1)}, u32[]{:S(2)}, u32[]{:S(2)}) collective-permute-start(bf16[12,32,128]{2,1,0:T(8,128)(2,1)S(1)} %get-tuple-element.32), channel_id=1, source_target_pairs={{0,24},{2,26},{4,28},{6,30},{8,16},{10,18},{12,20},{14,22},{16,8},... | collective-permute-start | bytes 294920 | tf_op jit(solution)/shard_map/ppermute | solution.py:110
  11.0 10.4 %collective-permute-start.1 = (bf16[12,32,128]{2,1,0:T(8,128)(2,1)S(1)}, bf16[12,32,128]{2,1,0:T(8,128)(2,1)S(1)}, u32[]{:S(2)}, u32[]{:S(2)}) collective-permute-start(bf16[12,32,128]{2,1,0:T(8,128)(2,1)S(1)} %get-tuple-element.33), channel_id=1, source_target_pairs={{0,16},{2,18},{4,20},{6,22},{8,24},{10,26},{12,28},{14,30},{16,0},... | collective-permute-start | bytes 294920 | tf_op jit(solution)/shard_map/ppermute | solution.py:110
  15.3 14.9 %collective-permute-start.7 = (bf16[12,32,128]{2,1,0:T(8,128)(2,1)S(1)}, bf16[12,32,128]{2,1,0:T(8,128)(2,1)S(1)}, u32[]{:S(2)}, u32[]{:S(2)}) collective-permute-start(bf16[12,32,128]{2,1,0:T(8,128)(2,1)S(1)} %get-tuple-element.47), channel_id=1, source_target_pairs={{0,8},{2,10},{4,12},{6,14},{8,0},{10,2},{12,4},{14,6},{16,24},{18,... | collective-permute-start | bytes 294920 | tf_op jit(solution)/shard_map/ppermute | solution.py:110
  16.9 26.4 %collective-permute-start.8 = (bf16[20,32,128]{2,1,0:T(8,128)(2,1)S(1)}, bf16[20,32,128]{2,1,0:T(8,128)(2,1)S(1)}, u32[]{:S(2)}, u32[]{:S(2)}) collective-permute-start(bf16[20,32,128]{2,1,0:T(8,128)(2,1)S(1)} %get-tuple-element.48), channel_id=1, source_target_pairs={{0,24},{2,26},{4,28},{6,30},{8,16},{10,18},{12,20},{14,22},{16,8},... | collective-permute-start | bytes 491528 | tf_op jit(solution)/shard_map/ppermute | solution.py:110
  19.5 23.9 %collective-permute-start.9 = (bf16[20,32,128]{2,1,0:T(8,128)(2,1)S(1)}, bf16[20,32,128]{2,1,0:T(8,128)(2,1)S(1)}, u32[]{:S(2)}, u32[]{:S(2)}) collective-permute-start(bf16[20,32,128]{2,1,0:T(8,128)(2,1)S(1)} %get-tuple-element.49), channel_id=1, source_target_pairs={{0,16},{2,18},{4,20},{6,22},{8,24},{10,26},{12,28},{14,30},{16,0},... | collective-permute-start | bytes 491528 | tf_op jit(solution)/shard_map/ppermute | solution.py:110
  19.7 23.7 %collective-permute-start.10 = (bf16[20,32,128]{2,1,0:T(8,128)(2,1)S(1)}, bf16[20,32,128]{2,1,0:T(8,128)(2,1)S(1)}, u32[]{:S(2)}, u32[]{:S(2)}) collective-permute-start(bf16[20,32,128]{2,1,0:T(8,128)(2,1)S(1)} %get-tuple-element.50), channel_id=1, source_target_pairs={{0,8},{2,10},{4,12},{6,14},{8,0},{10,2},{12,4},{14,6},{16,24},{18,... | collective-permute-start | bytes 491528 | tf_op jit(solution)/shard_map/ppermute | solution.py:110
  21.4 2.5 %collective-permute-start.6 = (s32[8,8]{1,0:T(8,128)}, s32[8,8]{1,0:T(8,128)S(1)}, u32[]{:S(2)}, u32[]{:S(2)}) collective-permute-start(s32[8,8]{1,0:T(8,128)} %refs_2_.1), channel_id=1, source_target_pairs={{0,1},{1,0},{2,3},{3,2},{4,5},{5,4},{6,7},{7,6},{8,9},{9,8},{10,11... | collective-permute-start | bytes 776 | tf_op jit(solution)/shard_map/ppermute | solution.py:129
  21.4 1.6 %copy-start = (bf16[8,8,128,128]{3,2,1,0:T(8,128)(2,1)S(1)}, bf16[8,8,128,128]{3,2,1,0:T(8,128)(2,1)}, u32[]{:S(2)}) copy-start(bf16[8,8,128,128]{3,2,1,0:T(8,128)(2,1)} %refs_3_.1) | copy-start | bytes 6291460
  23.0 0.7 %copy-start.2 = (s32[8,8]{1,0:T(8,128)S(1)}, s32[8,8]{1,0:T(8,128)}, u32[]{:S(2)}) copy-start(s32[8,8]{1,0:T(8,128)} %refs_2_.1) | copy-start | bytes 772
  23.9 8.7 %collective-permute-start.14 = (bf16[6,32,128]{2,1,0:T(8,128)(2,1)S(1)}, bf16[6,32,128]{2,1,0:T(8,128)(2,1)S(1)}, u32[]{:S(2)}, u32[]{:S(2)}) collective-permute-start(bf16[6,32,128]{2,1,0:T(8,128)(2,1)S(1)} %get-tuple-element.54), channel_id=1, source_target_pairs={{0,6},{2,4},{4,2},{6,0},{8,14},{10,12},{12,10},{14,8},{16,22},{18,... | collective-permute-start | bytes 147464 | tf_op jit(solution)/shard_map/ppermute | solution.py:110
  30.2 4.1 %collective-permute-start.15 = (bf16[6,32,128]{2,1,0:T(8,128)(2,1)S(1)}, bf16[6,32,128]{2,1,0:T(8,128)(2,1)S(1)}, u32[]{:S(2)}, u32[]{:S(2)}) collective-permute-start(bf16[6,32,128]{2,1,0:T(8,128)(2,1)S(1)} %get-tuple-element.55), channel_id=1, source_target_pairs={{0,4},{2,6},{4,0},{6,2},{8,12},{10,14},{12,8},{14,10},{16,20},{18,... | collective-permute-start | bytes 147464 | tf_op jit(solution)/shard_map/ppermute | solution.py:110
  32.6 4.1 %collective-permute-start.16 = (bf16[6,32,128]{2,1,0:T(8,128)(2,1)S(1)}, bf16[6,32,128]{2,1,0:T(8,128)(2,1)S(1)}, u32[]{:S(2)}, u32[]{:S(2)}) collective-permute-start(bf16[6,32,128]{2,1,0:T(8,128)(2,1)S(1)} %get-tuple-element.56), channel_id=1, source_target_pairs={{0,2},{2,0},{4,6},{6,4},{8,10},{10,8},{12,14},{14,12},{16,18},{18,... | collective-permute-start | bytes 147464 | tf_op jit(solution)/shard_map/ppermute | solution.py:110
  34.3 5.0 %collective-permute-start.11 = (bf16[6,32,128]{2,1,0:T(8,128)(2,1)S(1)}, bf16[6,32,128]{2,1,0:T(8,128)(2,1)S(1)}, u32[]{:S(2)}, u32[]{:S(2)}) collective-permute-start(bf16[6,32,128]{2,1,0:T(8,128)(2,1)S(1)} %get-tuple-element.51), channel_id=1, source_target_pairs={{0,6},{2,4},{4,2},{6,0},{8,14},{10,12},{12,10},{14,8},{16,22},{18,... | collective-permute-start | bytes 147464 | tf_op jit(solution)/shard_map/ppermute | solution.py:110
  36.7 4.1 %collective-permute-start.12 = (bf16[6,32,128]{2,1,0:T(8,128)(2,1)S(1)}, bf16[6,32,128]{2,1,0:T(8,128)(2,1)S(1)}, u32[]{:S(2)}, u32[]{:S(2)}) collective-permute-start(bf16[6,32,128]{2,1,0:T(8,128)(2,1)S(1)} %get-tuple-element.52), channel_id=1, source_target_pairs={{0,4},{2,6},{4,0},{6,2},{8,12},{10,14},{12,8},{14,10},{16,20},{18,... | collective-permute-start | bytes 147464 | tf_op jit(solution)/shard_map/ppermute | solution.py:110
  39.2 4.1 %collective-permute-start.13 = (bf16[6,32,128]{2,1,0:T(8,128)(2,1)S(1)}, bf16[6,32,128]{2,1,0:T(8,128)(2,1)S(1)}, u32[]{:S(2)}, u32[]{:S(2)}) collective-permute-start(bf16[6,32,128]{2,1,0:T(8,128)(2,1)S(1)} %get-tuple-element.53), channel_id=1, source_target_pairs={{0,2},{2,0},{4,6},{6,4},{8,10},{10,8},{12,14},{14,12},{16,18},{18,... | collective-permute-start | bytes 147464 | tf_op jit(solution)/shard_map/ppermute | solution.py:110

commit v10 on v5

--- a/solution.py
+++ b/solution.py
@@ -138,6 +138,7 @@
     second_along, blocks[-1] = lax.optimization_barrier((second_along, blocks[-1]))
     got_along[0], second_along[-1] = lax.optimization_barrier((got_along[0], second_along[-1]))
     last_along = [exchange(second_along[b - 1], near * b) for b in range(far - 1, 0, -1)]
+    got_along[0], places[-1] = lax.optimization_barrier((got_along[0], places[-1]))
     second_across, _ = regrouped(got_along, len(early), near - 1)
     last_across = [exchange(second_across[a - 1], a) for a in range(near - 1, 0, -1)]
     pieces = got_across + got_along[:1] + got_along[:0:-1] + last_along + last_across

time: 39.6 us -> 39.5 us (level)
  waiting for transfers between devices: 12.7 us -> 11.5 us
  starting transfers between devices: 19.2 us -> 20.1 us
  local copies, waits for them, and re-layouts: 3.29 us -> 3.97 us
  Pallas kernels: 4.13 us -> 3.61 us
    ppermute x12, waiting for transfers between devices: 12.7 us -> 10.3 us  [exchange(): return lax.ppermute(array, 'wide', [(d, d ^ partner) for d in range(wide)])]
    ppermute x1, waiting for transfers between devices: 0.01 us -> 1.16 us  [on_device(): places = [tile_positions, lax.ppermute(tile_positions, 'narrow', swap)]]
    ppermute x12, starting transfers between devices: 18.7 us -> 19.6 us  [exchange(): return lax.ppermute(array, 'wide', [(d, d ^ partner) for d in range(wide)])]
    unnamed x6 -> x8, local copies, waits for them, and re-layouts: 3.29 us -> 3.97 us
    pallas_call x2, Pallas kernels: 0.73 us -> 0.21 us  [regrouped(): pl.pallas_call(functools.partial(regroup, len(arrays), width, len(staged)...]
  transfers between devices with their start and end apart: 14 -> 14, of which waited for: 6 -> 7; matrix products, arithmetic and copies ran while one was open for 0% -> 0% of each run, Pallas kernels for 4% -> 2%
where the time goes in v10:
time: 39.5 us; the launch traced here: 39.2 us
  starting transfers between devices  20.1 us (51%)
  waiting for transfers between devices  11.5 us (29%)
  local copies, waits for them, and re-layouts  3.97 us (10%)
  Pallas kernels  3.61 us (9%)
    ppermute x12, starting transfers between devices, exchange(): return lax.ppermute(array, 'wide', [(d, d ^ partner) for d in range(wide)])  19.6 us
    ppermute x12, waiting for transfers between devices, exchange(): return lax.ppermute(array, 'wide', [(d, d ^ partner) for d in range(wide)])  10.3 us
    unnamed x8, local copies, waits for them, and re-layouts  3.97 us
    pallas_call x1, Pallas kernels, on_device(): pl.pallas_call(functools.partial(contract, origins, cap, count), out_shap...  2.72 us
    ppermute x1, waiting for transfers between devices, on_device(): places = [tile_positions, lax.ppermute(tile_positions, 'narrow', swap)]  1.16 us
  transfers between devices with their start and end apart: 14, of which 7 were waited for; matrix products, arithmetic and copies ran while one was open for 0% of the time, Pallas kernels for 2%

profile of v10, /device:TPU:0, one launch (start us, length us, event | category | flops | bytes accessed | tf_op | source)
XLA Modules:
  0.0 39.2 jit_solution(3928006697056279659)
XLA Ops:
  0.0 0.5 %collective-permute-start.3 = (bf16[8,8,128,128]{3,2,1,0:T(8,128)(2,1)}, bf16[8,8,128,128]{3,2,1,0:T(8,128)(2,1)S(1)}, u32[]{:S(2)}, u32[]{:S(2)}) collective-permute-start(bf16[8,8,128,128]{3,2,1,0:T(8,128)(2,1)} %refs_5_.1), channel_id=1, source_target_pairs={{0,1},{1,0},{2,3},{3,2},{4,5},{5,4},{6,7},{7,6},{8,9},{9,8},{10,11... | collective-permute-start | bytes 6291464 | tf_op jit(solution)/shard_map/ppermute | solution.py:124
  0.5 0.0 copy-start.1
  0.5 1.0 %copy-done.1 = bf16[16,128,128]{2,1,0:T(8,128)(2,1)S(1)} copy-done((bf16[16,128,128]{2,1,0:T(8,128)(2,1)S(1)}, bf16[16,128,128]{2,1,0:T(8,128)(2,1)}, u32[]{:S(2)}) %copy-start.1) | copy-done | bytes 524312
  1.5 0.0 copy-start.3
  1.5 0.7 %copy-done.3 = s32[1,32]{1,0:T(1,128)S(1)} copy-done((s32[1,32]{1,0:T(1,128)S(1)}, s32[1,32]{1,0:T(1,128)}, u32[]{:S(2)}) %copy-start.3) | copy-done | bytes 152
  2.2 0.7 %shard_map.46 = (bf16[4,128,128]{2,1,0:T(8,128)(2,1)S(1)}, bf16[4,128,128]{2,1,0:T(8,128)(2,1)S(1)}, bf16[4,128,128]{2,1,0:T(8,128)(2,1)S(1)}, bf16[4,128,128]{2...) custom-call(s32[1,32]{1,0:T(1,128)S(1)} %copy-done.3, ...), custom_call_target="tpu_custom_call" | custom-call | tf_op jit(solution)/shard_map/pallas_call | solution.py:109
  2.8 2.6 %collective-permute-start = (bf16[4,128,128]{2,1,0:T(8,128)(2,1)S(1)}, bf16[4,128,128]{2,1,0:T(8,128)(2,1)S(1)}, u32[]{:S(2)}, u32[]{:S(2)}) collective-permute-start(bf16[4,128,128]{2,1,0:T(8,128)(2,1)S(1)} %get-tuple-element.30), channel_id=1, source_target_pairs={{0,2},{2,0},{4,6},{6,4},{8,10},{10,8},{12,14},{14,12},{16,18},{18,... | collective-permute-start | bytes 393224 | tf_op jit(solution)/shard_map/ppermute | solution.py:104
  5.4 1.5 %collective-permute-start.1 = (bf16[4,128,128]{2,1,0:T(8,128)(2,1)S(1)}, bf16[4,128,128]{2,1,0:T(8,128)(2,1)S(1)}, u32[]{:S(2)}, u32[]{:S(2)}) collective-permute-start(bf16[4,128,128]{2,1,0:T(8,128)(2,1)S(1)} %get-tuple-element.31), channel_id=1, source_target_pairs={{0,4},{2,6},{4,0},{6,2},{8,12},{10,14},{12,8},{14,10},{16,20},{18,... | collective-permute-start | bytes 393224 | tf_op jit(solution)/shard_map/ppermute | solution.py:104
  6.9 0.0 collective-permute-start.2
  6.9 4.1 %collective-permute-start.5 = (bf16[4,128,128]{2,1,0:T(8,128)(2,1)S(1)}, bf16[4,128,128]{2,1,0:T(8,128)(2,1)S(1)}, u32[]{:S(2)}, u32[]{:S(2)}) collective-permute-start(bf16[4,128,128]{2,1,0:T(8,128)(2,1)S(1)} %get-tuple-element.42), channel_id=1, source_target_pairs={{0,24},{2,26},{4,28},{6,30},{8,16},{10,18},{12,20},{14,22},{16,8},... | collective-permute-start | bytes 393224 | tf_op jit(solution)/shard_map/ppermute | solution.py:104
  11.0 0.0 collective-permute-done.refs_1_.refs_3_
  11.0 1.8 %collective-permute-start.6 = (bf16[4,128,128]{2,1,0:T(8,128)(2,1)S(1)}, bf16[4,128,128]{2,1,0:T(8,128)(2,1)S(1)}, u32[]{:S(2)}, u32[]{:S(2)}) collective-permute-start(bf16[4,128,128]{2,1,0:T(8,128)(2,1)S(1)} %get-tuple-element.43), channel_id=1, source_target_pairs={{0,16},{2,18},{4,20},{6,22},{8,24},{10,26},{12,28},{14,30},{16,0},... | collective-permute-start | bytes 393224 | tf_op jit(solution)/shard_map/ppermute | solution.py:104
  12.8 1.0 %collective-permute-done.1.refs_2_.refs_4_ = bf16[4,128,128]{2,1,0:T(8,128)(2,1)S(1)} collective-permute-done((bf16[4,128,128]{2,1,0:T(8,128)(2,1)S(1)}, bf16[4,128,128]{2,1,0:T(8,128)(2,1)S(1)}, u32[]{:S(2)}, u32[]{:S(2)}) %collective-permute-start.1) | collective-permute-done | bytes 131104 | tf_op jit(solution)/shard_map/ppermute | solution.py:104
  13.8 1.6 %collective-permute-start.7 = (bf16[4,128,128]{2,1,0:T(8,128)(2,1)S(1)}, bf16[4,128,128]{2,1,0:T(8,128)(2,1)S(1)}, u32[]{:S(2)}, u32[]{:S(2)}) collective-permute-start(bf16[4,128,128]{2,1,0:T(8,128)(2,1)S(1)} %get-tuple-element.44), channel_id=1, source_target_pairs={{0,8},{2,10},{4,12},{6,14},{8,0},{10,2},{12,4},{14,6},{16,24},{18,... | collective-permute-start | bytes 393224 | tf_op jit(solution)/shard_map/ppermute | solution.py:104
  15.4 0.0 collective-permute-done.2.refs_3_.refs_5_
  15.4 0.0 copy-start
  15.4 1.6 %copy-done = bf16[8,8,128,128]{3,2,1,0:T(8,128)(2,1)S(1)} copy-done((bf16[8,8,128,128]{3,2,1,0:T(8,128)(2,1)S(1)}, bf16[8,8,128,128]{3,2,1,0:T(8,128)(2,1)}, u32[]{:S(2)}) %copy-start) | copy-done | bytes 2097176
  17.0 0.0 copy-start.2
  17.0 0.7 %copy-done.2 = s32[8,8]{1,0:T(8,128)S(1)} copy-done((s32[8,8]{1,0:T(8,128)S(1)}, s32[8,8]{1,0:T(8,128)}, u32[]{:S(2)}) %copy-start.2) | copy-done | bytes 280
  17.7 0.2 shard_map.47
  17.9 0.0 collective-permute-done.3.refs_17_
  17.9 2.5 %collective-permute-start.8 = (bf16[4,128,128]{2,1,0:T(8,128)(2,1)S(1)}, bf16[4,128,128]{2,1,0:T(8,128)(2,1)S(1)}, u32[]{:S(2)}, u32[]{:S(2)}) collective-permute-start(bf16[4,128,128]{2,1,0:T(8,128)(2,1)S(1)} %get-tuple-element.45), channel_id=1, source_target_pairs={{0,24},{2,26},{4,28},{6,30},{8,16},{10,18},{12,20},{14,22},{16,8},... | collective-permute-start | bytes 393224 | tf_op jit(solution)/shard_map/ppermute | solution.py:104
  20.4 0.0 collective-permute-start.4
  20.4 1.2 %collective-permute-done.4.refs_1_ = s32[8,8]{1,0:T(8,128)S(1)} collective-permute-done((s32[8,8]{1,0:T(8,128)S(1)}, s32[8,8]{1,0:T(8,128)S(1)}, u32[]{:S(2)}, u32[]{:S(2)}) %collective-permute-start.4) | collective-permute-done | bytes 288 | tf_op jit(solution)/shard_map/ppermute | solution.py:123
  21.6 0.2 collective-permute-start.9
  21.8 0.0 collective-permute-done.5.refs_3_.refs_7_
  21.8 1.7 %collective-permute-start.10 = (bf16[4,128,128]{2,1,0:T(8,128)(2,1)S(1)}, bf16[4,128,128]{2,1,0:T(8,128)(2,1)S(1)}, u32[]{:S(2)}, u32[]{:S(2)}) collective-permute-start(bf16[4,128,128]{2,1,0:T(8,128)(2,1)S(1)} %get-tuple-element.47), channel_id=1, source_target_pairs={{0,8},{2,10},{4,12},{6,14},{8,0},{10,2},{12,4},{14,6},{16,24},{18,... | collective-permute-start | bytes 393224 | tf_op jit(solution)/shard_map/ppermute | solution.py:104
  23.5 4.5 %collective-permute-done.6.refs_2_.refs_8_ = bf16[4,128,128]{2,1,0:T(8,128)(2,1)S(1)} collective-permute-done((bf16[4,128,128]{2,1,0:T(8,128)(2,1)S(1)}, bf16[4,128,128]{2,1,0:T(8,128)(2,1)S(1)}, u32[]{:S(2)}, u32[]{:S(2)}) %collective-permute-start.6) | collective-permute-done | bytes 131104 | tf_op jit(solution)/shard_map/ppermute | solution.py:104
  28.0 0.0 collective-permute-done.7.refs_1_.refs_9_
  28.0 3.0 %collective-permute-start.11 = (bf16[4,128,128]{2,1,0:T(8,128)(2,1)S(1)}, bf16[4,128,128]{2,1,0:T(8,128)(2,1)S(1)}, u32[]{:S(2)}, u32[]{:S(2)}) collective-permute-start(bf16[4,128,128]{2,1,0:T(8,128)(2,1)S(1)} %get-tuple-element.48), channel_id=1, source_target_pairs={{0,6},{2,4},{4,2},{6,0},{8,14},{10,12},{12,10},{14,8},{16,22},{18,... | collective-permute-start | bytes 393224 | tf_op jit(solution)/shard_map/ppermute | solution.py:104
  31.0 0.5 %collective-permute-start.12 = (bf16[4,128,128]{2,1,0:T(8,128)(2,1)S(1)}, bf16[4,128,128]{2,1,0:T(8,128)(2,1)S(1)}, u32[]{:S(2)}, u32[]{:S(2)}) collective-permute-start(bf16[4,128,128]{2,1,0:T(8,128)(2,1)S(1)} %get-tuple-element.49), channel_id=1, source_target_pairs={{0,4},{2,6},{4,0},{6,2},{8,12},{10,14},{12,8},{14,10},{16,20},{18,... | collective-permute-start | bytes 393224 | tf_op jit(solution)/shard_map/ppermute | solution.py:104
  31.5 0.0 collective-permute-done.8.refs_10_
  31.6 0.1 collective-permute-start.13
  31.7 1.4 %collective-permute-done.9.refs_11_ = bf16[4,128,128]{2,1,0:T(8,128)(2,1)S(1)} collective-permute-done((bf16[4,128,128]{2,1,0:T(8,128)(2,1)S(1)}, bf16[4,128,128]{2,1,0:T(8,128)(2,1)S(1)}, u32[]{:S(2)}, u32[]{:S(2)}) %collective-permute-start.9) | collective-permute-done | bytes 131104 | tf_op jit(solution)/shard_map/ppermute | solution.py:104
  33.1 0.0 collective-permute-done.10.refs_12_
  33.1 0.9 %collective-permute-done.11.refs_13_ = bf16[4,128,128]{2,1,0:T(8,128)(2,1)S(1)} collective-permute-done((bf16[4,128,128]{2,1,0:T(8,128)(2,1)S(1)}, bf16[4,128,128]{2,1,0:T(8,128)(2,1)S(1)}, u32[]{:S(2)}, u32[]{:S(2)}) %collective-permute-start.11) | collective-permute-done | bytes 131104 | tf_op jit(solution)/shard_map/ppermute | solution.py:104
  34.0 2.0 %collective-permute-done.12.refs_14_ = bf16[4,128,128]{2,1,0:T(8,128)(2,1)S(1)} collective-permute-done((bf16[4,128,128]{2,1,0:T(8,128)(2,1)S(1)}, bf16[4,128,128]{2,1,0:T(8,128)(2,1)S(1)}, u32[]{:S(2)}, u32[]{:S(2)}) %collective-permute-start.12) | collective-permute-done | bytes 131104 | tf_op jit(solution)/shard_map/ppermute | solution.py:104
  36.0 0.5 %collective-permute-done.13.refs_15_ = bf16[4,128,128]{2,1,0:T(8,128)(2,1)S(1)} collective-permute-done((bf16[4,128,128]{2,1,0:T(8,128)(2,1)S(1)}, bf16[4,128,128]{2,1,0:T(8,128)(2,1)S(1)}, u32[]{:S(2)}, u32[]{:S(2)}) %collective-permute-start.13) | collective-permute-done | bytes 131104 | tf_op jit(solution)/shard_map/ppermute | solution.py:104
  36.5 2.7 %shard_map.49 = bf16[8,128,128]{2,1,0:T(8,128)(2,1)} custom-call(s32[8,8]{1,0:T(8,128)S(1)} %get-tuple-element.33.refs_0_, s32[8,8]{1,0:T(8,128)S(1)} %collective-permute-done.4.refs_1_, bf16[4,128,128]{2,1,0:T(8,128)(2,1)S(1)} %get-tuple-element.29.refs_0_.refs_2_, bf16[4,128,128]{2,1,0:T(8,128)(2,1)S(1)} %collective-permute-done.refs_1_.refs_3_, ...), custom_call_target="tpu_custom_call" | custom-call | tf_op jit(solution)/shard_map/pallas_call | solution.py:150
  (1 shorter events, 0.0 us)
Async XLA Ops:
  0.0 17.9 %collective-permute-start.3 = (bf16[8,8,128,128]{3,2,1,0:T(8,128)(2,1)}, bf16[8,8,128,128]{3,2,1,0:T(8,128)(2,1)S(1)}, u32[]{:S(2)}, u32[]{:S(2)}) collective-permute-start(bf16[8,8,128,128]{3,2,1,0:T(8,128)(2,1)} %refs_5_.1), channel_id=1, source_target_pairs={{0,1},{1,0},{2,3},{3,2},{4,5},{5,4},{6,7},{7,6},{8,9},{9,8},{10,11... | collective-permute-start | bytes 6291464 | tf_op jit(solution)/shard_map/ppermute | solution.py:124
  0.5 1.0 %copy-start.1 = (bf16[16,128,128]{2,1,0:T(8,128)(2,1)S(1)}, bf16[16,128,128]{2,1,0:T(8,128)(2,1)}, u32[]{:S(2)}) copy-start(bf16[16,128,128]{2,1,0:T(8,128)(2,1)} %amplitudes_ref.1) | copy-start | bytes 1572868
  1.5 0.7 %copy-start.3 = (s32[1,32]{1,0:T(1,128)S(1)}, s32[1,32]{1,0:T(1,128)}, u32[]{:S(2)}) copy-start(s32[1,32]{1,0:T(1,128)} %send_ref.1) | copy-start | bytes 388
  2.8 8.2 %collective-permute-start = (bf16[4,128,128]{2,1,0:T(8,128)(2,1)S(1)}, bf16[4,128,128]{2,1,0:T(8,128)(2,1)S(1)}, u32[]{:S(2)}, u32[]{:S(2)}) collective-permute-start(bf16[4,128,128]{2,1,0:T(8,128)(2,1)S(1)} %get-tuple-element.30), channel_id=1, source_target_pairs={{0,2},{2,0},{4,6},{6,4},{8,10},{10,8},{12,14},{14,12},{16,18},{18,... | collective-permute-start | bytes 393224 | tf_op jit(solution)/shard_map/ppermute | solution.py:104
  5.4 8.4 %collective-permute-start.1 = (bf16[4,128,128]{2,1,0:T(8,128)(2,1)S(1)}, bf16[4,128,128]{2,1,0:T(8,128)(2,1)S(1)}, u32[]{:S(2)}, u32[]{:S(2)}) collective-permute-start(bf16[4,128,128]{2,1,0:T(8,128)(2,1)S(1)} %get-tuple-element.31), channel_id=1, source_target_pairs={{0,4},{2,6},{4,0},{6,2},{8,12},{10,14},{12,8},{14,10},{16,20},{18,... | collective-permute-start | bytes 393224 | tf_op jit(solution)/shard_map/ppermute | solution.py:104
  6.9 8.5 %collective-permute-start.2 = (bf16[4,128,128]{2,1,0:T(8,128)(2,1)S(1)}, bf16[4,128,128]{2,1,0:T(8,128)(2,1)S(1)}, u32[]{:S(2)}, u32[]{:S(2)}) collective-permute-start(bf16[4,128,128]{2,1,0:T(8,128)(2,1)S(1)} %get-tuple-element.32), channel_id=1, source_target_pairs={{0,6},{2,4},{4,2},{6,0},{8,14},{10,12},{12,10},{14,8},{16,22},{18,... | collective-permute-start | bytes 393224 | tf_op jit(solution)/shard_map/ppermute | solution.py:104
  6.9 14.9 %collective-permute-start.5 = (bf16[4,128,128]{2,1,0:T(8,128)(2,1)S(1)}, bf16[4,128,128]{2,1,0:T(8,128)(2,1)S(1)}, u32[]{:S(2)}, u32[]{:S(2)}) collective-permute-start(bf16[4,128,128]{2,1,0:T(8,128)(2,1)S(1)} %get-tuple-element.42), channel_id=1, source_target_pairs={{0,24},{2,26},{4,28},{6,30},{8,16},{10,18},{12,20},{14,22},{16,8},... | collective-permute-start | bytes 393224 | tf_op jit(solution)/shard_map/ppermute | solution.py:104
  11.0 17.0 %collective-permute-start.6 = (bf16[4,128,128]{2,1,0:T(8,128)(2,1)S(1)}, bf16[4,128,128]{2,1,0:T(8,128)(2,1)S(1)}, u32[]{:S(2)}, u32[]{:S(2)}) collective-permute-start(bf16[4,128,128]{2,1,0:T(8,128)(2,1)S(1)} %get-tuple-element.43), channel_id=1, source_target_pairs={{0,16},{2,18},{4,20},{6,22},{8,24},{10,26},{12,28},{14,30},{16,0},... | collective-permute-start | bytes 393224 | tf_op jit(solution)/shard_map/ppermute | solution.py:104
  13.8 14.2 %collective-permute-start.7 = (bf16[4,128,128]{2,1,0:T(8,128)(2,1)S(1)}, bf16[4,128,128]{2,1,0:T(8,128)(2,1)S(1)}, u32[]{:S(2)}, u32[]{:S(2)}) collective-permute-start(bf16[4,128,128]{2,1,0:T(8,128)(2,1)S(1)} %get-tuple-element.44), channel_id=1, source_target_pairs={{0,8},{2,10},{4,12},{6,14},{8,0},{10,2},{12,4},{14,6},{16,24},{18,... | collective-permute-start | bytes 393224 | tf_op jit(solution)/shard_map/ppermute | solution.py:104
  15.4 1.6 %copy-start = (bf16[8,8,128,128]{3,2,1,0:T(8,128)(2,1)S(1)}, bf16[8,8,128,128]{3,2,1,0:T(8,128)(2,1)}, u32[]{:S(2)}) copy-start(bf16[8,8,128,128]{3,2,1,0:T(8,128)(2,1)} %refs_5_.1) | copy-start | bytes 6291460
  17.0 0.7 %copy-start.2 = (s32[8,8]{1,0:T(8,128)S(1)}, s32[8,8]{1,0:T(8,128)}, u32[]{:S(2)}) copy-start(s32[8,8]{1,0:T(8,128)} %refs_4_.1) | copy-start | bytes 772
  17.9 13.7 %collective-permute-start.8 = (bf16[4,128,128]{2,1,0:T(8,128)(2,1)S(1)}, bf16[4,128,128]{2,1,0:T(8,128)(2,1)S(1)}, u32[]{:S(2)}, u32[]{:S(2)}) collective-permute-start(bf16[4,128,128]{2,1,0:T(8,128)(2,1)S(1)} %get-tuple-element.45), channel_id=1, source_target_pairs={{0,24},{2,26},{4,28},{6,30},{8,16},{10,18},{12,20},{14,22},{16,8},... | collective-permute-start | bytes 393224 | tf_op jit(solution)/shard_map/ppermute | solution.py:104
  20.4 1.2 %collective-permute-start.4 = (s32[8,8]{1,0:T(8,128)S(1)}, s32[8,8]{1,0:T(8,128)S(1)}, u32[]{:S(2)}, u32[]{:S(2)}) collective-permute-start(s32[8,8]{1,0:T(8,128)S(1)} %copy-done.2), channel_id=1, source_target_pairs={{0,1},{1,0},{2,3},{3,2},{4,5},{5,4},{6,7},{7,6},{8,9},{9,8},{10,11... | collective-permute-start | bytes 776 | tf_op jit(solution)/shard_map/ppermute | solution.py:123
  21.6 11.5 %collective-permute-start.9 = (bf16[4,128,128]{2,1,0:T(8,128)(2,1)S(1)}, bf16[4,128,128]{2,1,0:T(8,128)(2,1)S(1)}, u32[]{:S(2)}, u32[]{:S(2)}) collective-permute-start(bf16[4,128,128]{2,1,0:T(8,128)(2,1)S(1)} %get-tuple-element.46), channel_id=1, source_target_pairs={{0,16},{2,18},{4,20},{6,22},{8,24},{10,26},{12,28},{14,30},{16,0},... | collective-permute-start | bytes 393224 | tf_op jit(solution)/shard_map/ppermute | solution.py:104
  21.8 11.3 %collective-permute-start.10 = (bf16[4,128,128]{2,1,0:T(8,128)(2,1)S(1)}, bf16[4,128,128]{2,1,0:T(8,128)(2,1)S(1)}, u32[]{:S(2)}, u32[]{:S(2)}) collective-permute-start(bf16[4,128,128]{2,1,0:T(8,128)(2,1)S(1)} %get-tuple-element.47), channel_id=1, source_target_pairs={{0,8},{2,10},{4,12},{6,14},{8,0},{10,2},{12,4},{14,6},{16,24},{18,... | collective-permute-start | bytes 393224 | tf_op jit(solution)/shard_map/ppermute | solution.py:104
  28.0 6.0 %collective-permute-start.11 = (bf16[4,128,128]{2,1,0:T(8,128)(2,1)S(1)}, bf16[4,128,128]{2,1,0:T(8,128)(2,1)S(1)}, u32[]{:S(2)}, u32[]{:S(2)}) collective-permute-start(bf16[4,128,128]{2,1,0:T(8,128)(2,1)S(1)} %get-tuple-element.48), channel_id=1, source_target_pairs={{0,6},{2,4},{4,2},{6,0},{8,14},{10,12},{12,10},{14,8},{16,22},{18,... | collective-permute-start | bytes 393224 | tf_op jit(solution)/shard_map/ppermute | solution.py:104
  31.0 5.0 %collective-permute-start.12 = (bf16[4,128,128]{2,1,0:T(8,128)(2,1)S(1)}, bf16[4,128,128]{2,1,0:T(8,128)(2,1)S(1)}, u32[]{:S(2)}, u32[]{:S(2)}) collective-permute-start(bf16[4,128,128]{2,1,0:T(8,128)(2,1)S(1)} %get-tuple-element.49), channel_id=1, source_target_pairs={{0,4},{2,6},{4,0},{6,2},{8,12},{10,14},{12,8},{14,10},{16,20},{18,... | collective-permute-start | bytes 393224 | tf_op jit(solution)/shard_map/ppermute | solution.py:104
  31.6 5.0 %collective-permute-start.13 = (bf16[4,128,128]{2,1,0:T(8,128)(2,1)S(1)}, bf16[4,128,128]{2,1,0:T(8,128)(2,1)S(1)}, u32[]{:S(2)}, u32[]{:S(2)}) collective-permute-start(bf16[4,128,128]{2,1,0:T(8,128)(2,1)S(1)} %get-tuple-element.50), channel_id=1, source_target_pairs={{0,2},{2,0},{4,6},{6,4},{8,10},{10,8},{12,14},{14,12},{16,18},{18,... | collective-permute-start | bytes 393224 | tf_op jit(solution)/shard_map/ppermute | solution.py:104

commit v11 on v10

--- a/solution.py
+++ b/solution.py
@@ -125,18 +125,23 @@
     else:
         places = [lax.all_gather(tile_positions, "narrow", axis=1, tiled=True)]
         blocks = [lax.all_gather(integrals, "narrow", axis=1, tiled=True)]
-    first_along, first_across = outgoing[:far], outgoing[far:]
+    first_along, first_across = list(outgoing[:far]), outgoing[far:]
     got_across = [first_across[0]] + [None] * (near - 1)
     got_along = [first_along[0]] + [None] * (far - 1)
     for a in range(near - 1, 0, -1):
         got_across[a] = exchange(first_across[a], a)
     for b in range(far - 1, 0, -1):
+        if b == far // 2:
+            first_along[b], blocks[-1] = lax.optimization_barrier((first_along[b], blocks[-1]))
         got_along[b] = exchange(first_along[b], near * b)
     second_along, kept = regrouped(got_across, len(late), far - 1, (places[0], blocks[0]) if narrow == 2 else ())
     if narrow == 2:
         places[0], blocks[0] = kept
-    second_along, blocks[-1] = lax.optimization_barrier((second_along, blocks[-1]))
     got_along[0], second_along[-1] = lax.optimization_barrier((got_along[0], second_along[-1]))
+    middle = far // 2
+    got_along[middle], second_along[middle - 1] = lax.optimization_barrier(
+        (got_along[middle], second_along[middle - 1])
+    )
     last_along = [exchange(second_along[b - 1], near * b) for b in range(far - 1, 0, -1)]
     got_along[0], places[-1] = lax.optimization_barrier((got_along[0], places[-1]))
     second_across, _ = regrouped(got_along, len(early), near - 1)

time: 39.5 us -> 37.2 us (0.942)
  the two profiles are of different devices: /device:TPU:0 before, /device:TPU:18 now
where the time goes in v11:
time: 37.2 us; the launch traced here: 37 us
  waiting for transfers between devices  14.8 us (40%)
  starting transfers between devices  14.6 us (39%)
  local copies, waits for them, and re-layouts  3.97 us (11%)
  Pallas kernels  3.61 us (10%)
    ppermute x12, starting transfers between devices, exchange(): return lax.ppermute(array, 'wide', [(d, d ^ partner) for d in range(wide)])  14.6 us
    ppermute x12, waiting for transfers between devices, exchange(): return lax.ppermute(array, 'wide', [(d, d ^ partner) for d in range(wide)])  13.6 us
    unnamed x8, local copies, waits for them, and re-layouts  3.97 us
    pallas_call x1, Pallas kernels, on_device(): pl.pallas_call(functools.partial(contract, origins, cap, count), out_shap...  2.73 us
    ppermute x1, waiting for transfers between devices, on_device(): places = [tile_positions, lax.ppermute(tile_positions, 'narrow', swap)]  1.16 us
  transfers between devices with their start and end apart: 14, of which 8 were waited for; matrix products, arithmetic and copies ran while one was open for 0% of the time, Pallas kernels for 2%

profile of v11, /device:TPU:18, one launch (start us, length us, event | category | flops | bytes accessed | tf_op | source)
XLA Modules:
  0.0 37.0 jit_solution(8405914642125970531)
XLA Ops:
  0.0 0.0 collective-permute-start.5
  0.0 0.0 copy-start.1
  0.0 1.0 %copy-done.1 = bf16[16,128,128]{2,1,0:T(8,128)(2,1)S(1)} copy-done((bf16[16,128,128]{2,1,0:T(8,128)(2,1)S(1)}, bf16[16,128,128]{2,1,0:T(8,128)(2,1)}, u32[]{:S(2)}) %copy-start.1) | copy-done | bytes 524312
  1.0 0.0 copy-start.3
  1.0 0.7 %copy-done.3 = s32[1,32]{1,0:T(1,128)S(1)} copy-done((s32[1,32]{1,0:T(1,128)S(1)}, s32[1,32]{1,0:T(1,128)}, u32[]{:S(2)}) %copy-start.3) | copy-done | bytes 152
  1.7 0.7 %shard_map.46 = (bf16[4,128,128]{2,1,0:T(8,128)(2,1)S(1)}, bf16[4,128,128]{2,1,0:T(8,128)(2,1)S(1)}, bf16[4,128,128]{2,1,0:T(8,128)(2,1)S(1)}, bf16[4,128,128]{2...) custom-call(s32[1,32]{1,0:T(1,128)S(1)} %copy-done.3, ...), custom_call_target="tpu_custom_call" | custom-call | tf_op jit(solution)/shard_map/pallas_call | solution.py:109
  2.4 0.6 %collective-permute-start = (bf16[4,128,128]{2,1,0:T(8,128)(2,1)S(1)}, bf16[4,128,128]{2,1,0:T(8,128)(2,1)S(1)}, u32[]{:S(2)}, u32[]{:S(2)}) collective-permute-start(bf16[4,128,128]{2,1,0:T(8,128)(2,1)S(1)} %get-tuple-element.30), channel_id=1, source_target_pairs={{0,2},{2,0},{4,6},{6,4},{8,10},{10,8},{12,14},{14,12},{16,18},{18,... | collective-permute-start | bytes 393224 | tf_op jit(solution)/shard_map/ppermute | solution.py:104
  3.0 1.5 %collective-permute-start.1 = (bf16[4,128,128]{2,1,0:T(8,128)(2,1)S(1)}, bf16[4,128,128]{2,1,0:T(8,128)(2,1)S(1)}, u32[]{:S(2)}, u32[]{:S(2)}) collective-permute-start(bf16[4,128,128]{2,1,0:T(8,128)(2,1)S(1)} %get-tuple-element.31), channel_id=1, source_target_pairs={{0,4},{2,6},{4,0},{6,2},{8,12},{10,14},{12,8},{14,10},{16,20},{18,... | collective-permute-start | bytes 393224 | tf_op jit(solution)/shard_map/ppermute | solution.py:104
  4.5 1.4 %collective-permute-start.2 = (bf16[4,128,128]{2,1,0:T(8,128)(2,1)S(1)}, bf16[4,128,128]{2,1,0:T(8,128)(2,1)S(1)}, u32[]{:S(2)}, u32[]{:S(2)}) collective-permute-start(bf16[4,128,128]{2,1,0:T(8,128)(2,1)S(1)} %get-tuple-element.32), channel_id=1, source_target_pairs={{0,6},{2,4},{4,2},{6,0},{8,14},{10,12},{12,10},{14,8},{16,22},{18,... | collective-permute-start | bytes 393224 | tf_op jit(solution)/shard_map/ppermute | solution.py:104
  5.9 0.0 collective-permute-done.5.refs_17_
  5.9 0.3 collective-permute-start.6
  6.3 2.7 %collective-permute-start.4 = (bf16[4,128,128]{2,1,0:T(8,128)(2,1)S(1)}, bf16[4,128,128]{2,1,0:T(8,128)(2,1)S(1)}, u32[]{:S(2)}, u32[]{:S(2)}) collective-permute-start(bf16[4,128,128]{2,1,0:T(8,128)(2,1)S(1)} %get-tuple-element.39), channel_id=1, source_target_pairs={{0,24},{2,26},{4,28},{6,30},{8,16},{10,18},{12,20},{14,22},{16,8},... | collective-permute-start | bytes 393224 | tf_op jit(solution)/shard_map/ppermute | solution.py:104
  9.0 0.0 collective-permute-done.refs_1_.refs_3_
  9.0 1.3 %collective-permute-start.7 = (bf16[4,128,128]{2,1,0:T(8,128)(2,1)S(1)}, bf16[4,128,128]{2,1,0:T(8,128)(2,1)S(1)}, u32[]{:S(2)}, u32[]{:S(2)}) collective-permute-start(bf16[4,128,128]{2,1,0:T(8,128)(2,1)S(1)} %get-tuple-element.44), channel_id=1, source_target_pairs={{0,8},{2,10},{4,12},{6,14},{8,0},{10,2},{12,4},{14,6},{16,24},{18,... | collective-permute-start | bytes 393224 | tf_op jit(solution)/shard_map/ppermute | solution.py:104
  10.3 0.2 collective-permute-done.1.refs_2_.refs_4_
  10.5 1.6 %collective-permute-done.2.refs_3_.refs_5_ = bf16[4,128,128]{2,1,0:T(8,128)(2,1)S(1)} collective-permute-done((bf16[4,128,128]{2,1,0:T(8,128)(2,1)S(1)}, bf16[4,128,128]{2,1,0:T(8,128)(2,1)S(1)}, u32[]{:S(2)}, u32[]{:S(2)}) %collective-permute-start.2) | collective-permute-done | bytes 131104 | tf_op jit(solution)/shard_map/ppermute | solution.py:104
  12.1 0.0 copy-start
  12.1 1.6 %copy-done = bf16[8,8,128,128]{3,2,1,0:T(8,128)(2,1)S(1)} copy-done((bf16[8,8,128,128]{3,2,1,0:T(8,128)(2,1)S(1)}, bf16[8,8,128,128]{3,2,1,0:T(8,128)(2,1)}, u32[]{:S(2)}) %copy-start) | copy-done | bytes 2097176
  13.7 0.0 copy-start.2
  13.7 0.7 %copy-done.2 = s32[8,8]{1,0:T(8,128)S(1)} copy-done((s32[8,8]{1,0:T(8,128)S(1)}, s32[8,8]{1,0:T(8,128)}, u32[]{:S(2)}) %copy-start.2) | copy-done | bytes 280
  14.4 0.2 shard_map.47
  14.6 0.5 %collective-permute-start.8 = (bf16[4,128,128]{2,1,0:T(8,128)(2,1)S(1)}, bf16[4,128,128]{2,1,0:T(8,128)(2,1)S(1)}, u32[]{:S(2)}, u32[]{:S(2)}) collective-permute-start(bf16[4,128,128]{2,1,0:T(8,128)(2,1)S(1)} %get-tuple-element.45), channel_id=1, source_target_pairs={{0,24},{2,26},{4,28},{6,30},{8,16},{10,18},{12,20},{14,22},{16,8},... | collective-permute-start | bytes 393224 | tf_op jit(solution)/shard_map/ppermute | solution.py:104
  15.1 0.0 collective-permute-start.3
  15.1 1.2 %collective-permute-done.3.refs_1_ = s32[8,8]{1,0:T(8,128)S(1)} collective-permute-done((s32[8,8]{1,0:T(8,128)S(1)}, s32[8,8]{1,0:T(8,128)S(1)}, u32[]{:S(2)}, u32[]{:S(2)}) %collective-permute-start.3) | collective-permute-done | bytes 288 | tf_op jit(solution)/shard_map/ppermute | solution.py:123
  16.3 1.3 %collective-permute-start.10 = (bf16[4,128,128]{2,1,0:T(8,128)(2,1)S(1)}, bf16[4,128,128]{2,1,0:T(8,128)(2,1)S(1)}, u32[]{:S(2)}, u32[]{:S(2)}) collective-permute-start(bf16[4,128,128]{2,1,0:T(8,128)(2,1)S(1)} %get-tuple-element.47), channel_id=1, source_target_pairs={{0,8},{2,10},{4,12},{6,14},{8,0},{10,2},{12,4},{14,6},{16,24},{18,... | collective-permute-start | bytes 393224 | tf_op jit(solution)/shard_map/ppermute | solution.py:104
  17.6 0.0 collective-permute-done.6.refs_2_.refs_8_
  17.6 2.1 %collective-permute-start.9 = (bf16[4,128,128]{2,1,0:T(8,128)(2,1)S(1)}, bf16[4,128,128]{2,1,0:T(8,128)(2,1)S(1)}, u32[]{:S(2)}, u32[]{:S(2)}) collective-permute-start(bf16[4,128,128]{2,1,0:T(8,128)(2,1)S(1)} %get-tuple-element.46), channel_id=1, source_target_pairs={{0,16},{2,18},{4,20},{6,22},{8,24},{10,26},{12,28},{14,30},{16,0},... | collective-permute-start | bytes 393224 | tf_op jit(solution)/shard_map/ppermute | solution.py:104
  19.8 3.5 %collective-permute-done.4.refs_3_.refs_7_ = bf16[4,128,128]{2,1,0:T(8,128)(2,1)S(1)} collective-permute-done((bf16[4,128,128]{2,1,0:T(8,128)(2,1)S(1)}, bf16[4,128,128]{2,1,0:T(8,128)(2,1)S(1)}, u32[]{:S(2)}, u32[]{:S(2)}) %collective-permute-start.4) | collective-permute-done | bytes 131104 | tf_op jit(solution)/shard_map/ppermute | solution.py:104
  23.3 0.0 collective-permute-done.7.refs_1_.refs_9_
  23.3 1.6 %collective-permute-start.11 = (bf16[4,128,128]{2,1,0:T(8,128)(2,1)S(1)}, bf16[4,128,128]{2,1,0:T(8,128)(2,1)S(1)}, u32[]{:S(2)}, u32[]{:S(2)}) collective-permute-start(bf16[4,128,128]{2,1,0:T(8,128)(2,1)S(1)} %get-tuple-element.48), channel_id=1, source_target_pairs={{0,6},{2,4},{4,2},{6,0},{8,14},{10,12},{12,10},{14,8},{16,22},{18,... | collective-permute-start | bytes 393224 | tf_op jit(solution)/shard_map/ppermute | solution.py:104
  24.9 0.5 %collective-permute-start.12 = (bf16[4,128,128]{2,1,0:T(8,128)(2,1)S(1)}, bf16[4,128,128]{2,1,0:T(8,128)(2,1)S(1)}, u32[]{:S(2)}, u32[]{:S(2)}) collective-permute-start(bf16[4,128,128]{2,1,0:T(8,128)(2,1)S(1)} %get-tuple-element.49), channel_id=1, source_target_pairs={{0,4},{2,6},{4,0},{6,2},{8,12},{10,14},{12,8},{14,10},{16,20},{18,... | collective-permute-start | bytes 393224 | tf_op jit(solution)/shard_map/ppermute | solution.py:104
  25.4 3.5 %collective-permute-done.8.refs_10_ = bf16[4,128,128]{2,1,0:T(8,128)(2,1)S(1)} collective-permute-done((bf16[4,128,128]{2,1,0:T(8,128)(2,1)S(1)}, bf16[4,128,128]{2,1,0:T(8,128)(2,1)S(1)}, u32[]{:S(2)}, u32[]{:S(2)}) %collective-permute-start.8) | collective-permute-done | bytes 131104 | tf_op jit(solution)/shard_map/ppermute | solution.py:104
  28.9 0.5 %collective-permute-start.13 = (bf16[4,128,128]{2,1,0:T(8,128)(2,1)S(1)}, bf16[4,128,128]{2,1,0:T(8,128)(2,1)S(1)}, u32[]{:S(2)}, u32[]{:S(2)}) collective-permute-start(bf16[4,128,128]{2,1,0:T(8,128)(2,1)S(1)} %get-tuple-element.50), channel_id=1, source_target_pairs={{0,2},{2,0},{4,6},{6,4},{8,10},{10,8},{12,14},{14,12},{16,18},{18,... | collective-permute-start | bytes 393224 | tf_op jit(solution)/shard_map/ppermute | solution.py:104
  29.4 0.0 collective-permute-done.10.refs_12_
  29.4 0.0 collective-permute-done.9.refs_11_
  29.4 0.3 collective-permute-done.11.refs_13_
  29.7 2.7 %collective-permute-done.12.refs_14_ = bf16[4,128,128]{2,1,0:T(8,128)(2,1)S(1)} collective-permute-done((bf16[4,128,128]{2,1,0:T(8,128)(2,1)S(1)}, bf16[4,128,128]{2,1,0:T(8,128)(2,1)S(1)}, u32[]{:S(2)}, u32[]{:S(2)}) %collective-permute-start.12) | collective-permute-done | bytes 131104 | tf_op jit(solution)/shard_map/ppermute | solution.py:104
  32.4 1.8 %collective-permute-done.13.refs_15_ = bf16[4,128,128]{2,1,0:T(8,128)(2,1)S(1)} collective-permute-done((bf16[4,128,128]{2,1,0:T(8,128)(2,1)S(1)}, bf16[4,128,128]{2,1,0:T(8,128)(2,1)S(1)}, u32[]{:S(2)}, u32[]{:S(2)}) %collective-permute-start.13) | collective-permute-done | bytes 131104 | tf_op jit(solution)/shard_map/ppermute | solution.py:104
  34.2 2.7 %shard_map.49 = bf16[8,128,128]{2,1,0:T(8,128)(2,1)} custom-call(s32[8,8]{1,0:T(8,128)S(1)} %get-tuple-element.33.refs_0_, s32[8,8]{1,0:T(8,128)S(1)} %collective-permute-done.3.refs_1_, bf16[4,128,128]{2,1,0:T(8,128)(2,1)S(1)} %get-tuple-element.29.refs_0_.refs_2_, bf16[4,128,128]{2,1,0:T(8,128)(2,1)S(1)} %collective-permute-done.refs_1_.refs_3_, ...), custom_call_target="tpu_custom_call" | custom-call | tf_op jit(solution)/shard_map/pallas_call | solution.py:155
  (1 shorter events, 0.0 us)
Async XLA Ops:
  0.0 5.9 %collective-permute-start.5 = (bf16[8,8,128,128]{3,2,1,0:T(8,128)(2,1)}, bf16[8,8,128,128]{3,2,1,0:T(8,128)(2,1)S(1)}, u32[]{:S(2)}, u32[]{:S(2)}) collective-permute-start(bf16[8,8,128,128]{3,2,1,0:T(8,128)(2,1)} %refs_5_.1), channel_id=1, source_target_pairs={{0,1},{1,0},{2,3},{3,2},{4,5},{5,4},{6,7},{7,6},{8,9},{9,8},{10,11... | collective-permute-start | bytes 6291464 | tf_op jit(solution)/shard_map/ppermute | solution.py:124
  0.0 1.0 %copy-start.1 = (bf16[16,128,128]{2,1,0:T(8,128)(2,1)S(1)}, bf16[16,128,128]{2,1,0:T(8,128)(2,1)}, u32[]{:S(2)}) copy-start(bf16[16,128,128]{2,1,0:T(8,128)(2,1)} %amplitudes_ref.1) | copy-start | bytes 1572868
  1.0 0.7 %copy-start.3 = (s32[1,32]{1,0:T(1,128)S(1)}, s32[1,32]{1,0:T(1,128)}, u32[]{:S(2)}) copy-start(s32[1,32]{1,0:T(1,128)} %send_ref.1) | copy-start | bytes 388
  2.4 6.6 %collective-permute-start = (bf16[4,128,128]{2,1,0:T(8,128)(2,1)S(1)}, bf16[4,128,128]{2,1,0:T(8,128)(2,1)S(1)}, u32[]{:S(2)}, u32[]{:S(2)}) collective-permute-start(bf16[4,128,128]{2,1,0:T(8,128)(2,1)S(1)} %get-tuple-element.30), channel_id=1, source_target_pairs={{0,2},{2,0},{4,6},{6,4},{8,10},{10,8},{12,14},{14,12},{16,18},{18,... | collective-permute-start | bytes 393224 | tf_op jit(solution)/shard_map/ppermute | solution.py:104
  3.0 7.5 %collective-permute-start.1 = (bf16[4,128,128]{2,1,0:T(8,128)(2,1)S(1)}, bf16[4,128,128]{2,1,0:T(8,128)(2,1)S(1)}, u32[]{:S(2)}, u32[]{:S(2)}) collective-permute-start(bf16[4,128,128]{2,1,0:T(8,128)(2,1)S(1)} %get-tuple-element.31), channel_id=1, source_target_pairs={{0,4},{2,6},{4,0},{6,2},{8,12},{10,14},{12,8},{14,10},{16,20},{18,... | collective-permute-start | bytes 393224 | tf_op jit(solution)/shard_map/ppermute | solution.py:104
  4.5 7.6 %collective-permute-start.2 = (bf16[4,128,128]{2,1,0:T(8,128)(2,1)S(1)}, bf16[4,128,128]{2,1,0:T(8,128)(2,1)S(1)}, u32[]{:S(2)}, u32[]{:S(2)}) collective-permute-start(bf16[4,128,128]{2,1,0:T(8,128)(2,1)S(1)} %get-tuple-element.32), channel_id=1, source_target_pairs={{0,6},{2,4},{4,2},{6,0},{8,14},{10,12},{12,10},{14,8},{16,22},{18,... | collective-permute-start | bytes 393224 | tf_op jit(solution)/shard_map/ppermute | solution.py:104
  5.9 11.7 %collective-permute-start.6 = (bf16[4,128,128]{2,1,0:T(8,128)(2,1)S(1)}, bf16[4,128,128]{2,1,0:T(8,128)(2,1)S(1)}, u32[]{:S(2)}, u32[]{:S(2)}) collective-permute-start(bf16[4,128,128]{2,1,0:T(8,128)(2,1)S(1)} %get-tuple-element.41), channel_id=1, source_target_pairs={{0,16},{2,18},{4,20},{6,22},{8,24},{10,26},{12,28},{14,30},{16,0},... | collective-permute-start | bytes 393224 | tf_op jit(solution)/shard_map/ppermute | solution.py:104
  6.3 17.0 %collective-permute-start.4 = (bf16[4,128,128]{2,1,0:T(8,128)(2,1)S(1)}, bf16[4,128,128]{2,1,0:T(8,128)(2,1)S(1)}, u32[]{:S(2)}, u32[]{:S(2)}) collective-permute-start(bf16[4,128,128]{2,1,0:T(8,128)(2,1)S(1)} %get-tuple-element.39), channel_id=1, source_target_pairs={{0,24},{2,26},{4,28},{6,30},{8,16},{10,18},{12,20},{14,22},{16,8},... | collective-permute-start | bytes 393224 | tf_op jit(solution)/shard_map/ppermute | solution.py:104
  9.0 14.3 %collective-permute-start.7 = (bf16[4,128,128]{2,1,0:T(8,128)(2,1)S(1)}, bf16[4,128,128]{2,1,0:T(8,128)(2,1)S(1)}, u32[]{:S(2)}, u32[]{:S(2)}) collective-permute-start(bf16[4,128,128]{2,1,0:T(8,128)(2,1)S(1)} %get-tuple-element.44), channel_id=1, source_target_pairs={{0,8},{2,10},{4,12},{6,14},{8,0},{10,2},{12,4},{14,6},{16,24},{18,... | collective-permute-start | bytes 393224 | tf_op jit(solution)/shard_map/ppermute | solution.py:104
  12.1 1.6 %copy-start = (bf16[8,8,128,128]{3,2,1,0:T(8,128)(2,1)S(1)}, bf16[8,8,128,128]{3,2,1,0:T(8,128)(2,1)}, u32[]{:S(2)}) copy-start(bf16[8,8,128,128]{3,2,1,0:T(8,128)(2,1)} %refs_5_.1) | copy-start | bytes 6291460
  13.7 0.7 %copy-start.2 = (s32[8,8]{1,0:T(8,128)S(1)}, s32[8,8]{1,0:T(8,128)}, u32[]{:S(2)}) copy-start(s32[8,8]{1,0:T(8,128)} %refs_4_.1) | copy-start | bytes 772
  14.6 14.3 %collective-permute-start.8 = (bf16[4,128,128]{2,1,0:T(8,128)(2,1)S(1)}, bf16[4,128,128]{2,1,0:T(8,128)(2,1)S(1)}, u32[]{:S(2)}, u32[]{:S(2)}) collective-permute-start(bf16[4,128,128]{2,1,0:T(8,128)(2,1)S(1)} %get-tuple-element.45), channel_id=1, source_target_pairs={{0,24},{2,26},{4,28},{6,30},{8,16},{10,18},{12,20},{14,22},{16,8},... | collective-permute-start | bytes 393224 | tf_op jit(solution)/shard_map/ppermute | solution.py:104
  15.1 1.2 %collective-permute-start.3 = (s32[8,8]{1,0:T(8,128)S(1)}, s32[8,8]{1,0:T(8,128)S(1)}, u32[]{:S(2)}, u32[]{:S(2)}) collective-permute-start(s32[8,8]{1,0:T(8,128)S(1)} %copy-done.2), channel_id=1, source_target_pairs={{0,1},{1,0},{2,3},{3,2},{4,5},{5,4},{6,7},{7,6},{8,9},{9,8},{10,11... | collective-permute-start | bytes 776 | tf_op jit(solution)/shard_map/ppermute | solution.py:123
  16.3 13.2 %collective-permute-start.10 = (bf16[4,128,128]{2,1,0:T(8,128)(2,1)S(1)}, bf16[4,128,128]{2,1,0:T(8,128)(2,1)S(1)}, u32[]{:S(2)}, u32[]{:S(2)}) collective-permute-start(bf16[4,128,128]{2,1,0:T(8,128)(2,1)S(1)} %get-tuple-element.47), channel_id=1, source_target_pairs={{0,8},{2,10},{4,12},{6,14},{8,0},{10,2},{12,4},{14,6},{16,24},{18,... | collective-permute-start | bytes 393224 | tf_op jit(solution)/shard_map/ppermute | solution.py:104
  17.6 11.8 %collective-permute-start.9 = (bf16[4,128,128]{2,1,0:T(8,128)(2,1)S(1)}, bf16[4,128,128]{2,1,0:T(8,128)(2,1)S(1)}, u32[]{:S(2)}, u32[]{:S(2)}) collective-permute-start(bf16[4,128,128]{2,1,0:T(8,128)(2,1)S(1)} %get-tuple-element.46), channel_id=1, source_target_pairs={{0,16},{2,18},{4,20},{6,22},{8,24},{10,26},{12,28},{14,30},{16,0},... | collective-permute-start | bytes 393224 | tf_op jit(solution)/shard_map/ppermute | solution.py:104
  23.3 6.4 %collective-permute-start.11 = (bf16[4,128,128]{2,1,0:T(8,128)(2,1)S(1)}, bf16[4,128,128]{2,1,0:T(8,128)(2,1)S(1)}, u32[]{:S(2)}, u32[]{:S(2)}) collective-permute-start(bf16[4,128,128]{2,1,0:T(8,128)(2,1)S(1)} %get-tuple-element.48), channel_id=1, source_target_pairs={{0,6},{2,4},{4,2},{6,0},{8,14},{10,12},{12,10},{14,8},{16,22},{18,... | collective-permute-start | bytes 393224 | tf_op jit(solution)/shard_map/ppermute | solution.py:104
  24.9 7.5 %collective-permute-start.12 = (bf16[4,128,128]{2,1,0:T(8,128)(2,1)S(1)}, bf16[4,128,128]{2,1,0:T(8,128)(2,1)S(1)}, u32[]{:S(2)}, u32[]{:S(2)}) collective-permute-start(bf16[4,128,128]{2,1,0:T(8,128)(2,1)S(1)} %get-tuple-element.49), channel_id=1, source_target_pairs={{0,4},{2,6},{4,0},{6,2},{8,12},{10,14},{12,8},{14,10},{16,20},{18,... | collective-permute-start | bytes 393224 | tf_op jit(solution)/shard_map/ppermute | solution.py:104
  28.9 5.3 %collective-permute-start.13 = (bf16[4,128,128]{2,1,0:T(8,128)(2,1)S(1)}, bf16[4,128,128]{2,1,0:T(8,128)(2,1)S(1)}, u32[]{:S(2)}, u32[]{:S(2)}) collective-permute-start(bf16[4,128,128]{2,1,0:T(8,128)(2,1)S(1)} %get-tuple-element.50), channel_id=1, source_target_pairs={{0,2},{2,0},{4,6},{6,4},{8,10},{10,8},{12,14},{14,12},{16,18},{18,... | collective-permute-start | bytes 393224 | tf_op jit(solution)/shard_map/ppermute | solution.py:104

commit v12 on v11

--- a/solution.py
+++ b/solution.py
@@ -139,9 +139,7 @@
         places[0], blocks[0] = kept
     got_along[0], second_along[-1] = lax.optimization_barrier((got_along[0], second_along[-1]))
     middle = far // 2
-    got_along[middle], second_along[middle - 1] = lax.optimization_barrier(
-        (got_along[middle], second_along[middle - 1])
-    )
+    got_along[middle], second_along[0] = lax.optimization_barrier((got_along[middle], second_along[0]))
     last_along = [exchange(second_along[b - 1], near * b) for b in range(far - 1, 0, -1)]
     got_along[0], places[-1] = lax.optimization_barrier((got_along[0], places[-1]))
     second_across, _ = regrouped(got_along, len(early), near - 1)

time: 37.2 us -> 38.4 us (1.032)
  the two profiles are of different devices: /device:TPU:18 before, /device:TPU:19 now
where the time goes in v12:
time: 38.4 us; the launch traced here: 38.1 us
  waiting for transfers between devices  17.1 us (45%)
  starting transfers between devices  13.4 us (35%)
  local copies, waits for them, and re-layouts  3.97 us (10%)
  Pallas kernels  3.62 us (9%)
    ppermute x12, waiting for transfers between devices, exchange(): return lax.ppermute(array, 'wide', [(d, d ^ partner) for d in range(wide)])  16.3 us
    ppermute x12, starting transfers between devices, exchange(): return lax.ppermute(array, 'wide', [(d, d ^ partner) for d in range(wide)])  11.7 us
    unnamed x8, local copies, waits for them, and re-layouts  3.97 us
    pallas_call x1, Pallas kernels, on_device(): pl.pallas_call(functools.partial(contract, origins, cap, count), out_shap...  2.73 us
    ppermute x1, starting transfers between devices, on_device(): places = [tile_positions, lax.ppermute(tile_positions, 'narrow', swap)]  1.06 us
    ppermute x1, waiting for transfers between devices, on_device(): places = [tile_positions, lax.ppermute(tile_positions, 'narrow', swap)]  0.82 us
  transfers between devices with their start and end apart: 14, of which 6 were waited for; matrix products, arithmetic and copies ran while one was open for 0% of the time, Pallas kernels for 2%

profile of v12, /device:TPU:19, one launch (start us, length us, event | category | flops | bytes accessed | tf_op | source)
XLA Modules:
  0.0 38.1 jit_solution(6995540556334497879)
XLA Ops:
  0.0 0.7 %collective-permute-start.5 = (bf16[8,8,128,128]{3,2,1,0:T(8,128)(2,1)}, bf16[8,8,128,128]{3,2,1,0:T(8,128)(2,1)S(1)}, u32[]{:S(2)}, u32[]{:S(2)}) collective-permute-start(bf16[8,8,128,128]{3,2,1,0:T(8,128)(2,1)} %refs_5_.1), channel_id=1, source_target_pairs={{0,1},{1,0},{2,3},{3,2},{4,5},{5,4},{6,7},{7,6},{8,9},{9,8},{10,11... | collective-permute-start | bytes 6291464 | tf_op jit(solution)/shard_map/ppermute | solution.py:124
  0.7 0.0 copy-start.1
  0.7 1.0 %copy-done.1 = bf16[16,128,128]{2,1,0:T(8,128)(2,1)S(1)} copy-done((bf16[16,128,128]{2,1,0:T(8,128)(2,1)S(1)}, bf16[16,128,128]{2,1,0:T(8,128)(2,1)}, u32[]{:S(2)}) %copy-start.1) | copy-done | bytes 524312
  1.7 0.0 copy-start.3
  1.7 0.7 %copy-done.3 = s32[1,32]{1,0:T(1,128)S(1)} copy-done((s32[1,32]{1,0:T(1,128)S(1)}, s32[1,32]{1,0:T(1,128)}, u32[]{:S(2)}) %copy-start.3) | copy-done | bytes 152
  2.4 0.7 %shard_map.46 = (bf16[4,128,128]{2,1,0:T(8,128)(2,1)S(1)}, bf16[4,128,128]{2,1,0:T(8,128)(2,1)S(1)}, bf16[4,128,128]{2,1,0:T(8,128)(2,1)S(1)}, bf16[4,128,128]{2...) custom-call(s32[1,32]{1,0:T(1,128)S(1)} %copy-done.3, ...), custom_call_target="tpu_custom_call" | custom-call | tf_op jit(solution)/shard_map/pallas_call | solution.py:109
  3.1 0.3 collective-permute-start
  3.4 1.2 %collective-permute-start.1 = (bf16[4,128,128]{2,1,0:T(8,128)(2,1)S(1)}, bf16[4,128,128]{2,1,0:T(8,128)(2,1)S(1)}, u32[]{:S(2)}, u32[]{:S(2)}) collective-permute-start(bf16[4,128,128]{2,1,0:T(8,128)(2,1)S(1)} %get-tuple-element.31), channel_id=1, source_target_pairs={{0,4},{2,6},{4,0},{6,2},{8,12},{10,14},{12,8},{14,10},{16,20},{18,... | collective-permute-start | bytes 393224 | tf_op jit(solution)/shard_map/ppermute | solution.py:104
  4.6 1.2 %collective-permute-start.2 = (bf16[4,128,128]{2,1,0:T(8,128)(2,1)S(1)}, bf16[4,128,128]{2,1,0:T(8,128)(2,1)S(1)}, u32[]{:S(2)}, u32[]{:S(2)}) collective-permute-start(bf16[4,128,128]{2,1,0:T(8,128)(2,1)S(1)} %get-tuple-element.32), channel_id=1, source_target_pairs={{0,6},{2,4},{4,2},{6,0},{8,14},{10,12},{12,10},{14,8},{16,22},{18,... | collective-permute-start | bytes 393224 | tf_op jit(solution)/shard_map/ppermute | solution.py:104
  5.8 0.0 collective-permute-done.5.refs_17_
  5.8 0.1 collective-permute-start.6
  5.8 2.4 %collective-permute-start.4 = (bf16[4,128,128]{2,1,0:T(8,128)(2,1)S(1)}, bf16[4,128,128]{2,1,0:T(8,128)(2,1)S(1)}, u32[]{:S(2)}, u32[]{:S(2)}) collective-permute-start(bf16[4,128,128]{2,1,0:T(8,128)(2,1)S(1)} %get-tuple-element.39), channel_id=1, source_target_pairs={{0,24},{2,26},{4,28},{6,30},{8,16},{10,18},{12,20},{14,22},{16,8},... | collective-permute-start | bytes 393224 | tf_op jit(solution)/shard_map/ppermute | solution.py:104
  8.3 0.0 collective-permute-done.refs_1_.refs_3_
  8.3 1.3 %collective-permute-start.7 = (bf16[4,128,128]{2,1,0:T(8,128)(2,1)S(1)}, bf16[4,128,128]{2,1,0:T(8,128)(2,1)S(1)}, u32[]{:S(2)}, u32[]{:S(2)}) collective-permute-start(bf16[4,128,128]{2,1,0:T(8,128)(2,1)S(1)} %get-tuple-element.44), channel_id=1, source_target_pairs={{0,8},{2,10},{4,12},{6,14},{8,0},{10,2},{12,4},{14,6},{16,24},{18,... | collective-permute-start | bytes 393224 | tf_op jit(solution)/shard_map/ppermute | solution.py:104
  9.5 0.0 collective-permute-done.1.refs_2_.refs_4_
  9.6 2.5 %collective-permute-done.2.refs_3_.refs_5_ = bf16[4,128,128]{2,1,0:T(8,128)(2,1)S(1)} collective-permute-done((bf16[4,128,128]{2,1,0:T(8,128)(2,1)S(1)}, bf16[4,128,128]{2,1,0:T(8,128)(2,1)S(1)}, u32[]{:S(2)}, u32[]{:S(2)}) %collective-permute-start.2) | collective-permute-done | bytes 131104 | tf_op jit(solution)/shard_map/ppermute | solution.py:104
  12.0 0.0 copy-start
  12.0 1.6 %copy-done = bf16[8,8,128,128]{3,2,1,0:T(8,128)(2,1)S(1)} copy-done((bf16[8,8,128,128]{3,2,1,0:T(8,128)(2,1)S(1)}, bf16[8,8,128,128]{3,2,1,0:T(8,128)(2,1)}, u32[]{:S(2)}) %copy-start) | copy-done | bytes 2097176
  13.6 0.0 copy-start.2
  13.6 0.7 %copy-done.2 = s32[8,8]{1,0:T(8,128)S(1)} copy-done((s32[8,8]{1,0:T(8,128)S(1)}, s32[8,8]{1,0:T(8,128)}, u32[]{:S(2)}) %copy-start.2) | copy-done | bytes 280
  14.3 0.2 shard_map.47
  14.5 0.2 collective-permute-start.8
  14.7 1.1 %collective-permute-start.3 = (s32[8,8]{1,0:T(8,128)S(1)}, s32[8,8]{1,0:T(8,128)S(1)}, u32[]{:S(2)}, u32[]{:S(2)}) collective-permute-start(s32[8,8]{1,0:T(8,128)S(1)} %copy-done.2), channel_id=1, source_target_pairs={{0,1},{1,0},{2,3},{3,2},{4,5},{5,4},{6,7},{7,6},{8,9},{9,8},{10,11... | collective-permute-start | bytes 776 | tf_op jit(solution)/shard_map/ppermute | solution.py:123
  15.8 0.8 %collective-permute-done.3.refs_1_ = s32[8,8]{1,0:T(8,128)S(1)} collective-permute-done((s32[8,8]{1,0:T(8,128)S(1)}, s32[8,8]{1,0:T(8,128)S(1)}, u32[]{:S(2)}, u32[]{:S(2)}) %collective-permute-start.3) | collective-permute-done | bytes 288 | tf_op jit(solution)/shard_map/ppermute | solution.py:123
  16.6 3.2 %collective-permute-start.9 = (bf16[4,128,128]{2,1,0:T(8,128)(2,1)S(1)}, bf16[4,128,128]{2,1,0:T(8,128)(2,1)S(1)}, u32[]{:S(2)}, u32[]{:S(2)}) collective-permute-start(bf16[4,128,128]{2,1,0:T(8,128)(2,1)S(1)} %get-tuple-element.46), channel_id=1, source_target_pairs={{0,16},{2,18},{4,20},{6,22},{8,24},{10,26},{12,28},{14,30},{16,0},... | collective-permute-start | bytes 393224 | tf_op jit(solution)/shard_map/ppermute | solution.py:104
  19.8 0.0 collective-permute-done.6.refs_2_.refs_8_
  19.8 0.0 collective-permute-start.10
  19.8 6.4 %collective-permute-done.4.refs_3_.refs_7_ = bf16[4,128,128]{2,1,0:T(8,128)(2,1)S(1)} collective-permute-done((bf16[4,128,128]{2,1,0:T(8,128)(2,1)S(1)}, bf16[4,128,128]{2,1,0:T(8,128)(2,1)S(1)}, u32[]{:S(2)}, u32[]{:S(2)}) %collective-permute-start.4) | collective-permute-done | bytes 131104 | tf_op jit(solution)/shard_map/ppermute | solution.py:104
  26.2 0.0 collective-permute-done.7.refs_1_.refs_9_
  26.2 1.3 %collective-permute-start.11 = (bf16[4,128,128]{2,1,0:T(8,128)(2,1)S(1)}, bf16[4,128,128]{2,1,0:T(8,128)(2,1)S(1)}, u32[]{:S(2)}, u32[]{:S(2)}) collective-permute-start(bf16[4,128,128]{2,1,0:T(8,128)(2,1)S(1)} %get-tuple-element.48), channel_id=1, source_target_pairs={{0,6},{2,4},{4,2},{6,0},{8,14},{10,12},{12,10},{14,8},{16,22},{18,... | collective-permute-start | bytes 393224 | tf_op jit(solution)/shard_map/ppermute | solution.py:104
  27.5 0.2 collective-permute-start.12
  27.7 1.3 %collective-permute-done.8.refs_10_ = bf16[4,128,128]{2,1,0:T(8,128)(2,1)S(1)} collective-permute-done((bf16[4,128,128]{2,1,0:T(8,128)(2,1)S(1)}, bf16[4,128,128]{2,1,0:T(8,128)(2,1)S(1)}, u32[]{:S(2)}, u32[]{:S(2)}) %collective-permute-start.8) | collective-permute-done | bytes 131104 | tf_op jit(solution)/shard_map/ppermute | solution.py:104
  29.0 0.2 collective-permute-start.13
  29.2 0.0 collective-permute-done.9.refs_11_
  29.2 0.0 collective-permute-done.10.refs_12_
  29.3 2.4 %collective-permute-done.11.refs_13_ = bf16[4,128,128]{2,1,0:T(8,128)(2,1)S(1)} collective-permute-done((bf16[4,128,128]{2,1,0:T(8,128)(2,1)S(1)}, bf16[4,128,128]{2,1,0:T(8,128)(2,1)S(1)}, u32[]{:S(2)}, u32[]{:S(2)}) %collective-permute-start.11) | collective-permute-done | bytes 131104 | tf_op jit(solution)/shard_map/ppermute | solution.py:104
  31.6 3.8 %collective-permute-done.12.refs_14_ = bf16[4,128,128]{2,1,0:T(8,128)(2,1)S(1)} collective-permute-done((bf16[4,128,128]{2,1,0:T(8,128)(2,1)S(1)}, bf16[4,128,128]{2,1,0:T(8,128)(2,1)S(1)}, u32[]{:S(2)}, u32[]{:S(2)}) %collective-permute-start.12) | collective-permute-done | bytes 131104 | tf_op jit(solution)/shard_map/ppermute | solution.py:104
  35.4 0.0 collective-permute-done.13.refs_15_
  35.4 2.7 %shard_map.49 = bf16[8,128,128]{2,1,0:T(8,128)(2,1)} custom-call(s32[8,8]{1,0:T(8,128)S(1)} %get-tuple-element.33.refs_0_, s32[8,8]{1,0:T(8,128)S(1)} %collective-permute-done.3.refs_1_, bf16[4,128,128]{2,1,0:T(8,128)(2,1)S(1)} %get-tuple-element.29.refs_0_.refs_2_, bf16[4,128,128]{2,1,0:T(8,128)(2,1)S(1)} %collective-permute-done.refs_1_.refs_3_, ...), custom_call_target="tpu_custom_call" | custom-call | tf_op jit(solution)/shard_map/pallas_call | solution.py:153
  (1 shorter events, 0.0 us)
Async XLA Ops:
  0.0 5.8 %collective-permute-start.5 = (bf16[8,8,128,128]{3,2,1,0:T(8,128)(2,1)}, bf16[8,8,128,128]{3,2,1,0:T(8,128)(2,1)S(1)}, u32[]{:S(2)}, u32[]{:S(2)}) collective-permute-start(bf16[8,8,128,128]{3,2,1,0:T(8,128)(2,1)} %refs_5_.1), channel_id=1, source_target_pairs={{0,1},{1,0},{2,3},{3,2},{4,5},{5,4},{6,7},{7,6},{8,9},{9,8},{10,11... | collective-permute-start | bytes 6291464 | tf_op jit(solution)/shard_map/ppermute | solution.py:124
  0.7 1.0 %copy-start.1 = (bf16[16,128,128]{2,1,0:T(8,128)(2,1)S(1)}, bf16[16,128,128]{2,1,0:T(8,128)(2,1)}, u32[]{:S(2)}) copy-start(bf16[16,128,128]{2,1,0:T(8,128)(2,1)} %amplitudes_ref.1) | copy-start | bytes 1572868
  1.7 0.7 %copy-start.3 = (s32[1,32]{1,0:T(1,128)S(1)}, s32[1,32]{1,0:T(1,128)}, u32[]{:S(2)}) copy-start(s32[1,32]{1,0:T(1,128)} %send_ref.1) | copy-start | bytes 388
  3.1 5.2 %collective-permute-start = (bf16[4,128,128]{2,1,0:T(8,128)(2,1)S(1)}, bf16[4,128,128]{2,1,0:T(8,128)(2,1)S(1)}, u32[]{:S(2)}, u32[]{:S(2)}) collective-permute-start(bf16[4,128,128]{2,1,0:T(8,128)(2,1)S(1)} %get-tuple-element.30), channel_id=1, source_target_pairs={{0,2},{2,0},{4,6},{6,4},{8,10},{10,8},{12,14},{14,12},{16,18},{18,... | collective-permute-start | bytes 393224 | tf_op jit(solution)/shard_map/ppermute | solution.py:104
  3.4 6.2 %collective-permute-start.1 = (bf16[4,128,128]{2,1,0:T(8,128)(2,1)S(1)}, bf16[4,128,128]{2,1,0:T(8,128)(2,1)S(1)}, u32[]{:S(2)}, u32[]{:S(2)}) collective-permute-start(bf16[4,128,128]{2,1,0:T(8,128)(2,1)S(1)} %get-tuple-element.31), channel_id=1, source_target_pairs={{0,4},{2,6},{4,0},{6,2},{8,12},{10,14},{12,8},{14,10},{16,20},{18,... | collective-permute-start | bytes 393224 | tf_op jit(solution)/shard_map/ppermute | solution.py:104
  4.6 7.4 %collective-permute-start.2 = (bf16[4,128,128]{2,1,0:T(8,128)(2,1)S(1)}, bf16[4,128,128]{2,1,0:T(8,128)(2,1)S(1)}, u32[]{:S(2)}, u32[]{:S(2)}) collective-permute-start(bf16[4,128,128]{2,1,0:T(8,128)(2,1)S(1)} %get-tuple-element.32), channel_id=1, source_target_pairs={{0,6},{2,4},{4,2},{6,0},{8,14},{10,12},{12,10},{14,8},{16,22},{18,... | collective-permute-start | bytes 393224 | tf_op jit(solution)/shard_map/ppermute | solution.py:104
  5.8 14.1 %collective-permute-start.6 = (bf16[4,128,128]{2,1,0:T(8,128)(2,1)S(1)}, bf16[4,128,128]{2,1,0:T(8,128)(2,1)S(1)}, u32[]{:S(2)}, u32[]{:S(2)}) collective-permute-start(bf16[4,128,128]{2,1,0:T(8,128)(2,1)S(1)} %get-tuple-element.41), channel_id=1, source_target_pairs={{0,16},{2,18},{4,20},{6,22},{8,24},{10,26},{12,28},{14,30},{16,0},... | collective-permute-start | bytes 393224 | tf_op jit(solution)/shard_map/ppermute | solution.py:104
  5.8 20.4 %collective-permute-start.4 = (bf16[4,128,128]{2,1,0:T(8,128)(2,1)S(1)}, bf16[4,128,128]{2,1,0:T(8,128)(2,1)S(1)}, u32[]{:S(2)}, u32[]{:S(2)}) collective-permute-start(bf16[4,128,128]{2,1,0:T(8,128)(2,1)S(1)} %get-tuple-element.39), channel_id=1, source_target_pairs={{0,24},{2,26},{4,28},{6,30},{8,16},{10,18},{12,20},{14,22},{16,8},... | collective-permute-start | bytes 393224 | tf_op jit(solution)/shard_map/ppermute | solution.py:104
  8.3 17.9 %collective-permute-start.7 = (bf16[4,128,128]{2,1,0:T(8,128)(2,1)S(1)}, bf16[4,128,128]{2,1,0:T(8,128)(2,1)S(1)}, u32[]{:S(2)}, u32[]{:S(2)}) collective-permute-start(bf16[4,128,128]{2,1,0:T(8,128)(2,1)S(1)} %get-tuple-element.44), channel_id=1, source_target_pairs={{0,8},{2,10},{4,12},{6,14},{8,0},{10,2},{12,4},{14,6},{16,24},{18,... | collective-permute-start | bytes 393224 | tf_op jit(solution)/shard_map/ppermute | solution.py:104
  12.0 1.6 %copy-start = (bf16[8,8,128,128]{3,2,1,0:T(8,128)(2,1)S(1)}, bf16[8,8,128,128]{3,2,1,0:T(8,128)(2,1)}, u32[]{:S(2)}) copy-start(bf16[8,8,128,128]{3,2,1,0:T(8,128)(2,1)} %refs_5_.1) | copy-start | bytes 6291460
  13.6 0.7 %copy-start.2 = (s32[8,8]{1,0:T(8,128)S(1)}, s32[8,8]{1,0:T(8,128)}, u32[]{:S(2)}) copy-start(s32[8,8]{1,0:T(8,128)} %refs_4_.1) | copy-start | bytes 772
  14.5 14.5 %collective-permute-start.8 = (bf16[4,128,128]{2,1,0:T(8,128)(2,1)S(1)}, bf16[4,128,128]{2,1,0:T(8,128)(2,1)S(1)}, u32[]{:S(2)}, u32[]{:S(2)}) collective-permute-start(bf16[4,128,128]{2,1,0:T(8,128)(2,1)S(1)} %get-tuple-element.45), channel_id=1, source_target_pairs={{0,24},{2,26},{4,28},{6,30},{8,16},{10,18},{12,20},{14,22},{16,8},... | collective-permute-start | bytes 393224 | tf_op jit(solution)/shard_map/ppermute | solution.py:104
  14.7 1.9 %collective-permute-start.3 = (s32[8,8]{1,0:T(8,128)S(1)}, s32[8,8]{1,0:T(8,128)S(1)}, u32[]{:S(2)}, u32[]{:S(2)}) collective-permute-start(s32[8,8]{1,0:T(8,128)S(1)} %copy-done.2), channel_id=1, source_target_pairs={{0,1},{1,0},{2,3},{3,2},{4,5},{5,4},{6,7},{7,6},{8,9},{9,8},{10,11... | collective-permute-start | bytes 776 | tf_op jit(solution)/shard_map/ppermute | solution.py:123
  16.6 12.6 %collective-permute-start.9 = (bf16[4,128,128]{2,1,0:T(8,128)(2,1)S(1)}, bf16[4,128,128]{2,1,0:T(8,128)(2,1)S(1)}, u32[]{:S(2)}, u32[]{:S(2)}) collective-permute-start(bf16[4,128,128]{2,1,0:T(8,128)(2,1)S(1)} %get-tuple-element.46), channel_id=1, source_target_pairs={{0,16},{2,18},{4,20},{6,22},{8,24},{10,26},{12,28},{14,30},{16,0},... | collective-permute-start | bytes 393224 | tf_op jit(solution)/shard_map/ppermute | solution.py:104
  19.8 9.4 %collective-permute-start.10 = (bf16[4,128,128]{2,1,0:T(8,128)(2,1)S(1)}, bf16[4,128,128]{2,1,0:T(8,128)(2,1)S(1)}, u32[]{:S(2)}, u32[]{:S(2)}) collective-permute-start(bf16[4,128,128]{2,1,0:T(8,128)(2,1)S(1)} %get-tuple-element.47), channel_id=1, source_target_pairs={{0,8},{2,10},{4,12},{6,14},{8,0},{10,2},{12,4},{14,6},{16,24},{18,... | collective-permute-start | bytes 393224 | tf_op jit(solution)/shard_map/ppermute | solution.py:104
  26.2 5.4 %collective-permute-start.11 = (bf16[4,128,128]{2,1,0:T(8,128)(2,1)S(1)}, bf16[4,128,128]{2,1,0:T(8,128)(2,1)S(1)}, u32[]{:S(2)}, u32[]{:S(2)}) collective-permute-start(bf16[4,128,128]{2,1,0:T(8,128)(2,1)S(1)} %get-tuple-element.48), channel_id=1, source_target_pairs={{0,6},{2,4},{4,2},{6,0},{8,14},{10,12},{12,10},{14,8},{16,22},{18,... | collective-permute-start | bytes 393224 | tf_op jit(solution)/shard_map/ppermute | solution.py:104
  27.5 7.9 %collective-permute-start.12 = (bf16[4,128,128]{2,1,0:T(8,128)(2,1)S(1)}, bf16[4,128,128]{2,1,0:T(8,128)(2,1)S(1)}, u32[]{:S(2)}, u32[]{:S(2)}) collective-permute-start(bf16[4,128,128]{2,1,0:T(8,128)(2,1)S(1)} %get-tuple-element.49), channel_id=1, source_target_pairs={{0,4},{2,6},{4,0},{6,2},{8,12},{10,14},{12,8},{14,10},{16,20},{18,... | collective-permute-start | bytes 393224 | tf_op jit(solution)/shard_map/ppermute | solution.py:104
  29.0 6.4 %collective-permute-start.13 = (bf16[4,128,128]{2,1,0:T(8,128)(2,1)S(1)}, bf16[4,128,128]{2,1,0:T(8,128)(2,1)S(1)}, u32[]{:S(2)}, u32[]{:S(2)}) collective-permute-start(bf16[4,128,128]{2,1,0:T(8,128)(2,1)S(1)} %get-tuple-element.50), channel_id=1, source_target_pairs={{0,2},{2,0},{4,6},{6,4},{8,10},{10,8},{12,14},{14,12},{16,18},{18,... | collective-permute-start | bytes 393224 | tf_op jit(solution)/shard_map/ppermute | solution.py:104

commit v13 on v11

--- a/solution.py
+++ b/solution.py
@@ -92,6 +92,26 @@
     return list(outs[:count]), list(outs[count:])
 
 
+def copy_all(*refs):
+    half = len(refs) // 2
+    copies = [pltpu.make_async_copy(refs[i], refs[half + i], refs[-1].at[i]) for i in range(half)]
+    for copy in copies:
+        copy.start()
+    for copy in copies:
+        copy.wait()
+
+
+def staged_copy(*arrays):
+    return pl.pallas_call(
+        copy_all,
+        out_shape=[jax.ShapeDtypeStruct(a.shape, a.dtype) for a in arrays],
+        in_specs=[ANYWHERE] * len(arrays),
+        out_specs=[VMEM] * len(arrays),
+        scratch_shapes=[pltpu.SemaphoreType.DMA((len(arrays),))],
+        compiler_params=GRANT,
+    )(*arrays)
+
+
 def on_device(wide, narrow, amplitudes, send_list, tile_positions, integrals):
     cap = send_list.shape[1] // wide
     pairs, columns = amplitudes.shape[1:]
@@ -134,9 +154,7 @@
         if b == far // 2:
             first_along[b], blocks[-1] = lax.optimization_barrier((first_along[b], blocks[-1]))
         got_along[b] = exchange(first_along[b], near * b)
-    second_along, kept = regrouped(got_across, len(late), far - 1, (places[0], blocks[0]) if narrow == 2 else ())
-    if narrow == 2:
-        places[0], blocks[0] = kept
+    second_along, _ = regrouped(got_across, len(late), far - 1)
     got_along[0], second_along[-1] = lax.optimization_barrier((got_along[0], second_along[-1]))
     middle = far // 2
     got_along[middle], second_along[middle - 1] = lax.optimization_barrier(
@@ -144,6 +162,10 @@
     )
     last_along = [exchange(second_along[b - 1], near * b) for b in range(far - 1, 0, -1)]
     got_along[0], places[-1] = lax.optimization_barrier((got_along[0], places[-1]))
+    if narrow == 2:
+        source, got_along[middle] = lax.optimization_barrier((blocks[0], got_along[middle]))
+        places[0], blocks[0] = staged_copy(places[0], source)
+        got_along[0], blocks[0] = lax.optimization_barrier((got_along[0], blocks[0]))
     second_across, _ = regrouped(got_along, len(early), near - 1)
     last_across = [exchange(second_across[a - 1], a) for a in range(near - 1, 0, -1)]
     pieces = got_across + got_along[:1] + got_along[:0:-1] + last_along + last_across

time: 37.2 us -> 37.9 us (1.019)
  starting transfers between devices: 14.6 us -> 17.9 us
  waiting for transfers between devices: 14.8 us -> 12.1 us
    ppermute x12, starting transfers between devices: 14.6 us -> 17.9 us  [exchange(): return lax.ppermute(array, 'wide', [(d, d ^ partner) for d in range(wide)])]
    ppermute x12, waiting for transfers between devices: 13.6 us -> 10.7 us  [exchange(): return lax.ppermute(array, 'wide', [(d, d ^ partner) for d in range(wide)])]
  transfers between devices with their start and end apart: 14 -> 14, of which waited for: 8 -> 9; matrix products, arithmetic and copies ran while one was open for 0% -> 0% of each run, Pallas kernels for 2% -> 2%
where the time goes in v13:
time: 37.9 us; the launch traced here: 37.7 us
  starting transfers between devices  17.9 us (47%)
  waiting for transfers between devices  12.1 us (32%)
  local copies, waits for them, and re-layouts  3.97 us (10%)
  Pallas kernels  3.62 us (10%)
    ppermute x12, starting transfers between devices, exchange(): return lax.ppermute(array, 'wide', [(d, d ^ partner) for d in range(wide)])  17.9 us
    ppermute x12, waiting for transfers between devices, exchange(): return lax.ppermute(array, 'wide', [(d, d ^ partner) for d in range(wide)])  10.7 us
    unnamed x8, local copies, waits for them, and re-layouts  3.97 us
    pallas_call x1, Pallas kernels, on_device(): pl.pallas_call(functools.partial(contract, origins, cap, count), out_shap...  2.72 us
    ppermute x1, waiting for transfers between devices, on_device(): places = [tile_positions, lax.ppermute(tile_positions, 'narrow', swap)]  1.37 us
  transfers between devices with their start and end apart: 14, of which 9 were waited for; matrix products, arithmetic and copies ran while one was open for 0% of the time, Pallas kernels for 2%

profile of v13, /device:TPU:18, one launch (start us, length us, event | category | flops | bytes accessed | tf_op | source)
XLA Modules:
  0.0 37.7 jit_solution(10873557270571068886)
XLA Ops:
  0.0 0.0 collective-permute-start
  0.0 0.0 copy-start.1
  0.0 1.0 %copy-done.1 = bf16[16,128,128]{2,1,0:T(8,128)(2,1)S(1)} copy-done((bf16[16,128,128]{2,1,0:T(8,128)(2,1)S(1)}, bf16[16,128,128]{2,1,0:T(8,128)(2,1)}, u32[]{:S(2)}) %copy-start.1) | copy-done | bytes 524312
  1.0 0.0 copy-start.3
  1.0 0.7 %copy-done.3 = s32[1,32]{1,0:T(1,128)S(1)} copy-done((s32[1,32]{1,0:T(1,128)S(1)}, s32[1,32]{1,0:T(1,128)}, u32[]{:S(2)}) %copy-start.3) | copy-done | bytes 152
  1.7 0.7 %shard_map.46 = (bf16[4,128,128]{2,1,0:T(8,128)(2,1)S(1)}, bf16[4,128,128]{2,1,0:T(8,128)(2,1)S(1)}, bf16[4,128,128]{2,1,0:T(8,128)(2,1)S(1)}, bf16[4,128,128]{2...) custom-call(s32[1,32]{1,0:T(1,128)S(1)} %copy-done.3, ...), custom_call_target="tpu_custom_call" | custom-call | tf_op jit(solution)/shard_map/pallas_call | solution.py:129
  2.4 0.6 %collective-permute-start.2 = (bf16[4,128,128]{2,1,0:T(8,128)(2,1)S(1)}, bf16[4,128,128]{2,1,0:T(8,128)(2,1)S(1)}, u32[]{:S(2)}, u32[]{:S(2)}) collective-permute-start(bf16[4,128,128]{2,1,0:T(8,128)(2,1)S(1)} %get-tuple-element.36), channel_id=1, source_target_pairs={{0,2},{2,0},{4,6},{6,4},{8,10},{10,8},{12,14},{14,12},{16,18},{18,... | collective-permute-start | bytes 393224 | tf_op jit(solution)/shard_map/ppermute | solution.py:124
  3.0 1.5 %collective-permute-start.3 = (bf16[4,128,128]{2,1,0:T(8,128)(2,1)S(1)}, bf16[4,128,128]{2,1,0:T(8,128)(2,1)S(1)}, u32[]{:S(2)}, u32[]{:S(2)}) collective-permute-start(bf16[4,128,128]{2,1,0:T(8,128)(2,1)S(1)} %get-tuple-element.37), channel_id=1, source_target_pairs={{0,4},{2,6},{4,0},{6,2},{8,12},{10,14},{12,8},{14,10},{16,20},{18,... | collective-permute-start | bytes 393224 | tf_op jit(solution)/shard_map/ppermute | solution.py:124
  4.5 1.4 %collective-permute-start.4 = (bf16[4,128,128]{2,1,0:T(8,128)(2,1)S(1)}, bf16[4,128,128]{2,1,0:T(8,128)(2,1)S(1)}, u32[]{:S(2)}, u32[]{:S(2)}) collective-permute-start(bf16[4,128,128]{2,1,0:T(8,128)(2,1)S(1)} %get-tuple-element.38), channel_id=1, source_target_pairs={{0,6},{2,4},{4,2},{6,0},{8,14},{10,12},{12,10},{14,8},{16,22},{18,... | collective-permute-start | bytes 393224 | tf_op jit(solution)/shard_map/ppermute | solution.py:124
  5.9 0.0 collective-permute-done.refs_17_
  5.9 0.3 collective-permute-start.1
  6.3 2.7 %collective-permute-start.6 = (bf16[4,128,128]{2,1,0:T(8,128)(2,1)S(1)}, bf16[4,128,128]{2,1,0:T(8,128)(2,1)S(1)}, u32[]{:S(2)}, u32[]{:S(2)}) collective-permute-start(bf16[4,128,128]{2,1,0:T(8,128)(2,1)S(1)} %get-tuple-element.50), channel_id=1, source_target_pairs={{0,24},{2,26},{4,28},{6,30},{8,16},{10,18},{12,20},{14,22},{16,8},... | collective-permute-start | bytes 393224 | tf_op jit(solution)/shard_map/ppermute | solution.py:124
  9.0 0.0 collective-permute-done.2.refs_1_.refs_3_
  9.0 1.3 %collective-permute-start.7 = (bf16[4,128,128]{2,1,0:T(8,128)(2,1)S(1)}, bf16[4,128,128]{2,1,0:T(8,128)(2,1)S(1)}, u32[]{:S(2)}, u32[]{:S(2)}) collective-permute-start(bf16[4,128,128]{2,1,0:T(8,128)(2,1)S(1)} %get-tuple-element.52), channel_id=1, source_target_pairs={{0,8},{2,10},{4,12},{6,14},{8,0},{10,2},{12,4},{14,6},{16,24},{18,... | collective-permute-start | bytes 393224 | tf_op jit(solution)/shard_map/ppermute | solution.py:124
  10.3 0.2 collective-permute-done.3.refs_2_.refs_4_
  10.5 1.6 %collective-permute-done.4.refs_3_.refs_5_ = bf16[4,128,128]{2,1,0:T(8,128)(2,1)S(1)} collective-permute-done((bf16[4,128,128]{2,1,0:T(8,128)(2,1)S(1)}, bf16[4,128,128]{2,1,0:T(8,128)(2,1)S(1)}, u32[]{:S(2)}, u32[]{:S(2)}) %collective-permute-start.4) | collective-permute-done | bytes 131104 | tf_op jit(solution)/shard_map/ppermute | solution.py:124
  12.2 0.5 %collective-permute-start.8 = (bf16[4,128,128]{2,1,0:T(8,128)(2,1)S(1)}, bf16[4,128,128]{2,1,0:T(8,128)(2,1)S(1)}, u32[]{:S(2)}, u32[]{:S(2)}) collective-permute-start(bf16[4,128,128]{2,1,0:T(8,128)(2,1)S(1)} %get-tuple-element.53), channel_id=1, source_target_pairs={{0,24},{2,26},{4,28},{6,30},{8,16},{10,18},{12,20},{14,22},{16,8},... | collective-permute-start | bytes 393224 | tf_op jit(solution)/shard_map/ppermute | solution.py:124
  12.7 0.0 collective-permute-start.5
  12.7 1.4 %collective-permute-done.5.refs_1_ = s32[8,8]{1,0:T(8,128)S(1)} collective-permute-done((s32[8,8]{1,0:T(8,128)}, s32[8,8]{1,0:T(8,128)S(1)}, u32[]{:S(2)}, u32[]{:S(2)}) %collective-permute-start.5) | collective-permute-done | bytes 288 | tf_op jit(solution)/shard_map/ppermute | solution.py:143
  14.0 1.3 %collective-permute-start.10 = (bf16[4,128,128]{2,1,0:T(8,128)(2,1)S(1)}, bf16[4,128,128]{2,1,0:T(8,128)(2,1)S(1)}, u32[]{:S(2)}, u32[]{:S(2)}) collective-permute-start(bf16[4,128,128]{2,1,0:T(8,128)(2,1)S(1)} %get-tuple-element.55), channel_id=1, source_target_pairs={{0,8},{2,10},{4,12},{6,14},{8,0},{10,2},{12,4},{14,6},{16,24},{18,... | collective-permute-start | bytes 393224 | tf_op jit(solution)/shard_map/ppermute | solution.py:124
  15.4 0.8 %collective-permute-done.1.refs_2_.refs_8_ = bf16[4,128,128]{2,1,0:T(8,128)(2,1)S(1)} collective-permute-done((bf16[4,128,128]{2,1,0:T(8,128)(2,1)S(1)}, bf16[4,128,128]{2,1,0:T(8,128)(2,1)S(1)}, u32[]{:S(2)}, u32[]{:S(2)}) %collective-permute-start.1) | collective-permute-done | bytes 131104 | tf_op jit(solution)/shard_map/ppermute | solution.py:124
  16.2 3.8 %collective-permute-start.9 = (bf16[4,128,128]{2,1,0:T(8,128)(2,1)S(1)}, bf16[4,128,128]{2,1,0:T(8,128)(2,1)S(1)}, u32[]{:S(2)}, u32[]{:S(2)}) collective-permute-start(bf16[4,128,128]{2,1,0:T(8,128)(2,1)S(1)} %get-tuple-element.54), channel_id=1, source_target_pairs={{0,16},{2,18},{4,20},{6,22},{8,24},{10,26},{12,28},{14,30},{16,0},... | collective-permute-start | bytes 393224 | tf_op jit(solution)/shard_map/ppermute | solution.py:124
  20.0 0.0 copy-start
  20.0 1.6 %copy-done = bf16[8,8,128,128]{3,2,1,0:T(8,128)(2,1)S(1)} copy-done((bf16[8,8,128,128]{3,2,1,0:T(8,128)(2,1)S(1)}, bf16[8,8,128,128]{3,2,1,0:T(8,128)(2,1)}, u32[]{:S(2)}) %copy-start) | copy-done | bytes 2097176
  21.6 0.0 copy-start.2
  21.6 0.7 %copy-done.2 = s32[8,8]{1,0:T(8,128)S(1)} copy-done((s32[8,8]{1,0:T(8,128)S(1)}, s32[8,8]{1,0:T(8,128)}, u32[]{:S(2)}) %copy-start.2) | copy-done | bytes 280
  22.3 0.2 shard_map.48
  22.5 1.9 %collective-permute-done.6.refs_3_.refs_7_ = bf16[4,128,128]{2,1,0:T(8,128)(2,1)S(1)} collective-permute-done((bf16[4,128,128]{2,1,0:T(8,128)(2,1)S(1)}, bf16[4,128,128]{2,1,0:T(8,128)(2,1)S(1)}, u32[]{:S(2)}, u32[]{:S(2)}) %collective-permute-start.6) | collective-permute-done | bytes 131104 | tf_op jit(solution)/shard_map/ppermute | solution.py:124
  24.4 0.0 collective-permute-done.7.refs_1_.refs_9_
  24.4 1.6 %collective-permute-start.11 = (bf16[4,128,128]{2,1,0:T(8,128)(2,1)S(1)}, bf16[4,128,128]{2,1,0:T(8,128)(2,1)S(1)}, u32[]{:S(2)}, u32[]{:S(2)}) collective-permute-start(bf16[4,128,128]{2,1,0:T(8,128)(2,1)S(1)} %get-tuple-element.56), channel_id=1, source_target_pairs={{0,6},{2,4},{4,2},{6,0},{8,14},{10,12},{12,10},{14,8},{16,22},{18,... | collective-permute-start | bytes 393224 | tf_op jit(solution)/shard_map/ppermute | solution.py:124
  26.0 2.2 %collective-permute-start.12 = (bf16[4,128,128]{2,1,0:T(8,128)(2,1)S(1)}, bf16[4,128,128]{2,1,0:T(8,128)(2,1)S(1)}, u32[]{:S(2)}, u32[]{:S(2)}) collective-permute-start(bf16[4,128,128]{2,1,0:T(8,128)(2,1)S(1)} %get-tuple-element.57), channel_id=1, source_target_pairs={{0,4},{2,6},{4,0},{6,2},{8,12},{10,14},{12,8},{14,10},{16,20},{18,... | collective-permute-start | bytes 393224 | tf_op jit(solution)/shard_map/ppermute | solution.py:124
  28.2 0.7 %collective-permute-done.8.refs_10_ = bf16[4,128,128]{2,1,0:T(8,128)(2,1)S(1)} collective-permute-done((bf16[4,128,128]{2,1,0:T(8,128)(2,1)S(1)}, bf16[4,128,128]{2,1,0:T(8,128)(2,1)S(1)}, u32[]{:S(2)}, u32[]{:S(2)}) %collective-permute-start.8) | collective-permute-done | bytes 131104 | tf_op jit(solution)/shard_map/ppermute | solution.py:124
  28.9 0.5 %collective-permute-start.13 = (bf16[4,128,128]{2,1,0:T(8,128)(2,1)S(1)}, bf16[4,128,128]{2,1,0:T(8,128)(2,1)S(1)}, u32[]{:S(2)}, u32[]{:S(2)}) collective-permute-start(bf16[4,128,128]{2,1,0:T(8,128)(2,1)S(1)} %get-tuple-element.58), channel_id=1, source_target_pairs={{0,2},{2,0},{4,6},{6,4},{8,10},{10,8},{12,14},{14,12},{16,18},{18,... | collective-permute-start | bytes 393224 | tf_op jit(solution)/shard_map/ppermute | solution.py:124
  29.4 0.0 collective-permute-done.10.refs_12_
  29.4 0.0 collective-permute-done.9.refs_11_
  29.4 1.2 %collective-permute-done.11.refs_13_ = bf16[4,128,128]{2,1,0:T(8,128)(2,1)S(1)} collective-permute-done((bf16[4,128,128]{2,1,0:T(8,128)(2,1)S(1)}, bf16[4,128,128]{2,1,0:T(8,128)(2,1)S(1)}, u32[]{:S(2)}, u32[]{:S(2)}) %collective-permute-start.11) | collective-permute-done | bytes 131104 | tf_op jit(solution)/shard_map/ppermute | solution.py:124
  30.7 2.7 %collective-permute-done.12.refs_14_ = bf16[4,128,128]{2,1,0:T(8,128)(2,1)S(1)} collective-permute-done((bf16[4,128,128]{2,1,0:T(8,128)(2,1)S(1)}, bf16[4,128,128]{2,1,0:T(8,128)(2,1)S(1)}, u32[]{:S(2)}, u32[]{:S(2)}) %collective-permute-start.12) | collective-permute-done | bytes 131104 | tf_op jit(solution)/shard_map/ppermute | solution.py:124
  33.4 1.6 %collective-permute-done.13.refs_15_ = bf16[4,128,128]{2,1,0:T(8,128)(2,1)S(1)} collective-permute-done((bf16[4,128,128]{2,1,0:T(8,128)(2,1)S(1)}, bf16[4,128,128]{2,1,0:T(8,128)(2,1)S(1)}, u32[]{:S(2)}, u32[]{:S(2)}) %collective-permute-start.13) | collective-permute-done | bytes 131104 | tf_op jit(solution)/shard_map/ppermute | solution.py:124
  34.9 2.7 %shard_map.50 = bf16[8,128,128]{2,1,0:T(8,128)(2,1)} custom-call(s32[8,8]{1,0:T(8,128)S(1)} %get-tuple-element.42.refs_0_, s32[8,8]{1,0:T(8,128)S(1)} %collective-permute-done.5.refs_1_, bf16[4,128,128]{2,1,0:T(8,128)(2,1)S(1)} %get-tuple-element.35.refs_0_.refs_2_, bf16[4,128,128]{2,1,0:T(8,128)(2,1)S(1)} %collective-permute-done.2.refs_1_.refs_3_, ...), custom_call_target="tpu_custom_call" | custom-call | tf_op jit(solution)/shard_map/pallas_call | solution.py:177
  (2 shorter events, 0.1 us)
Async XLA Ops:
  0.0 5.9 %collective-permute-start = (bf16[8,8,128,128]{3,2,1,0:T(8,128)(2,1)}, bf16[8,8,128,128]{3,2,1,0:T(8,128)(2,1)S(1)}, u32[]{:S(2)}, u32[]{:S(2)}) collective-permute-start(bf16[8,8,128,128]{3,2,1,0:T(8,128)(2,1)} %refs_1_), channel_id=1, source_target_pairs={{0,1},{1,0},{2,3},{3,2},{4,5},{5,4},{6,7},{7,6},{8,9},{9,8},{10,11... | collective-permute-start | bytes 6291464 | tf_op jit(solution)/shard_map/ppermute | solution.py:144
  0.0 1.0 %copy-start.1 = (bf16[16,128,128]{2,1,0:T(8,128)(2,1)S(1)}, bf16[16,128,128]{2,1,0:T(8,128)(2,1)}, u32[]{:S(2)}) copy-start(bf16[16,128,128]{2,1,0:T(8,128)(2,1)} %amplitudes_ref.1) | copy-start | bytes 1572868
  1.0 0.7 %copy-start.3 = (s32[1,32]{1,0:T(1,128)S(1)}, s32[1,32]{1,0:T(1,128)}, u32[]{:S(2)}) copy-start(s32[1,32]{1,0:T(1,128)} %send_ref.1) | copy-start | bytes 388
  2.4 6.6 %collective-permute-start.2 = (bf16[4,128,128]{2,1,0:T(8,128)(2,1)S(1)}, bf16[4,128,128]{2,1,0:T(8,128)(2,1)S(1)}, u32[]{:S(2)}, u32[]{:S(2)}) collective-permute-start(bf16[4,128,128]{2,1,0:T(8,128)(2,1)S(1)} %get-tuple-element.36), channel_id=1, source_target_pairs={{0,2},{2,0},{4,6},{6,4},{8,10},{10,8},{12,14},{14,12},{16,18},{18,... | collective-permute-start | bytes 393224 | tf_op jit(solution)/shard_map/ppermute | solution.py:124
  3.0 7.5 %collective-permute-start.3 = (bf16[4,128,128]{2,1,0:T(8,128)(2,1)S(1)}, bf16[4,128,128]{2,1,0:T(8,128)(2,1)S(1)}, u32[]{:S(2)}, u32[]{:S(2)}) collective-permute-start(bf16[4,128,128]{2,1,0:T(8,128)(2,1)S(1)} %get-tuple-element.37), channel_id=1, source_target_pairs={{0,4},{2,6},{4,0},{6,2},{8,12},{10,14},{12,8},{14,10},{16,20},{18,... | collective-permute-start | bytes 393224 | tf_op jit(solution)/shard_map/ppermute | solution.py:124
  4.5 7.6 %collective-permute-start.4 = (bf16[4,128,128]{2,1,0:T(8,128)(2,1)S(1)}, bf16[4,128,128]{2,1,0:T(8,128)(2,1)S(1)}, u32[]{:S(2)}, u32[]{:S(2)}) collective-permute-start(bf16[4,128,128]{2,1,0:T(8,128)(2,1)S(1)} %get-tuple-element.38), channel_id=1, source_target_pairs={{0,6},{2,4},{4,2},{6,0},{8,14},{10,12},{12,10},{14,8},{16,22},{18,... | collective-permute-start | bytes 393224 | tf_op jit(solution)/shard_map/ppermute | solution.py:124
  5.9 10.3 %collective-permute-start.1 = (bf16[4,128,128]{2,1,0:T(8,128)(2,1)S(1)}, bf16[4,128,128]{2,1,0:T(8,128)(2,1)S(1)}, u32[]{:S(2)}, u32[]{:S(2)}) collective-permute-start(bf16[4,128,128]{2,1,0:T(8,128)(2,1)S(1)} %get-tuple-element.34), channel_id=1, source_target_pairs={{0,16},{2,18},{4,20},{6,22},{8,24},{10,26},{12,28},{14,30},{16,0},... | collective-permute-start | bytes 393224 | tf_op jit(solution)/shard_map/ppermute | solution.py:124
  6.3 18.1 %collective-permute-start.6 = (bf16[4,128,128]{2,1,0:T(8,128)(2,1)S(1)}, bf16[4,128,128]{2,1,0:T(8,128)(2,1)S(1)}, u32[]{:S(2)}, u32[]{:S(2)}) collective-permute-start(bf16[4,128,128]{2,1,0:T(8,128)(2,1)S(1)} %get-tuple-element.50), channel_id=1, source_target_pairs={{0,24},{2,26},{4,28},{6,30},{8,16},{10,18},{12,20},{14,22},{16,8},... | collective-permute-start | bytes 393224 | tf_op jit(solution)/shard_map/ppermute | solution.py:124
  9.0 15.4 %collective-permute-start.7 = (bf16[4,128,128]{2,1,0:T(8,128)(2,1)S(1)}, bf16[4,128,128]{2,1,0:T(8,128)(2,1)S(1)}, u32[]{:S(2)}, u32[]{:S(2)}) collective-permute-start(bf16[4,128,128]{2,1,0:T(8,128)(2,1)S(1)} %get-tuple-element.52), channel_id=1, source_target_pairs={{0,8},{2,10},{4,12},{6,14},{8,0},{10,2},{12,4},{14,6},{16,24},{18,... | collective-permute-start | bytes 393224 | tf_op jit(solution)/shard_map/ppermute | solution.py:124
  12.2 16.8 %collective-permute-start.8 = (bf16[4,128,128]{2,1,0:T(8,128)(2,1)S(1)}, bf16[4,128,128]{2,1,0:T(8,128)(2,1)S(1)}, u32[]{:S(2)}, u32[]{:S(2)}) collective-permute-start(bf16[4,128,128]{2,1,0:T(8,128)(2,1)S(1)} %get-tuple-element.53), channel_id=1, source_target_pairs={{0,24},{2,26},{4,28},{6,30},{8,16},{10,18},{12,20},{14,22},{16,8},... | collective-permute-start | bytes 393224 | tf_op jit(solution)/shard_map/ppermute | solution.py:124
  12.7 1.4 %collective-permute-start.5 = (s32[8,8]{1,0:T(8,128)}, s32[8,8]{1,0:T(8,128)S(1)}, u32[]{:S(2)}, u32[]{:S(2)}) collective-permute-start(s32[8,8]{1,0:T(8,128)} %refs_0_.1), channel_id=1, source_target_pairs={{0,1},{1,0},{2,3},{3,2},{4,5},{5,4},{6,7},{7,6},{8,9},{9,8},{10,11... | collective-permute-start | bytes 776 | tf_op jit(solution)/shard_map/ppermute | solution.py:143
  14.0 15.4 %collective-permute-start.10 = (bf16[4,128,128]{2,1,0:T(8,128)(2,1)S(1)}, bf16[4,128,128]{2,1,0:T(8,128)(2,1)S(1)}, u32[]{:S(2)}, u32[]{:S(2)}) collective-permute-start(bf16[4,128,128]{2,1,0:T(8,128)(2,1)S(1)} %get-tuple-element.55), channel_id=1, source_target_pairs={{0,8},{2,10},{4,12},{6,14},{8,0},{10,2},{12,4},{14,6},{16,24},{18,... | collective-permute-start | bytes 393224 | tf_op jit(solution)/shard_map/ppermute | solution.py:124
  16.2 13.2 %collective-permute-start.9 = (bf16[4,128,128]{2,1,0:T(8,128)(2,1)S(1)}, bf16[4,128,128]{2,1,0:T(8,128)(2,1)S(1)}, u32[]{:S(2)}, u32[]{:S(2)}) collective-permute-start(bf16[4,128,128]{2,1,0:T(8,128)(2,1)S(1)} %get-tuple-element.54), channel_id=1, source_target_pairs={{0,16},{2,18},{4,20},{6,22},{8,24},{10,26},{12,28},{14,30},{16,0},... | collective-permute-start | bytes 393224 | tf_op jit(solution)/shard_map/ppermute | solution.py:124
  20.0 1.6 %copy-start = (bf16[8,8,128,128]{3,2,1,0:T(8,128)(2,1)S(1)}, bf16[8,8,128,128]{3,2,1,0:T(8,128)(2,1)}, u32[]{:S(2)}) copy-start(bf16[8,8,128,128]{3,2,1,0:T(8,128)(2,1)} %refs_1_) | copy-start | bytes 6291460
  21.6 0.7 %copy-start.2 = (s32[8,8]{1,0:T(8,128)S(1)}, s32[8,8]{1,0:T(8,128)}, u32[]{:S(2)}) copy-start(s32[8,8]{1,0:T(8,128)} %refs_0_.1) | copy-start | bytes 772
  24.4 6.3 %collective-permute-start.11 = (bf16[4,128,128]{2,1,0:T(8,128)(2,1)S(1)}, bf16[4,128,128]{2,1,0:T(8,128)(2,1)S(1)}, u32[]{:S(2)}, u32[]{:S(2)}) collective-permute-start(bf16[4,128,128]{2,1,0:T(8,128)(2,1)S(1)} %get-tuple-element.56), channel_id=1, source_target_pairs={{0,6},{2,4},{4,2},{6,0},{8,14},{10,12},{12,10},{14,8},{16,22},{18,... | collective-permute-start | bytes 393224 | tf_op jit(solution)/shard_map/ppermute | solution.py:124
  26.0 7.4 %collective-permute-start.12 = (bf16[4,128,128]{2,1,0:T(8,128)(2,1)S(1)}, bf16[4,128,128]{2,1,0:T(8,128)(2,1)S(1)}, u32[]{:S(2)}, u32[]{:S(2)}) collective-permute-start(bf16[4,128,128]{2,1,0:T(8,128)(2,1)S(1)} %get-tuple-element.57), channel_id=1, source_target_pairs={{0,4},{2,6},{4,0},{6,2},{8,12},{10,14},{12,8},{14,10},{16,20},{18,... | collective-permute-start | bytes 393224 | tf_op jit(solution)/shard_map/ppermute | solution.py:124
  28.9 6.0 %collective-permute-start.13 = (bf16[4,128,128]{2,1,0:T(8,128)(2,1)S(1)}, bf16[4,128,128]{2,1,0:T(8,128)(2,1)S(1)}, u32[]{:S(2)}, u32[]{:S(2)}) collective-permute-start(bf16[4,128,128]{2,1,0:T(8,128)(2,1)S(1)} %get-tuple-element.58), channel_id=1, source_target_pairs={{0,2},{2,0},{4,6},{6,4},{8,10},{10,8},{12,14},{14,12},{16,18},{18,... | collective-permute-start | bytes 393224 | tf_op jit(solution)/shard_map/ppermute | solution.py:124

commit v14 on v11

--- a/solution.py
+++ b/solution.py
@@ -18,17 +18,14 @@
 
 def pick_outgoing(plan, cap, send_ref, amplitudes_ref, *refs):
     out_refs = refs[: len(plan)]
-    sends, held, sems = refs[len(plan) :]
-    fetch_sends = pltpu.make_async_copy(send_ref, sends, sems.at[0])
-    fetch_tiles = pltpu.make_async_copy(amplitudes_ref, held, sems.at[1])
-    fetch_tiles.start()
+    sends, sem = refs[len(plan) :]
+    fetch_sends = pltpu.make_async_copy(send_ref, sends, sem)
     fetch_sends.start()
     fetch_sends.wait()
-    fetch_tiles.wait()
     me = lax.axis_index("wide")
     for wanted, out_ref in zip(plan, out_refs):
         for place, (partner, slot) in enumerate(wanted):
-            out_ref[place] = held[sends[0, (me ^ partner) * cap + slot]]
+            out_ref[place] = amplitudes_ref[sends[0, (me ^ partner) * cap + slot]]
 
 
 def regroup(ins, width, staged, *refs):
@@ -109,12 +106,11 @@
     outgoing = pl.pallas_call(
         functools.partial(pick_outgoing, plan, cap),
         out_shape=[jax.ShapeDtypeStruct((len(p), pairs, columns), amplitudes.dtype) for p in plan],
-        in_specs=[ANYWHERE, ANYWHERE],
+        in_specs=[ANYWHERE, VMEM],
         out_specs=[VMEM] * len(plan),
         scratch_shapes=[
             pltpu.SMEM(send_list.shape, send_list.dtype),
-            pltpu.VMEM(amplitudes.shape, amplitudes.dtype),
-            pltpu.SemaphoreType.DMA((2,)),
+            pltpu.SemaphoreType.DMA,
         ],
         compiler_params=GRANT,
     )(send_list, amplitudes)

time: 37.2 us -> 37.1 us (level)
  the two profiles are of different devices: /device:TPU:18 before, /device:TPU:22 now
where the time goes in v14:
time: 37.1 us; the launch traced here: 36.9 us
  starting transfers between devices  14.7 us (40%)
  waiting for transfers between devices  14.6 us (39%)
  local copies, waits for them, and re-layouts  3.97 us (11%)
  Pallas kernels  3.57 us (10%)
    ppermute x12, starting transfers between devices, exchange(): return lax.ppermute(array, 'wide', [(d, d ^ partner) for d in range(wide)])  14.7 us
    ppermute x12, waiting for transfers between devices, exchange(): return lax.ppermute(array, 'wide', [(d, d ^ partner) for d in range(wide)])  13.5 us
    unnamed x8, local copies, waits for them, and re-layouts  3.97 us
    pallas_call x1, Pallas kernels, on_device(): pl.pallas_call(functools.partial(contract, origins, cap, count), out_shap...  2.72 us
    ppermute x1, waiting for transfers between devices, on_device(): places = [tile_positions, lax.ppermute(tile_positions, 'narrow', swap)]  1.16 us
  transfers between devices with their start and end apart: 14, of which 7 were waited for; matrix products, arithmetic and copies ran while one was open for 0% of the time, Pallas kernels for 2%

profile of v14, /device:TPU:22, one launch (start us, length us, event | category | flops | bytes accessed | tf_op | source)
XLA Modules:
  0.0 36.9 jit_solution(13329180817791354699)
XLA Ops:
  0.0 0.0 collective-permute-start.5
  0.0 0.0 copy-start.1
  0.0 1.0 %copy-done.1 = bf16[16,128,128]{2,1,0:T(8,128)(2,1)S(1)} copy-done((bf16[16,128,128]{2,1,0:T(8,128)(2,1)S(1)}, bf16[16,128,128]{2,1,0:T(8,128)(2,1)}, u32[]{:S(2)}) %copy-start.1) | copy-done | bytes 524312
  1.0 0.0 copy-start.3
  1.0 0.7 %copy-done.3 = s32[1,32]{1,0:T(1,128)S(1)} copy-done((s32[1,32]{1,0:T(1,128)S(1)}, s32[1,32]{1,0:T(1,128)}, u32[]{:S(2)}) %copy-start.3) | copy-done | bytes 152
  1.7 0.6 %shard_map.46 = (bf16[4,128,128]{2,1,0:T(8,128)(2,1)S(1)}, bf16[4,128,128]{2,1,0:T(8,128)(2,1)S(1)}, bf16[4,128,128]{2,1,0:T(8,128)(2,1)S(1)}, bf16[4,128,128]{2...) custom-call(s32[1,32]{1,0:T(1,128)S(1)} %copy-done.3, ...), custom_call_target="tpu_custom_call" | custom-call | tf_op jit(solution)/shard_map/pallas_call | solution.py:106
  2.3 0.6 %collective-permute-start = (bf16[4,128,128]{2,1,0:T(8,128)(2,1)S(1)}, bf16[4,128,128]{2,1,0:T(8,128)(2,1)S(1)}, u32[]{:S(2)}, u32[]{:S(2)}) collective-permute-start(bf16[4,128,128]{2,1,0:T(8,128)(2,1)S(1)} %get-tuple-element.30), channel_id=1, source_target_pairs={{0,2},{2,0},{4,6},{6,4},{8,10},{10,8},{12,14},{14,12},{16,18},{18,... | collective-permute-start | bytes 393224 | tf_op jit(solution)/shard_map/ppermute | solution.py:101
  2.9 0.5 %collective-permute-start.1 = (bf16[4,128,128]{2,1,0:T(8,128)(2,1)S(1)}, bf16[4,128,128]{2,1,0:T(8,128)(2,1)S(1)}, u32[]{:S(2)}, u32[]{:S(2)}) collective-permute-start(bf16[4,128,128]{2,1,0:T(8,128)(2,1)S(1)} %get-tuple-element.31), channel_id=1, source_target_pairs={{0,4},{2,6},{4,0},{6,2},{8,12},{10,14},{12,8},{14,10},{16,20},{18,... | collective-permute-start | bytes 393224 | tf_op jit(solution)/shard_map/ppermute | solution.py:101
  3.4 2.4 %collective-permute-start.2 = (bf16[4,128,128]{2,1,0:T(8,128)(2,1)S(1)}, bf16[4,128,128]{2,1,0:T(8,128)(2,1)S(1)}, u32[]{:S(2)}, u32[]{:S(2)}) collective-permute-start(bf16[4,128,128]{2,1,0:T(8,128)(2,1)S(1)} %get-tuple-element.32), channel_id=1, source_target_pairs={{0,6},{2,4},{4,2},{6,0},{8,14},{10,12},{12,10},{14,8},{16,22},{18,... | collective-permute-start | bytes 393224 | tf_op jit(solution)/shard_map/ppermute | solution.py:101
  5.9 0.0 collective-permute-done.5.refs_17_
  5.9 0.3 collective-permute-start.6
  6.2 2.7 %collective-permute-start.4 = (bf16[4,128,128]{2,1,0:T(8,128)(2,1)S(1)}, bf16[4,128,128]{2,1,0:T(8,128)(2,1)S(1)}, u32[]{:S(2)}, u32[]{:S(2)}) collective-permute-start(bf16[4,128,128]{2,1,0:T(8,128)(2,1)S(1)} %get-tuple-element.39), channel_id=1, source_target_pairs={{0,24},{2,26},{4,28},{6,30},{8,16},{10,18},{12,20},{14,22},{16,8},... | collective-permute-start | bytes 393224 | tf_op jit(solution)/shard_map/ppermute | solution.py:101
  8.9 0.0 collective-permute-done.refs_1_.refs_3_
  8.9 1.3 %collective-permute-start.7 = (bf16[4,128,128]{2,1,0:T(8,128)(2,1)S(1)}, bf16[4,128,128]{2,1,0:T(8,128)(2,1)S(1)}, u32[]{:S(2)}, u32[]{:S(2)}) collective-permute-start(bf16[4,128,128]{2,1,0:T(8,128)(2,1)S(1)} %get-tuple-element.44), channel_id=1, source_target_pairs={{0,8},{2,10},{4,12},{6,14},{8,0},{10,2},{12,4},{14,6},{16,24},{18,... | collective-permute-start | bytes 393224 | tf_op jit(solution)/shard_map/ppermute | solution.py:101
  10.3 1.1 %collective-permute-done.1.refs_2_.refs_4_ = bf16[4,128,128]{2,1,0:T(8,128)(2,1)S(1)} collective-permute-done((bf16[4,128,128]{2,1,0:T(8,128)(2,1)S(1)}, bf16[4,128,128]{2,1,0:T(8,128)(2,1)S(1)}, u32[]{:S(2)}, u32[]{:S(2)}) %collective-permute-start.1) | collective-permute-done | bytes 131104 | tf_op jit(solution)/shard_map/ppermute | solution.py:101
  11.4 0.0 collective-permute-done.2.refs_3_.refs_5_
  11.4 0.0 copy-start
  11.4 1.6 %copy-done = bf16[8,8,128,128]{3,2,1,0:T(8,128)(2,1)S(1)} copy-done((bf16[8,8,128,128]{3,2,1,0:T(8,128)(2,1)S(1)}, bf16[8,8,128,128]{3,2,1,0:T(8,128)(2,1)}, u32[]{:S(2)}) %copy-start) | copy-done | bytes 2097176
  13.0 0.0 copy-start.2
  13.0 0.7 %copy-done.2 = s32[8,8]{1,0:T(8,128)S(1)} copy-done((s32[8,8]{1,0:T(8,128)S(1)}, s32[8,8]{1,0:T(8,128)}, u32[]{:S(2)}) %copy-start.2) | copy-done | bytes 280
  13.7 0.2 shard_map.47
  13.9 0.5 %collective-permute-start.8 = (bf16[4,128,128]{2,1,0:T(8,128)(2,1)S(1)}, bf16[4,128,128]{2,1,0:T(8,128)(2,1)S(1)}, u32[]{:S(2)}, u32[]{:S(2)}) collective-permute-start(bf16[4,128,128]{2,1,0:T(8,128)(2,1)S(1)} %get-tuple-element.45), channel_id=1, source_target_pairs={{0,24},{2,26},{4,28},{6,30},{8,16},{10,18},{12,20},{14,22},{16,8},... | collective-permute-start | bytes 393224 | tf_op jit(solution)/shard_map/ppermute | solution.py:101
  14.4 0.0 collective-permute-start.3
  14.4 1.2 %collective-permute-done.3.refs_1_ = s32[8,8]{1,0:T(8,128)S(1)} collective-permute-done((s32[8,8]{1,0:T(8,128)S(1)}, s32[8,8]{1,0:T(8,128)S(1)}, u32[]{:S(2)}, u32[]{:S(2)}) %collective-permute-start.3) | collective-permute-done | bytes 288 | tf_op jit(solution)/shard_map/ppermute | solution.py:119
  15.5 1.3 %collective-permute-start.10 = (bf16[4,128,128]{2,1,0:T(8,128)(2,1)S(1)}, bf16[4,128,128]{2,1,0:T(8,128)(2,1)S(1)}, u32[]{:S(2)}, u32[]{:S(2)}) collective-permute-start(bf16[4,128,128]{2,1,0:T(8,128)(2,1)S(1)} %get-tuple-element.47), channel_id=1, source_target_pairs={{0,8},{2,10},{4,12},{6,14},{8,0},{10,2},{12,4},{14,6},{16,24},{18,... | collective-permute-start | bytes 393224 | tf_op jit(solution)/shard_map/ppermute | solution.py:101
  16.9 0.0 collective-permute-done.6.refs_2_.refs_8_
  16.9 2.7 %collective-permute-start.9 = (bf16[4,128,128]{2,1,0:T(8,128)(2,1)S(1)}, bf16[4,128,128]{2,1,0:T(8,128)(2,1)S(1)}, u32[]{:S(2)}, u32[]{:S(2)}) collective-permute-start(bf16[4,128,128]{2,1,0:T(8,128)(2,1)S(1)} %get-tuple-element.46), channel_id=1, source_target_pairs={{0,16},{2,18},{4,20},{6,22},{8,24},{10,26},{12,28},{14,30},{16,0},... | collective-permute-start | bytes 393224 | tf_op jit(solution)/shard_map/ppermute | solution.py:101
  19.6 4.1 %collective-permute-done.4.refs_3_.refs_7_ = bf16[4,128,128]{2,1,0:T(8,128)(2,1)S(1)} collective-permute-done((bf16[4,128,128]{2,1,0:T(8,128)(2,1)S(1)}, bf16[4,128,128]{2,1,0:T(8,128)(2,1)S(1)}, u32[]{:S(2)}, u32[]{:S(2)}) %collective-permute-start.4) | collective-permute-done | bytes 131104 | tf_op jit(solution)/shard_map/ppermute | solution.py:101
  23.7 0.0 collective-permute-done.7.refs_1_.refs_9_
  23.7 0.1 collective-permute-start.11
  23.8 1.5 %collective-permute-start.12 = (bf16[4,128,128]{2,1,0:T(8,128)(2,1)S(1)}, bf16[4,128,128]{2,1,0:T(8,128)(2,1)S(1)}, u32[]{:S(2)}, u32[]{:S(2)}) collective-permute-start(bf16[4,128,128]{2,1,0:T(8,128)(2,1)S(1)} %get-tuple-element.49), channel_id=1, source_target_pairs={{0,4},{2,6},{4,0},{6,2},{8,12},{10,14},{12,8},{14,10},{16,20},{18,... | collective-permute-start | bytes 393224 | tf_op jit(solution)/shard_map/ppermute | solution.py:101
  25.3 3.5 %collective-permute-done.8.refs_10_ = bf16[4,128,128]{2,1,0:T(8,128)(2,1)S(1)} collective-permute-done((bf16[4,128,128]{2,1,0:T(8,128)(2,1)S(1)}, bf16[4,128,128]{2,1,0:T(8,128)(2,1)S(1)}, u32[]{:S(2)}, u32[]{:S(2)}) %collective-permute-start.8) | collective-permute-done | bytes 131104 | tf_op jit(solution)/shard_map/ppermute | solution.py:101
  28.9 0.5 %collective-permute-start.13 = (bf16[4,128,128]{2,1,0:T(8,128)(2,1)S(1)}, bf16[4,128,128]{2,1,0:T(8,128)(2,1)S(1)}, u32[]{:S(2)}, u32[]{:S(2)}) collective-permute-start(bf16[4,128,128]{2,1,0:T(8,128)(2,1)S(1)} %get-tuple-element.50), channel_id=1, source_target_pairs={{0,2},{2,0},{4,6},{6,4},{8,10},{10,8},{12,14},{14,12},{16,18},{18,... | collective-permute-start | bytes 393224 | tf_op jit(solution)/shard_map/ppermute | solution.py:101
  29.4 0.0 collective-permute-done.10.refs_12_
  29.4 0.0 collective-permute-done.9.refs_11_
  29.4 0.5 %collective-permute-done.11.refs_13_ = bf16[4,128,128]{2,1,0:T(8,128)(2,1)S(1)} collective-permute-done((bf16[4,128,128]{2,1,0:T(8,128)(2,1)S(1)}, bf16[4,128,128]{2,1,0:T(8,128)(2,1)S(1)}, u32[]{:S(2)}, u32[]{:S(2)}) %collective-permute-start.11) | collective-permute-done | bytes 131104 | tf_op jit(solution)/shard_map/ppermute | solution.py:101
  29.9 1.9 %collective-permute-done.12.refs_14_ = bf16[4,128,128]{2,1,0:T(8,128)(2,1)S(1)} collective-permute-done((bf16[4,128,128]{2,1,0:T(8,128)(2,1)S(1)}, bf16[4,128,128]{2,1,0:T(8,128)(2,1)S(1)}, u32[]{:S(2)}, u32[]{:S(2)}) %collective-permute-start.12) | collective-permute-done | bytes 131104 | tf_op jit(solution)/shard_map/ppermute | solution.py:101
  31.8 2.4 %collective-permute-done.13.refs_15_ = bf16[4,128,128]{2,1,0:T(8,128)(2,1)S(1)} collective-permute-done((bf16[4,128,128]{2,1,0:T(8,128)(2,1)S(1)}, bf16[4,128,128]{2,1,0:T(8,128)(2,1)S(1)}, u32[]{:S(2)}, u32[]{:S(2)}) %collective-permute-start.13) | collective-permute-done | bytes 131104 | tf_op jit(solution)/shard_map/ppermute | solution.py:101
  34.2 2.7 %shard_map.49 = bf16[8,128,128]{2,1,0:T(8,128)(2,1)} custom-call(s32[8,8]{1,0:T(8,128)S(1)} %get-tuple-element.33.refs_0_, s32[8,8]{1,0:T(8,128)S(1)} %collective-permute-done.3.refs_1_, bf16[4,128,128]{2,1,0:T(8,128)(2,1)S(1)} %get-tuple-element.29.refs_0_.refs_2_, bf16[4,128,128]{2,1,0:T(8,128)(2,1)S(1)} %collective-permute-done.refs_1_.refs_3_, ...), custom_call_target="tpu_custom_call" | custom-call | tf_op jit(solution)/shard_map/pallas_call | solution.py:151
  (1 shorter events, 0.0 us)
Async XLA Ops:
  0.0 5.9 %collective-permute-start.5 = (bf16[8,8,128,128]{3,2,1,0:T(8,128)(2,1)}, bf16[8,8,128,128]{3,2,1,0:T(8,128)(2,1)S(1)}, u32[]{:S(2)}, u32[]{:S(2)}) collective-permute-start(bf16[8,8,128,128]{3,2,1,0:T(8,128)(2,1)} %refs_5_.1), channel_id=1, source_target_pairs={{0,1},{1,0},{2,3},{3,2},{4,5},{5,4},{6,7},{7,6},{8,9},{9,8},{10,11... | collective-permute-start | bytes 6291464 | tf_op jit(solution)/shard_map/ppermute | solution.py:120
  0.0 1.0 %copy-start.1 = (bf16[16,128,128]{2,1,0:T(8,128)(2,1)S(1)}, bf16[16,128,128]{2,1,0:T(8,128)(2,1)}, u32[]{:S(2)}) copy-start(bf16[16,128,128]{2,1,0:T(8,128)(2,1)} %amplitudes_ref.1) | copy-start | bytes 1572868
  1.0 0.7 %copy-start.3 = (s32[1,32]{1,0:T(1,128)S(1)}, s32[1,32]{1,0:T(1,128)}, u32[]{:S(2)}) copy-start(s32[1,32]{1,0:T(1,128)} %send_ref.1) | copy-start | bytes 388
  2.3 6.6 %collective-permute-start = (bf16[4,128,128]{2,1,0:T(8,128)(2,1)S(1)}, bf16[4,128,128]{2,1,0:T(8,128)(2,1)S(1)}, u32[]{:S(2)}, u32[]{:S(2)}) collective-permute-start(bf16[4,128,128]{2,1,0:T(8,128)(2,1)S(1)} %get-tuple-element.30), channel_id=1, source_target_pairs={{0,2},{2,0},{4,6},{6,4},{8,10},{10,8},{12,14},{14,12},{16,18},{18,... | collective-permute-start | bytes 393224 | tf_op jit(solution)/shard_map/ppermute | solution.py:101
  2.9 8.4 %collective-permute-start.1 = (bf16[4,128,128]{2,1,0:T(8,128)(2,1)S(1)}, bf16[4,128,128]{2,1,0:T(8,128)(2,1)S(1)}, u32[]{:S(2)}, u32[]{:S(2)}) collective-permute-start(bf16[4,128,128]{2,1,0:T(8,128)(2,1)S(1)} %get-tuple-element.31), channel_id=1, source_target_pairs={{0,4},{2,6},{4,0},{6,2},{8,12},{10,14},{12,8},{14,10},{16,20},{18,... | collective-permute-start | bytes 393224 | tf_op jit(solution)/shard_map/ppermute | solution.py:101
  3.4 7.9 %collective-permute-start.2 = (bf16[4,128,128]{2,1,0:T(8,128)(2,1)S(1)}, bf16[4,128,128]{2,1,0:T(8,128)(2,1)S(1)}, u32[]{:S(2)}, u32[]{:S(2)}) collective-permute-start(bf16[4,128,128]{2,1,0:T(8,128)(2,1)S(1)} %get-tuple-element.32), channel_id=1, source_target_pairs={{0,6},{2,4},{4,2},{6,0},{8,14},{10,12},{12,10},{14,8},{16,22},{18,... | collective-permute-start | bytes 393224 | tf_op jit(solution)/shard_map/ppermute | solution.py:101
  5.9 11.0 %collective-permute-start.6 = (bf16[4,128,128]{2,1,0:T(8,128)(2,1)S(1)}, bf16[4,128,128]{2,1,0:T(8,128)(2,1)S(1)}, u32[]{:S(2)}, u32[]{:S(2)}) collective-permute-start(bf16[4,128,128]{2,1,0:T(8,128)(2,1)S(1)} %get-tuple-element.41), channel_id=1, source_target_pairs={{0,16},{2,18},{4,20},{6,22},{8,24},{10,26},{12,28},{14,30},{16,0},... | collective-permute-start | bytes 393224 | tf_op jit(solution)/shard_map/ppermute | solution.py:101
  6.2 17.4 %collective-permute-start.4 = (bf16[4,128,128]{2,1,0:T(8,128)(2,1)S(1)}, bf16[4,128,128]{2,1,0:T(8,128)(2,1)S(1)}, u32[]{:S(2)}, u32[]{:S(2)}) collective-permute-start(bf16[4,128,128]{2,1,0:T(8,128)(2,1)S(1)} %get-tuple-element.39), channel_id=1, source_target_pairs={{0,24},{2,26},{4,28},{6,30},{8,16},{10,18},{12,20},{14,22},{16,8},... | collective-permute-start | bytes 393224 | tf_op jit(solution)/shard_map/ppermute | solution.py:101
  8.9 14.7 %collective-permute-start.7 = (bf16[4,128,128]{2,1,0:T(8,128)(2,1)S(1)}, bf16[4,128,128]{2,1,0:T(8,128)(2,1)S(1)}, u32[]{:S(2)}, u32[]{:S(2)}) collective-permute-start(bf16[4,128,128]{2,1,0:T(8,128)(2,1)S(1)} %get-tuple-element.44), channel_id=1, source_target_pairs={{0,8},{2,10},{4,12},{6,14},{8,0},{10,2},{12,4},{14,6},{16,24},{18,... | collective-permute-start | bytes 393224 | tf_op jit(solution)/shard_map/ppermute | solution.py:101
  11.4 1.6 %copy-start = (bf16[8,8,128,128]{3,2,1,0:T(8,128)(2,1)S(1)}, bf16[8,8,128,128]{3,2,1,0:T(8,128)(2,1)}, u32[]{:S(2)}) copy-start(bf16[8,8,128,128]{3,2,1,0:T(8,128)(2,1)} %refs_5_.1) | copy-start | bytes 6291460
  13.0 0.7 %copy-start.2 = (s32[8,8]{1,0:T(8,128)S(1)}, s32[8,8]{1,0:T(8,128)}, u32[]{:S(2)}) copy-start(s32[8,8]{1,0:T(8,128)} %refs_4_.1) | copy-start | bytes 772
  13.9 15.0 %collective-permute-start.8 = (bf16[4,128,128]{2,1,0:T(8,128)(2,1)S(1)}, bf16[4,128,128]{2,1,0:T(8,128)(2,1)S(1)}, u32[]{:S(2)}, u32[]{:S(2)}) collective-permute-start(bf16[4,128,128]{2,1,0:T(8,128)(2,1)S(1)} %get-tuple-element.45), channel_id=1, source_target_pairs={{0,24},{2,26},{4,28},{6,30},{8,16},{10,18},{12,20},{14,22},{16,8},... | collective-permute-start | bytes 393224 | tf_op jit(solution)/shard_map/ppermute | solution.py:101
  14.4 1.2 %collective-permute-start.3 = (s32[8,8]{1,0:T(8,128)S(1)}, s32[8,8]{1,0:T(8,128)S(1)}, u32[]{:S(2)}, u32[]{:S(2)}) collective-permute-start(s32[8,8]{1,0:T(8,128)S(1)} %copy-done.2), channel_id=1, source_target_pairs={{0,1},{1,0},{2,3},{3,2},{4,5},{5,4},{6,7},{7,6},{8,9},{9,8},{10,11... | collective-permute-start | bytes 776 | tf_op jit(solution)/shard_map/ppermute | solution.py:119
  15.5 13.9 %collective-permute-start.10 = (bf16[4,128,128]{2,1,0:T(8,128)(2,1)S(1)}, bf16[4,128,128]{2,1,0:T(8,128)(2,1)S(1)}, u32[]{:S(2)}, u32[]{:S(2)}) collective-permute-start(bf16[4,128,128]{2,1,0:T(8,128)(2,1)S(1)} %get-tuple-element.47), channel_id=1, source_target_pairs={{0,8},{2,10},{4,12},{6,14},{8,0},{10,2},{12,4},{14,6},{16,24},{18,... | collective-permute-start | bytes 393224 | tf_op jit(solution)/shard_map/ppermute | solution.py:101
  16.9 12.5 %collective-permute-start.9 = (bf16[4,128,128]{2,1,0:T(8,128)(2,1)S(1)}, bf16[4,128,128]{2,1,0:T(8,128)(2,1)S(1)}, u32[]{:S(2)}, u32[]{:S(2)}) collective-permute-start(bf16[4,128,128]{2,1,0:T(8,128)(2,1)S(1)} %get-tuple-element.46), channel_id=1, source_target_pairs={{0,16},{2,18},{4,20},{6,22},{8,24},{10,26},{12,28},{14,30},{16,0},... | collective-permute-start | bytes 393224 | tf_op jit(solution)/shard_map/ppermute | solution.py:101
  23.7 6.2 %collective-permute-start.11 = (bf16[4,128,128]{2,1,0:T(8,128)(2,1)S(1)}, bf16[4,128,128]{2,1,0:T(8,128)(2,1)S(1)}, u32[]{:S(2)}, u32[]{:S(2)}) collective-permute-start(bf16[4,128,128]{2,1,0:T(8,128)(2,1)S(1)} %get-tuple-element.48), channel_id=1, source_target_pairs={{0,6},{2,4},{4,2},{6,0},{8,14},{10,12},{12,10},{14,8},{16,22},{18,... | collective-permute-start | bytes 393224 | tf_op jit(solution)/shard_map/ppermute | solution.py:101
  23.8 8.0 %collective-permute-start.12 = (bf16[4,128,128]{2,1,0:T(8,128)(2,1)S(1)}, bf16[4,128,128]{2,1,0:T(8,128)(2,1)S(1)}, u32[]{:S(2)}, u32[]{:S(2)}) collective-permute-start(bf16[4,128,128]{2,1,0:T(8,128)(2,1)S(1)} %get-tuple-element.49), channel_id=1, source_target_pairs={{0,4},{2,6},{4,0},{6,2},{8,12},{10,14},{12,8},{14,10},{16,20},{18,... | collective-permute-start | bytes 393224 | tf_op jit(solution)/shard_map/ppermute | solution.py:101
  28.9 5.3 %collective-permute-start.13 = (bf16[4,128,128]{2,1,0:T(8,128)(2,1)S(1)}, bf16[4,128,128]{2,1,0:T(8,128)(2,1)S(1)}, u32[]{:S(2)}, u32[]{:S(2)}) collective-permute-start(bf16[4,128,128]{2,1,0:T(8,128)(2,1)S(1)} %get-tuple-element.50), channel_id=1, source_target_pairs={{0,2},{2,0},{4,6},{6,4},{8,10},{10,8},{12,14},{14,12},{16,18},{18,... | collective-permute-start | bytes 393224 | tf_op jit(solution)/shard_map/ppermute | solution.py:101
